TPU v7x, 32 devices: a whole 2x2x4 slice. The times are simulated.
32 devices in a mesh: gx: 8 (over y, x, core), gy: 4 (over z).
Axes of the slice: x: 2, y: 2, z: 4, core: 2. Of those that a mesh axis runs over, the one named last changes fastest.
Arguments:
- hidden_in: bfloat16 [256, 16384], P(('gx', 'gy')), may hold values from -6 to 6
- norm_gain: float32 [16384], replicated, may hold values from 0.1 to 1.9
- w_qkv: bfloat16 [16384, 18432], P('gy', 'gx'), may hold values from -0.046875 to 0.046875
- k_cache: bfloat16 [256, 512, 1024], P(('gx', 'gy')), may hold values from -60 to 60
- v_cache: bfloat16 [256, 512, 1024], P(('gx', 'gy')), may hold values from -6 to 6
- lengths: int32 [256], P(('gx', 'gy')), may hold values from 1 to 512, as said below
- w_out: bfloat16 [16384, 16384], P('gy', 'gx'), may hold values from -0.375 to 0.375
Outputs:
- attn_out: bfloat16 [256, 16384], P(('gx', 'gy'))
Inputs may be any that keep to these rules, and one draw needn't show every extreme that they name: Row b attends to its first lengths[b] cached positions; some row has 512.
All inputs are finite; a program needn't handle non-finite values.
Results may differ from a plain program's by a relative error of at most 0.015.
The roundings to bfloat16 on the way count: a program that leaves them out, or rounds other values in their place, can miss the bound.
Values may be sent and summed in bfloat16 or wider, within the bound.
No kernel may reach another device: no remote copies, remote signals or barrier semaphores. Data moves between devices by JAX's collectives and lax.ppermute only.
A program may use at most 128 MiB of HBM per device.

v0:
```python
import math

import jax
import jax.numpy as jnp
from jax import lax
from jax.sharding import PartitionSpec as P

HQ = 128
KVH = 8
HD = 128


eps = 1e-05
theta = 500000.0


def rotate(values, position, head_size):
    half = head_size // 2
    index = jnp.arange(half, dtype=jnp.float32)
    freqs = theta ** (-2.0 * index / head_size)
    angle = position[:, None, None] * freqs[None, None, :]
    cosine = jnp.cos(angle)
    sine = jnp.sin(angle)
    first = values[..., :half]
    second = values[..., half:]
    return jnp.concatenate(
        [first * cosine - second * sine, second * cosine + first * sine], axis=-1
    )


def normalize(scores, fresh):
    top = jnp.maximum(jnp.max(scores, axis=-1), fresh)
    probs = jnp.exp(scores - top[..., None])
    pnew = jnp.exp(fresh - top)
    total = jnp.sum(probs, axis=-1) + pnew
    return ((probs / total[..., None]).astype(jnp.bfloat16), (pnew / total).astype(jnp.bfloat16))


def attend_local(owned, k_cache, v_cache, lengths):
    rows = owned.shape[0]
    span = k_cache.shape[1]
    share = HQ // KVH
    query = owned[:, : HQ * HD].reshape(rows, HQ, HD).astype(jnp.float32)
    key_new = owned[:, HQ * HD : (HQ + KVH) * HD].reshape(rows, KVH, HD).astype(jnp.float32)
    value_new = owned[:, (HQ + KVH) * HD :].reshape(rows, KVH, HD).astype(jnp.float32)
    position = lengths.astype(jnp.float32)
    grouped = rotate(query, position, HD).astype(jnp.bfloat16).reshape(rows, KVH, share, HD)
    key_new = rotate(key_new, position, HD).astype(jnp.bfloat16)
    keys = k_cache.reshape(rows, span, KVH, HD)
    values = v_cache.reshape(rows, span, KVH, HD)
    scale = 1.0 / math.sqrt(HD)
    fresh = (
        jnp.einsum("rgsd,rgd->rgs", grouped, key_new, preferred_element_type=jnp.float32) * scale
    )
    scores = (
        jnp.einsum("rgsd,rtgd->rgst", grouped, keys, preferred_element_type=jnp.float32) * scale
    )
    valid = jnp.arange(span, dtype=jnp.int32)[None, :] < lengths[:, None]
    scores = jnp.where(valid[:, None, None, :], scores, -jnp.inf)
    weights, wnew = normalize(scores, fresh)
    mixed = jnp.einsum("rgst,rtgd->rgsd", weights, values, preferred_element_type=jnp.float32)
    mixed = mixed + wnew.astype(jnp.float32)[..., None] * value_new[:, :, None, :]
    return mixed.reshape(rows, HQ * HD).astype(jnp.bfloat16)


def on_device(hidden_in, norm_gain, w_qkv, k_cache, v_cache, lengths, w_out):
    widened = hidden_in.astype(jnp.float32)
    normed = (
        widened * lax.rsqrt(jnp.mean(widened * widened, axis=-1, keepdims=True) + eps) * norm_gain
    ).astype(jnp.bfloat16)
    grouped_in = lax.all_gather(normed, "gx", axis=0, tiled=True)
    spread_in = lax.all_to_all(grouped_in, "gy", split_axis=1, concat_axis=0, tiled=True)
    picked = spread_in
    partial_qkv = lax.psum_scatter(
        jnp.dot(picked, w_qkv, preferred_element_type=jnp.float32),
        "gy",
        scatter_dimension=0,
        tiled=True,
    )
    owned = lax.all_to_all(
        partial_qkv.astype(jnp.bfloat16), "gx", split_axis=0, concat_axis=1, tiled=True
    )
    attended = attend_local(owned, k_cache, v_cache, lengths)
    grouped_out = lax.all_gather(attended, "gx", axis=0, tiled=True)
    spread_out = lax.all_to_all(grouped_out, "gy", split_axis=1, concat_axis=0, tiled=True)
    picked = spread_out
    partial_out = lax.psum_scatter(
        jnp.dot(picked, w_out, preferred_element_type=jnp.float32).astype(jnp.bfloat16),
        "gy",
        scatter_dimension=0,
        tiled=True,
    )
    return lax.all_to_all(partial_out, "gx", split_axis=0, concat_axis=1, tiled=True)


def solution(mesh):
    return jax.shard_map(
        on_device,
        mesh=mesh,
        in_specs=(
            P(("gx", "gy"), None),
            P(),
            P("gy", "gx"),
            P(("gx", "gy"), None, None),
            P(("gx", "gy"), None, None),
            P(("gx", "gy")),
            P("gy", "gx"),
        ),
        out_specs=P(("gx", "gy"), None),
        check_vma=False,
    )
```

profile of v0, /device:TPU:0, one launch (start us, length us, event | category | flops | bytes accessed | tf_op | source)
XLA Modules:
  0.0 308.4 jit_solution(7281891384599900363)
XLA Ops:
  6.5 0.0 all-gather.3.cloned.1.call-start
  6.5 1.2 fusion.19
  7.7 1.8 fusion.21
  9.5 0.0 all-gather.3.cloned.1.call-update
  9.6 0.0 reduce-scatter.3.cloned.1.call-start
  9.6 30.7 %all-gather.3.cloned.1.call-done = bf16[64,16384]{1,0:T(8,128)(2,1)} async-done(((bf16[8,16384]{1,0:T(8,128)(2,1)}), bf16[64,16384]{1,0:T(8,128)(2,1)}) %all-gather.3.cloned.1.call-update) | async-done | bytes 2097168 | tf_op jit(solution)/shard_map/all_gather | solution.py:71
  40.3 1.7 copy.51
  42.0 53.0 %all_to_all.76 = bf16[64,4,4096]{2,0,1:T(8,128)(2,1)S(1)} all-to-all(bf16[64,4,4096]{2,0,1:T(8,128)(2,1)S(1)} %bitcast.73), channel_id=1, replica_groups=mesh['gx'=8,'gy'=4] {'gy'}, dimensions={1} | all-to-all | bytes 4194304 | tf_op jit(solution)/shard_map/all_to_all | solution.py:72
  95.1 10.4 %fusion.31 = f32[256,2304]{1,0:T(8,128)} fusion(bf16[256,4096]{1,0:T(8,128)(2,1)S(1)} %bitcast.78, bf16[4096,2304]{1,0:T(8,128)(2,1)} %param.9), kind=kOutput, calls=%fused_computation.56 | convolution fusion | flops 4831838208 | bytes 23330816 | tf_op jit(solution)/shard_map/dot_general | solution.py:75
  105.4 0.0 copy-start
  105.4 0.0 reduce-scatter.3.cloned.1.call-update
  105.5 0.6 copy-done
  106.1 0.1 iota_compare_fusion
  106.2 45.6 %reduce-scatter.3.cloned.1.call-done = f32[64,2304]{1,0:T(8,128)} async-done(((f32[256,2304]{1,0:T(8,128)}), f32[64,2304]{1,0:T(8,128)}) %reduce-scatter.3.cloned.1.call-update) | async-done | bytes 589840 | tf_op jit(solution)/shard_map/reduce_scatter | solution.py:74
  151.8 1.8 convert_bitcast_fusion.1
  153.6 3.7 %all-to-all-start.1 = ((bf16[8,8,2304]{2,1,0:T(8,128)(2,1)}), bf16[8,8,2304]{2,1,0:T(8,128)(2,1)S(1)}, u32[]{:S(2)}, u32[]{:S(2)}) async-start(bf16[8,8,2304]{2,1,0:T(8,128)(2,1)} %convert_bitcast_fusion.1), calls=%async_computation.2 | async-start | bytes 589824 | tf_op jit(solution)/shard_map/all_to_all | solution.py:80
  157.2 0.0 all-gather.5.cloned.1.call-start
  157.3 0.1 multiply_cosine_fusion
  157.4 7.1 %all-to-all-done.1 = bf16[8,8,2304]{2,1,0:T(8,128)(2,1)S(1)} async-done(((bf16[8,8,2304]{2,1,0:T(8,128)(2,1)}), bf16[8,8,2304]{2,1,0:T(8,128)(2,1)S(1)}, u32[]{:S(2)}, u32[]{:S(2)}) %all-to-all-start.1) | async-done | bytes 294944 | tf_op jit(solution)/shard_map/all_to_all | solution.py:80
  164.6 0.1 copy.52
  164.7 0.1 subtract_convert_fusion.1
  164.8 0.0 slice-start
  164.8 0.2 subtract_convert_fusion
  165.0 0.1 maximum_bitcast_fusion
  165.1 0.3 fusion.22
  165.4 0.0 slice-start.1
  165.5 6.1 %fusion.6 = (f32[8,8,16]{2,1,0:T(8,128)S(1)}, f32[8,8,16,512]{3,2,1,0:T(8,128)S(1)}) fusion(pred[8,512]{1,0:T(8,128)(4,1)S(1)} %iota_compare_fusion, bf16[8,8,16,64]{3,2,1,0:T(8,128)(2,1)S(1)} %bitcast.85, bf16[8,8,16,64]{3,2,1,0:T(8,128)(2,1)S(1)} %bitcast.83, bf16[8,512,1024]{2,1,0:T(8,128)(2,1)} %param.10), kind=kOutput, calls=%fused_computation.12 | convolution fusion | flops 136313856 | bytes 10756096 | tf_op jit(solution)/shard_map/rgsd,rtgd->rgst/dot_general | solution.py:56
  171.6 0.7 fusion.7
  172.3 0.0 slice-done
  172.3 0.0 slice-done.1
  172.3 2.2 fusion.11
  174.5 0.9 copy.53
  175.4 0.0 all-gather.5.cloned.1.call-update
  175.4 0.0 reduce-scatter.5.cloned.1.call-start
  175.4 25.7 %all-gather.5.cloned.1.call-done = bf16[64,16384]{1,0:T(8,128)(2,1)} async-done(((bf16[8,16384]{1,0:T(8,128)(2,1)}), bf16[64,16384]{1,0:T(8,128)(2,1)}) %all-gather.5.cloned.1.call-update) | async-done | bytes 2097168 | tf_op jit(solution)/shard_map/all_gather | solution.py:84
  201.1 1.7 copy.50
  202.9 53.0 %all_to_all.77 = bf16[64,4,4096]{2,0,1:T(8,128)(2,1)S(1)} all-to-all(bf16[64,4,4096]{2,0,1:T(8,128)(2,1)S(1)} %bitcast.74), channel_id=1, replica_groups=mesh['gx'=8,'gy'=4] {'gy'}, dimensions={1} | all-to-all | bytes 4194304 | tf_op jit(solution)/shard_map/all_to_all | solution.py:85
  255.9 9.2 %convolution_convert_fusion = bf16[256,2048]{1,0:T(8,128)(2,1)} fusion(bf16[256,4096]{1,0:T(8,128)(2,1)S(1)} %bitcast.79, bf16[4096,2048]{1,0:T(8,128)(2,1)} %param.13), kind=kOutput, calls=%fused_computation.6 | convolution fusion | flops 4295491584 | bytes 19922944 | tf_op jit(solution)/shard_map/dot_general | solution.py:88
  265.1 0.0 reduce-scatter.5.cloned.1.call-update
  265.1 25.4 %reduce-scatter.5.cloned.1.call-done = bf16[64,2048]{1,0:T(8,128)(2,1)} async-done(((bf16[256,2048]{1,0:T(8,128)(2,1)}), bf16[64,2048]{1,0:T(8,128)(2,1)}) %reduce-scatter.5.cloned.1.call-update) | async-done | bytes 262160 | tf_op jit(solution)/shard_map/reduce_scatter | solution.py:87
  290.6 10.6 %all_to_all.78 = bf16[8,8,2048]{2,1,0:T(8,128)(2,1)S(1)} all-to-all(bf16[8,8,2048]{2,1,0:T(8,128)(2,1)} %bitcast.88), channel_id=1, replica_groups=mesh['gx'=8,'gy'=4] {'gx'}, dimensions={0} | all-to-all | bytes 524288 | tf_op jit(solution)/shard_map/all_to_all | solution.py:93
  301.1 0.7 copy.56
  (9 shorter events, 0.1 us)
Async XLA Ops:
  6.5 33.8 %all-gather.3.cloned.1.call-start = ((), (), s32[]{:S(2)}) async-start(), calls=%async_computation.6 | async-start | bytes 2359296 | tf_op jit(solution)/shard_map/all_gather | solution.py:71
  9.6 142.2 %reduce-scatter.3.cloned.1.call-start = ((), (), s32[]{:S(2)}) async-start(), calls=%async_computation.7 | async-start | bytes 2949120 | tf_op jit(solution)/shard_map/reduce_scatter | solution.py:74
  105.4 0.7 copy-start
  153.6 10.9 %all-to-all-start.1 = ((bf16[8,8,2304]{2,1,0:T(8,128)(2,1)}), bf16[8,8,2304]{2,1,0:T(8,128)(2,1)S(1)}, u32[]{:S(2)}, u32[]{:S(2)}) async-start(bf16[8,8,2304]{2,1,0:T(8,128)(2,1)} %convert_bitcast_fusion.1), calls=%async_computation.2 | async-start | bytes 589824 | tf_op jit(solution)/shard_map/all_to_all | solution.py:80
  157.2 43.9 %all-gather.5.cloned.1.call-start = ((), (), s32[]{:S(2)}) async-start(), calls=%async_computation.8 | async-start | bytes 2359296 | tf_op jit(solution)/shard_map/all_gather | solution.py:84
  164.8 7.5 %slice-start = ((s8[8388608]{0:T(1024)(128)(4,1)}), s8[4194304]{0:T(1024)(128)(4,1)S(1)}, s32[]{:S(2)}) async-start(s8[8388608]{0:T(1024)(128)(4,1)} %bitcast.93), calls=%async_computation.10 | async-start | bytes 8388608
  165.4 6.9 %slice-start.1 = ((s8[8388608]{0:T(1024)(128)(4,1)}), s8[4194304]{0:T(1024)(128)(4,1)S(1)}, s32[]{:S(2)}) async-start(s8[8388608]{0:T(1024)(128)(4,1)} %bitcast.93), calls=%async_computation.11 | async-start | bytes 8388608
  175.4 115.2 %reduce-scatter.5.cloned.1.call-start = ((), (), s32[]{:S(2)}) async-start(), calls=%async_computation.9 | async-start | bytes 1310720 | tf_op jit(solution)/shard_map/reduce_scatter | solution.py:87
Sparse Core Ops, SparseCore 0:
  9.7 30.5 all-gather.2
  105.6 46.1 reduce-scatter.2
  175.5 25.5 all-gather.4
  265.3 25.2 reduce-scatter.4
where the time goes:
time: 309 us; the launch traced here: 308 us
  waiting for transfers between devices  135 us (44%)
  blocking collectives  117 us (38%)
  matrix products  28.2 us (9%)
  between operations  13.3 us (4%)
  other arithmetic  6.13 us (2%)
  local copies, waits for them, and re-layouts  5.79 us (2%)
  starting transfers between devices  3.78 us (1%)
    all_to_all x1, blocking collectives, on_device(): lax.all_to_all(grouped_out, 'gy', split_axis=1, concat_axis=0, tiled=True)  53 us
    all_to_all x1, blocking collectives, on_device(): lax.all_to_all(grouped_in, 'gy', split_axis=1, concat_axis=0, tiled=True)  53 us
    reduce_scatter x1, waiting for transfers between devices, on_device(): lax.psum_scatter(jnp.dot(picked, w_qkv, preferred_element_type=jnp.float3...  45.6 us
    all_gather x1, waiting for transfers between devices, on_device(): grouped_in = lax.all_gather(normed, 'gx', axis=0, tiled=True)  30.7 us
    all_gather x1, waiting for transfers between devices, on_device(): grouped_out = lax.all_gather(attended, 'gx', axis=0, tiled=True)  25.7 us
    reduce_scatter x1, waiting for transfers between devices, on_device(): lax.psum_scatter(jnp.dot(picked, w_out, preferred_element_type=jnp.float3...  25.4 us
    all_to_all x1, blocking collectives, on_device(): lax.all_to_all(partial_out, 'gx', split_axis=0, concat_axis=1, tiled=True)  10.6 us
    dot_general x1, matrix products, on_device(): jnp.dot(picked, w_qkv, preferred_element_type=jnp.float32)  10.4 us
  transfers between devices with their start and end apart: 5, of which 5 were waited for; matrix products, arithmetic and copies ran while one was open for 0% of the time, Pallas kernels for 0%

commit v1 on v0

v1 whole, which is shorter than its diff:
```python
import math

import jax
import jax.numpy as jnp
from jax import lax
from jax.experimental import pallas as pl
from jax.experimental.pallas import tpu as pltpu
from jax.sharding import PartitionSpec as P

HQ = 128
KVH = 8
HD = 128


eps = 1e-05
theta = 500000.0
ROOM = 50 * 2**20


def rotate(values, position, head_size):
    half = head_size // 2
    index = jnp.arange(half, dtype=jnp.float32)
    freqs = theta ** (-2.0 * index / head_size)
    angle = position[:, None, None] * freqs[None, None, :]
    cosine = jnp.cos(angle)
    sine = jnp.sin(angle)
    first = values[..., :half]
    second = values[..., half:]
    return jnp.concatenate(
        [first * cosine - second * sine, second * cosine + first * sine], axis=-1
    )


PART = 128


def attend_kernel(lengths, query, key_new, value_new, k_cache, v_cache, out, keys, values, wide, sems):
    rows, span = keys.shape[:2]
    share = HQ // KVH
    parts = span // PART
    scale = 1.0 / math.sqrt(HD)

    def copies(row, part):
        some = pl.ds(part * PART, PART)
        return (
            pltpu.make_async_copy(
                k_cache.at[row, some], keys.at[row, some], sems.at[row, part, 0]
            ),
            pltpu.make_async_copy(
                v_cache.at[row, some], values.at[row, some], sems.at[row, part, 1]
            ),
        )

    for row in range(rows):
        for part in range(parts):

            @pl.when(part * PART < lengths[row])
            def _():
                for copy in copies(row, part):
                    copy.start()

    wide[...] = jnp.zeros_like(wide)

    def one_row(row, used):
        count = used * PART
        for part in range(used):
            for copy in copies(row, part):
                copy.wait()
        for group in range(KVH):
            heads = pl.ds(group * share, share)
            wide[heads, group * HD : (group + 1) * HD] = query[row, heads]
        scores = lax.dot_general(
            wide[...],
            keys[row, :count],
            (((1,), (1,)), ((), ())),
            preferred_element_type=jnp.float32,
        )
        position = lax.broadcasted_iota(jnp.int32, scores.shape, 1)
        scores = jnp.where(position < lengths[row], scores * scale, -jnp.inf)
        fresh_key = jnp.broadcast_to(key_new[row][:, None, :], (KVH, share, HD))
        fresh_key = fresh_key.reshape(HQ, HD).astype(jnp.float32)
        fresh = jnp.sum(query[row].astype(jnp.float32) * fresh_key, axis=1, keepdims=True) * scale
        top = jnp.maximum(jnp.max(scores, axis=1, keepdims=True), fresh)
        probs = jnp.exp(scores - top)
        pnew = jnp.exp(fresh - top)
        unit = 1.0 / (jnp.sum(probs, axis=1, keepdims=True) + pnew)
        weights = (probs * unit).astype(jnp.bfloat16)
        wnew = (pnew * unit).astype(jnp.bfloat16).astype(jnp.float32)
        mixed = jnp.dot(weights, values[row, :count], preferred_element_type=jnp.float32)
        for group in range(KVH):
            heads = slice(group * share, (group + 1) * share)
            own = mixed[heads, group * HD : (group + 1) * HD]
            own = own + wnew[heads] * value_new[row, group : group + 1]
            out[row, heads] = own.astype(out.dtype)

    @pl.loop(0, rows)
    def _(row):
        used = (lengths[row] + PART - 1) // PART
        for case in range(1, parts + 1):

            @pl.when(used == case)
            def _():
                one_row(row, case)


def attend_local(owned, k_cache, v_cache, lengths):
    rows = owned.shape[0]
    query = owned[:, : HQ * HD].reshape(rows, HQ, HD).astype(jnp.float32)
    key_new = owned[:, HQ * HD : (HQ + KVH) * HD].reshape(rows, KVH, HD).astype(jnp.float32)
    value_new = owned[:, (HQ + KVH) * HD :].reshape(rows, KVH, HD).astype(jnp.float32)
    position = lengths.astype(jnp.float32)
    query = rotate(query, position, HD).astype(jnp.bfloat16)
    key_new = rotate(key_new, position, HD).astype(jnp.bfloat16)
    span, width = k_cache.shape[1:]
    vmem = pl.BlockSpec(memory_space=pltpu.VMEM)
    anywhere = pl.BlockSpec(memory_space=pl.ANY)
    mixed = pl.pallas_call(
        attend_kernel,
        in_specs=[
            pl.BlockSpec(memory_space=pltpu.SMEM),
            vmem,
            vmem,
            vmem,
            anywhere,
            anywhere,
        ],
        out_specs=vmem,
        out_shape=jax.ShapeDtypeStruct((rows, HQ, HD), jnp.bfloat16),
        scratch_shapes=[
            pltpu.VMEM((rows, span, width), jnp.bfloat16),
            pltpu.VMEM((rows, span, width), jnp.bfloat16),
            pltpu.VMEM((HQ, width), jnp.bfloat16),
            pltpu.SemaphoreType.DMA((rows, span // PART, 2)),
        ],
        compiler_params=pltpu.CompilerParams(vmem_limit_bytes=ROOM),
        cost_estimate=pl.CostEstimate(
            flops=4 * rows * span * width * HQ,
            bytes_accessed=2 * rows * span * width,
            transcendentals=rows * span * HQ,
        ),
    )(lengths, query, key_new, value_new, k_cache, v_cache)
    return mixed.reshape(rows, HQ * HD)


def swap(block, axis, bit):
    count = lax.axis_size(axis)
    return lax.ppermute(block, axis, [(i, i ^ bit) for i in range(count)])


def all_rows(block):
    if lax.axis_size("gx") != 8:
        pieces = lax.all_gather(block, "gx", axis=0)
        count, rows, width = pieces.shape
        return pieces.reshape(count, 2, rows // 2, width).transpose(1, 0, 2, 3)
    mine = [block] + [swap(block, "gx", chip) for chip in (2, 4, 6)]
    theirs = [swap(piece, "gx", 1) for piece in mine]
    pieces = [piece for pair in zip(mine, theirs) for piece in pair]
    halves = [piece.reshape(2, 1, -1, block.shape[1]) for piece in pieces]
    return jnp.concatenate(halves, axis=1)


def multiply_kernel(rows_ref, weights_ref, out_ref):
    out_ref[...] = jnp.dot(
        rows_ref[...], weights_ref[...], preferred_element_type=jnp.float32
    )


def multiply(rows, weights):
    count, depth = rows.shape
    columns = weights.shape[1]
    tile = 256 if columns % 256 == 0 else columns
    return pl.pallas_call(
        multiply_kernel,
        grid=(columns // tile,),
        in_specs=[
            pl.BlockSpec(memory_space=pltpu.VMEM),
            pl.BlockSpec((depth, tile), lambda j: (0, j)),
        ],
        out_specs=pl.BlockSpec((count, tile), lambda j: (0, j)),
        out_shape=jax.ShapeDtypeStruct((count, columns), jnp.float32),
        compiler_params=pltpu.CompilerParams(vmem_limit_bytes=ROOM),
        cost_estimate=pl.CostEstimate(
            flops=2 * count * depth * columns,
            bytes_accessed=2 * depth * columns,
            transcendentals=0,
        ),
    )(rows, weights)


def project(rows, weights, scale):
    width = weights.shape[0]
    here = lax.axis_index("gy")

    def features(owner):
        return lax.dynamic_slice_in_dim(rows, owner * width, width, axis=1)

    def send(values, bit):
        packed = (values * scale).astype(jnp.float16)
        return swap(packed, "gy", bit).astype(jnp.float32) * (1.0 / scale)

    far = jnp.concatenate([swap(features(here ^ bit), "gy", bit) for bit in (2, 3)])
    near, far = lax.optimization_barrier((features(here ^ 1), far))
    near = jnp.concatenate([features(here), swap(near, "gy", 1)])
    far = all_rows(far)
    near = all_rows(near)
    shape = far.shape[:3] + weights.shape[1:]
    far = multiply(far.reshape(-1, width), weights).reshape(shape)
    pair = far[0] + send(far[1], 1)
    near = multiply(near.reshape(-1, width), weights).reshape(shape)
    return near[0] + send(near[1], 1) + send(pair, 2)


def deliver(columns):
    count, rows, width = columns.shape
    if count != 8:
        owned = lax.all_to_all(columns, "gx", split_axis=0, concat_axis=0)
    else:
        pairs = [columns[:2]] + [
            swap(columns[chip : chip + 2], "gx", chip) for chip in (2, 4, 6)
        ]
        theirs = swap(jnp.stack([pair[1] for pair in pairs]), "gx", 1)
        owned = jnp.stack([pair[0] for pair in pairs])
        owned = jnp.stack([owned, theirs], axis=1).reshape(count, rows, width)
        owned = owned[jnp.arange(count) ^ lax.axis_index("gx")]
    return owned.transpose(1, 0, 2).reshape(rows, count * width)


def level(rows):
    rows = rows.astype(jnp.float32)
    top = jnp.max(jnp.abs(rows), axis=-1, keepdims=True)
    scale = jnp.ones_like(top)
    unit = jnp.ones_like(top)
    for power in (64, 32, 16, 8, 4, 2, 1):
        large = top * scale > 2.0 ** (power - 1)
        scale = jnp.where(large, scale * 2.0**-power, scale)
        unit = jnp.where(large, unit * 2.0**power, unit)
    for power in (64, 32, 16, 8, 4, 2, 1):
        small = top * scale <= 2.0**-power
        scale = jnp.where(small, scale * 2.0**power, scale)
        unit = jnp.where(small, unit * 2.0**-power, unit)
    return (rows * scale).astype(jnp.bfloat16), unit


def on_device(hidden_in, norm_gain, w_qkv, k_cache, v_cache, lengths, w_out):
    widened = hidden_in.astype(jnp.float32)
    normed = (
        widened * lax.rsqrt(jnp.mean(widened * widened, axis=-1, keepdims=True) + eps) * norm_gain
    ).astype(jnp.bfloat16)
    qkv = project(normed, w_qkv, 32.0)
    owned = deliver(qkv.astype(jnp.bfloat16))
    attended = attend_local(owned, k_cache, v_cache, lengths)
    scaled, unit = level(attended)
    out = deliver(project(scaled, w_out, 8.0).astype(jnp.bfloat16))
    return (out.astype(jnp.float32) * unit).astype(jnp.bfloat16)


def solution(mesh):
    return jax.shard_map(
        on_device,
        mesh=mesh,
        in_specs=(
            P(("gx", "gy"), None),
            P(),
            P("gy", "gx"),
            P(("gx", "gy"), None, None),
            P(("gx", "gy"), None, None),
            P(("gx", "gy")),
            P("gy", "gx"),
        ),
        out_specs=P(("gx", "gy"), None),
        check_vma=False,
    )
```

time: 309 us -> 161 us (0.52)
  blocking collectives: 117 us -> 0 us
  waiting for transfers between devices: 135 us -> 56.3 us
  Pallas kernels: 0 us -> 48 us
  starting transfers between devices: 3.78 us -> 48.2 us
  matrix products: 28.2 us -> 0 us
  between operations: 13.3 us -> 0.7 us
  local copies, waits for them, and re-layouts: 5.79 us -> 1.71 us
    all_to_all x3 -> x0, blocking collectives: 117 us -> none  [the longest x1 53 us: on_device(): lax.all_to_all(grouped_out, 'gy', split_axis=1, concat_axis=0, tiled=True)]
    reduce_scatter x2 -> x0, waiting for transfers between devices: 71 us -> none  [the longest x1 45.6 us: on_device(): lax.psum_scatter(jnp.dot(picked, w_qkv, preferred_element_type=jnp.float3...]
    all_gather x2 -> x0, waiting for transfers between devices: 56.4 us -> none  [the longest x1 30.7 us: on_device(): grouped_in = lax.all_gather(normed, 'gx', axis=0, tiled=True)]
    ppermute x0 -> x48, waiting for transfers between devices: none -> 56.3 us  [swap(): return lax.ppermute(block, axis, [(i, i ^ bit) for i in range(count)])]
    ppermute x0 -> x48, starting transfers between devices: none -> 48.2 us  [swap(): return lax.ppermute(block, axis, [(i, i ^ bit) for i in range(count)])]
    pallas_call x0 -> x5, Pallas kernels: none -> 48 us  [the longest x4 39.9 us: multiply(): pl.pallas_call(multiply_kernel, grid=(columns // tile,), in_specs=[pl.Blo...]
    dot_general x5 -> x0, matrix products: 28.2 us -> none  [the longest x1 10.4 us: on_device(): jnp.dot(picked, w_qkv, preferred_element_type=jnp.float32)]
    all_to_all x1 -> x0, waiting for transfers between devices: 7.11 us -> none  [on_device(): lax.all_to_all(partial_qkv.astype(jnp.bfloat16), 'gx', split_axis=0, conc...]
  transfers between devices with their start and end apart: 5 -> 48, of which waited for: 5 -> 24; matrix products, arithmetic and copies ran while one was open for 0% -> 1% of each run, Pallas kernels for 0% -> 25%
where the time goes in v1:
time: 161 us; the launch traced here: 160 us
  waiting for transfers between devices  56.3 us (35%)
  starting transfers between devices  48.2 us (30%)
  Pallas kernels  48 us (30%)
  other arithmetic  5.25 us (3%)
  local copies, waits for them, and re-layouts  1.71 us (1%)
    ppermute x48, waiting for transfers between devices, swap(): return lax.ppermute(block, axis, [(i, i ^ bit) for i in range(count)])  56.3 us
    ppermute x48, starting transfers between devices, swap(): return lax.ppermute(block, axis, [(i, i ^ bit) for i in range(count)])  48.2 us
    pallas_call x4, Pallas kernels, multiply(): pl.pallas_call(multiply_kernel, grid=(columns // tile,), in_specs=[pl.Blo...  39.9 us
    pallas_call x1, Pallas kernels, attend_local(): pl.pallas_call(attend_kernel, in_specs=[pl.BlockSpec(memory_space=pltpu.S...  8.09 us
  transfers between devices with their start and end apart: 48, of which 24 were waited for; matrix products, arithmetic and copies ran while one was open for 1% of the time, Pallas kernels for 25%

profile of v1, /device:TPU:0, one launch (start us, length us, event | category | flops | bytes accessed | tf_op | source)
XLA Modules:
  0.0 160.1 jit_solution(1147623166085052075)
XLA Ops:
  0.0 1.2 fusion.8
  1.2 1.1 fusion.10
  2.4 4.1 %collective-permute-start = (bf16[8,4096]{1,0:T(8,128)(2,1)S(1)}, bf16[8,4096]{1,0:T(8,128)(2,1)S(1)}, u32[]{:S(2)}, u32[]{:S(2)}) collective-permute-start(bf16[8,4096]{1,0:T(8,128)(2,1)S(1)} %get-tuple-element.37), channel_id=1, source_target_pairs={{0,2},{1,3},{2,0},{3,1},{4,6},{5,7},{6,4},{7,5},{8,10},{9,11},{10,... | collective-permute-start | bytes 196616 | tf_op jit(solution)/shard_map/ppermute | solution.py:147
  6.5 1.3 collective-permute-start.1
  7.8 2.3 %collective-permute-done = bf16[8,4096]{1,0:T(8,128)(2,1)S(1)} collective-permute-done((bf16[8,4096]{1,0:T(8,128)(2,1)S(1)}, bf16[8,4096]{1,0:T(8,128)(2,1)S(1)}, u32[]{:S(2)}, u32[]{:S(2)}) %collective-permute-start) | collective-permute-done | bytes 65568 | tf_op jit(solution)/shard_map/ppermute | solution.py:147
  10.1 2.5 %collective-permute-done.1 = bf16[8,4096]{1,0:T(8,128)(2,1)S(1)} collective-permute-done((bf16[8,4096]{1,0:T(8,128)(2,1)S(1)}, bf16[8,4096]{1,0:T(8,128)(2,1)S(1)}, u32[]{:S(2)}, u32[]{:S(2)}) %collective-permute-start.1) | collective-permute-done | bytes 65568 | tf_op jit(solution)/shard_map/ppermute | solution.py:147
  12.7 0.9 collective-permute-start.2
  13.7 1.8 %collective-permute-start.12 = (bf16[16,4096]{1,0:T(8,128)(2,1)S(1)}, bf16[16,4096]{1,0:T(8,128)(2,1)S(1)}, u32[]{:S(2)}, u32[]{:S(2)}) collective-permute-start(bf16[16,4096]{1,0:T(8,128)(2,1)S(1)} %pad_maximum_fusion.4), channel_id=1, source_target_pairs={{0,8},{4,12},{8,0},{12,4},{16,24},{20,28},{24,16},{28,20},{1,9},{5... | collective-permute-start | bytes 393224 | tf_op jit(solution)/shard_map/ppermute | solution.py:147
  15.4 1.5 collective-permute-start.14
  17.3 1.8 %collective-permute-start.4 = (bf16[16,4096]{1,0:T(8,128)(2,1)S(1)}, bf16[16,4096]{1,0:T(8,128)(2,1)S(1)}, u32[]{:S(2)}, u32[]{:S(2)}) collective-permute-start(bf16[16,4096]{1,0:T(8,128)(2,1)S(1)} %pad_maximum_fusion.5), channel_id=1, source_target_pairs={{0,8},{4,12},{8,0},{12,4},{16,24},{20,28},{24,16},{28,20},{1,9},{5... | collective-permute-start | bytes 393224 | tf_op jit(solution)/shard_map/ppermute | solution.py:147
  19.7 1.9 %collective-permute-start.6 = (bf16[16,4096]{1,0:T(8,128)(2,1)S(1)}, bf16[16,4096]{1,0:T(8,128)(2,1)S(1)}, u32[]{:S(2)}, u32[]{:S(2)}) collective-permute-start(bf16[16,4096]{1,0:T(8,128)(2,1)S(1)} %pad_maximum_fusion.5), channel_id=1, source_target_pairs={{0,16},{4,20},{8,24},{12,28},{16,0},{20,4},{24,8},{28,12},{1,17},{... | collective-permute-start | bytes 393224 | tf_op jit(solution)/shard_map/ppermute | solution.py:147
  21.7 1.6 %collective-permute-start.8 = (bf16[16,4096]{1,0:T(8,128)(2,1)S(1)}, bf16[16,4096]{1,0:T(8,128)(2,1)S(1)}, u32[]{:S(2)}, u32[]{:S(2)}) collective-permute-start(bf16[16,4096]{1,0:T(8,128)(2,1)S(1)} %pad_maximum_fusion.5), channel_id=1, source_target_pairs={{0,24},{4,28},{8,16},{12,20},{16,8},{20,12},{24,0},{28,4},{1,25},{... | collective-permute-start | bytes 393224 | tf_op jit(solution)/shard_map/ppermute | solution.py:147
  24.3 1.8 %collective-permute-done.4 = bf16[16,4096]{1,0:T(8,128)(2,1)S(1)} collective-permute-done((bf16[16,4096]{1,0:T(8,128)(2,1)S(1)}, bf16[16,4096]{1,0:T(8,128)(2,1)S(1)}, u32[]{:S(2)}, u32[]{:S(2)}) %collective-permute-start.4) | collective-permute-done | bytes 131104 | tf_op jit(solution)/shard_map/ppermute | solution.py:147
  26.1 3.3 %collective-permute-done.6 = bf16[16,4096]{1,0:T(8,128)(2,1)S(1)} collective-permute-done((bf16[16,4096]{1,0:T(8,128)(2,1)S(1)}, bf16[16,4096]{1,0:T(8,128)(2,1)S(1)}, u32[]{:S(2)}, u32[]{:S(2)}) %collective-permute-start.6) | collective-permute-done | bytes 131104 | tf_op jit(solution)/shard_map/ppermute | solution.py:147
  30.1 10.6 %shard_map.74 = f32[128,2304]{1,0:T(8,128)S(1)} custom-call(bf16[128,4096]{1,0:T(8,128)(2,1)S(1)} %bitcast.179, bf16[4096,2304]{1,0:T(8,128)(2,1)} %weights_ref.5), custom_call_target="tpu_custom_call" | custom-call | flops 2415919104 | bytes 18874368 | tf_op jit(solution)/shard_map/pallas_call | solution.py:172
  40.8 1.0 collective-permute-start.18
  41.9 10.6 %shard_map.73 = f32[128,2304]{1,0:T(8,128)S(1)} custom-call(bf16[128,4096]{1,0:T(8,128)(2,1)S(1)} %bitcast.181, bf16[4096,2304]{1,0:T(8,128)(2,1)} %weights_ref.5), custom_call_target="tpu_custom_call" | custom-call | flops 2415919104 | bytes 18874368 | tf_op jit(solution)/shard_map/pallas_call | solution.py:172
  52.6 1.1 collective-permute-start.10
  53.8 2.2 %collective-permute-start.19 = (f16[8,8,2304]{2,1,0:T(8,128)(2,1)S(1)}, f16[8,8,2304]{2,1,0:T(8,128)(2,1)S(1)}, u32[]{:S(2)}, u32[]{:S(2)}) collective-permute-start(f16[8,8,2304]{2,1,0:T(8,128)(2,1)S(1)} %fusion.3), channel_id=1, source_target_pairs={{0,2},{1,3},{2,0},{3,1},{4,6},{5,7},{6,4},{7,5},{8,10},{9,11},{10,... | collective-permute-start | bytes 884744 | tf_op jit(solution)/shard_map/ppermute | solution.py:147
  56.2 11.9 %collective-permute-done.10 = f16[8,8,2304]{2,1,0:T(8,128)(2,1)S(1)} collective-permute-done((f16[8,8,2304]{2,1,0:T(8,128)(2,1)S(1)}, f16[8,8,2304]{2,1,0:T(8,128)(2,1)S(1)}, u32[]{:S(2)}, u32[]{:S(2)}) %collective-permute-start.10) | collective-permute-done | bytes 294944 | tf_op jit(solution)/shard_map/ppermute | solution.py:147
  69.0 1.3 collective-permute-start.21
  70.3 1.4 collective-permute-start.22
  71.8 1.3 collective-permute-done.20
  73.1 1.1 collective-permute-done.21
  74.2 1.4 collective-permute-done.22
  75.7 1.3 collective-permute-done.23
  78.4 8.1 %shard_map.75 = bf16[8,128,128]{2,1,0:T(8,128)(2,1)S(1)} custom-call(s32[8]{0:T(128)S(1)} %copy-done, bf16[8,128,128]{2,1,0:T(8,128)(2,1)S(1)} %pad_maximum_fusion.1.query, bf16[8,8,128]{2,1,0:T(8,128)(2,1)S(1)} %pad_maximum_fusion.9.key_new, f32[8,8,128]{2,1,0:T(8,128)S(1)} %get-tuple-element.55.value_new, bf16[8,512,1024]{2,1,0:T(8,128)(2,1)} %k_cache.1, ...), custom_call_target="tpu_custom_call" | custom-call | flops 2147483648 | bytes 8388608 | tf_op jit(solution)/shard_map/pallas_call | solution.py:117
  87.1 3.4 %collective-permute-start.24 = (bf16[8,4096]{1,0:T(8,128)(2,1)S(1)}, bf16[8,4096]{1,0:T(8,128)(2,1)S(1)}, u32[]{:S(2)}, u32[]{:S(2)}) collective-permute-start(bf16[8,4096]{1,0:T(8,128)(2,1)S(1)} %get-tuple-element.33), channel_id=1, source_target_pairs={{0,2},{1,3},{2,0},{3,1},{4,6},{5,7},{6,4},{7,5},{8,10},{9,11},{10,... | collective-permute-start | bytes 196616 | tf_op jit(solution)/shard_map/ppermute | solution.py:147
  90.5 1.8 %collective-permute-start.25 = (bf16[8,4096]{1,0:T(8,128)(2,1)S(1)}, bf16[8,4096]{1,0:T(8,128)(2,1)S(1)}, u32[]{:S(2)}, u32[]{:S(2)}) collective-permute-start(bf16[8,4096]{1,0:T(8,128)(2,1)S(1)} %get-tuple-element.32), channel_id=1, source_target_pairs={{0,3},{1,2},{2,1},{3,0},{4,7},{5,6},{6,5},{7,4},{8,11},{9,10},{10,... | collective-permute-start | bytes 196616 | tf_op jit(solution)/shard_map/ppermute | solution.py:147
  92.7 3.9 %collective-permute-done.25 = bf16[8,4096]{1,0:T(8,128)(2,1)S(1)} collective-permute-done((bf16[8,4096]{1,0:T(8,128)(2,1)S(1)}, bf16[8,4096]{1,0:T(8,128)(2,1)S(1)}, u32[]{:S(2)}, u32[]{:S(2)}) %collective-permute-start.25) | collective-permute-done | bytes 65568 | tf_op jit(solution)/shard_map/ppermute | solution.py:147
  96.7 1.2 collective-permute-start.26
  98.0 2.1 %collective-permute-start.36 = (bf16[16,4096]{1,0:T(8,128)(2,1)S(1)}, bf16[16,4096]{1,0:T(8,128)(2,1)S(1)}, u32[]{:S(2)}, u32[]{:S(2)}) collective-permute-start(bf16[16,4096]{1,0:T(8,128)(2,1)S(1)} %pad_maximum_fusion.6), channel_id=1, source_target_pairs={{0,8},{4,12},{8,0},{12,4},{16,24},{20,28},{24,16},{28,20},{1,9},{5... | collective-permute-start | bytes 393224 | tf_op jit(solution)/shard_map/ppermute | solution.py:147
  100.4 1.2 collective-permute-start.40
  101.7 2.0 %collective-permute-start.28 = (bf16[16,4096]{1,0:T(8,128)(2,1)S(1)}, bf16[16,4096]{1,0:T(8,128)(2,1)S(1)}, u32[]{:S(2)}, u32[]{:S(2)}) collective-permute-start(bf16[16,4096]{1,0:T(8,128)(2,1)S(1)} %pad_maximum_fusion.7), channel_id=1, source_target_pairs={{0,8},{4,12},{8,0},{12,4},{16,24},{20,28},{24,16},{28,20},{1,9},{5... | collective-permute-start | bytes 393224 | tf_op jit(solution)/shard_map/ppermute | solution.py:147
  105.2 2.7 %collective-permute-start.32 = (bf16[16,4096]{1,0:T(8,128)(2,1)S(1)}, bf16[16,4096]{1,0:T(8,128)(2,1)S(1)}, u32[]{:S(2)}, u32[]{:S(2)}) collective-permute-start(bf16[16,4096]{1,0:T(8,128)(2,1)S(1)} %pad_maximum_fusion.7), channel_id=1, source_target_pairs={{0,24},{4,28},{8,16},{12,20},{16,8},{20,12},{24,0},{28,4},{1,25},{... | collective-permute-start | bytes 393224 | tf_op jit(solution)/shard_map/ppermute | solution.py:147
  107.9 1.3 collective-permute-done.38
  109.7 1.0 collective-permute-done.28
  110.8 3.3 %collective-permute-done.30 = bf16[16,4096]{1,0:T(8,128)(2,1)S(1)} collective-permute-done((bf16[16,4096]{1,0:T(8,128)(2,1)S(1)}, bf16[16,4096]{1,0:T(8,128)(2,1)S(1)}, u32[]{:S(2)}, u32[]{:S(2)}) %collective-permute-start.30) | collective-permute-done | bytes 131104 | tf_op jit(solution)/shard_map/ppermute | solution.py:147
  114.8 9.3 %shard_map.77 = f32[128,2048]{1,0:T(8,128)S(1)} custom-call(bf16[128,4096]{1,0:T(8,128)(2,1)S(1)} %bitcast.180, bf16[4096,2048]{1,0:T(8,128)(2,1)} %weights_ref.7), custom_call_target="tpu_custom_call" | custom-call | flops 2147483648 | bytes 16777216 | tf_op jit(solution)/shard_map/pallas_call | solution.py:172
  124.4 9.3 %shard_map.76 = f32[128,2048]{1,0:T(8,128)S(1)} custom-call(bf16[128,4096]{1,0:T(8,128)(2,1)S(1)} %bitcast.182, bf16[4096,2048]{1,0:T(8,128)(2,1)} %weights_ref.7), custom_call_target="tpu_custom_call" | custom-call | flops 2147483648 | bytes 16777216 | tf_op jit(solution)/shard_map/pallas_call | solution.py:172
  133.8 2.1 %collective-permute-start.34 = (f16[8,8,2048]{2,1,0:T(8,128)(2,1)S(1)}, f16[8,8,2048]{2,1,0:T(8,128)(2,1)S(1)}, u32[]{:S(2)}, u32[]{:S(2)}) collective-permute-start(f16[8,8,2048]{2,1,0:T(8,128)(2,1)S(1)} %fusion.23), channel_id=1, source_target_pairs={{0,1},{1,0},{2,3},{3,2},{4,5},{5,4},{6,7},{7,6},{8,9},{9,8},{10,11... | collective-permute-start | bytes 786440 | tf_op jit(solution)/shard_map/ppermute | solution.py:147
  135.9 1.5 collective-permute-start.43
  137.5 10.1 %collective-permute-done.34 = f16[8,8,2048]{2,1,0:T(8,128)(2,1)S(1)} collective-permute-done((f16[8,8,2048]{2,1,0:T(8,128)(2,1)S(1)}, f16[8,8,2048]{2,1,0:T(8,128)(2,1)S(1)}, u32[]{:S(2)}, u32[]{:S(2)}) %collective-permute-start.34) | collective-permute-done | bytes 262176 | tf_op jit(solution)/shard_map/ppermute | solution.py:147
  147.6 3.1 %collective-permute-done.43 = f16[8,8,2048]{2,1,0:T(8,128)(2,1)S(1)} collective-permute-done((f16[8,8,2048]{2,1,0:T(8,128)(2,1)S(1)}, f16[8,8,2048]{2,1,0:T(8,128)(2,1)S(1)}, u32[]{:S(2)}, u32[]{:S(2)}) %collective-permute-start.43) | collective-permute-done | bytes 262176 | tf_op jit(solution)/shard_map/ppermute | solution.py:147
  150.9 1.2 collective-permute-start.45
  152.1 2.3 %collective-permute-start.46 = (bf16[2,8,2048]{2,1,0:T(8,128)(2,1)S(1)}, bf16[2,8,2048]{2,1,0:T(8,128)(2,1)S(1)}, u32[]{:S(2)}, u32[]{:S(2)}) collective-permute-start(bf16[2,8,2048]{2,1,0:T(8,128)(2,1)S(1)} %get-tuple-element.29), channel_id=1, source_target_pairs={{0,24},{4,28},{8,16},{12,20},{16,8},{20,12},{24,0},{28,4},{1,25},{... | collective-permute-start | bytes 196616 | tf_op jit(solution)/shard_map/ppermute | solution.py:147
  155.2 2.0 %collective-permute-done.46 = bf16[2,8,2048]{2,1,0:T(8,128)(2,1)S(1)} collective-permute-done((bf16[2,8,2048]{2,1,0:T(8,128)(2,1)S(1)}, bf16[2,8,2048]{2,1,0:T(8,128)(2,1)S(1)}, u32[]{:S(2)}, u32[]{:S(2)}) %collective-permute-start.46) | collective-permute-done | bytes 65568 | tf_op jit(solution)/shard_map/ppermute | solution.py:147
  157.4 1.3 collective-permute-done.47
  (143 shorter events, 12.6 us)
Async XLA Ops:
  2.4 7.8 %collective-permute-start = (bf16[8,4096]{1,0:T(8,128)(2,1)S(1)}, bf16[8,4096]{1,0:T(8,128)(2,1)S(1)}, u32[]{:S(2)}, u32[]{:S(2)}) collective-permute-start(bf16[8,4096]{1,0:T(8,128)(2,1)S(1)} %get-tuple-element.37), channel_id=1, source_target_pairs={{0,2},{1,3},{2,0},{3,1},{4,6},{5,7},{6,4},{7,5},{8,10},{9,11},{10,... | collective-permute-start | bytes 196616 | tf_op jit(solution)/shard_map/ppermute | solution.py:147
  6.5 6.2 %collective-permute-start.1 = (bf16[8,4096]{1,0:T(8,128)(2,1)S(1)}, bf16[8,4096]{1,0:T(8,128)(2,1)S(1)}, u32[]{:S(2)}, u32[]{:S(2)}) collective-permute-start(bf16[8,4096]{1,0:T(8,128)(2,1)S(1)} %get-tuple-element.36), channel_id=1, source_target_pairs={{0,3},{1,2},{2,1},{3,0},{4,7},{5,6},{6,5},{7,4},{8,11},{9,10},{10,... | collective-permute-start | bytes 196616 | tf_op jit(solution)/shard_map/ppermute | solution.py:147
  12.7 4.6 %collective-permute-start.2 = (bf16[8,4096]{1,0:T(8,128)(2,1)S(1)}, bf16[8,4096]{1,0:T(8,128)(2,1)S(1)}, u32[]{:S(2)}, u32[]{:S(2)}) collective-permute-start(bf16[8,4096]{1,0:T(8,128)(2,1)S(1)} %get-tuple-element.9), channel_id=1, source_target_pairs={{0,1},{1,0},{2,3},{3,2},{4,5},{5,4},{6,7},{7,6},{8,9},{9,8},{10,11... | collective-permute-start | bytes 196616 | tf_op jit(solution)/shard_map/ppermute | solution.py:147
  13.6 3.8 %collective-permute-start.11 = (bf16[16,4096]{1,0:T(8,128)(2,1)S(1)}, bf16[16,4096]{1,0:T(8,128)(2,1)S(1)}, u32[]{:S(2)}, u32[]{:S(2)}) collective-permute-start(bf16[16,4096]{1,0:T(8,128)(2,1)S(1)} %pad_maximum_fusion.4), channel_id=1, source_target_pairs={{0,4},{4,0},{8,12},{12,8},{16,20},{20,16},{24,28},{28,24},{1,5},{5... | collective-permute-start | bytes 393224 | tf_op jit(solution)/shard_map/ppermute | solution.py:147
  13.7 6.1 %collective-permute-start.12 = (bf16[16,4096]{1,0:T(8,128)(2,1)S(1)}, bf16[16,4096]{1,0:T(8,128)(2,1)S(1)}, u32[]{:S(2)}, u32[]{:S(2)}) collective-permute-start(bf16[16,4096]{1,0:T(8,128)(2,1)S(1)} %pad_maximum_fusion.4), channel_id=1, source_target_pairs={{0,8},{4,12},{8,0},{12,4},{16,24},{20,28},{24,16},{28,20},{1,9},{5... | collective-permute-start | bytes 393224 | tf_op jit(solution)/shard_map/ppermute | solution.py:147
  15.4 8.1 %collective-permute-start.14 = (bf16[16,4096]{1,0:T(8,128)(2,1)S(1)}, bf16[16,4096]{1,0:T(8,128)(2,1)S(1)}, u32[]{:S(2)}, u32[]{:S(2)}) collective-permute-start(bf16[16,4096]{1,0:T(8,128)(2,1)S(1)} %pad_maximum_fusion.4), channel_id=1, source_target_pairs={{0,16},{4,20},{8,24},{12,28},{16,0},{20,4},{24,8},{28,12},{1,17},{... | collective-permute-start | bytes 393224 | tf_op jit(solution)/shard_map/ppermute | solution.py:147
  16.9 7.3 %collective-permute-start.16 = (bf16[16,4096]{1,0:T(8,128)(2,1)S(1)}, bf16[16,4096]{1,0:T(8,128)(2,1)S(1)}, u32[]{:S(2)}, u32[]{:S(2)}) collective-permute-start(bf16[16,4096]{1,0:T(8,128)(2,1)S(1)} %pad_maximum_fusion.4), channel_id=1, source_target_pairs={{0,24},{4,28},{8,16},{12,20},{16,8},{20,12},{24,0},{28,4},{1,25},{... | collective-permute-start | bytes 393224 | tf_op jit(solution)/shard_map/ppermute | solution.py:147
  17.2 4.4 %collective-permute-start.3 = (bf16[16,4096]{1,0:T(8,128)(2,1)S(1)}, bf16[16,4096]{1,0:T(8,128)(2,1)S(1)}, u32[]{:S(2)}, u32[]{:S(2)}) collective-permute-start(bf16[16,4096]{1,0:T(8,128)(2,1)S(1)} %pad_maximum_fusion.5), channel_id=1, source_target_pairs={{0,4},{4,0},{8,12},{12,8},{16,20},{20,16},{24,28},{28,24},{1,5},{5... | collective-permute-start | bytes 393224 | tf_op jit(solution)/shard_map/ppermute | solution.py:147
  17.3 8.8 %collective-permute-start.4 = (bf16[16,4096]{1,0:T(8,128)(2,1)S(1)}, bf16[16,4096]{1,0:T(8,128)(2,1)S(1)}, u32[]{:S(2)}, u32[]{:S(2)}) collective-permute-start(bf16[16,4096]{1,0:T(8,128)(2,1)S(1)} %pad_maximum_fusion.5), channel_id=1, source_target_pairs={{0,8},{4,12},{8,0},{12,4},{16,24},{20,28},{24,16},{28,20},{1,9},{5... | collective-permute-start | bytes 393224 | tf_op jit(solution)/shard_map/ppermute | solution.py:147
  19.7 9.7 %collective-permute-start.6 = (bf16[16,4096]{1,0:T(8,128)(2,1)S(1)}, bf16[16,4096]{1,0:T(8,128)(2,1)S(1)}, u32[]{:S(2)}, u32[]{:S(2)}) collective-permute-start(bf16[16,4096]{1,0:T(8,128)(2,1)S(1)} %pad_maximum_fusion.5), channel_id=1, source_target_pairs={{0,16},{4,20},{8,24},{12,28},{16,0},{20,4},{24,8},{28,12},{1,17},{... | collective-permute-start | bytes 393224 | tf_op jit(solution)/shard_map/ppermute | solution.py:147
  21.7 7.8 %collective-permute-start.8 = (bf16[16,4096]{1,0:T(8,128)(2,1)S(1)}, bf16[16,4096]{1,0:T(8,128)(2,1)S(1)}, u32[]{:S(2)}, u32[]{:S(2)}) collective-permute-start(bf16[16,4096]{1,0:T(8,128)(2,1)S(1)} %pad_maximum_fusion.5), channel_id=1, source_target_pairs={{0,24},{4,28},{8,16},{12,20},{16,8},{20,12},{24,0},{28,4},{1,25},{... | collective-permute-start | bytes 393224 | tf_op jit(solution)/shard_map/ppermute | solution.py:147
  23.5 6.4 %collective-permute-start.13 = (bf16[16,4096]{1,0:T(8,128)(2,1)S(1)}, bf16[16,4096]{1,0:T(8,128)(2,1)S(1)}, u32[]{:S(2)}, u32[]{:S(2)}) collective-permute-start(bf16[16,4096]{1,0:T(8,128)(2,1)S(1)} %collective-permute-done.12), channel_id=1, source_target_pairs={{0,4},{4,0},{8,12},{12,8},{16,20},{20,16},{24,28},{28,24},{1,5},{5... | collective-permute-start | bytes 393224 | tf_op jit(solution)/shard_map/ppermute | solution.py:147
  24.3 5.8 %collective-permute-start.15 = (bf16[16,4096]{1,0:T(8,128)(2,1)S(1)}, bf16[16,4096]{1,0:T(8,128)(2,1)S(1)}, u32[]{:S(2)}, u32[]{:S(2)}) collective-permute-start(bf16[16,4096]{1,0:T(8,128)(2,1)S(1)} %collective-permute-done.14), channel_id=1, source_target_pairs={{0,4},{4,0},{8,12},{12,8},{16,20},{20,16},{24,28},{28,24},{1,5},{5... | collective-permute-start | bytes 393224 | tf_op jit(solution)/shard_map/ppermute | solution.py:147
  26.1 4.0 %collective-permute-start.17 = (bf16[16,4096]{1,0:T(8,128)(2,1)S(1)}, bf16[16,4096]{1,0:T(8,128)(2,1)S(1)}, u32[]{:S(2)}, u32[]{:S(2)}) collective-permute-start(bf16[16,4096]{1,0:T(8,128)(2,1)S(1)} %collective-permute-done.16), channel_id=1, source_target_pairs={{0,4},{4,0},{8,12},{12,8},{16,20},{20,16},{24,28},{28,24},{1,5},{5... | collective-permute-start | bytes 393224 | tf_op jit(solution)/shard_map/ppermute | solution.py:147
  29.4 12.4 %collective-permute-start.5 = (bf16[16,4096]{1,0:T(8,128)(2,1)S(1)}, bf16[16,4096]{1,0:T(8,128)(2,1)S(1)}, u32[]{:S(2)}, u32[]{:S(2)}) collective-permute-start(bf16[16,4096]{1,0:T(8,128)(2,1)S(1)} %collective-permute-done.4), channel_id=1, source_target_pairs={{0,4},{4,0},{8,12},{12,8},{16,20},{20,16},{24,28},{28,24},{1,5},{5... | collective-permute-start | bytes 393224 | tf_op jit(solution)/shard_map/ppermute | solution.py:147
  29.4 12.4 %collective-permute-start.7 = (bf16[16,4096]{1,0:T(8,128)(2,1)S(1)}, bf16[16,4096]{1,0:T(8,128)(2,1)S(1)}, u32[]{:S(2)}, u32[]{:S(2)}) collective-permute-start(bf16[16,4096]{1,0:T(8,128)(2,1)S(1)} %collective-permute-done.6), channel_id=1, source_target_pairs={{0,4},{4,0},{8,12},{12,8},{16,20},{20,16},{24,28},{28,24},{1,5},{5... | collective-permute-start | bytes 393224 | tf_op jit(solution)/shard_map/ppermute | solution.py:147
  29.9 12.0 %collective-permute-start.9 = (bf16[16,4096]{1,0:T(8,128)(2,1)S(1)}, bf16[16,4096]{1,0:T(8,128)(2,1)S(1)}, u32[]{:S(2)}, u32[]{:S(2)}) collective-permute-start(bf16[16,4096]{1,0:T(8,128)(2,1)S(1)} %collective-permute-done.8), channel_id=1, source_target_pairs={{0,4},{4,0},{8,12},{12,8},{16,20},{20,16},{24,28},{28,24},{1,5},{5... | collective-permute-start | bytes 393224 | tf_op jit(solution)/shard_map/ppermute | solution.py:147
  40.8 12.9 %collective-permute-start.18 = (f16[8,8,2304]{2,1,0:T(8,128)(2,1)S(1)}, f16[8,8,2304]{2,1,0:T(8,128)(2,1)S(1)}, u32[]{:S(2)}, u32[]{:S(2)}) collective-permute-start(f16[8,8,2304]{2,1,0:T(8,128)(2,1)S(1)} %fusion.22), channel_id=1, source_target_pairs={{0,1},{1,0},{2,3},{3,2},{4,5},{5,4},{6,7},{7,6},{8,9},{9,8},{10,11... | collective-permute-start | bytes 884744 | tf_op jit(solution)/shard_map/ppermute | solution.py:147
  52.6 15.5 %collective-permute-start.10 = (f16[8,8,2304]{2,1,0:T(8,128)(2,1)S(1)}, f16[8,8,2304]{2,1,0:T(8,128)(2,1)S(1)}, u32[]{:S(2)}, u32[]{:S(2)}) collective-permute-start(f16[8,8,2304]{2,1,0:T(8,128)(2,1)S(1)} %fusion.21), channel_id=1, source_target_pairs={{0,1},{1,0},{2,3},{3,2},{4,5},{5,4},{6,7},{7,6},{8,9},{9,8},{10,11... | collective-permute-start | bytes 884744 | tf_op jit(solution)/shard_map/ppermute | solution.py:147
  53.8 14.2 %collective-permute-start.19 = (f16[8,8,2304]{2,1,0:T(8,128)(2,1)S(1)}, f16[8,8,2304]{2,1,0:T(8,128)(2,1)S(1)}, u32[]{:S(2)}, u32[]{:S(2)}) collective-permute-start(f16[8,8,2304]{2,1,0:T(8,128)(2,1)S(1)} %fusion.3), channel_id=1, source_target_pairs={{0,2},{1,3},{2,0},{3,1},{4,6},{5,7},{6,4},{7,5},{8,10},{9,11},{10,... | collective-permute-start | bytes 884744 | tf_op jit(solution)/shard_map/ppermute | solution.py:147
  68.2 4.9 %collective-permute-start.20 = (bf16[2,8,2304]{2,1,0:T(8,128)(2,1)S(1)}, bf16[2,8,2304]{2,1,0:T(8,128)(2,1)S(1)}, u32[]{:S(2)}, u32[]{:S(2)}) collective-permute-start(bf16[2,8,2304]{2,1,0:T(8,128)(2,1)S(1)} %get-tuple-element.23), channel_id=1, source_target_pairs={{0,8},{4,12},{8,0},{12,4},{16,24},{20,28},{24,16},{28,20},{1,9},{5... | collective-permute-start | bytes 221192 | tf_op jit(solution)/shard_map/ppermute | solution.py:147
  69.0 5.1 %collective-permute-start.21 = (bf16[2,8,2304]{2,1,0:T(8,128)(2,1)S(1)}, bf16[2,8,2304]{2,1,0:T(8,128)(2,1)S(1)}, u32[]{:S(2)}, u32[]{:S(2)}) collective-permute-start(bf16[2,8,2304]{2,1,0:T(8,128)(2,1)S(1)} %get-tuple-element.25), channel_id=1, source_target_pairs={{0,16},{4,20},{8,24},{12,28},{16,0},{20,4},{24,8},{28,12},{1,17},{... | collective-permute-start | bytes 221192 | tf_op jit(solution)/shard_map/ppermute | solution.py:147
  70.3 5.3 %collective-permute-start.22 = (bf16[2,8,2304]{2,1,0:T(8,128)(2,1)S(1)}, bf16[2,8,2304]{2,1,0:T(8,128)(2,1)S(1)}, u32[]{:S(2)}, u32[]{:S(2)}) collective-permute-start(bf16[2,8,2304]{2,1,0:T(8,128)(2,1)S(1)} %get-tuple-element.24), channel_id=1, source_target_pairs={{0,24},{4,28},{8,16},{12,20},{16,8},{20,12},{24,0},{28,4},{1,25},{... | collective-permute-start | bytes 221192 | tf_op jit(solution)/shard_map/ppermute | solution.py:147
  75.6 1.4 collective-permute-start.23
  87.1 5.6 %collective-permute-start.24 = (bf16[8,4096]{1,0:T(8,128)(2,1)S(1)}, bf16[8,4096]{1,0:T(8,128)(2,1)S(1)}, u32[]{:S(2)}, u32[]{:S(2)}) collective-permute-start(bf16[8,4096]{1,0:T(8,128)(2,1)S(1)} %get-tuple-element.33), channel_id=1, source_target_pairs={{0,2},{1,3},{2,0},{3,1},{4,6},{5,7},{6,4},{7,5},{8,10},{9,11},{10,... | collective-permute-start | bytes 196616 | tf_op jit(solution)/shard_map/ppermute | solution.py:147
  90.5 6.2 %collective-permute-start.25 = (bf16[8,4096]{1,0:T(8,128)(2,1)S(1)}, bf16[8,4096]{1,0:T(8,128)(2,1)S(1)}, u32[]{:S(2)}, u32[]{:S(2)}) collective-permute-start(bf16[8,4096]{1,0:T(8,128)(2,1)S(1)} %get-tuple-element.32), channel_id=1, source_target_pairs={{0,3},{1,2},{2,1},{3,0},{4,7},{5,6},{6,5},{7,4},{8,11},{9,10},{10,... | collective-permute-start | bytes 196616 | tf_op jit(solution)/shard_map/ppermute | solution.py:147
  96.7 4.9 %collective-permute-start.26 = (bf16[8,4096]{1,0:T(8,128)(2,1)S(1)}, bf16[8,4096]{1,0:T(8,128)(2,1)S(1)}, u32[]{:S(2)}, u32[]{:S(2)}) collective-permute-start(bf16[8,4096]{1,0:T(8,128)(2,1)S(1)} %get-tuple-element.11), channel_id=1, source_target_pairs={{0,1},{1,0},{2,3},{3,2},{4,5},{5,4},{6,7},{7,6},{8,9},{9,8},{10,11... | collective-permute-start | bytes 196616 | tf_op jit(solution)/shard_map/ppermute | solution.py:147
  97.9 3.8 %collective-permute-start.35 = (bf16[16,4096]{1,0:T(8,128)(2,1)S(1)}, bf16[16,4096]{1,0:T(8,128)(2,1)S(1)}, u32[]{:S(2)}, u32[]{:S(2)}) collective-permute-start(bf16[16,4096]{1,0:T(8,128)(2,1)S(1)} %pad_maximum_fusion.6), channel_id=1, source_target_pairs={{0,4},{4,0},{8,12},{12,8},{16,20},{20,16},{24,28},{28,24},{1,5},{5... | collective-permute-start | bytes 393224 | tf_op jit(solution)/shard_map/ppermute | solution.py:147
  98.0 6.3 %collective-permute-start.36 = (bf16[16,4096]{1,0:T(8,128)(2,1)S(1)}, bf16[16,4096]{1,0:T(8,128)(2,1)S(1)}, u32[]{:S(2)}, u32[]{:S(2)}) collective-permute-start(bf16[16,4096]{1,0:T(8,128)(2,1)S(1)} %pad_maximum_fusion.6), channel_id=1, source_target_pairs={{0,8},{4,12},{8,0},{12,4},{16,24},{20,28},{24,16},{28,20},{1,9},{5... | collective-permute-start | bytes 393224 | tf_op jit(solution)/shard_map/ppermute | solution.py:147
  100.1 9.2 %collective-permute-start.38 = (bf16[16,4096]{1,0:T(8,128)(2,1)S(1)}, bf16[16,4096]{1,0:T(8,128)(2,1)S(1)}, u32[]{:S(2)}, u32[]{:S(2)}) collective-permute-start(bf16[16,4096]{1,0:T(8,128)(2,1)S(1)} %pad_maximum_fusion.6), channel_id=1, source_target_pairs={{0,16},{4,20},{8,24},{12,28},{16,0},{20,4},{24,8},{28,12},{1,17},{... | collective-permute-start | bytes 393224 | tf_op jit(solution)/shard_map/ppermute | solution.py:147
  100.4 8.8 %collective-permute-start.40 = (bf16[16,4096]{1,0:T(8,128)(2,1)S(1)}, bf16[16,4096]{1,0:T(8,128)(2,1)S(1)}, u32[]{:S(2)}, u32[]{:S(2)}) collective-permute-start(bf16[16,4096]{1,0:T(8,128)(2,1)S(1)} %pad_maximum_fusion.6), channel_id=1, source_target_pairs={{0,24},{4,28},{8,16},{12,20},{16,8},{20,12},{24,0},{28,4},{1,25},{... | collective-permute-start | bytes 393224 | tf_op jit(solution)/shard_map/ppermute | solution.py:147
  101.6 3.5 %collective-permute-start.27 = (bf16[16,4096]{1,0:T(8,128)(2,1)S(1)}, bf16[16,4096]{1,0:T(8,128)(2,1)S(1)}, u32[]{:S(2)}, u32[]{:S(2)}) collective-permute-start(bf16[16,4096]{1,0:T(8,128)(2,1)S(1)} %pad_maximum_fusion.7), channel_id=1, source_target_pairs={{0,4},{4,0},{8,12},{12,8},{16,20},{20,16},{24,28},{28,24},{1,5},{5... | collective-permute-start | bytes 393224 | tf_op jit(solution)/shard_map/ppermute | solution.py:147
  101.7 9.0 %collective-permute-start.28 = (bf16[16,4096]{1,0:T(8,128)(2,1)S(1)}, bf16[16,4096]{1,0:T(8,128)(2,1)S(1)}, u32[]{:S(2)}, u32[]{:S(2)}) collective-permute-start(bf16[16,4096]{1,0:T(8,128)(2,1)S(1)} %pad_maximum_fusion.7), channel_id=1, source_target_pairs={{0,8},{4,12},{8,0},{12,4},{16,24},{20,28},{24,16},{28,20},{1,9},{5... | collective-permute-start | bytes 393224 | tf_op jit(solution)/shard_map/ppermute | solution.py:147
  104.2 9.8 %collective-permute-start.30 = (bf16[16,4096]{1,0:T(8,128)(2,1)S(1)}, bf16[16,4096]{1,0:T(8,128)(2,1)S(1)}, u32[]{:S(2)}, u32[]{:S(2)}) collective-permute-start(bf16[16,4096]{1,0:T(8,128)(2,1)S(1)} %pad_maximum_fusion.7), channel_id=1, source_target_pairs={{0,16},{4,20},{8,24},{12,28},{16,0},{20,4},{24,8},{28,12},{1,17},{... | collective-permute-start | bytes 393224 | tf_op jit(solution)/shard_map/ppermute | solution.py:147
  105.2 8.9 %collective-permute-start.32 = (bf16[16,4096]{1,0:T(8,128)(2,1)S(1)}, bf16[16,4096]{1,0:T(8,128)(2,1)S(1)}, u32[]{:S(2)}, u32[]{:S(2)}) collective-permute-start(bf16[16,4096]{1,0:T(8,128)(2,1)S(1)} %pad_maximum_fusion.7), channel_id=1, source_target_pairs={{0,24},{4,28},{8,16},{12,20},{16,8},{20,12},{24,0},{28,4},{1,25},{... | collective-permute-start | bytes 393224 | tf_op jit(solution)/shard_map/ppermute | solution.py:147
  109.2 5.4 %collective-permute-start.37 = (bf16[16,4096]{1,0:T(8,128)(2,1)S(1)}, bf16[16,4096]{1,0:T(8,128)(2,1)S(1)}, u32[]{:S(2)}, u32[]{:S(2)}) collective-permute-start(bf16[16,4096]{1,0:T(8,128)(2,1)S(1)} %collective-permute-done.36), channel_id=1, source_target_pairs={{0,4},{4,0},{8,12},{12,8},{16,20},{20,16},{24,28},{28,24},{1,5},{5... | collective-permute-start | bytes 393224 | tf_op jit(solution)/shard_map/ppermute | solution.py:147
  109.2 5.5 %collective-permute-start.39 = (bf16[16,4096]{1,0:T(8,128)(2,1)S(1)}, bf16[16,4096]{1,0:T(8,128)(2,1)S(1)}, u32[]{:S(2)}, u32[]{:S(2)}) collective-permute-start(bf16[16,4096]{1,0:T(8,128)(2,1)S(1)} %collective-permute-done.38), channel_id=1, source_target_pairs={{0,4},{4,0},{8,12},{12,8},{16,20},{20,16},{24,28},{28,24},{1,5},{5... | collective-permute-start | bytes 393224 | tf_op jit(solution)/shard_map/ppermute | solution.py:147
  110.8 4.0 %collective-permute-start.41 = (bf16[16,4096]{1,0:T(8,128)(2,1)S(1)}, bf16[16,4096]{1,0:T(8,128)(2,1)S(1)}, u32[]{:S(2)}, u32[]{:S(2)}) collective-permute-start(bf16[16,4096]{1,0:T(8,128)(2,1)S(1)} %collective-permute-done.40), channel_id=1, source_target_pairs={{0,4},{4,0},{8,12},{12,8},{16,20},{20,16},{24,28},{28,24},{1,5},{5... | collective-permute-start | bytes 393224 | tf_op jit(solution)/shard_map/ppermute | solution.py:147
  114.1 10.2 %collective-permute-start.29 = (bf16[16,4096]{1,0:T(8,128)(2,1)S(1)}, bf16[16,4096]{1,0:T(8,128)(2,1)S(1)}, u32[]{:S(2)}, u32[]{:S(2)}) collective-permute-start(bf16[16,4096]{1,0:T(8,128)(2,1)S(1)} %collective-permute-done.28), channel_id=1, source_target_pairs={{0,4},{4,0},{8,12},{12,8},{16,20},{20,16},{24,28},{28,24},{1,5},{5... | collective-permute-start | bytes 393224 | tf_op jit(solution)/shard_map/ppermute | solution.py:147
  114.1 10.2 %collective-permute-start.31 = (bf16[16,4096]{1,0:T(8,128)(2,1)S(1)}, bf16[16,4096]{1,0:T(8,128)(2,1)S(1)}, u32[]{:S(2)}, u32[]{:S(2)}) collective-permute-start(bf16[16,4096]{1,0:T(8,128)(2,1)S(1)} %collective-permute-done.30), channel_id=1, source_target_pairs={{0,4},{4,0},{8,12},{12,8},{16,20},{20,16},{24,28},{28,24},{1,5},{5... | collective-permute-start | bytes 393224 | tf_op jit(solution)/shard_map/ppermute | solution.py:147
  114.6 9.8 %collective-permute-start.33 = (bf16[16,4096]{1,0:T(8,128)(2,1)S(1)}, bf16[16,4096]{1,0:T(8,128)(2,1)S(1)}, u32[]{:S(2)}, u32[]{:S(2)}) collective-permute-start(bf16[16,4096]{1,0:T(8,128)(2,1)S(1)} %collective-permute-done.32), channel_id=1, source_target_pairs={{0,4},{4,0},{8,12},{12,8},{16,20},{20,16},{24,28},{28,24},{1,5},{5... | collective-permute-start | bytes 393224 | tf_op jit(solution)/shard_map/ppermute | solution.py:147
  124.2 11.7 %collective-permute-start.42 = (f16[8,8,2048]{2,1,0:T(8,128)(2,1)S(1)}, f16[8,8,2048]{2,1,0:T(8,128)(2,1)S(1)}, u32[]{:S(2)}, u32[]{:S(2)}) collective-permute-start(f16[8,8,2048]{2,1,0:T(8,128)(2,1)S(1)} %fusion.24), channel_id=1, source_target_pairs={{0,1},{1,0},{2,3},{3,2},{4,5},{5,4},{6,7},{7,6},{8,9},{9,8},{10,11... | collective-permute-start | bytes 786440 | tf_op jit(solution)/shard_map/ppermute | solution.py:147
  133.8 13.8 %collective-permute-start.34 = (f16[8,8,2048]{2,1,0:T(8,128)(2,1)S(1)}, f16[8,8,2048]{2,1,0:T(8,128)(2,1)S(1)}, u32[]{:S(2)}, u32[]{:S(2)}) collective-permute-start(f16[8,8,2048]{2,1,0:T(8,128)(2,1)S(1)} %fusion.23), channel_id=1, source_target_pairs={{0,1},{1,0},{2,3},{3,2},{4,5},{5,4},{6,7},{7,6},{8,9},{9,8},{10,11... | collective-permute-start | bytes 786440 | tf_op jit(solution)/shard_map/ppermute | solution.py:147
  135.9 14.7 %collective-permute-start.43 = (f16[8,8,2048]{2,1,0:T(8,128)(2,1)S(1)}, f16[8,8,2048]{2,1,0:T(8,128)(2,1)S(1)}, u32[]{:S(2)}, u32[]{:S(2)}) collective-permute-start(f16[8,8,2048]{2,1,0:T(8,128)(2,1)S(1)} %fusion.16), channel_id=1, source_target_pairs={{0,2},{1,3},{2,0},{3,1},{4,6},{5,7},{6,4},{7,5},{8,10},{9,11},{10,... | collective-permute-start | bytes 786440 | tf_op jit(solution)/shard_map/ppermute | solution.py:147
  150.8 4.3 %collective-permute-start.44 = (bf16[2,8,2048]{2,1,0:T(8,128)(2,1)S(1)}, bf16[2,8,2048]{2,1,0:T(8,128)(2,1)S(1)}, u32[]{:S(2)}, u32[]{:S(2)}) collective-permute-start(bf16[2,8,2048]{2,1,0:T(8,128)(2,1)S(1)} %get-tuple-element.28), channel_id=1, source_target_pairs={{0,8},{4,12},{8,0},{12,4},{16,24},{20,28},{24,16},{28,20},{1,9},{5... | collective-permute-start | bytes 196616 | tf_op jit(solution)/shard_map/ppermute | solution.py:147
  150.9 4.3 %collective-permute-start.45 = (bf16[2,8,2048]{2,1,0:T(8,128)(2,1)S(1)}, bf16[2,8,2048]{2,1,0:T(8,128)(2,1)S(1)}, u32[]{:S(2)}, u32[]{:S(2)}) collective-permute-start(bf16[2,8,2048]{2,1,0:T(8,128)(2,1)S(1)} %get-tuple-element.30), channel_id=1, source_target_pairs={{0,16},{4,20},{8,24},{12,28},{16,0},{20,4},{24,8},{28,12},{1,17},{... | collective-permute-start | bytes 196616 | tf_op jit(solution)/shard_map/ppermute | solution.py:147
  152.1 5.2 %collective-permute-start.46 = (bf16[2,8,2048]{2,1,0:T(8,128)(2,1)S(1)}, bf16[2,8,2048]{2,1,0:T(8,128)(2,1)S(1)}, u32[]{:S(2)}, u32[]{:S(2)}) collective-permute-start(bf16[2,8,2048]{2,1,0:T(8,128)(2,1)S(1)} %get-tuple-element.29), channel_id=1, source_target_pairs={{0,24},{4,28},{8,16},{12,20},{16,8},{20,12},{24,0},{28,4},{1,25},{... | collective-permute-start | bytes 196616 | tf_op jit(solution)/shard_map/ppermute | solution.py:147
  157.3 1.4 collective-permute-start.47
  (1 other events, 7.8 us)

commit v2 on v1

--- a/solution.py
+++ b/solution.py
@@ -1,3 +1,4 @@
+import functools
 import math
 
 import jax
@@ -32,6 +33,7 @@
 
 
 PART = 128
+GROUP = 4
 
 
 def attend_kernel(lengths, query, key_new, value_new, k_cache, v_cache, out, keys, values, wide, sems):
@@ -40,32 +42,31 @@
     parts = span // PART
     scale = 1.0 / math.sqrt(HD)
 
-    def copies(row, part):
-        some = pl.ds(part * PART, PART)
+    def copies(row, count):
+        some = pl.ds(0, count)
         return (
-            pltpu.make_async_copy(
-                k_cache.at[row, some], keys.at[row, some], sems.at[row, part, 0]
-            ),
-            pltpu.make_async_copy(
-                v_cache.at[row, some], values.at[row, some], sems.at[row, part, 1]
-            ),
+            pltpu.make_async_copy(k_cache.at[row, some], keys.at[row, some], sems.at[row, 0]),
+            pltpu.make_async_copy(v_cache.at[row, some], values.at[row, some], sems.at[row, 1]),
         )
 
-    for row in range(rows):
-        for part in range(parts):
-
-            @pl.when(part * PART < lengths[row])
-            def _():
-                for copy in copies(row, part):
-                    copy.start()
-
-    wide[...] = jnp.zeros_like(wide)
-
-    def one_row(row, used):
-        count = used * PART
-        for part in range(used):
-            for copy in copies(row, part):
-                copy.wait()
+    def by_length(length, act):
+        for case in range(1, parts + 1):
+            pl.when((length + PART - 1) // PART == case)(functools.partial(act, case * PART))
+
+    def fetch(row, count):
+        for copy in copies(row, count):
+            copy.start()
+
+    def arrive(row, count):
+        for copy in copies(row, count):
+            copy.wait()
+
+    def clear(row, part):
+        values[row, part * PART : (part + 1) * PART] = jnp.zeros(
+            (PART, values.shape[2]), values.dtype
+        )
+
+    def score(row, wide, count):
         for group in range(KVH):
             heads = pl.ds(group * share, share)
             wide[heads, group * HD : (group + 1) * HD] = query[row, heads]
@@ -76,7 +77,9 @@
             preferred_element_type=jnp.float32,
         )
         position = lax.broadcasted_iota(jnp.int32, scores.shape, 1)
-        scores = jnp.where(position < lengths[row], scores * scale, -jnp.inf)
+        return jnp.where(position < lengths[row], scores * scale, -jnp.inf)
+
+    def weigh(row, scores):
         fresh_key = jnp.broadcast_to(key_new[row][:, None, :], (KVH, share, HD))
         fresh_key = fresh_key.reshape(HQ, HD).astype(jnp.float32)
         fresh = jnp.sum(query[row].astype(jnp.float32) * fresh_key, axis=1, keepdims=True) * scale
@@ -85,7 +88,9 @@
         pnew = jnp.exp(fresh - top)
         unit = 1.0 / (jnp.sum(probs, axis=1, keepdims=True) + pnew)
         weights = (probs * unit).astype(jnp.bfloat16)
-        wnew = (pnew * unit).astype(jnp.bfloat16).astype(jnp.float32)
+        return weights, (pnew * unit).astype(jnp.bfloat16).astype(jnp.float32)
+
+    def mix(row, weights, wnew, count):
         mixed = jnp.dot(weights, values[row, :count], preferred_element_type=jnp.float32)
         for group in range(KVH):
             heads = slice(group * share, (group + 1) * share)
@@ -93,14 +98,30 @@
             own = own + wnew[heads] * value_new[row, group : group + 1]
             out[row, heads] = own.astype(out.dtype)
 
+    def group(row, count):
+        each = [row + at for at in range(GROUP)]
+        for one in each:
+            by_length(lengths[one], functools.partial(arrive, one))
+            for part in range(1, count // PART):
+                pl.when(lengths[one] <= part * PART)(functools.partial(clear, one, part))
+        scores = [score(one, wide.at[at], count) for at, one in enumerate(each)]
+        weighed = [weigh(one, of_one) for one, of_one in zip(each, scores)]
+        for one, (weights, wnew) in zip(each, weighed):
+            mix(one, weights, wnew, count)
+
     @pl.loop(0, rows)
     def _(row):
-        used = (lengths[row] + PART - 1) // PART
-        for case in range(1, parts + 1):
-
-            @pl.when(used == case)
-            def _():
-                one_row(row, case)
+        by_length(lengths[row], functools.partial(fetch, row))
+
+    wide[...] = jnp.zeros_like(wide)
+
+    @pl.loop(0, rows // GROUP)
+    def _(index):
+        row = index * GROUP
+        longest = lengths[row]
+        for at in range(1, GROUP):
+            longest = jnp.maximum(longest, lengths[row + at])
+        by_length(longest, functools.partial(group, row))
 
 
 def attend_local(owned, k_cache, v_cache, lengths):
@@ -129,8 +150,8 @@
         scratch_shapes=[
             pltpu.VMEM((rows, span, width), jnp.bfloat16),
             pltpu.VMEM((rows, span, width), jnp.bfloat16),
-            pltpu.VMEM((HQ, width), jnp.bfloat16),
-            pltpu.SemaphoreType.DMA((rows, span // PART, 2)),
+            pltpu.VMEM((GROUP, HQ, width), jnp.bfloat16),
+            pltpu.SemaphoreType.DMA((rows, 2)),
         ],
         compiler_params=pltpu.CompilerParams(vmem_limit_bytes=ROOM),
         cost_estimate=pl.CostEstimate(
@@ -159,68 +180,104 @@
     return jnp.concatenate(halves, axis=1)
 
 
-def multiply_kernel(rows_ref, weights_ref, out_ref):
-    out_ref[...] = jnp.dot(
-        rows_ref[...], weights_ref[...], preferred_element_type=jnp.float32
-    )
-
-
-def multiply(rows, weights):
-    count, depth = rows.shape
-    columns = weights.shape[1]
-    tile = 256 if columns % 256 == 0 else columns
+def multiply_kernel(start, far, near, weights, out, held, sems):
+    parts, depth, columns = held.shape
+
+    def copy(part):
+        return pltpu.make_async_copy(
+            weights.at[pl.ds(part * depth, depth), pl.ds(start, columns)],
+            held.at[part],
+            sems.at[part],
+        )
+
+    for part in range(parts):
+        copy(part).start()
+    out[...] = jnp.zeros_like(out)
+
+    @pl.loop(0, parts)
+    def _(part):
+        copy(part).wait()
+        some = pl.ds(pl.multiple_of(part * depth, depth), depth)
+        rows = jnp.concatenate([far[:, some], near[:, some]], axis=0)
+        out[...] += jnp.dot(rows, held[part], preferred_element_type=jnp.float32)
+
+
+def multiply(far, near, weights, start, columns):
+    half, width = far.shape
+    depth = 512
+    vmem = pl.BlockSpec(memory_space=pltpu.VMEM)
     return pl.pallas_call(
-        multiply_kernel,
-        grid=(columns // tile,),
-        in_specs=[
-            pl.BlockSpec(memory_space=pltpu.VMEM),
-            pl.BlockSpec((depth, tile), lambda j: (0, j)),
+        functools.partial(multiply_kernel, start),
+        in_specs=[vmem, vmem, pl.BlockSpec(memory_space=pl.ANY)],
+        out_specs=vmem,
+        out_shape=jax.ShapeDtypeStruct((2 * half, columns), jnp.float32),
+        scratch_shapes=[
+            pltpu.VMEM((width // depth, depth, columns), jnp.bfloat16),
+            pltpu.SemaphoreType.DMA((width // depth,)),
         ],
-        out_specs=pl.BlockSpec((count, tile), lambda j: (0, j)),
-        out_shape=jax.ShapeDtypeStruct((count, columns), jnp.float32),
         compiler_params=pltpu.CompilerParams(vmem_limit_bytes=ROOM),
         cost_estimate=pl.CostEstimate(
-            flops=2 * count * depth * columns,
-            bytes_accessed=2 * depth * columns,
+            flops=4 * half * width * columns,
+            bytes_accessed=2 * width * columns,
             transcendentals=0,
         ),
-    )(rows, weights)
+    )(far, near, weights)
 
 
 def project(rows, weights, scale):
-    width = weights.shape[0]
+    width, columns = weights.shape
     here = lax.axis_index("gy")
 
     def features(owner):
         return lax.dynamic_slice_in_dim(rows, owner * width, width, axis=1)
 
-    def send(values, bit):
-        packed = (values * scale).astype(jnp.float16)
+    def pack(values):
+        return (values * scale).astype(jnp.float16)
+
+    def send(packed, bit):
         return swap(packed, "gy", bit).astype(jnp.float32) * (1.0 / scale)
 
-    far = jnp.concatenate([swap(features(here ^ bit), "gy", bit) for bit in (2, 3)])
-    near, far = lax.optimization_barrier((features(here ^ 1), far))
-    near = jnp.concatenate([features(here), swap(near, "gy", 1)])
-    far = all_rows(far)
+    near, far, last = (swap(features(here ^ bit), "gy", bit) for bit in (1, 2, 3))
+    near = jnp.concatenate([features(here), near])
+    far = all_rows(jnp.concatenate([far, last]))
     near = all_rows(near)
-    shape = far.shape[:3] + weights.shape[1:]
-    far = multiply(far.reshape(-1, width), weights).reshape(shape)
-    pair = far[0] + send(far[1], 1)
-    near = multiply(near.reshape(-1, width), weights).reshape(shape)
-    return near[0] + send(near[1], 1) + send(pair, 2)
-
-
-def deliver(columns):
+    shape = (2, 2) + far.shape[1:3]
+    far = far.reshape(-1, width)
+    near = near.reshape(-1, width)
+    first = columns // 512 * 256 if columns % 256 == 0 else columns
+    left = multiply(far, near, weights, 0, first).reshape(shape + (first,))
+    go_left = pack(left[:, 1])
+    go_left, far, near = lax.optimization_barrier((go_left, far, near))
+    left = left[:, 0] + send(go_left, 1)
+    if first == columns:
+        return [left[1] + send(pack(left[0]), 2)]
+    right = multiply(far, near, weights, first, columns - first)
+    right = right.reshape(shape + (columns - first,))
+    go_far = pack(right[0, 1])
+    across, go_near = lax.optimization_barrier((pack(left[0]), pack(right[1, 1])))
+    left = left[1] + send(across, 2)
+    across = pack(right[0, 0] + send(go_far, 1))
+    right = right[1, 0] + send(go_near, 1) + send(across, 2)
+    return [left, right]
+
+
+def collect(columns):
+    columns = columns.astype(jnp.bfloat16)
     count, rows, width = columns.shape
     if count != 8:
-        owned = lax.all_to_all(columns, "gx", split_axis=0, concat_axis=0)
-    else:
-        pairs = [columns[:2]] + [
-            swap(columns[chip : chip + 2], "gx", chip) for chip in (2, 4, 6)
-        ]
-        theirs = swap(jnp.stack([pair[1] for pair in pairs]), "gx", 1)
-        owned = jnp.stack([pair[0] for pair in pairs])
-        owned = jnp.stack([owned, theirs], axis=1).reshape(count, rows, width)
+        return lax.all_to_all(columns, "gx", split_axis=0, concat_axis=0)
+    pairs = [columns[:2]] + [
+        swap(columns[chip : chip + 2], "gx", chip) for chip in (2, 4, 6)
+    ]
+    theirs = swap(jnp.stack([pair[1] for pair in pairs]), "gx", 1)
+    owned = jnp.stack([pair[0] for pair in pairs])
+    return jnp.stack([owned, theirs], axis=1).reshape(count, rows, width)
+
+
+def deliver(parts):
+    owned = jnp.concatenate([collect(part) for part in parts], axis=-1)
+    count, rows, width = owned.shape
+    if count == 8:
         owned = owned[jnp.arange(count) ^ lax.axis_index("gx")]
     return owned.transpose(1, 0, 2).reshape(rows, count * width)
 
@@ -247,10 +304,10 @@
         widened * lax.rsqrt(jnp.mean(widened * widened, axis=-1, keepdims=True) + eps) * norm_gain
     ).astype(jnp.bfloat16)
     qkv = project(normed, w_qkv, 32.0)
-    owned = deliver(qkv.astype(jnp.bfloat16))
+    owned = deliver(qkv)
     attended = attend_local(owned, k_cache, v_cache, lengths)
     scaled, unit = level(attended)
-    out = deliver(project(scaled, w_out, 8.0).astype(jnp.bfloat16))
+    out = deliver(project(scaled, w_out, 8.0))
     return (out.astype(jnp.float32) * unit).astype(jnp.bfloat16)
 
 

time: 161 us -> 138 us (0.86)
  Pallas kernels: 48 us -> 24.7 us
  waiting for transfers between devices: 56.3 us -> 42.9 us
  starting transfers between devices: 48.2 us -> 61.4 us
    pallas_call x4, Pallas kernels: 39.9 us -> 20.3 us  [multiply(): pl.pallas_call(functools.partial(multiply_kernel, start), in_specs=[vmem,...]
    ppermute x48 -> x60, waiting for transfers between devices: 56.3 us -> 42.9 us  [swap(): return lax.ppermute(block, axis, [(i, i ^ bit) for i in range(count)])]
    ppermute x48 -> x60, starting transfers between devices: 48.2 us -> 61.4 us  [swap(): return lax.ppermute(block, axis, [(i, i ^ bit) for i in range(count)])]
    pallas_call x1, Pallas kernels: 8.09 us -> 4.41 us  [attend_local(): pl.pallas_call(attend_kernel, in_specs=[pl.BlockSpec(memory_space=pltpu.S...]
  transfers between devices with their start and end apart: 48 -> 60, of which waited for: 24 -> 27; matrix products, arithmetic and copies ran while one was open for 1% -> 1% of each run, Pallas kernels for 25% -> 8%
where the time goes in v2:
time: 138 us
  starting transfers between devices  61.4 us (44%)
  waiting for transfers between devices  42.9 us (31%)
  Pallas kernels  24.7 us (18%)
  other arithmetic  6.03 us (4%)
  local copies, waits for them, and re-layouts  1.76 us (1%)
    ppermute x60, starting transfers between devices, swap(): return lax.ppermute(block, axis, [(i, i ^ bit) for i in range(count)])  61.4 us
    ppermute x60, waiting for transfers between devices, swap(): return lax.ppermute(block, axis, [(i, i ^ bit) for i in range(count)])  42.9 us
    pallas_call x4, Pallas kernels, multiply(): pl.pallas_call(functools.partial(multiply_kernel, start), in_specs=[vmem,...  20.3 us
    pallas_call x1, Pallas kernels, attend_local(): pl.pallas_call(attend_kernel, in_specs=[pl.BlockSpec(memory_space=pltpu.S...  4.41 us
  transfers between devices with their start and end apart: 60, of which 27 were waited for; matrix products, arithmetic and copies ran while one was open for 1% of the time, Pallas kernels for 8%

profile of v2, /device:TPU:0, one launch (start us, length us, event | category | flops | bytes accessed | tf_op | source)
XLA Modules:
  0.0 137.8 jit_solution(10951684692658893874)
XLA Ops:
  0.0 1.2 fusion
  1.2 1.1 fusion.2
  2.3 3.1 %collective-permute-start.9 = (bf16[8,4096]{1,0:T(8,128)(2,1)S(1)}, bf16[8,4096]{1,0:T(8,128)(2,1)S(1)}, u32[]{:S(2)}, u32[]{:S(2)}) collective-permute-start(bf16[8,4096]{1,0:T(8,128)(2,1)S(1)} %get-tuple-element.42), channel_id=1, source_target_pairs={{0,1},{1,0},{2,3},{3,2},{4,5},{5,4},{6,7},{7,6},{8,9},{9,8},{10,11... | collective-permute-start | bytes 196616 | tf_op jit(solution)/shard_map/ppermute | solution.py:168
  5.4 2.6 %collective-permute-start = (bf16[8,4096]{1,0:T(8,128)(2,1)S(1)}, bf16[8,4096]{1,0:T(8,128)(2,1)S(1)}, u32[]{:S(2)}, u32[]{:S(2)}) collective-permute-start(bf16[8,4096]{1,0:T(8,128)(2,1)S(1)} %get-tuple-element.44), channel_id=1, source_target_pairs={{0,2},{1,3},{2,0},{3,1},{4,6},{5,7},{6,4},{7,5},{8,10},{9,11},{10,... | collective-permute-start | bytes 196616 | tf_op jit(solution)/shard_map/ppermute | solution.py:168
  8.9 1.8 %collective-permute-start.11 = (bf16[16,4096]{1,0:T(8,128)(2,1)S(1)}, bf16[16,4096]{1,0:T(8,128)(2,1)S(1)}, u32[]{:S(2)}, u32[]{:S(2)}) collective-permute-start(bf16[16,4096]{1,0:T(8,128)(2,1)S(1)} %pad_maximum_fusion.4), channel_id=1, source_target_pairs={{0,8},{4,12},{8,0},{12,4},{16,24},{20,28},{24,16},{28,20},{1,9},{5... | collective-permute-start | bytes 393224 | tf_op jit(solution)/shard_map/ppermute | solution.py:168
  10.7 1.5 %collective-permute-start.13 = (bf16[16,4096]{1,0:T(8,128)(2,1)S(1)}, bf16[16,4096]{1,0:T(8,128)(2,1)S(1)}, u32[]{:S(2)}, u32[]{:S(2)}) collective-permute-start(bf16[16,4096]{1,0:T(8,128)(2,1)S(1)} %pad_maximum_fusion.4), channel_id=1, source_target_pairs={{0,16},{4,20},{8,24},{12,28},{16,0},{20,4},{24,8},{28,12},{1,17},{... | collective-permute-start | bytes 393224 | tf_op jit(solution)/shard_map/ppermute | solution.py:168
  12.7 2.4 %collective-permute-start.15 = (bf16[16,4096]{1,0:T(8,128)(2,1)S(1)}, bf16[16,4096]{1,0:T(8,128)(2,1)S(1)}, u32[]{:S(2)}, u32[]{:S(2)}) collective-permute-start(bf16[16,4096]{1,0:T(8,128)(2,1)S(1)} %pad_maximum_fusion.4), channel_id=1, source_target_pairs={{0,24},{4,28},{8,16},{12,20},{16,8},{20,12},{24,0},{28,4},{1,25},{... | collective-permute-start | bytes 393224 | tf_op jit(solution)/shard_map/ppermute | solution.py:168
  15.9 1.5 %collective-permute-start.5 = (bf16[16,4096]{1,0:T(8,128)(2,1)S(1)}, bf16[16,4096]{1,0:T(8,128)(2,1)S(1)}, u32[]{:S(2)}, u32[]{:S(2)}) collective-permute-start(bf16[16,4096]{1,0:T(8,128)(2,1)S(1)} %constant_dynamic-update-slice_fusion), channel_id=1, source_target_pairs={{0,16},{4,20},{8,24},{12,28},{16,0},{20,4},{24,8},{28,12},{1,17},{... | collective-permute-start | bytes 393224 | tf_op jit(solution)/shard_map/ppermute | solution.py:168
  17.4 1.6 %collective-permute-start.7 = (bf16[16,4096]{1,0:T(8,128)(2,1)S(1)}, bf16[16,4096]{1,0:T(8,128)(2,1)S(1)}, u32[]{:S(2)}, u32[]{:S(2)}) collective-permute-start(bf16[16,4096]{1,0:T(8,128)(2,1)S(1)} %constant_dynamic-update-slice_fusion), channel_id=1, source_target_pairs={{0,24},{4,28},{8,16},{12,20},{16,8},{20,12},{24,0},{28,4},{1,25},{... | collective-permute-start | bytes 393224 | tf_op jit(solution)/shard_map/ppermute | solution.py:168
  19.0 2.7 %collective-permute-done.3 = bf16[16,4096]{1,0:T(8,128)(2,1)S(1)} collective-permute-done((bf16[16,4096]{1,0:T(8,128)(2,1)S(1)}, bf16[16,4096]{1,0:T(8,128)(2,1)S(1)}, u32[]{:S(2)}, u32[]{:S(2)}) %collective-permute-start.3) | collective-permute-done | bytes 131104 | tf_op jit(solution)/shard_map/ppermute | solution.py:168
  22.4 2.3 %collective-permute-done.5 = bf16[16,4096]{1,0:T(8,128)(2,1)S(1)} collective-permute-done((bf16[16,4096]{1,0:T(8,128)(2,1)S(1)}, bf16[16,4096]{1,0:T(8,128)(2,1)S(1)}, u32[]{:S(2)}, u32[]{:S(2)}) %collective-permute-start.5) | collective-permute-done | bytes 131104 | tf_op jit(solution)/shard_map/ppermute | solution.py:168
  26.6 4.9 %shard_map.73 = f32[256,1024]{1,0:T(8,128)S(1)} custom-call(bf16[128,4096]{1,0:T(8,128)(2,1)S(1)} %bitcast.248, bf16[128,4096]{1,0:T(8,128)(2,1)S(1)} %bitcast.250, bf16[4096,2304]{1,0:T(8,128)(2,1)} %weights.5), custom_call_target="tpu_custom_call" | custom-call | flops 2147483648 | bytes 8388608 | tf_op jit(solution)/shard_map/pallas_call | solution.py:209
  32.3 5.6 %shard_map.74 = f32[256,1280]{1,0:T(8,128)S(1)} custom-call(bf16[128,4096]{1,0:T(8,128)(2,1)S(1)} %bitcast.249, bf16[128,4096]{1,0:T(8,128)(2,1)S(1)} %bitcast.251, bf16[4096,2304]{1,0:T(8,128)(2,1)} %weights.5), custom_call_target="tpu_custom_call" | custom-call | flops 2684354560 | bytes 10485760 | tf_op jit(solution)/shard_map/pallas_call | solution.py:209
  38.0 1.4 %collective-permute-start.24 = (f16[8,8,1280]{2,1,0:T(8,128)(2,1)S(1)}, f16[8,8,1280]{2,1,0:T(8,128)(2,1)S(1)}, u32[]{:S(2)}, u32[]{:S(2)}) collective-permute-start(f16[8,8,1280]{2,1,0:T(8,128)(2,1)S(1)} %get-tuple-element.30), channel_id=1, source_target_pairs={{0,1},{1,0},{2,3},{3,2},{4,5},{5,4},{6,7},{7,6},{8,9},{9,8},{10,11... | collective-permute-start | bytes 491528 | tf_op jit(solution)/shard_map/ppermute | solution.py:168
  40.1 2.5 %collective-permute-start.18 = (f16[8,8,1024]{2,1,0:T(8,128)(2,1)S(1)}, f16[8,8,1024]{2,1,0:T(8,128)(2,1)S(1)}, u32[]{:S(2)}, u32[]{:S(2)}) collective-permute-start(f16[8,8,1024]{2,1,0:T(8,128)(2,1)S(1)} %fusion.37), channel_id=1, source_target_pairs={{0,2},{1,3},{2,0},{3,1},{4,6},{5,7},{6,4},{7,5},{8,10},{9,11},{10,... | collective-permute-start | bytes 393224 | tf_op jit(solution)/shard_map/ppermute | solution.py:168
  42.6 4.2 %collective-permute-done.24 = f16[8,8,1280]{2,1,0:T(8,128)(2,1)S(1)} collective-permute-done((f16[8,8,1280]{2,1,0:T(8,128)(2,1)S(1)}, f16[8,8,1280]{2,1,0:T(8,128)(2,1)S(1)}, u32[]{:S(2)}, u32[]{:S(2)}) %collective-permute-start.24) | collective-permute-done | bytes 163872 | tf_op jit(solution)/shard_map/ppermute | solution.py:168
  46.9 1.8 %collective-permute-start.25 = (f16[8,8,1280]{2,1,0:T(8,128)(2,1)S(1)}, f16[8,8,1280]{2,1,0:T(8,128)(2,1)S(1)}, u32[]{:S(2)}, u32[]{:S(2)}) collective-permute-start(f16[8,8,1280]{2,1,0:T(8,128)(2,1)S(1)} %fusion.14), channel_id=1, source_target_pairs={{0,2},{1,3},{2,0},{3,1},{4,6},{5,7},{6,4},{7,5},{8,10},{9,11},{10,... | collective-permute-start | bytes 491528 | tf_op jit(solution)/shard_map/ppermute | solution.py:168
  48.8 1.4 %collective-permute-start.19 = (bf16[2,8,1024]{2,1,0:T(8,128)(2,1)S(1)}, bf16[2,8,1024]{2,1,0:T(8,128)(2,1)S(1)}, u32[]{:S(2)}, u32[]{:S(2)}) collective-permute-start(bf16[2,8,1024]{2,1,0:T(8,128)(2,1)S(1)} %get-tuple-element.62), channel_id=1, source_target_pairs={{0,8},{4,12},{8,0},{12,4},{16,24},{20,28},{24,16},{28,20},{1,9},{5... | collective-permute-start | bytes 98312 | tf_op jit(solution)/shard_map/ppermute | solution.py:168
  51.1 1.3 collective-permute-start.21
  52.4 4.3 %collective-permute-done.25 = f16[8,8,1280]{2,1,0:T(8,128)(2,1)S(1)} collective-permute-done((f16[8,8,1280]{2,1,0:T(8,128)(2,1)S(1)}, f16[8,8,1280]{2,1,0:T(8,128)(2,1)S(1)}, u32[]{:S(2)}, u32[]{:S(2)}) %collective-permute-start.25) | collective-permute-done | bytes 163872 | tf_op jit(solution)/shard_map/ppermute | solution.py:168
  57.4 1.4 %collective-permute-start.26 = (bf16[2,8,1280]{2,1,0:T(8,128)(2,1)S(1)}, bf16[2,8,1280]{2,1,0:T(8,128)(2,1)S(1)}, u32[]{:S(2)}, u32[]{:S(2)}) collective-permute-start(bf16[2,8,1280]{2,1,0:T(8,128)(2,1)S(1)} %get-tuple-element.47), channel_id=1, source_target_pairs={{0,8},{4,12},{8,0},{12,4},{16,24},{20,28},{24,16},{28,20},{1,9},{5... | collective-permute-start | bytes 122888 | tf_op jit(solution)/shard_map/ppermute | solution.py:168
  59.7 1.3 collective-permute-start.28
  61.4 1.5 %collective-permute-done.27 = bf16[2,8,1280]{2,1,0:T(8,128)(2,1)S(1)} collective-permute-done((bf16[2,8,1280]{2,1,0:T(8,128)(2,1)S(1)}, bf16[2,8,1280]{2,1,0:T(8,128)(2,1)S(1)}, u32[]{:S(2)}, u32[]{:S(2)}) %collective-permute-start.27) | collective-permute-done | bytes 40992 | tf_op jit(solution)/shard_map/ppermute | solution.py:168
  62.9 1.7 %collective-permute-done.28 = bf16[2,8,1280]{2,1,0:T(8,128)(2,1)S(1)} collective-permute-done((bf16[2,8,1280]{2,1,0:T(8,128)(2,1)S(1)}, bf16[2,8,1280]{2,1,0:T(8,128)(2,1)S(1)}, u32[]{:S(2)}, u32[]{:S(2)}) %collective-permute-start.28) | collective-permute-done | bytes 40992 | tf_op jit(solution)/shard_map/ppermute | solution.py:168
  64.7 1.2 collective-permute-done.29
  67.3 4.4 %shard_map.75 = bf16[8,128,128]{2,1,0:T(8,128)(2,1)S(1)} custom-call(s32[8]{0:T(128)S(1)} %copy-done, bf16[8,128,128]{2,1,0:T(8,128)(2,1)S(1)} %pad_maximum_fusion.1.query, bf16[8,8,128]{2,1,0:T(8,128)(2,1)S(1)} %pad_maximum_fusion.13.key_new, f32[8,8,128]{2,1,0:T(8,128)S(1)} %get-tuple-element.93.value_new, bf16[8,512,1024]{2,1,0:T(8,128)(2,1)} %k_cache.1, ...), custom_call_target="tpu_custom_call" | custom-call | flops 2147483648 | bytes 8388608 | tf_op jit(solution)/shard_map/pallas_call | solution.py:138
  72.3 3.0 %collective-permute-start.39 = (bf16[8,4096]{1,0:T(8,128)(2,1)S(1)}, bf16[8,4096]{1,0:T(8,128)(2,1)S(1)}, u32[]{:S(2)}, u32[]{:S(2)}) collective-permute-start(bf16[8,4096]{1,0:T(8,128)(2,1)S(1)} %get-tuple-element.38), channel_id=1, source_target_pairs={{0,1},{1,0},{2,3},{3,2},{4,5},{5,4},{6,7},{7,6},{8,9},{9,8},{10,11... | collective-permute-start | bytes 196616 | tf_op jit(solution)/shard_map/ppermute | solution.py:168
  75.3 2.9 %collective-permute-start.30 = (bf16[8,4096]{1,0:T(8,128)(2,1)S(1)}, bf16[8,4096]{1,0:T(8,128)(2,1)S(1)}, u32[]{:S(2)}, u32[]{:S(2)}) collective-permute-start(bf16[8,4096]{1,0:T(8,128)(2,1)S(1)} %get-tuple-element.40), channel_id=1, source_target_pairs={{0,2},{1,3},{2,0},{3,1},{4,6},{5,7},{6,4},{7,5},{8,10},{9,11},{10,... | collective-permute-start | bytes 196616 | tf_op jit(solution)/shard_map/ppermute | solution.py:168
  78.9 1.5 %collective-permute-start.41 = (bf16[16,4096]{1,0:T(8,128)(2,1)S(1)}, bf16[16,4096]{1,0:T(8,128)(2,1)S(1)}, u32[]{:S(2)}, u32[]{:S(2)}) collective-permute-start(bf16[16,4096]{1,0:T(8,128)(2,1)S(1)} %pad_maximum_fusion.6), channel_id=1, source_target_pairs={{0,8},{4,12},{8,0},{12,4},{16,24},{20,28},{24,16},{28,20},{1,9},{5... | collective-permute-start | bytes 393224 | tf_op jit(solution)/shard_map/ppermute | solution.py:168
  80.4 1.4 %collective-permute-start.43 = (bf16[16,4096]{1,0:T(8,128)(2,1)S(1)}, bf16[16,4096]{1,0:T(8,128)(2,1)S(1)}, u32[]{:S(2)}, u32[]{:S(2)}) collective-permute-start(bf16[16,4096]{1,0:T(8,128)(2,1)S(1)} %pad_maximum_fusion.6), channel_id=1, source_target_pairs={{0,16},{4,20},{8,24},{12,28},{16,0},{20,4},{24,8},{28,12},{1,17},{... | collective-permute-start | bytes 393224 | tf_op jit(solution)/shard_map/ppermute | solution.py:168
  82.5 2.2 %collective-permute-done.31 = bf16[8,4096]{1,0:T(8,128)(2,1)S(1)} collective-permute-done((bf16[8,4096]{1,0:T(8,128)(2,1)S(1)}, bf16[8,4096]{1,0:T(8,128)(2,1)S(1)}, u32[]{:S(2)}, u32[]{:S(2)}) %collective-permute-start.31) | collective-permute-done | bytes 65568 | tf_op jit(solution)/shard_map/ppermute | solution.py:168
  84.9 1.8 %collective-permute-start.33 = (bf16[16,4096]{1,0:T(8,128)(2,1)S(1)}, bf16[16,4096]{1,0:T(8,128)(2,1)S(1)}, u32[]{:S(2)}, u32[]{:S(2)}) collective-permute-start(bf16[16,4096]{1,0:T(8,128)(2,1)S(1)} %constant_dynamic-update-slice_fusion.2), channel_id=1, source_target_pairs={{0,8},{4,12},{8,0},{12,4},{16,24},{20,28},{24,16},{28,20},{1,9},{5... | collective-permute-start | bytes 393224 | tf_op jit(solution)/shard_map/ppermute | solution.py:168
  86.7 1.8 %collective-permute-start.37 = (bf16[16,4096]{1,0:T(8,128)(2,1)S(1)}, bf16[16,4096]{1,0:T(8,128)(2,1)S(1)}, u32[]{:S(2)}, u32[]{:S(2)}) collective-permute-start(bf16[16,4096]{1,0:T(8,128)(2,1)S(1)} %constant_dynamic-update-slice_fusion.2), channel_id=1, source_target_pairs={{0,24},{4,28},{8,16},{12,20},{16,8},{20,12},{24,0},{28,4},{1,25},{... | collective-permute-start | bytes 393224 | tf_op jit(solution)/shard_map/ppermute | solution.py:168
  88.6 2.2 %collective-permute-done.33 = bf16[16,4096]{1,0:T(8,128)(2,1)S(1)} collective-permute-done((bf16[16,4096]{1,0:T(8,128)(2,1)S(1)}, bf16[16,4096]{1,0:T(8,128)(2,1)S(1)}, u32[]{:S(2)}, u32[]{:S(2)}) %collective-permute-start.33) | collective-permute-done | bytes 131104 | tf_op jit(solution)/shard_map/ppermute | solution.py:168
  91.5 3.6 %collective-permute-done.35 = bf16[16,4096]{1,0:T(8,128)(2,1)S(1)} collective-permute-done((bf16[16,4096]{1,0:T(8,128)(2,1)S(1)}, bf16[16,4096]{1,0:T(8,128)(2,1)S(1)}, u32[]{:S(2)}, u32[]{:S(2)}) %collective-permute-start.35) | collective-permute-done | bytes 131104 | tf_op jit(solution)/shard_map/ppermute | solution.py:168
  97.0 4.9 %shard_map.76 = f32[256,1024]{1,0:T(8,128)S(1)} custom-call(bf16[128,4096]{1,0:T(8,128)(2,1)S(1)} %bitcast.244, bf16[128,4096]{1,0:T(8,128)(2,1)S(1)} %bitcast.246, bf16[4096,2048]{1,0:T(8,128)(2,1)} %weights.7), custom_call_target="tpu_custom_call" | custom-call | flops 2147483648 | bytes 8388608 | tf_op jit(solution)/shard_map/pallas_call | solution.py:209
  102.8 4.9 %shard_map.77 = f32[256,1024]{1,0:T(8,128)S(1)} custom-call(bf16[128,4096]{1,0:T(8,128)(2,1)S(1)} %bitcast.245, bf16[128,4096]{1,0:T(8,128)(2,1)S(1)} %bitcast.247, bf16[4096,2048]{1,0:T(8,128)(2,1)} %weights.7), custom_call_target="tpu_custom_call" | custom-call | flops 2147483648 | bytes 8388608 | tf_op jit(solution)/shard_map/pallas_call | solution.py:209
  107.8 1.3 collective-permute-start.54
  109.1 1.3 collective-permute-done.47
  110.6 2.8 %collective-permute-start.48 = (f16[8,8,1024]{2,1,0:T(8,128)(2,1)S(1)}, f16[8,8,1024]{2,1,0:T(8,128)(2,1)S(1)}, u32[]{:S(2)}, u32[]{:S(2)}) collective-permute-start(f16[8,8,1024]{2,1,0:T(8,128)(2,1)S(1)} %fusion.38), channel_id=1, source_target_pairs={{0,2},{1,3},{2,0},{3,1},{4,6},{5,7},{6,4},{7,5},{8,10},{9,11},{10,... | collective-permute-start | bytes 393224 | tf_op jit(solution)/shard_map/ppermute | solution.py:168
  113.4 4.6 %collective-permute-start.55 = (f16[8,8,1024]{2,1,0:T(8,128)(2,1)S(1)}, f16[8,8,1024]{2,1,0:T(8,128)(2,1)S(1)}, u32[]{:S(2)}, u32[]{:S(2)}) collective-permute-start(f16[8,8,1024]{2,1,0:T(8,128)(2,1)S(1)} %fusion.24), channel_id=1, source_target_pairs={{0,2},{1,3},{2,0},{3,1},{4,6},{5,7},{6,4},{7,5},{8,10},{9,11},{10,... | collective-permute-start | bytes 393224 | tf_op jit(solution)/shard_map/ppermute | solution.py:168
  118.1 4.6 %collective-permute-done.48 = f16[8,8,1024]{2,1,0:T(8,128)(2,1)S(1)} collective-permute-done((f16[8,8,1024]{2,1,0:T(8,128)(2,1)S(1)}, f16[8,8,1024]{2,1,0:T(8,128)(2,1)S(1)}, u32[]{:S(2)}, u32[]{:S(2)}) %collective-permute-start.48) | collective-permute-done | bytes 131104 | tf_op jit(solution)/shard_map/ppermute | solution.py:168
  122.8 1.1 collective-permute-start.49
  123.8 1.4 %collective-permute-done.55 = f16[8,8,1024]{2,1,0:T(8,128)(2,1)S(1)} collective-permute-done((f16[8,8,1024]{2,1,0:T(8,128)(2,1)S(1)}, f16[8,8,1024]{2,1,0:T(8,128)(2,1)S(1)}, u32[]{:S(2)}, u32[]{:S(2)}) %collective-permute-start.55) | collective-permute-done | bytes 131104 | tf_op jit(solution)/shard_map/ppermute | solution.py:168
  126.6 1.8 %collective-permute-start.51 = (bf16[2,8,1024]{2,1,0:T(8,128)(2,1)S(1)}, bf16[2,8,1024]{2,1,0:T(8,128)(2,1)S(1)}, u32[]{:S(2)}, u32[]{:S(2)}) collective-permute-start(bf16[2,8,1024]{2,1,0:T(8,128)(2,1)S(1)} %get-tuple-element.53), channel_id=1, source_target_pairs={{0,24},{4,28},{8,16},{12,20},{16,8},{20,12},{24,0},{28,4},{1,25},{... | collective-permute-start | bytes 98312 | tf_op jit(solution)/shard_map/ppermute | solution.py:168
  130.1 1.8 %collective-permute-start.58 = (bf16[2,8,1024]{2,1,0:T(8,128)(2,1)S(1)}, bf16[2,8,1024]{2,1,0:T(8,128)(2,1)S(1)}, u32[]{:S(2)}, u32[]{:S(2)}) collective-permute-start(bf16[2,8,1024]{2,1,0:T(8,128)(2,1)S(1)} %get-tuple-element.58), channel_id=1, source_target_pairs={{0,24},{4,28},{8,16},{12,20},{16,8},{20,12},{24,0},{28,4},{1,25},{... | collective-permute-start | bytes 98312 | tf_op jit(solution)/shard_map/ppermute | solution.py:168
  133.4 1.6 %collective-permute-done.58 = bf16[2,8,1024]{2,1,0:T(8,128)(2,1)S(1)} collective-permute-done((bf16[2,8,1024]{2,1,0:T(8,128)(2,1)S(1)}, bf16[2,8,1024]{2,1,0:T(8,128)(2,1)S(1)}, u32[]{:S(2)}, u32[]{:S(2)}) %collective-permute-start.58) | collective-permute-done | bytes 32800 | tf_op jit(solution)/shard_map/ppermute | solution.py:168
  135.1 1.2 collective-permute-done.59
  (194 shorter events, 22.3 us)
Async XLA Ops:
  2.3 6.5 %collective-permute-start.9 = (bf16[8,4096]{1,0:T(8,128)(2,1)S(1)}, bf16[8,4096]{1,0:T(8,128)(2,1)S(1)}, u32[]{:S(2)}, u32[]{:S(2)}) collective-permute-start(bf16[8,4096]{1,0:T(8,128)(2,1)S(1)} %get-tuple-element.42), channel_id=1, source_target_pairs={{0,1},{1,0},{2,3},{3,2},{4,5},{5,4},{6,7},{7,6},{8,9},{9,8},{10,11... | collective-permute-start | bytes 196616 | tf_op jit(solution)/shard_map/ppermute | solution.py:168
  5.4 7.3 %collective-permute-start = (bf16[8,4096]{1,0:T(8,128)(2,1)S(1)}, bf16[8,4096]{1,0:T(8,128)(2,1)S(1)}, u32[]{:S(2)}, u32[]{:S(2)}) collective-permute-start(bf16[8,4096]{1,0:T(8,128)(2,1)S(1)} %get-tuple-element.44), channel_id=1, source_target_pairs={{0,2},{1,3},{2,0},{3,1},{4,6},{5,7},{6,4},{7,5},{8,10},{9,11},{10,... | collective-permute-start | bytes 196616 | tf_op jit(solution)/shard_map/ppermute | solution.py:168
  8.0 7.1 %collective-permute-start.1 = (bf16[8,4096]{1,0:T(8,128)(2,1)S(1)}, bf16[8,4096]{1,0:T(8,128)(2,1)S(1)}, u32[]{:S(2)}, u32[]{:S(2)}) collective-permute-start(bf16[8,4096]{1,0:T(8,128)(2,1)S(1)} %get-tuple-element.43), channel_id=1, source_target_pairs={{0,3},{1,2},{2,1},{3,0},{4,7},{5,6},{6,5},{7,4},{8,11},{9,10},{10,... | collective-permute-start | bytes 196616 | tf_op jit(solution)/shard_map/ppermute | solution.py:168
  8.9 6.4 %collective-permute-start.10 = (bf16[16,4096]{1,0:T(8,128)(2,1)S(1)}, bf16[16,4096]{1,0:T(8,128)(2,1)S(1)}, u32[]{:S(2)}, u32[]{:S(2)}) collective-permute-start(bf16[16,4096]{1,0:T(8,128)(2,1)S(1)} %pad_maximum_fusion.4), channel_id=1, source_target_pairs={{0,4},{4,0},{8,12},{12,8},{16,20},{20,16},{24,28},{28,24},{1,5},{5... | collective-permute-start | bytes 393224 | tf_op jit(solution)/shard_map/ppermute | solution.py:168
  8.9 7.0 %collective-permute-start.11 = (bf16[16,4096]{1,0:T(8,128)(2,1)S(1)}, bf16[16,4096]{1,0:T(8,128)(2,1)S(1)}, u32[]{:S(2)}, u32[]{:S(2)}) collective-permute-start(bf16[16,4096]{1,0:T(8,128)(2,1)S(1)} %pad_maximum_fusion.4), channel_id=1, source_target_pairs={{0,8},{4,12},{8,0},{12,4},{16,24},{20,28},{24,16},{28,20},{1,9},{5... | collective-permute-start | bytes 393224 | tf_op jit(solution)/shard_map/ppermute | solution.py:168
  10.7 11.0 %collective-permute-start.13 = (bf16[16,4096]{1,0:T(8,128)(2,1)S(1)}, bf16[16,4096]{1,0:T(8,128)(2,1)S(1)}, u32[]{:S(2)}, u32[]{:S(2)}) collective-permute-start(bf16[16,4096]{1,0:T(8,128)(2,1)S(1)} %pad_maximum_fusion.4), channel_id=1, source_target_pairs={{0,16},{4,20},{8,24},{12,28},{16,0},{20,4},{24,8},{28,12},{1,17},{... | collective-permute-start | bytes 393224 | tf_op jit(solution)/shard_map/ppermute | solution.py:168
  12.7 9.6 %collective-permute-start.15 = (bf16[16,4096]{1,0:T(8,128)(2,1)S(1)}, bf16[16,4096]{1,0:T(8,128)(2,1)S(1)}, u32[]{:S(2)}, u32[]{:S(2)}) collective-permute-start(bf16[16,4096]{1,0:T(8,128)(2,1)S(1)} %pad_maximum_fusion.4), channel_id=1, source_target_pairs={{0,24},{4,28},{8,16},{12,20},{16,8},{20,12},{24,0},{28,4},{1,25},{... | collective-permute-start | bytes 393224 | tf_op jit(solution)/shard_map/ppermute | solution.py:168
  15.3 6.4 %collective-permute-start.3 = (bf16[16,4096]{1,0:T(8,128)(2,1)S(1)}, bf16[16,4096]{1,0:T(8,128)(2,1)S(1)}, u32[]{:S(2)}, u32[]{:S(2)}) collective-permute-start(bf16[16,4096]{1,0:T(8,128)(2,1)S(1)} %constant_dynamic-update-slice_fusion), channel_id=1, source_target_pairs={{0,8},{4,12},{8,0},{12,4},{16,24},{20,28},{24,16},{28,20},{1,9},{5... | collective-permute-start | bytes 393224 | tf_op jit(solution)/shard_map/ppermute | solution.py:168
  15.9 8.8 %collective-permute-start.5 = (bf16[16,4096]{1,0:T(8,128)(2,1)S(1)}, bf16[16,4096]{1,0:T(8,128)(2,1)S(1)}, u32[]{:S(2)}, u32[]{:S(2)}) collective-permute-start(bf16[16,4096]{1,0:T(8,128)(2,1)S(1)} %constant_dynamic-update-slice_fusion), channel_id=1, source_target_pairs={{0,16},{4,20},{8,24},{12,28},{16,0},{20,4},{24,8},{28,12},{1,17},{... | collective-permute-start | bytes 393224 | tf_op jit(solution)/shard_map/ppermute | solution.py:168
  17.4 7.3 %collective-permute-start.7 = (bf16[16,4096]{1,0:T(8,128)(2,1)S(1)}, bf16[16,4096]{1,0:T(8,128)(2,1)S(1)}, u32[]{:S(2)}, u32[]{:S(2)}) collective-permute-start(bf16[16,4096]{1,0:T(8,128)(2,1)S(1)} %constant_dynamic-update-slice_fusion), channel_id=1, source_target_pairs={{0,24},{4,28},{8,16},{12,20},{16,8},{20,12},{24,0},{28,4},{1,25},{... | collective-permute-start | bytes 393224 | tf_op jit(solution)/shard_map/ppermute | solution.py:168
  21.8 3.6 %collective-permute-start.4 = (bf16[16,4096]{1,0:T(8,128)(2,1)S(1)}, bf16[16,4096]{1,0:T(8,128)(2,1)S(1)}, u32[]{:S(2)}, u32[]{:S(2)}) collective-permute-start(bf16[16,4096]{1,0:T(8,128)(2,1)S(1)} %collective-permute-done.3), channel_id=1, source_target_pairs={{0,4},{4,0},{8,12},{12,8},{16,20},{20,16},{24,28},{28,24},{1,5},{5... | collective-permute-start | bytes 393224 | tf_op jit(solution)/shard_map/ppermute | solution.py:168
  31.6 8.5 %collective-permute-start.17 = (f16[2,8,8,1024]{3,2,1,0:T(8,128)(2,1)S(1)}, f16[2,8,8,1024]{3,2,1,0:T(8,128)(2,1)S(1)}, u32[]{:S(2)}, u32[]{:S(2)}) collective-permute-start(f16[2,8,8,1024]{3,2,1,0:T(8,128)(2,1)S(1)} %fusion.19), channel_id=1, source_target_pairs={{0,1},{1,0},{2,3},{3,2},{4,5},{5,4},{6,7},{7,6},{8,9},{9,8},{10,11... | collective-permute-start | bytes 786440 | tf_op jit(solution)/shard_map/ppermute | solution.py:168
  38.0 8.9 %collective-permute-start.24 = (f16[8,8,1280]{2,1,0:T(8,128)(2,1)S(1)}, f16[8,8,1280]{2,1,0:T(8,128)(2,1)S(1)}, u32[]{:S(2)}, u32[]{:S(2)}) collective-permute-start(f16[8,8,1280]{2,1,0:T(8,128)(2,1)S(1)} %get-tuple-element.30), channel_id=1, source_target_pairs={{0,1},{1,0},{2,3},{3,2},{4,5},{5,4},{6,7},{7,6},{8,9},{9,8},{10,11... | collective-permute-start | bytes 491528 | tf_op jit(solution)/shard_map/ppermute | solution.py:168
  40.1 8.6 %collective-permute-start.18 = (f16[8,8,1024]{2,1,0:T(8,128)(2,1)S(1)}, f16[8,8,1024]{2,1,0:T(8,128)(2,1)S(1)}, u32[]{:S(2)}, u32[]{:S(2)}) collective-permute-start(f16[8,8,1024]{2,1,0:T(8,128)(2,1)S(1)} %fusion.37), channel_id=1, source_target_pairs={{0,2},{1,3},{2,0},{3,1},{4,6},{5,7},{6,4},{7,5},{8,10},{9,11},{10,... | collective-permute-start | bytes 393224 | tf_op jit(solution)/shard_map/ppermute | solution.py:168
  46.9 9.8 %collective-permute-start.25 = (f16[8,8,1280]{2,1,0:T(8,128)(2,1)S(1)}, f16[8,8,1280]{2,1,0:T(8,128)(2,1)S(1)}, u32[]{:S(2)}, u32[]{:S(2)}) collective-permute-start(f16[8,8,1280]{2,1,0:T(8,128)(2,1)S(1)} %fusion.14), channel_id=1, source_target_pairs={{0,2},{1,3},{2,0},{3,1},{4,6},{5,7},{6,4},{7,5},{8,10},{9,11},{10,... | collective-permute-start | bytes 491528 | tf_op jit(solution)/shard_map/ppermute | solution.py:168
  48.7 8.5 %collective-permute-start.23 = (f16[8,8,1280]{2,1,0:T(8,128)(2,1)S(1)}, f16[8,8,1280]{2,1,0:T(8,128)(2,1)S(1)}, u32[]{:S(2)}, u32[]{:S(2)}) collective-permute-start(f16[8,8,1280]{2,1,0:T(8,128)(2,1)S(1)} %get-tuple-element.19), channel_id=1, source_target_pairs={{0,1},{1,0},{2,3},{3,2},{4,5},{5,4},{6,7},{7,6},{8,9},{9,8},{10,11... | collective-permute-start | bytes 491528 | tf_op jit(solution)/shard_map/ppermute | solution.py:168
  48.8 10.9 %collective-permute-start.19 = (bf16[2,8,1024]{2,1,0:T(8,128)(2,1)S(1)}, bf16[2,8,1024]{2,1,0:T(8,128)(2,1)S(1)}, u32[]{:S(2)}, u32[]{:S(2)}) collective-permute-start(bf16[2,8,1024]{2,1,0:T(8,128)(2,1)S(1)} %get-tuple-element.62), channel_id=1, source_target_pairs={{0,8},{4,12},{8,0},{12,4},{16,24},{20,28},{24,16},{28,20},{1,9},{5... | collective-permute-start | bytes 98312 | tf_op jit(solution)/shard_map/ppermute | solution.py:168
  50.3 10.7 %collective-permute-start.20 = (bf16[2,8,1024]{2,1,0:T(8,128)(2,1)S(1)}, bf16[2,8,1024]{2,1,0:T(8,128)(2,1)S(1)}, u32[]{:S(2)}, u32[]{:S(2)}) collective-permute-start(bf16[2,8,1024]{2,1,0:T(8,128)(2,1)S(1)} %get-tuple-element.64), channel_id=1, source_target_pairs={{0,16},{4,20},{8,24},{12,28},{16,0},{20,4},{24,8},{28,12},{1,17},{... | collective-permute-start | bytes 98312 | tf_op jit(solution)/shard_map/ppermute | solution.py:168
  51.1 9.8 %collective-permute-start.21 = (bf16[2,8,1024]{2,1,0:T(8,128)(2,1)S(1)}, bf16[2,8,1024]{2,1,0:T(8,128)(2,1)S(1)}, u32[]{:S(2)}, u32[]{:S(2)}) collective-permute-start(bf16[2,8,1024]{2,1,0:T(8,128)(2,1)S(1)} %get-tuple-element.63), channel_id=1, source_target_pairs={{0,24},{4,28},{8,16},{12,20},{16,8},{20,12},{24,0},{28,4},{1,25},{... | collective-permute-start | bytes 98312 | tf_op jit(solution)/shard_map/ppermute | solution.py:168
  57.4 4.1 %collective-permute-start.26 = (bf16[2,8,1280]{2,1,0:T(8,128)(2,1)S(1)}, bf16[2,8,1280]{2,1,0:T(8,128)(2,1)S(1)}, u32[]{:S(2)}, u32[]{:S(2)}) collective-permute-start(bf16[2,8,1280]{2,1,0:T(8,128)(2,1)S(1)} %get-tuple-element.47), channel_id=1, source_target_pairs={{0,8},{4,12},{8,0},{12,4},{16,24},{20,28},{24,16},{28,20},{1,9},{5... | collective-permute-start | bytes 122888 | tf_op jit(solution)/shard_map/ppermute | solution.py:168
  58.8 4.1 %collective-permute-start.27 = (bf16[2,8,1280]{2,1,0:T(8,128)(2,1)S(1)}, bf16[2,8,1280]{2,1,0:T(8,128)(2,1)S(1)}, u32[]{:S(2)}, u32[]{:S(2)}) collective-permute-start(bf16[2,8,1280]{2,1,0:T(8,128)(2,1)S(1)} %get-tuple-element.49), channel_id=1, source_target_pairs={{0,16},{4,20},{8,24},{12,28},{16,0},{20,4},{24,8},{28,12},{1,17},{... | collective-permute-start | bytes 122888 | tf_op jit(solution)/shard_map/ppermute | solution.py:168
  59.7 4.9 %collective-permute-start.28 = (bf16[2,8,1280]{2,1,0:T(8,128)(2,1)S(1)}, bf16[2,8,1280]{2,1,0:T(8,128)(2,1)S(1)}, u32[]{:S(2)}, u32[]{:S(2)}) collective-permute-start(bf16[2,8,1280]{2,1,0:T(8,128)(2,1)S(1)} %get-tuple-element.48), channel_id=1, source_target_pairs={{0,24},{4,28},{8,16},{12,20},{16,8},{20,12},{24,0},{28,4},{1,25},{... | collective-permute-start | bytes 122888 | tf_op jit(solution)/shard_map/ppermute | solution.py:168
  61.0 3.7 %collective-permute-start.22 = (bf16[4,8,1024]{2,1,0:T(8,128)(2,1)S(1)}, bf16[4,8,1024]{2,1,0:T(8,128)(2,1)S(1)}, u32[]{:S(2)}, u32[]{:S(2)}) collective-permute-start(bf16[4,8,1024]{2,1,0:T(8,128)(2,1)S(1)} %pad_maximum_fusion.10), channel_id=1, source_target_pairs={{0,4},{4,0},{8,12},{12,8},{16,20},{20,16},{24,28},{28,24},{1,5},{5... | collective-permute-start | bytes 196616 | tf_op jit(solution)/shard_map/ppermute | solution.py:168
  72.3 6.0 %collective-permute-start.39 = (bf16[8,4096]{1,0:T(8,128)(2,1)S(1)}, bf16[8,4096]{1,0:T(8,128)(2,1)S(1)}, u32[]{:S(2)}, u32[]{:S(2)}) collective-permute-start(bf16[8,4096]{1,0:T(8,128)(2,1)S(1)} %get-tuple-element.38), channel_id=1, source_target_pairs={{0,1},{1,0},{2,3},{3,2},{4,5},{5,4},{6,7},{7,6},{8,9},{9,8},{10,11... | collective-permute-start | bytes 196616 | tf_op jit(solution)/shard_map/ppermute | solution.py:168
  75.3 7.2 %collective-permute-start.30 = (bf16[8,4096]{1,0:T(8,128)(2,1)S(1)}, bf16[8,4096]{1,0:T(8,128)(2,1)S(1)}, u32[]{:S(2)}, u32[]{:S(2)}) collective-permute-start(bf16[8,4096]{1,0:T(8,128)(2,1)S(1)} %get-tuple-element.40), channel_id=1, source_target_pairs={{0,2},{1,3},{2,0},{3,1},{4,6},{5,7},{6,4},{7,5},{8,10},{9,11},{10,... | collective-permute-start | bytes 196616 | tf_op jit(solution)/shard_map/ppermute | solution.py:168
  78.3 6.4 %collective-permute-start.31 = (bf16[8,4096]{1,0:T(8,128)(2,1)S(1)}, bf16[8,4096]{1,0:T(8,128)(2,1)S(1)}, u32[]{:S(2)}, u32[]{:S(2)}) collective-permute-start(bf16[8,4096]{1,0:T(8,128)(2,1)S(1)} %get-tuple-element.39), channel_id=1, source_target_pairs={{0,3},{1,2},{2,1},{3,0},{4,7},{5,6},{6,5},{7,4},{8,11},{9,10},{10,... | collective-permute-start | bytes 196616 | tf_op jit(solution)/shard_map/ppermute | solution.py:168
  78.3 6.5 %collective-permute-start.40 = (bf16[16,4096]{1,0:T(8,128)(2,1)S(1)}, bf16[16,4096]{1,0:T(8,128)(2,1)S(1)}, u32[]{:S(2)}, u32[]{:S(2)}) collective-permute-start(bf16[16,4096]{1,0:T(8,128)(2,1)S(1)} %pad_maximum_fusion.6), channel_id=1, source_target_pairs={{0,4},{4,0},{8,12},{12,8},{16,20},{20,16},{24,28},{28,24},{1,5},{5... | collective-permute-start | bytes 393224 | tf_op jit(solution)/shard_map/ppermute | solution.py:168
  78.9 7.7 %collective-permute-start.41 = (bf16[16,4096]{1,0:T(8,128)(2,1)S(1)}, bf16[16,4096]{1,0:T(8,128)(2,1)S(1)}, u32[]{:S(2)}, u32[]{:S(2)}) collective-permute-start(bf16[16,4096]{1,0:T(8,128)(2,1)S(1)} %pad_maximum_fusion.6), channel_id=1, source_target_pairs={{0,8},{4,12},{8,0},{12,4},{16,24},{20,28},{24,16},{28,20},{1,9},{5... | collective-permute-start | bytes 393224 | tf_op jit(solution)/shard_map/ppermute | solution.py:168
  80.4 10.4 %collective-permute-start.43 = (bf16[16,4096]{1,0:T(8,128)(2,1)S(1)}, bf16[16,4096]{1,0:T(8,128)(2,1)S(1)}, u32[]{:S(2)}, u32[]{:S(2)}) collective-permute-start(bf16[16,4096]{1,0:T(8,128)(2,1)S(1)} %pad_maximum_fusion.6), channel_id=1, source_target_pairs={{0,16},{4,20},{8,24},{12,28},{16,0},{20,4},{24,8},{28,12},{1,17},{... | collective-permute-start | bytes 393224 | tf_op jit(solution)/shard_map/ppermute | solution.py:168
  82.5 8.9 %collective-permute-start.45 = (bf16[16,4096]{1,0:T(8,128)(2,1)S(1)}, bf16[16,4096]{1,0:T(8,128)(2,1)S(1)}, u32[]{:S(2)}, u32[]{:S(2)}) collective-permute-start(bf16[16,4096]{1,0:T(8,128)(2,1)S(1)} %pad_maximum_fusion.6), channel_id=1, source_target_pairs={{0,24},{4,28},{8,16},{12,20},{16,8},{20,12},{24,0},{28,4},{1,25},{... | collective-permute-start | bytes 393224 | tf_op jit(solution)/shard_map/ppermute | solution.py:168
  84.9 6.0 %collective-permute-start.33 = (bf16[16,4096]{1,0:T(8,128)(2,1)S(1)}, bf16[16,4096]{1,0:T(8,128)(2,1)S(1)}, u32[]{:S(2)}, u32[]{:S(2)}) collective-permute-start(bf16[16,4096]{1,0:T(8,128)(2,1)S(1)} %constant_dynamic-update-slice_fusion.2), channel_id=1, source_target_pairs={{0,8},{4,12},{8,0},{12,4},{16,24},{20,28},{24,16},{28,20},{1,9},{5... | collective-permute-start | bytes 393224 | tf_op jit(solution)/shard_map/ppermute | solution.py:168
  86.6 8.5 %collective-permute-start.35 = (bf16[16,4096]{1,0:T(8,128)(2,1)S(1)}, bf16[16,4096]{1,0:T(8,128)(2,1)S(1)}, u32[]{:S(2)}, u32[]{:S(2)}) collective-permute-start(bf16[16,4096]{1,0:T(8,128)(2,1)S(1)} %constant_dynamic-update-slice_fusion.2), channel_id=1, source_target_pairs={{0,16},{4,20},{8,24},{12,28},{16,0},{20,4},{24,8},{28,12},{1,17},{... | collective-permute-start | bytes 393224 | tf_op jit(solution)/shard_map/ppermute | solution.py:168
  86.7 8.4 %collective-permute-start.37 = (bf16[16,4096]{1,0:T(8,128)(2,1)S(1)}, bf16[16,4096]{1,0:T(8,128)(2,1)S(1)}, u32[]{:S(2)}, u32[]{:S(2)}) collective-permute-start(bf16[16,4096]{1,0:T(8,128)(2,1)S(1)} %constant_dynamic-update-slice_fusion.2), channel_id=1, source_target_pairs={{0,24},{4,28},{8,16},{12,20},{16,8},{20,12},{24,0},{28,4},{1,25},{... | collective-permute-start | bytes 393224 | tf_op jit(solution)/shard_map/ppermute | solution.py:168
  90.8 4.8 %collective-permute-start.42 = (bf16[16,4096]{1,0:T(8,128)(2,1)S(1)}, bf16[16,4096]{1,0:T(8,128)(2,1)S(1)}, u32[]{:S(2)}, u32[]{:S(2)}) collective-permute-start(bf16[16,4096]{1,0:T(8,128)(2,1)S(1)} %collective-permute-done.41), channel_id=1, source_target_pairs={{0,4},{4,0},{8,12},{12,8},{16,20},{20,16},{24,28},{28,24},{1,5},{5... | collective-permute-start | bytes 393224 | tf_op jit(solution)/shard_map/ppermute | solution.py:168
  90.8 4.9 %collective-permute-start.34 = (bf16[16,4096]{1,0:T(8,128)(2,1)S(1)}, bf16[16,4096]{1,0:T(8,128)(2,1)S(1)}, u32[]{:S(2)}, u32[]{:S(2)}) collective-permute-start(bf16[16,4096]{1,0:T(8,128)(2,1)S(1)} %collective-permute-done.33), channel_id=1, source_target_pairs={{0,4},{4,0},{8,12},{12,8},{16,20},{20,16},{24,28},{28,24},{1,5},{5... | collective-permute-start | bytes 393224 | tf_op jit(solution)/shard_map/ppermute | solution.py:168
  91.4 4.3 %collective-permute-start.44 = (bf16[16,4096]{1,0:T(8,128)(2,1)S(1)}, bf16[16,4096]{1,0:T(8,128)(2,1)S(1)}, u32[]{:S(2)}, u32[]{:S(2)}) collective-permute-start(bf16[16,4096]{1,0:T(8,128)(2,1)S(1)} %collective-permute-done.43), channel_id=1, source_target_pairs={{0,4},{4,0},{8,12},{12,8},{16,20},{20,16},{24,28},{28,24},{1,5},{5... | collective-permute-start | bytes 393224 | tf_op jit(solution)/shard_map/ppermute | solution.py:168
  102.0 8.5 %collective-permute-start.47 = (f16[2,8,8,1024]{3,2,1,0:T(8,128)(2,1)S(1)}, f16[2,8,8,1024]{3,2,1,0:T(8,128)(2,1)S(1)}, u32[]{:S(2)}, u32[]{:S(2)}) collective-permute-start(f16[2,8,8,1024]{3,2,1,0:T(8,128)(2,1)S(1)} %fusion.20), channel_id=1, source_target_pairs={{0,1},{1,0},{2,3},{3,2},{4,5},{5,4},{6,7},{7,6},{8,9},{9,8},{10,11... | collective-permute-start | bytes 786440 | tf_op jit(solution)/shard_map/ppermute | solution.py:168
  107.8 5.5 %collective-permute-start.54 = (f16[8,8,1024]{2,1,0:T(8,128)(2,1)S(1)}, f16[8,8,1024]{2,1,0:T(8,128)(2,1)S(1)}, u32[]{:S(2)}, u32[]{:S(2)}) collective-permute-start(f16[8,8,1024]{2,1,0:T(8,128)(2,1)S(1)} %get-tuple-element.32), channel_id=1, source_target_pairs={{0,1},{1,0},{2,3},{3,2},{4,5},{5,4},{6,7},{7,6},{8,9},{9,8},{10,11... | collective-permute-start | bytes 393224 | tf_op jit(solution)/shard_map/ppermute | solution.py:168
  110.6 12.1 %collective-permute-start.48 = (f16[8,8,1024]{2,1,0:T(8,128)(2,1)S(1)}, f16[8,8,1024]{2,1,0:T(8,128)(2,1)S(1)}, u32[]{:S(2)}, u32[]{:S(2)}) collective-permute-start(f16[8,8,1024]{2,1,0:T(8,128)(2,1)S(1)} %fusion.38), channel_id=1, source_target_pairs={{0,2},{1,3},{2,0},{3,1},{4,6},{5,7},{6,4},{7,5},{8,10},{9,11},{10,... | collective-permute-start | bytes 393224 | tf_op jit(solution)/shard_map/ppermute | solution.py:168
  113.4 11.8 %collective-permute-start.55 = (f16[8,8,1024]{2,1,0:T(8,128)(2,1)S(1)}, f16[8,8,1024]{2,1,0:T(8,128)(2,1)S(1)}, u32[]{:S(2)}, u32[]{:S(2)}) collective-permute-start(f16[8,8,1024]{2,1,0:T(8,128)(2,1)S(1)} %fusion.24), channel_id=1, source_target_pairs={{0,2},{1,3},{2,0},{3,1},{4,6},{5,7},{6,4},{7,5},{8,10},{9,11},{10,... | collective-permute-start | bytes 393224 | tf_op jit(solution)/shard_map/ppermute | solution.py:168
  118.1 7.8 %collective-permute-start.53 = (f16[8,8,1024]{2,1,0:T(8,128)(2,1)S(1)}, f16[8,8,1024]{2,1,0:T(8,128)(2,1)S(1)}, u32[]{:S(2)}, u32[]{:S(2)}) collective-permute-start(f16[8,8,1024]{2,1,0:T(8,128)(2,1)S(1)} %get-tuple-element.24), channel_id=1, source_target_pairs={{0,1},{1,0},{2,3},{3,2},{4,5},{5,4},{6,7},{7,6},{8,9},{9,8},{10,11... | collective-permute-start | bytes 393224 | tf_op jit(solution)/shard_map/ppermute | solution.py:168
  122.8 7.4 %collective-permute-start.49 = (bf16[2,8,1024]{2,1,0:T(8,128)(2,1)S(1)}, bf16[2,8,1024]{2,1,0:T(8,128)(2,1)S(1)}, u32[]{:S(2)}, u32[]{:S(2)}) collective-permute-start(bf16[2,8,1024]{2,1,0:T(8,128)(2,1)S(1)} %get-tuple-element.52), channel_id=1, source_target_pairs={{0,8},{4,12},{8,0},{12,4},{16,24},{20,28},{24,16},{28,20},{1,9},{5... | collective-permute-start | bytes 98312 | tf_op jit(solution)/shard_map/ppermute | solution.py:168
  125.9 6.0 %collective-permute-start.50 = (bf16[2,8,1024]{2,1,0:T(8,128)(2,1)S(1)}, bf16[2,8,1024]{2,1,0:T(8,128)(2,1)S(1)}, u32[]{:S(2)}, u32[]{:S(2)}) collective-permute-start(bf16[2,8,1024]{2,1,0:T(8,128)(2,1)S(1)} %get-tuple-element.54), channel_id=1, source_target_pairs={{0,16},{4,20},{8,24},{12,28},{16,0},{20,4},{24,8},{28,12},{1,17},{... | collective-permute-start | bytes 98312 | tf_op jit(solution)/shard_map/ppermute | solution.py:168
  126.6 5.3 %collective-permute-start.51 = (bf16[2,8,1024]{2,1,0:T(8,128)(2,1)S(1)}, bf16[2,8,1024]{2,1,0:T(8,128)(2,1)S(1)}, u32[]{:S(2)}, u32[]{:S(2)}) collective-permute-start(bf16[2,8,1024]{2,1,0:T(8,128)(2,1)S(1)} %get-tuple-element.53), channel_id=1, source_target_pairs={{0,24},{4,28},{8,16},{12,20},{16,8},{20,12},{24,0},{28,4},{1,25},{... | collective-permute-start | bytes 98312 | tf_op jit(solution)/shard_map/ppermute | solution.py:168
  128.4 3.9 %collective-permute-start.56 = (bf16[2,8,1024]{2,1,0:T(8,128)(2,1)S(1)}, bf16[2,8,1024]{2,1,0:T(8,128)(2,1)S(1)}, u32[]{:S(2)}, u32[]{:S(2)}) collective-permute-start(bf16[2,8,1024]{2,1,0:T(8,128)(2,1)S(1)} %get-tuple-element.57), channel_id=1, source_target_pairs={{0,8},{4,12},{8,0},{12,4},{16,24},{20,28},{24,16},{28,20},{1,9},{5... | collective-permute-start | bytes 98312 | tf_op jit(solution)/shard_map/ppermute | solution.py:168
  129.5 3.9 %collective-permute-start.57 = (bf16[2,8,1024]{2,1,0:T(8,128)(2,1)S(1)}, bf16[2,8,1024]{2,1,0:T(8,128)(2,1)S(1)}, u32[]{:S(2)}, u32[]{:S(2)}) collective-permute-start(bf16[2,8,1024]{2,1,0:T(8,128)(2,1)S(1)} %get-tuple-element.59), channel_id=1, source_target_pairs={{0,16},{4,20},{8,24},{12,28},{16,0},{20,4},{24,8},{28,12},{1,17},{... | collective-permute-start | bytes 98312 | tf_op jit(solution)/shard_map/ppermute | solution.py:168
  130.1 4.8 %collective-permute-start.58 = (bf16[2,8,1024]{2,1,0:T(8,128)(2,1)S(1)}, bf16[2,8,1024]{2,1,0:T(8,128)(2,1)S(1)}, u32[]{:S(2)}, u32[]{:S(2)}) collective-permute-start(bf16[2,8,1024]{2,1,0:T(8,128)(2,1)S(1)} %get-tuple-element.58), channel_id=1, source_target_pairs={{0,24},{4,28},{8,16},{12,20},{16,8},{20,12},{24,0},{28,4},{1,25},{... | collective-permute-start | bytes 98312 | tf_op jit(solution)/shard_map/ppermute | solution.py:168
  132.0 4.3 %collective-permute-start.52 = (bf16[4,8,1024]{2,1,0:T(8,128)(2,1)S(1)}, bf16[4,8,1024]{2,1,0:T(8,128)(2,1)S(1)}, u32[]{:S(2)}, u32[]{:S(2)}) collective-permute-start(bf16[4,8,1024]{2,1,0:T(8,128)(2,1)S(1)} %pad_maximum_fusion.11), channel_id=1, source_target_pairs={{0,4},{4,0},{8,12},{12,8},{16,20},{20,16},{24,28},{28,24},{1,5},{5... | collective-permute-start | bytes 196616 | tf_op jit(solution)/shard_map/ppermute | solution.py:168
  (13 other events, 51.7 us)

commit v3 on v2

--- a/solution.py
+++ b/solution.py
@@ -42,24 +42,22 @@
     parts = span // PART
     scale = 1.0 / math.sqrt(HD)
 
-    def copies(row, count):
+    def copy(cache, row, count):
+        source, target = ((k_cache, keys), (v_cache, values))[cache]
         some = pl.ds(0, count)
-        return (
-            pltpu.make_async_copy(k_cache.at[row, some], keys.at[row, some], sems.at[row, 0]),
-            pltpu.make_async_copy(v_cache.at[row, some], values.at[row, some], sems.at[row, 1]),
+        return pltpu.make_async_copy(
+            source.at[row, some], target.at[row, some], sems.at[row, cache]
         )
 
     def by_length(length, act):
         for case in range(1, parts + 1):
             pl.when((length + PART - 1) // PART == case)(functools.partial(act, case * PART))
 
-    def fetch(row, count):
-        for copy in copies(row, count):
-            copy.start()
-
-    def arrive(row, count):
-        for copy in copies(row, count):
-            copy.wait()
+    def start(cache, row):
+        by_length(lengths[row], lambda count: copy(cache, row, count).start())
+
+    def wait(cache, row):
+        by_length(lengths[row], lambda count: copy(cache, row, count).wait())
 
     def clear(row, part):
         values[row, part * PART : (part + 1) * PART] = jnp.zeros(
@@ -101,17 +99,23 @@
     def group(row, count):
         each = [row + at for at in range(GROUP)]
         for one in each:
-            by_length(lengths[one], functools.partial(arrive, one))
+            wait(0, one)
             for part in range(1, count // PART):
                 pl.when(lengths[one] <= part * PART)(functools.partial(clear, one, part))
         scores = [score(one, wide.at[at], count) for at, one in enumerate(each)]
         weighed = [weigh(one, of_one) for one, of_one in zip(each, scores)]
+        for one in each:
+            wait(1, one)
         for one, (weights, wnew) in zip(each, weighed):
             mix(one, weights, wnew, count)
 
-    @pl.loop(0, rows)
-    def _(row):
-        by_length(lengths[row], functools.partial(fetch, row))
+    @pl.loop(0, rows // GROUP)
+    def _(index):
+        for cache in range(2):
+
+            @pl.loop(0, GROUP)
+            def _(at):
+                start(cache, index * GROUP + at)
 
     wide[...] = jnp.zeros_like(wide)
 
@@ -298,16 +302,44 @@
     return (rows * scale).astype(jnp.bfloat16), unit
 
 
+def norm_kernel(hidden_hbm, gain_hbm, out, hidden, gain, sems):
+    copies = (
+        pltpu.make_async_copy(hidden_hbm, hidden, sems.at[0]),
+        pltpu.make_async_copy(gain_hbm, gain, sems.at[1]),
+    )
+    for copy in copies:
+        copy.start()
+    for copy in copies:
+        copy.wait()
+    widened = hidden[...].astype(jnp.float32)
+    mean = jnp.mean(widened * widened, axis=-1, keepdims=True)
+    out[...] = (widened * lax.rsqrt(mean + eps) * gain[...]).astype(out.dtype)
+
+
+def norm(hidden_in, norm_gain):
+    anywhere = pl.BlockSpec(memory_space=pl.ANY)
+    gain = norm_gain.reshape(1, -1)
+    return pl.pallas_call(
+        norm_kernel,
+        in_specs=[anywhere, anywhere],
+        out_specs=pl.BlockSpec(memory_space=pltpu.VMEM),
+        out_shape=jax.ShapeDtypeStruct(hidden_in.shape, jnp.bfloat16),
+        scratch_shapes=[
+            pltpu.VMEM(hidden_in.shape, hidden_in.dtype),
+            pltpu.VMEM(gain.shape, gain.dtype),
+            pltpu.SemaphoreType.DMA((2,)),
+        ],
+        compiler_params=pltpu.CompilerParams(vmem_limit_bytes=62 * 2**20),
+    )(hidden_in, gain)
+
+
 def on_device(hidden_in, norm_gain, w_qkv, k_cache, v_cache, lengths, w_out):
-    widened = hidden_in.astype(jnp.float32)
-    normed = (
-        widened * lax.rsqrt(jnp.mean(widened * widened, axis=-1, keepdims=True) + eps) * norm_gain
-    ).astype(jnp.bfloat16)
+    normed = norm(hidden_in, norm_gain)
     qkv = project(normed, w_qkv, 32.0)
     owned = deliver(qkv)
     attended = attend_local(owned, k_cache, v_cache, lengths)
     scaled, unit = level(attended)
-    out = deliver(project(scaled, w_out, 8.0))
+    out = deliver([jnp.concatenate(project(scaled, w_out, 8.0), axis=-1)])
     return (out.astype(jnp.float32) * unit).astype(jnp.bfloat16)
 
 

time: 138 us -> 136 us (0.986)
  starting transfers between devices: 61.4 us -> 52.4 us
  waiting for transfers between devices: 42.9 us -> 48.9 us
  Pallas kernels: 24.7 us -> 27.6 us
  other arithmetic: 6.03 us -> 3.7 us
    ppermute x60 -> x56, starting transfers between devices: 61.4 us -> 52.4 us  [swap(): return lax.ppermute(block, axis, [(i, i ^ bit) for i in range(count)])]
    ppermute x60 -> x56, waiting for transfers between devices: 42.9 us -> 48.9 us  [swap(): return lax.ppermute(block, axis, [(i, i ^ bit) for i in range(count)])]
    pallas_call x0 -> x1, Pallas kernels: none -> 1.98 us  [norm(): pl.pallas_call(norm_kernel, in_specs=[anywhere, anywhere], out_specs=pl.B...]
  transfers between devices with their start and end apart: 60 -> 56, of which waited for: 27 -> 29; matrix products, arithmetic and copies ran while one was open for 1% -> 1% of each run, Pallas kernels for 8% -> 8%
where the time goes in v3:
time: 136 us
  starting transfers between devices  52.4 us (39%)
  waiting for transfers between devices  48.9 us (36%)
  Pallas kernels  27.6 us (20%)
  other arithmetic  3.7 us (3%)
  local copies, waits for them, and re-layouts  2.65 us (2%)
    ppermute x56, starting transfers between devices, swap(): return lax.ppermute(block, axis, [(i, i ^ bit) for i in range(count)])  52.4 us
    ppermute x56, waiting for transfers between devices, swap(): return lax.ppermute(block, axis, [(i, i ^ bit) for i in range(count)])  48.9 us
    pallas_call x4, Pallas kernels, multiply(): pl.pallas_call(functools.partial(multiply_kernel, start), in_specs=[vmem,...  20.3 us
    pallas_call x1, Pallas kernels, attend_local(): pl.pallas_call(attend_kernel, in_specs=[pl.BlockSpec(memory_space=pltpu.S...  5.24 us
  transfers between devices with their start and end apart: 56, of which 29 were waited for; matrix products, arithmetic and copies ran while one was open for 1% of the time, Pallas kernels for 8%

profile of v3, /device:TPU:0, one launch (start us, length us, event | category | flops | bytes accessed | tf_op | source)
XLA Modules:
  0.0 136.0 jit_solution(18327247092455086696)
XLA Ops:
  0.0 2.0 %shard_map.73 = bf16[8,16384]{1,0:T(8,128)(2,1)} custom-call(bf16[8,16384]{1,0:T(8,128)(2,1)} %hidden_hbm.1, f32[1,16384]{1,0:T(1,128)} %bitcast.265), custom_call_target="tpu_custom_call" | custom-call | tf_op jit(solution)/shard_map/pallas_call | solution.py:322
  2.0 1.0 constant_dynamic-slice_fusion.5
  3.0 3.1 %collective-permute-start.9 = (bf16[8,4096]{1,0:T(8,128)(2,1)S(1)}, bf16[8,4096]{1,0:T(8,128)(2,1)S(1)}, u32[]{:S(2)}, u32[]{:S(2)}) collective-permute-start(bf16[8,4096]{1,0:T(8,128)(2,1)S(1)} %get-tuple-element.47), channel_id=1, source_target_pairs={{0,1},{1,0},{2,3},{3,2},{4,5},{5,4},{6,7},{7,6},{8,9},{9,8},{10,11... | collective-permute-start | bytes 196616 | tf_op jit(solution)/shard_map/ppermute | solution.py:172
  6.0 2.6 %collective-permute-start = (bf16[8,4096]{1,0:T(8,128)(2,1)S(1)}, bf16[8,4096]{1,0:T(8,128)(2,1)S(1)}, u32[]{:S(2)}, u32[]{:S(2)}) collective-permute-start(bf16[8,4096]{1,0:T(8,128)(2,1)S(1)} %get-tuple-element.49), channel_id=1, source_target_pairs={{0,2},{1,3},{2,0},{3,1},{4,6},{5,7},{6,4},{7,5},{8,10},{9,11},{10,... | collective-permute-start | bytes 196616 | tf_op jit(solution)/shard_map/ppermute | solution.py:172
  9.6 1.8 %collective-permute-start.11 = (bf16[16,4096]{1,0:T(8,128)(2,1)S(1)}, bf16[16,4096]{1,0:T(8,128)(2,1)S(1)}, u32[]{:S(2)}, u32[]{:S(2)}) collective-permute-start(bf16[16,4096]{1,0:T(8,128)(2,1)S(1)} %pad_maximum_fusion.4), channel_id=1, source_target_pairs={{0,8},{4,12},{8,0},{12,4},{16,24},{20,28},{24,16},{28,20},{1,9},{5... | collective-permute-start | bytes 393224 | tf_op jit(solution)/shard_map/ppermute | solution.py:172
  11.3 1.5 %collective-permute-start.13 = (bf16[16,4096]{1,0:T(8,128)(2,1)S(1)}, bf16[16,4096]{1,0:T(8,128)(2,1)S(1)}, u32[]{:S(2)}, u32[]{:S(2)}) collective-permute-start(bf16[16,4096]{1,0:T(8,128)(2,1)S(1)} %pad_maximum_fusion.4), channel_id=1, source_target_pairs={{0,16},{4,20},{8,24},{12,28},{16,0},{20,4},{24,8},{28,12},{1,17},{... | collective-permute-start | bytes 393224 | tf_op jit(solution)/shard_map/ppermute | solution.py:172
  13.3 2.4 %collective-permute-start.15 = (bf16[16,4096]{1,0:T(8,128)(2,1)S(1)}, bf16[16,4096]{1,0:T(8,128)(2,1)S(1)}, u32[]{:S(2)}, u32[]{:S(2)}) collective-permute-start(bf16[16,4096]{1,0:T(8,128)(2,1)S(1)} %pad_maximum_fusion.4), channel_id=1, source_target_pairs={{0,24},{4,28},{8,16},{12,20},{16,8},{20,12},{24,0},{28,4},{1,25},{... | collective-permute-start | bytes 393224 | tf_op jit(solution)/shard_map/ppermute | solution.py:172
  16.5 1.5 %collective-permute-start.5 = (bf16[16,4096]{1,0:T(8,128)(2,1)S(1)}, bf16[16,4096]{1,0:T(8,128)(2,1)S(1)}, u32[]{:S(2)}, u32[]{:S(2)}) collective-permute-start(bf16[16,4096]{1,0:T(8,128)(2,1)S(1)} %constant_dynamic-update-slice_fusion), channel_id=1, source_target_pairs={{0,16},{4,20},{8,24},{12,28},{16,0},{20,4},{24,8},{28,12},{1,17},{... | collective-permute-start | bytes 393224 | tf_op jit(solution)/shard_map/ppermute | solution.py:172
  18.0 1.6 %collective-permute-start.7 = (bf16[16,4096]{1,0:T(8,128)(2,1)S(1)}, bf16[16,4096]{1,0:T(8,128)(2,1)S(1)}, u32[]{:S(2)}, u32[]{:S(2)}) collective-permute-start(bf16[16,4096]{1,0:T(8,128)(2,1)S(1)} %constant_dynamic-update-slice_fusion), channel_id=1, source_target_pairs={{0,24},{4,28},{8,16},{12,20},{16,8},{20,12},{24,0},{28,4},{1,25},{... | collective-permute-start | bytes 393224 | tf_op jit(solution)/shard_map/ppermute | solution.py:172
  19.7 2.7 %collective-permute-done.3 = bf16[16,4096]{1,0:T(8,128)(2,1)S(1)} collective-permute-done((bf16[16,4096]{1,0:T(8,128)(2,1)S(1)}, bf16[16,4096]{1,0:T(8,128)(2,1)S(1)}, u32[]{:S(2)}, u32[]{:S(2)}) %collective-permute-start.3) | collective-permute-done | bytes 131104 | tf_op jit(solution)/shard_map/ppermute | solution.py:172
  23.0 2.3 %collective-permute-done.5 = bf16[16,4096]{1,0:T(8,128)(2,1)S(1)} collective-permute-done((bf16[16,4096]{1,0:T(8,128)(2,1)S(1)}, bf16[16,4096]{1,0:T(8,128)(2,1)S(1)}, u32[]{:S(2)}, u32[]{:S(2)}) %collective-permute-start.5) | collective-permute-done | bytes 131104 | tf_op jit(solution)/shard_map/ppermute | solution.py:172
  27.2 4.9 %shard_map.74 = f32[256,1024]{1,0:T(8,128)S(1)} custom-call(bf16[128,4096]{1,0:T(8,128)(2,1)S(1)} %bitcast.245, bf16[128,4096]{1,0:T(8,128)(2,1)S(1)} %bitcast.247, bf16[4096,2304]{1,0:T(8,128)(2,1)} %weights.5), custom_call_target="tpu_custom_call" | custom-call | flops 2147483648 | bytes 8388608 | tf_op jit(solution)/shard_map/pallas_call | solution.py:213
  32.9 5.6 %shard_map.75 = f32[256,1280]{1,0:T(8,128)S(1)} custom-call(bf16[128,4096]{1,0:T(8,128)(2,1)S(1)} %bitcast.246, bf16[128,4096]{1,0:T(8,128)(2,1)S(1)} %bitcast.248, bf16[4096,2304]{1,0:T(8,128)(2,1)} %weights.5), custom_call_target="tpu_custom_call" | custom-call | flops 2684354560 | bytes 10485760 | tf_op jit(solution)/shard_map/pallas_call | solution.py:213
  38.6 1.4 %collective-permute-start.24 = (f16[8,8,1280]{2,1,0:T(8,128)(2,1)S(1)}, f16[8,8,1280]{2,1,0:T(8,128)(2,1)S(1)}, u32[]{:S(2)}, u32[]{:S(2)}) collective-permute-start(f16[8,8,1280]{2,1,0:T(8,128)(2,1)S(1)} %get-tuple-element.30), channel_id=1, source_target_pairs={{0,1},{1,0},{2,3},{3,2},{4,5},{5,4},{6,7},{7,6},{8,9},{9,8},{10,11... | collective-permute-start | bytes 491528 | tf_op jit(solution)/shard_map/ppermute | solution.py:172
  40.8 2.5 %collective-permute-start.18 = (f16[8,8,1024]{2,1,0:T(8,128)(2,1)S(1)}, f16[8,8,1024]{2,1,0:T(8,128)(2,1)S(1)}, u32[]{:S(2)}, u32[]{:S(2)}) collective-permute-start(f16[8,8,1024]{2,1,0:T(8,128)(2,1)S(1)} %fusion.38), channel_id=1, source_target_pairs={{0,2},{1,3},{2,0},{3,1},{4,6},{5,7},{6,4},{7,5},{8,10},{9,11},{10,... | collective-permute-start | bytes 393224 | tf_op jit(solution)/shard_map/ppermute | solution.py:172
  43.3 4.2 %collective-permute-done.24 = f16[8,8,1280]{2,1,0:T(8,128)(2,1)S(1)} collective-permute-done((f16[8,8,1280]{2,1,0:T(8,128)(2,1)S(1)}, f16[8,8,1280]{2,1,0:T(8,128)(2,1)S(1)}, u32[]{:S(2)}, u32[]{:S(2)}) %collective-permute-start.24) | collective-permute-done | bytes 163872 | tf_op jit(solution)/shard_map/ppermute | solution.py:172
  47.6 1.8 %collective-permute-start.25 = (f16[8,8,1280]{2,1,0:T(8,128)(2,1)S(1)}, f16[8,8,1280]{2,1,0:T(8,128)(2,1)S(1)}, u32[]{:S(2)}, u32[]{:S(2)}) collective-permute-start(f16[8,8,1280]{2,1,0:T(8,128)(2,1)S(1)} %fusion.11), channel_id=1, source_target_pairs={{0,2},{1,3},{2,0},{3,1},{4,6},{5,7},{6,4},{7,5},{8,10},{9,11},{10,... | collective-permute-start | bytes 491528 | tf_op jit(solution)/shard_map/ppermute | solution.py:172
  49.4 1.5 %collective-permute-start.19 = (bf16[2,8,1024]{2,1,0:T(8,128)(2,1)S(1)}, bf16[2,8,1024]{2,1,0:T(8,128)(2,1)S(1)}, u32[]{:S(2)}, u32[]{:S(2)}) collective-permute-start(bf16[2,8,1024]{2,1,0:T(8,128)(2,1)S(1)} %get-tuple-element.57), channel_id=1, source_target_pairs={{0,8},{4,12},{8,0},{12,4},{16,24},{20,28},{24,16},{28,20},{1,9},{5... | collective-permute-start | bytes 98312 | tf_op jit(solution)/shard_map/ppermute | solution.py:172
  51.7 1.3 collective-permute-start.21
  53.0 4.3 %collective-permute-done.25 = f16[8,8,1280]{2,1,0:T(8,128)(2,1)S(1)} collective-permute-done((f16[8,8,1280]{2,1,0:T(8,128)(2,1)S(1)}, f16[8,8,1280]{2,1,0:T(8,128)(2,1)S(1)}, u32[]{:S(2)}, u32[]{:S(2)}) %collective-permute-start.25) | collective-permute-done | bytes 163872 | tf_op jit(solution)/shard_map/ppermute | solution.py:172
  58.0 1.5 %collective-permute-start.26 = (bf16[2,8,1280]{2,1,0:T(8,128)(2,1)S(1)}, bf16[2,8,1280]{2,1,0:T(8,128)(2,1)S(1)}, u32[]{:S(2)}, u32[]{:S(2)}) collective-permute-start(bf16[2,8,1280]{2,1,0:T(8,128)(2,1)S(1)} %get-tuple-element.52), channel_id=1, source_target_pairs={{0,8},{4,12},{8,0},{12,4},{16,24},{20,28},{24,16},{28,20},{1,9},{5... | collective-permute-start | bytes 122888 | tf_op jit(solution)/shard_map/ppermute | solution.py:172
  60.2 1.3 collective-permute-start.28
  62.0 1.4 %collective-permute-done.27 = bf16[2,8,1280]{2,1,0:T(8,128)(2,1)S(1)} collective-permute-done((bf16[2,8,1280]{2,1,0:T(8,128)(2,1)S(1)}, bf16[2,8,1280]{2,1,0:T(8,128)(2,1)S(1)}, u32[]{:S(2)}, u32[]{:S(2)}) %collective-permute-start.27) | collective-permute-done | bytes 40992 | tf_op jit(solution)/shard_map/ppermute | solution.py:172
  63.4 1.7 %collective-permute-done.28 = bf16[2,8,1280]{2,1,0:T(8,128)(2,1)S(1)} collective-permute-done((bf16[2,8,1280]{2,1,0:T(8,128)(2,1)S(1)}, bf16[2,8,1280]{2,1,0:T(8,128)(2,1)S(1)}, u32[]{:S(2)}, u32[]{:S(2)}) %collective-permute-start.28) | collective-permute-done | bytes 40992 | tf_op jit(solution)/shard_map/ppermute | solution.py:172
  65.3 1.2 collective-permute-done.29
  67.9 5.2 %shard_map.76 = bf16[8,128,128]{2,1,0:T(8,128)(2,1)S(1)} custom-call(s32[8]{0:T(128)S(1)} %copy-done, bf16[8,128,128]{2,1,0:T(8,128)(2,1)S(1)} %pad_maximum_fusion.1.query, bf16[8,8,128]{2,1,0:T(8,128)(2,1)S(1)} %pad_maximum_fusion.9.key_new, f32[8,8,128]{2,1,0:T(8,128)S(1)} %get-tuple-element.82.value_new, bf16[8,512,1024]{2,1,0:T(8,128)(2,1)} %k_cache.1, ...), custom_call_target="tpu_custom_call" | custom-call | flops 2147483648 | bytes 8388608 | tf_op jit(solution)/shard_map/pallas_call | solution.py:142
  73.8 1.4 %collective-permute-start.39 = (bf16[8,4096]{1,0:T(8,128)(2,1)S(1)}, bf16[8,4096]{1,0:T(8,128)(2,1)S(1)}, u32[]{:S(2)}, u32[]{:S(2)}) collective-permute-start(bf16[8,4096]{1,0:T(8,128)(2,1)S(1)} %get-tuple-element.43), channel_id=1, source_target_pairs={{0,1},{1,0},{2,3},{3,2},{4,5},{5,4},{6,7},{7,6},{8,9},{9,8},{10,11... | collective-permute-start | bytes 196616 | tf_op jit(solution)/shard_map/ppermute | solution.py:172
  75.2 5.1 %collective-permute-start.30 = (bf16[8,4096]{1,0:T(8,128)(2,1)S(1)}, bf16[8,4096]{1,0:T(8,128)(2,1)S(1)}, u32[]{:S(2)}, u32[]{:S(2)}) collective-permute-start(bf16[8,4096]{1,0:T(8,128)(2,1)S(1)} %get-tuple-element.45), channel_id=1, source_target_pairs={{0,2},{1,3},{2,0},{3,1},{4,6},{5,7},{6,4},{7,5},{8,10},{9,11},{10,... | collective-permute-start | bytes 196616 | tf_op jit(solution)/shard_map/ppermute | solution.py:172
  80.6 3.6 %collective-permute-done.30 = bf16[8,4096]{1,0:T(8,128)(2,1)S(1)} collective-permute-done((bf16[8,4096]{1,0:T(8,128)(2,1)S(1)}, bf16[8,4096]{1,0:T(8,128)(2,1)S(1)}, u32[]{:S(2)}, u32[]{:S(2)}) %collective-permute-start.30) | collective-permute-done | bytes 65568 | tf_op jit(solution)/shard_map/ppermute | solution.py:172
  84.1 2.2 %collective-permute-done.31 = bf16[8,4096]{1,0:T(8,128)(2,1)S(1)} collective-permute-done((bf16[8,4096]{1,0:T(8,128)(2,1)S(1)}, bf16[8,4096]{1,0:T(8,128)(2,1)S(1)}, u32[]{:S(2)}, u32[]{:S(2)}) %collective-permute-start.31) | collective-permute-done | bytes 65568 | tf_op jit(solution)/shard_map/ppermute | solution.py:172
  86.7 1.2 collective-permute-start.35
  87.9 2.2 %collective-permute-start.37 = (bf16[16,4096]{1,0:T(8,128)(2,1)S(1)}, bf16[16,4096]{1,0:T(8,128)(2,1)S(1)}, u32[]{:S(2)}, u32[]{:S(2)}) collective-permute-start(bf16[16,4096]{1,0:T(8,128)(2,1)S(1)} %constant_dynamic-update-slice_fusion.2), channel_id=1, source_target_pairs={{0,24},{4,28},{8,16},{12,20},{16,8},{20,12},{24,0},{28,4},{1,25},{... | collective-permute-start | bytes 393224 | tf_op jit(solution)/shard_map/ppermute | solution.py:172
  90.2 2.6 %collective-permute-done.33 = bf16[16,4096]{1,0:T(8,128)(2,1)S(1)} collective-permute-done((bf16[16,4096]{1,0:T(8,128)(2,1)S(1)}, bf16[16,4096]{1,0:T(8,128)(2,1)S(1)}, u32[]{:S(2)}, u32[]{:S(2)}) %collective-permute-start.33) | collective-permute-done | bytes 131104 | tf_op jit(solution)/shard_map/ppermute | solution.py:172
  93.5 2.7 %collective-permute-done.35 = bf16[16,4096]{1,0:T(8,128)(2,1)S(1)} collective-permute-done((bf16[16,4096]{1,0:T(8,128)(2,1)S(1)}, bf16[16,4096]{1,0:T(8,128)(2,1)S(1)}, u32[]{:S(2)}, u32[]{:S(2)}) %collective-permute-start.35) | collective-permute-done | bytes 131104 | tf_op jit(solution)/shard_map/ppermute | solution.py:172
  98.0 4.9 %shard_map.77 = f32[256,1024]{1,0:T(8,128)S(1)} custom-call(bf16[128,4096]{1,0:T(8,128)(2,1)S(1)} %bitcast.241, bf16[128,4096]{1,0:T(8,128)(2,1)S(1)} %bitcast.243, bf16[4096,2048]{1,0:T(8,128)(2,1)} %weights.7), custom_call_target="tpu_custom_call" | custom-call | flops 2147483648 | bytes 8388608 | tf_op jit(solution)/shard_map/pallas_call | solution.py:213
  103.1 4.9 %shard_map.78 = f32[256,1024]{1,0:T(8,128)S(1)} custom-call(bf16[128,4096]{1,0:T(8,128)(2,1)S(1)} %bitcast.242, bf16[128,4096]{1,0:T(8,128)(2,1)S(1)} %bitcast.244, bf16[4096,2048]{1,0:T(8,128)(2,1)} %weights.7), custom_call_target="tpu_custom_call" | custom-call | flops 2147483648 | bytes 8388608 | tf_op jit(solution)/shard_map/pallas_call | solution.py:213
  108.1 2.1 %collective-permute-start.50 = (f16[8,8,1024]{2,1,0:T(8,128)(2,1)S(1)}, f16[8,8,1024]{2,1,0:T(8,128)(2,1)S(1)}, u32[]{:S(2)}, u32[]{:S(2)}) collective-permute-start(f16[8,8,1024]{2,1,0:T(8,128)(2,1)S(1)} %get-tuple-element.32), channel_id=1, source_target_pairs={{0,1},{1,0},{2,3},{3,2},{4,5},{5,4},{6,7},{7,6},{8,9},{9,8},{10,11... | collective-permute-start | bytes 393224 | tf_op jit(solution)/shard_map/ppermute | solution.py:172
  110.1 1.8 %collective-permute-done.47 = f16[2,8,8,1024]{3,2,1,0:T(8,128)(2,1)S(1)} collective-permute-done((f16[2,8,8,1024]{3,2,1,0:T(8,128)(2,1)S(1)}, f16[2,8,8,1024]{3,2,1,0:T(8,128)(2,1)S(1)}, u32[]{:S(2)}, u32[]{:S(2)}) %collective-permute-start.47) | collective-permute-done | bytes 262176 | tf_op jit(solution)/shard_map/ppermute | solution.py:172
  112.1 1.2 collective-permute-start.48
  113.3 1.0 collective-permute-done.50
  114.3 3.6 %collective-permute-start.51 = (f16[8,8,1024]{2,1,0:T(8,128)(2,1)S(1)}, f16[8,8,1024]{2,1,0:T(8,128)(2,1)S(1)}, u32[]{:S(2)}, u32[]{:S(2)}) collective-permute-start(f16[8,8,1024]{2,1,0:T(8,128)(2,1)S(1)} %fusion.25), channel_id=1, source_target_pairs={{0,2},{1,3},{2,0},{3,1},{4,6},{5,7},{6,4},{7,5},{8,10},{9,11},{10,... | collective-permute-start | bytes 393224 | tf_op jit(solution)/shard_map/ppermute | solution.py:172
  118.0 6.1 %collective-permute-done.48 = f16[8,8,1024]{2,1,0:T(8,128)(2,1)S(1)} collective-permute-done((f16[8,8,1024]{2,1,0:T(8,128)(2,1)S(1)}, f16[8,8,1024]{2,1,0:T(8,128)(2,1)S(1)}, u32[]{:S(2)}, u32[]{:S(2)}) %collective-permute-start.48) | collective-permute-done | bytes 131104 | tf_op jit(solution)/shard_map/ppermute | solution.py:172
  124.1 1.8 %collective-permute-done.51 = f16[8,8,1024]{2,1,0:T(8,128)(2,1)S(1)} collective-permute-done((f16[8,8,1024]{2,1,0:T(8,128)(2,1)S(1)}, f16[8,8,1024]{2,1,0:T(8,128)(2,1)S(1)}, u32[]{:S(2)}, u32[]{:S(2)}) %collective-permute-start.51) | collective-permute-done | bytes 131104 | tf_op jit(solution)/shard_map/ppermute | solution.py:172
  126.5 1.1 collective-permute-start.52
  128.0 2.1 %collective-permute-start.54 = (bf16[2,8,2048]{2,1,0:T(8,128)(2,1)S(1)}, bf16[2,8,2048]{2,1,0:T(8,128)(2,1)S(1)}, u32[]{:S(2)}, u32[]{:S(2)}) collective-permute-start(bf16[2,8,2048]{2,1,0:T(8,128)(2,1)S(1)} %get-tuple-element.41), channel_id=1, source_target_pairs={{0,24},{4,28},{8,16},{12,20},{16,8},{20,12},{24,0},{28,4},{1,25},{... | collective-permute-start | bytes 196616 | tf_op jit(solution)/shard_map/ppermute | solution.py:172
  130.1 1.0 collective-permute-done.52
  131.9 1.2 collective-permute-done.54
  133.2 1.3 collective-permute-done.55
  (172 shorter events, 17.8 us)
Async XLA Ops:
  3.0 6.5 %collective-permute-start.9 = (bf16[8,4096]{1,0:T(8,128)(2,1)S(1)}, bf16[8,4096]{1,0:T(8,128)(2,1)S(1)}, u32[]{:S(2)}, u32[]{:S(2)}) collective-permute-start(bf16[8,4096]{1,0:T(8,128)(2,1)S(1)} %get-tuple-element.47), channel_id=1, source_target_pairs={{0,1},{1,0},{2,3},{3,2},{4,5},{5,4},{6,7},{7,6},{8,9},{9,8},{10,11... | collective-permute-start | bytes 196616 | tf_op jit(solution)/shard_map/ppermute | solution.py:172
  6.0 7.3 %collective-permute-start = (bf16[8,4096]{1,0:T(8,128)(2,1)S(1)}, bf16[8,4096]{1,0:T(8,128)(2,1)S(1)}, u32[]{:S(2)}, u32[]{:S(2)}) collective-permute-start(bf16[8,4096]{1,0:T(8,128)(2,1)S(1)} %get-tuple-element.49), channel_id=1, source_target_pairs={{0,2},{1,3},{2,0},{3,1},{4,6},{5,7},{6,4},{7,5},{8,10},{9,11},{10,... | collective-permute-start | bytes 196616 | tf_op jit(solution)/shard_map/ppermute | solution.py:172
  8.6 7.1 %collective-permute-start.1 = (bf16[8,4096]{1,0:T(8,128)(2,1)S(1)}, bf16[8,4096]{1,0:T(8,128)(2,1)S(1)}, u32[]{:S(2)}, u32[]{:S(2)}) collective-permute-start(bf16[8,4096]{1,0:T(8,128)(2,1)S(1)} %get-tuple-element.48), channel_id=1, source_target_pairs={{0,3},{1,2},{2,1},{3,0},{4,7},{5,6},{6,5},{7,4},{8,11},{9,10},{10,... | collective-permute-start | bytes 196616 | tf_op jit(solution)/shard_map/ppermute | solution.py:172
  9.5 6.4 %collective-permute-start.10 = (bf16[16,4096]{1,0:T(8,128)(2,1)S(1)}, bf16[16,4096]{1,0:T(8,128)(2,1)S(1)}, u32[]{:S(2)}, u32[]{:S(2)}) collective-permute-start(bf16[16,4096]{1,0:T(8,128)(2,1)S(1)} %pad_maximum_fusion.4), channel_id=1, source_target_pairs={{0,4},{4,0},{8,12},{12,8},{16,20},{20,16},{24,28},{28,24},{1,5},{5... | collective-permute-start | bytes 393224 | tf_op jit(solution)/shard_map/ppermute | solution.py:172
  9.6 7.0 %collective-permute-start.11 = (bf16[16,4096]{1,0:T(8,128)(2,1)S(1)}, bf16[16,4096]{1,0:T(8,128)(2,1)S(1)}, u32[]{:S(2)}, u32[]{:S(2)}) collective-permute-start(bf16[16,4096]{1,0:T(8,128)(2,1)S(1)} %pad_maximum_fusion.4), channel_id=1, source_target_pairs={{0,8},{4,12},{8,0},{12,4},{16,24},{20,28},{24,16},{28,20},{1,9},{5... | collective-permute-start | bytes 393224 | tf_op jit(solution)/shard_map/ppermute | solution.py:172
  11.3 11.0 %collective-permute-start.13 = (bf16[16,4096]{1,0:T(8,128)(2,1)S(1)}, bf16[16,4096]{1,0:T(8,128)(2,1)S(1)}, u32[]{:S(2)}, u32[]{:S(2)}) collective-permute-start(bf16[16,4096]{1,0:T(8,128)(2,1)S(1)} %pad_maximum_fusion.4), channel_id=1, source_target_pairs={{0,16},{4,20},{8,24},{12,28},{16,0},{20,4},{24,8},{28,12},{1,17},{... | collective-permute-start | bytes 393224 | tf_op jit(solution)/shard_map/ppermute | solution.py:172
  13.3 9.6 %collective-permute-start.15 = (bf16[16,4096]{1,0:T(8,128)(2,1)S(1)}, bf16[16,4096]{1,0:T(8,128)(2,1)S(1)}, u32[]{:S(2)}, u32[]{:S(2)}) collective-permute-start(bf16[16,4096]{1,0:T(8,128)(2,1)S(1)} %pad_maximum_fusion.4), channel_id=1, source_target_pairs={{0,24},{4,28},{8,16},{12,20},{16,8},{20,12},{24,0},{28,4},{1,25},{... | collective-permute-start | bytes 393224 | tf_op jit(solution)/shard_map/ppermute | solution.py:172
  15.8 2.2 %collective-permute-start.2 = (bf16[16,4096]{1,0:T(8,128)(2,1)S(1)}, bf16[16,4096]{1,0:T(8,128)(2,1)S(1)}, u32[]{:S(2)}, u32[]{:S(2)}) collective-permute-start(bf16[16,4096]{1,0:T(8,128)(2,1)S(1)} %constant_dynamic-update-slice_fusion), channel_id=1, source_target_pairs={{0,4},{4,0},{8,12},{12,8},{16,20},{20,16},{24,28},{28,24},{1,5},{5... | collective-permute-start | bytes 393224 | tf_op jit(solution)/shard_map/ppermute | solution.py:172
  15.9 6.4 %collective-permute-start.3 = (bf16[16,4096]{1,0:T(8,128)(2,1)S(1)}, bf16[16,4096]{1,0:T(8,128)(2,1)S(1)}, u32[]{:S(2)}, u32[]{:S(2)}) collective-permute-start(bf16[16,4096]{1,0:T(8,128)(2,1)S(1)} %constant_dynamic-update-slice_fusion), channel_id=1, source_target_pairs={{0,8},{4,12},{8,0},{12,4},{16,24},{20,28},{24,16},{28,20},{1,9},{5... | collective-permute-start | bytes 393224 | tf_op jit(solution)/shard_map/ppermute | solution.py:172
  16.5 8.8 %collective-permute-start.5 = (bf16[16,4096]{1,0:T(8,128)(2,1)S(1)}, bf16[16,4096]{1,0:T(8,128)(2,1)S(1)}, u32[]{:S(2)}, u32[]{:S(2)}) collective-permute-start(bf16[16,4096]{1,0:T(8,128)(2,1)S(1)} %constant_dynamic-update-slice_fusion), channel_id=1, source_target_pairs={{0,16},{4,20},{8,24},{12,28},{16,0},{20,4},{24,8},{28,12},{1,17},{... | collective-permute-start | bytes 393224 | tf_op jit(solution)/shard_map/ppermute | solution.py:172
  18.0 7.3 %collective-permute-start.7 = (bf16[16,4096]{1,0:T(8,128)(2,1)S(1)}, bf16[16,4096]{1,0:T(8,128)(2,1)S(1)}, u32[]{:S(2)}, u32[]{:S(2)}) collective-permute-start(bf16[16,4096]{1,0:T(8,128)(2,1)S(1)} %constant_dynamic-update-slice_fusion), channel_id=1, source_target_pairs={{0,24},{4,28},{8,16},{12,20},{16,8},{20,12},{24,0},{28,4},{1,25},{... | collective-permute-start | bytes 393224 | tf_op jit(solution)/shard_map/ppermute | solution.py:172
  22.3 3.5 %collective-permute-start.12 = (bf16[16,4096]{1,0:T(8,128)(2,1)S(1)}, bf16[16,4096]{1,0:T(8,128)(2,1)S(1)}, u32[]{:S(2)}, u32[]{:S(2)}) collective-permute-start(bf16[16,4096]{1,0:T(8,128)(2,1)S(1)} %collective-permute-done.11), channel_id=1, source_target_pairs={{0,4},{4,0},{8,12},{12,8},{16,20},{20,16},{24,28},{28,24},{1,5},{5... | collective-permute-start | bytes 393224 | tf_op jit(solution)/shard_map/ppermute | solution.py:172
  22.4 3.6 %collective-permute-start.4 = (bf16[16,4096]{1,0:T(8,128)(2,1)S(1)}, bf16[16,4096]{1,0:T(8,128)(2,1)S(1)}, u32[]{:S(2)}, u32[]{:S(2)}) collective-permute-start(bf16[16,4096]{1,0:T(8,128)(2,1)S(1)} %collective-permute-done.3), channel_id=1, source_target_pairs={{0,4},{4,0},{8,12},{12,8},{16,20},{20,16},{24,28},{28,24},{1,5},{5... | collective-permute-start | bytes 393224 | tf_op jit(solution)/shard_map/ppermute | solution.py:172
  22.9 3.0 %collective-permute-start.14 = (bf16[16,4096]{1,0:T(8,128)(2,1)S(1)}, bf16[16,4096]{1,0:T(8,128)(2,1)S(1)}, u32[]{:S(2)}, u32[]{:S(2)}) collective-permute-start(bf16[16,4096]{1,0:T(8,128)(2,1)S(1)} %collective-permute-done.13), channel_id=1, source_target_pairs={{0,4},{4,0},{8,12},{12,8},{16,20},{20,16},{24,28},{28,24},{1,5},{5... | collective-permute-start | bytes 393224 | tf_op jit(solution)/shard_map/ppermute | solution.py:172
  32.2 8.5 %collective-permute-start.17 = (f16[2,8,8,1024]{3,2,1,0:T(8,128)(2,1)S(1)}, f16[2,8,8,1024]{3,2,1,0:T(8,128)(2,1)S(1)}, u32[]{:S(2)}, u32[]{:S(2)}) collective-permute-start(f16[2,8,8,1024]{3,2,1,0:T(8,128)(2,1)S(1)} %fusion.16), channel_id=1, source_target_pairs={{0,1},{1,0},{2,3},{3,2},{4,5},{5,4},{6,7},{7,6},{8,9},{9,8},{10,11... | collective-permute-start | bytes 786440 | tf_op jit(solution)/shard_map/ppermute | solution.py:172
  38.6 8.9 %collective-permute-start.24 = (f16[8,8,1280]{2,1,0:T(8,128)(2,1)S(1)}, f16[8,8,1280]{2,1,0:T(8,128)(2,1)S(1)}, u32[]{:S(2)}, u32[]{:S(2)}) collective-permute-start(f16[8,8,1280]{2,1,0:T(8,128)(2,1)S(1)} %get-tuple-element.30), channel_id=1, source_target_pairs={{0,1},{1,0},{2,3},{3,2},{4,5},{5,4},{6,7},{7,6},{8,9},{9,8},{10,11... | collective-permute-start | bytes 491528 | tf_op jit(solution)/shard_map/ppermute | solution.py:172
  40.8 8.6 %collective-permute-start.18 = (f16[8,8,1024]{2,1,0:T(8,128)(2,1)S(1)}, f16[8,8,1024]{2,1,0:T(8,128)(2,1)S(1)}, u32[]{:S(2)}, u32[]{:S(2)}) collective-permute-start(f16[8,8,1024]{2,1,0:T(8,128)(2,1)S(1)} %fusion.38), channel_id=1, source_target_pairs={{0,2},{1,3},{2,0},{3,1},{4,6},{5,7},{6,4},{7,5},{8,10},{9,11},{10,... | collective-permute-start | bytes 393224 | tf_op jit(solution)/shard_map/ppermute | solution.py:172
  47.6 9.7 %collective-permute-start.25 = (f16[8,8,1280]{2,1,0:T(8,128)(2,1)S(1)}, f16[8,8,1280]{2,1,0:T(8,128)(2,1)S(1)}, u32[]{:S(2)}, u32[]{:S(2)}) collective-permute-start(f16[8,8,1280]{2,1,0:T(8,128)(2,1)S(1)} %fusion.11), channel_id=1, source_target_pairs={{0,2},{1,3},{2,0},{3,1},{4,6},{5,7},{6,4},{7,5},{8,10},{9,11},{10,... | collective-permute-start | bytes 491528 | tf_op jit(solution)/shard_map/ppermute | solution.py:172
  49.3 8.5 %collective-permute-start.23 = (f16[8,8,1280]{2,1,0:T(8,128)(2,1)S(1)}, f16[8,8,1280]{2,1,0:T(8,128)(2,1)S(1)}, u32[]{:S(2)}, u32[]{:S(2)}) collective-permute-start(f16[8,8,1280]{2,1,0:T(8,128)(2,1)S(1)} %get-tuple-element.19), channel_id=1, source_target_pairs={{0,1},{1,0},{2,3},{3,2},{4,5},{5,4},{6,7},{7,6},{8,9},{9,8},{10,11... | collective-permute-start | bytes 491528 | tf_op jit(solution)/shard_map/ppermute | solution.py:172
  49.4 10.8 %collective-permute-start.19 = (bf16[2,8,1024]{2,1,0:T(8,128)(2,1)S(1)}, bf16[2,8,1024]{2,1,0:T(8,128)(2,1)S(1)}, u32[]{:S(2)}, u32[]{:S(2)}) collective-permute-start(bf16[2,8,1024]{2,1,0:T(8,128)(2,1)S(1)} %get-tuple-element.57), channel_id=1, source_target_pairs={{0,8},{4,12},{8,0},{12,4},{16,24},{20,28},{24,16},{28,20},{1,9},{5... | collective-permute-start | bytes 98312 | tf_op jit(solution)/shard_map/ppermute | solution.py:172
  50.9 10.7 %collective-permute-start.20 = (bf16[2,8,1024]{2,1,0:T(8,128)(2,1)S(1)}, bf16[2,8,1024]{2,1,0:T(8,128)(2,1)S(1)}, u32[]{:S(2)}, u32[]{:S(2)}) collective-permute-start(bf16[2,8,1024]{2,1,0:T(8,128)(2,1)S(1)} %get-tuple-element.59), channel_id=1, source_target_pairs={{0,16},{4,20},{8,24},{12,28},{16,0},{20,4},{24,8},{28,12},{1,17},{... | collective-permute-start | bytes 98312 | tf_op jit(solution)/shard_map/ppermute | solution.py:172
  51.7 9.8 %collective-permute-start.21 = (bf16[2,8,1024]{2,1,0:T(8,128)(2,1)S(1)}, bf16[2,8,1024]{2,1,0:T(8,128)(2,1)S(1)}, u32[]{:S(2)}, u32[]{:S(2)}) collective-permute-start(bf16[2,8,1024]{2,1,0:T(8,128)(2,1)S(1)} %get-tuple-element.58), channel_id=1, source_target_pairs={{0,24},{4,28},{8,16},{12,20},{16,8},{20,12},{24,0},{28,4},{1,25},{... | collective-permute-start | bytes 98312 | tf_op jit(solution)/shard_map/ppermute | solution.py:172
  58.0 4.1 %collective-permute-start.26 = (bf16[2,8,1280]{2,1,0:T(8,128)(2,1)S(1)}, bf16[2,8,1280]{2,1,0:T(8,128)(2,1)S(1)}, u32[]{:S(2)}, u32[]{:S(2)}) collective-permute-start(bf16[2,8,1280]{2,1,0:T(8,128)(2,1)S(1)} %get-tuple-element.52), channel_id=1, source_target_pairs={{0,8},{4,12},{8,0},{12,4},{16,24},{20,28},{24,16},{28,20},{1,9},{5... | collective-permute-start | bytes 122888 | tf_op jit(solution)/shard_map/ppermute | solution.py:172
  59.4 4.0 %collective-permute-start.27 = (bf16[2,8,1280]{2,1,0:T(8,128)(2,1)S(1)}, bf16[2,8,1280]{2,1,0:T(8,128)(2,1)S(1)}, u32[]{:S(2)}, u32[]{:S(2)}) collective-permute-start(bf16[2,8,1280]{2,1,0:T(8,128)(2,1)S(1)} %get-tuple-element.54), channel_id=1, source_target_pairs={{0,16},{4,20},{8,24},{12,28},{16,0},{20,4},{24,8},{28,12},{1,17},{... | collective-permute-start | bytes 122888 | tf_op jit(solution)/shard_map/ppermute | solution.py:172
  60.2 4.9 %collective-permute-start.28 = (bf16[2,8,1280]{2,1,0:T(8,128)(2,1)S(1)}, bf16[2,8,1280]{2,1,0:T(8,128)(2,1)S(1)}, u32[]{:S(2)}, u32[]{:S(2)}) collective-permute-start(bf16[2,8,1280]{2,1,0:T(8,128)(2,1)S(1)} %get-tuple-element.53), channel_id=1, source_target_pairs={{0,24},{4,28},{8,16},{12,20},{16,8},{20,12},{24,0},{28,4},{1,25},{... | collective-permute-start | bytes 122888 | tf_op jit(solution)/shard_map/ppermute | solution.py:172
  61.6 3.7 %collective-permute-start.22 = (bf16[4,8,1024]{2,1,0:T(8,128)(2,1)S(1)}, bf16[4,8,1024]{2,1,0:T(8,128)(2,1)S(1)}, u32[]{:S(2)}, u32[]{:S(2)}) collective-permute-start(bf16[4,8,1024]{2,1,0:T(8,128)(2,1)S(1)} %pad_maximum_fusion.8), channel_id=1, source_target_pairs={{0,4},{4,0},{8,12},{12,8},{16,20},{20,16},{24,28},{28,24},{1,5},{5... | collective-permute-start | bytes 196616 | tf_op jit(solution)/shard_map/ppermute | solution.py:172
  73.8 6.5 %collective-permute-start.39 = (bf16[8,4096]{1,0:T(8,128)(2,1)S(1)}, bf16[8,4096]{1,0:T(8,128)(2,1)S(1)}, u32[]{:S(2)}, u32[]{:S(2)}) collective-permute-start(bf16[8,4096]{1,0:T(8,128)(2,1)S(1)} %get-tuple-element.43), channel_id=1, source_target_pairs={{0,1},{1,0},{2,3},{3,2},{4,5},{5,4},{6,7},{7,6},{8,9},{9,8},{10,11... | collective-permute-start | bytes 196616 | tf_op jit(solution)/shard_map/ppermute | solution.py:172
  75.2 8.9 %collective-permute-start.30 = (bf16[8,4096]{1,0:T(8,128)(2,1)S(1)}, bf16[8,4096]{1,0:T(8,128)(2,1)S(1)}, u32[]{:S(2)}, u32[]{:S(2)}) collective-permute-start(bf16[8,4096]{1,0:T(8,128)(2,1)S(1)} %get-tuple-element.45), channel_id=1, source_target_pairs={{0,2},{1,3},{2,0},{3,1},{4,6},{5,7},{6,4},{7,5},{8,10},{9,11},{10,... | collective-permute-start | bytes 196616 | tf_op jit(solution)/shard_map/ppermute | solution.py:172
  80.3 6.1 %collective-permute-start.31 = (bf16[8,4096]{1,0:T(8,128)(2,1)S(1)}, bf16[8,4096]{1,0:T(8,128)(2,1)S(1)}, u32[]{:S(2)}, u32[]{:S(2)}) collective-permute-start(bf16[8,4096]{1,0:T(8,128)(2,1)S(1)} %get-tuple-element.44), channel_id=1, source_target_pairs={{0,3},{1,2},{2,1},{3,0},{4,7},{5,6},{6,5},{7,4},{8,11},{9,10},{10,... | collective-permute-start | bytes 196616 | tf_op jit(solution)/shard_map/ppermute | solution.py:172
  80.3 6.2 %collective-permute-start.40 = (bf16[16,4096]{1,0:T(8,128)(2,1)S(1)}, bf16[16,4096]{1,0:T(8,128)(2,1)S(1)}, u32[]{:S(2)}, u32[]{:S(2)}) collective-permute-start(bf16[16,4096]{1,0:T(8,128)(2,1)S(1)} %pad_maximum_fusion.6), channel_id=1, source_target_pairs={{0,4},{4,0},{8,12},{12,8},{16,20},{20,16},{24,28},{28,24},{1,5},{5... | collective-permute-start | bytes 393224 | tf_op jit(solution)/shard_map/ppermute | solution.py:172
  80.4 6.4 %collective-permute-start.41 = (bf16[16,4096]{1,0:T(8,128)(2,1)S(1)}, bf16[16,4096]{1,0:T(8,128)(2,1)S(1)}, u32[]{:S(2)}, u32[]{:S(2)}) collective-permute-start(bf16[16,4096]{1,0:T(8,128)(2,1)S(1)} %pad_maximum_fusion.6), channel_id=1, source_target_pairs={{0,8},{4,12},{8,0},{12,4},{16,24},{20,28},{24,16},{28,20},{1,9},{5... | collective-permute-start | bytes 393224 | tf_op jit(solution)/shard_map/ppermute | solution.py:172
  80.4 12.4 %collective-permute-start.43 = (bf16[16,4096]{1,0:T(8,128)(2,1)S(1)}, bf16[16,4096]{1,0:T(8,128)(2,1)S(1)}, u32[]{:S(2)}, u32[]{:S(2)}) collective-permute-start(bf16[16,4096]{1,0:T(8,128)(2,1)S(1)} %pad_maximum_fusion.6), channel_id=1, source_target_pairs={{0,16},{4,20},{8,24},{12,28},{16,0},{20,4},{24,8},{28,12},{1,17},{... | collective-permute-start | bytes 393224 | tf_op jit(solution)/shard_map/ppermute | solution.py:172
  84.1 9.3 %collective-permute-start.45 = (bf16[16,4096]{1,0:T(8,128)(2,1)S(1)}, bf16[16,4096]{1,0:T(8,128)(2,1)S(1)}, u32[]{:S(2)}, u32[]{:S(2)}) collective-permute-start(bf16[16,4096]{1,0:T(8,128)(2,1)S(1)} %pad_maximum_fusion.6), channel_id=1, source_target_pairs={{0,24},{4,28},{8,16},{12,20},{16,8},{20,12},{24,0},{28,4},{1,25},{... | collective-permute-start | bytes 393224 | tf_op jit(solution)/shard_map/ppermute | solution.py:172
  86.3 1.6 %collective-permute-start.32 = (bf16[16,4096]{1,0:T(8,128)(2,1)S(1)}, bf16[16,4096]{1,0:T(8,128)(2,1)S(1)}, u32[]{:S(2)}, u32[]{:S(2)}) collective-permute-start(bf16[16,4096]{1,0:T(8,128)(2,1)S(1)} %constant_dynamic-update-slice_fusion.2), channel_id=1, source_target_pairs={{0,4},{4,0},{8,12},{12,8},{16,20},{20,16},{24,28},{28,24},{1,5},{5... | collective-permute-start | bytes 393224 | tf_op jit(solution)/shard_map/ppermute | solution.py:172
  86.4 6.4 %collective-permute-start.33 = (bf16[16,4096]{1,0:T(8,128)(2,1)S(1)}, bf16[16,4096]{1,0:T(8,128)(2,1)S(1)}, u32[]{:S(2)}, u32[]{:S(2)}) collective-permute-start(bf16[16,4096]{1,0:T(8,128)(2,1)S(1)} %constant_dynamic-update-slice_fusion.2), channel_id=1, source_target_pairs={{0,8},{4,12},{8,0},{12,4},{16,24},{20,28},{24,16},{28,20},{1,9},{5... | collective-permute-start | bytes 393224 | tf_op jit(solution)/shard_map/ppermute | solution.py:172
  86.7 9.4 %collective-permute-start.35 = (bf16[16,4096]{1,0:T(8,128)(2,1)S(1)}, bf16[16,4096]{1,0:T(8,128)(2,1)S(1)}, u32[]{:S(2)}, u32[]{:S(2)}) collective-permute-start(bf16[16,4096]{1,0:T(8,128)(2,1)S(1)} %constant_dynamic-update-slice_fusion.2), channel_id=1, source_target_pairs={{0,16},{4,20},{8,24},{12,28},{16,0},{20,4},{24,8},{28,12},{1,17},{... | collective-permute-start | bytes 393224 | tf_op jit(solution)/shard_map/ppermute | solution.py:172
  87.9 8.2 %collective-permute-start.37 = (bf16[16,4096]{1,0:T(8,128)(2,1)S(1)}, bf16[16,4096]{1,0:T(8,128)(2,1)S(1)}, u32[]{:S(2)}, u32[]{:S(2)}) collective-permute-start(bf16[16,4096]{1,0:T(8,128)(2,1)S(1)} %constant_dynamic-update-slice_fusion.2), channel_id=1, source_target_pairs={{0,24},{4,28},{8,16},{12,20},{16,8},{20,12},{24,0},{28,4},{1,25},{... | collective-permute-start | bytes 393224 | tf_op jit(solution)/shard_map/ppermute | solution.py:172
  92.8 3.9 %collective-permute-start.42 = (bf16[16,4096]{1,0:T(8,128)(2,1)S(1)}, bf16[16,4096]{1,0:T(8,128)(2,1)S(1)}, u32[]{:S(2)}, u32[]{:S(2)}) collective-permute-start(bf16[16,4096]{1,0:T(8,128)(2,1)S(1)} %collective-permute-done.41), channel_id=1, source_target_pairs={{0,4},{4,0},{8,12},{12,8},{16,20},{20,16},{24,28},{28,24},{1,5},{5... | collective-permute-start | bytes 393224 | tf_op jit(solution)/shard_map/ppermute | solution.py:172
  92.8 4.0 %collective-permute-start.34 = (bf16[16,4096]{1,0:T(8,128)(2,1)S(1)}, bf16[16,4096]{1,0:T(8,128)(2,1)S(1)}, u32[]{:S(2)}, u32[]{:S(2)}) collective-permute-start(bf16[16,4096]{1,0:T(8,128)(2,1)S(1)} %collective-permute-done.33), channel_id=1, source_target_pairs={{0,4},{4,0},{8,12},{12,8},{16,20},{20,16},{24,28},{28,24},{1,5},{5... | collective-permute-start | bytes 393224 | tf_op jit(solution)/shard_map/ppermute | solution.py:172
  93.4 3.4 %collective-permute-start.44 = (bf16[16,4096]{1,0:T(8,128)(2,1)S(1)}, bf16[16,4096]{1,0:T(8,128)(2,1)S(1)}, u32[]{:S(2)}, u32[]{:S(2)}) collective-permute-start(bf16[16,4096]{1,0:T(8,128)(2,1)S(1)} %collective-permute-done.43), channel_id=1, source_target_pairs={{0,4},{4,0},{8,12},{12,8},{16,20},{20,16},{24,28},{28,24},{1,5},{5... | collective-permute-start | bytes 393224 | tf_op jit(solution)/shard_map/ppermute | solution.py:172
  103.0 8.9 %collective-permute-start.47 = (f16[2,8,8,1024]{3,2,1,0:T(8,128)(2,1)S(1)}, f16[2,8,8,1024]{3,2,1,0:T(8,128)(2,1)S(1)}, u32[]{:S(2)}, u32[]{:S(2)}) collective-permute-start(f16[2,8,8,1024]{3,2,1,0:T(8,128)(2,1)S(1)} %fusion.17), channel_id=1, source_target_pairs={{0,1},{1,0},{2,3},{3,2},{4,5},{5,4},{6,7},{7,6},{8,9},{9,8},{10,11... | collective-permute-start | bytes 786440 | tf_op jit(solution)/shard_map/ppermute | solution.py:172
  108.1 6.2 %collective-permute-start.50 = (f16[8,8,1024]{2,1,0:T(8,128)(2,1)S(1)}, f16[8,8,1024]{2,1,0:T(8,128)(2,1)S(1)}, u32[]{:S(2)}, u32[]{:S(2)}) collective-permute-start(f16[8,8,1024]{2,1,0:T(8,128)(2,1)S(1)} %get-tuple-element.32), channel_id=1, source_target_pairs={{0,1},{1,0},{2,3},{3,2},{4,5},{5,4},{6,7},{7,6},{8,9},{9,8},{10,11... | collective-permute-start | bytes 393224 | tf_op jit(solution)/shard_map/ppermute | solution.py:172
  112.1 12.0 %collective-permute-start.48 = (f16[8,8,1024]{2,1,0:T(8,128)(2,1)S(1)}, f16[8,8,1024]{2,1,0:T(8,128)(2,1)S(1)}, u32[]{:S(2)}, u32[]{:S(2)}) collective-permute-start(f16[8,8,1024]{2,1,0:T(8,128)(2,1)S(1)} %fusion.39), channel_id=1, source_target_pairs={{0,2},{1,3},{2,0},{3,1},{4,6},{5,7},{6,4},{7,5},{8,10},{9,11},{10,... | collective-permute-start | bytes 393224 | tf_op jit(solution)/shard_map/ppermute | solution.py:172
  114.3 11.5 %collective-permute-start.51 = (f16[8,8,1024]{2,1,0:T(8,128)(2,1)S(1)}, f16[8,8,1024]{2,1,0:T(8,128)(2,1)S(1)}, u32[]{:S(2)}, u32[]{:S(2)}) collective-permute-start(f16[8,8,1024]{2,1,0:T(8,128)(2,1)S(1)} %fusion.25), channel_id=1, source_target_pairs={{0,2},{1,3},{2,0},{3,1},{4,6},{5,7},{6,4},{7,5},{8,10},{9,11},{10,... | collective-permute-start | bytes 393224 | tf_op jit(solution)/shard_map/ppermute | solution.py:172
  118.0 8.5 %collective-permute-start.49 = (f16[8,8,1024]{2,1,0:T(8,128)(2,1)S(1)}, f16[8,8,1024]{2,1,0:T(8,128)(2,1)S(1)}, u32[]{:S(2)}, u32[]{:S(2)}) collective-permute-start(f16[8,8,1024]{2,1,0:T(8,128)(2,1)S(1)} %get-tuple-element.24), channel_id=1, source_target_pairs={{0,1},{1,0},{2,3},{3,2},{4,5},{5,4},{6,7},{7,6},{8,9},{9,8},{10,11... | collective-permute-start | bytes 393224 | tf_op jit(solution)/shard_map/ppermute | solution.py:172
  126.5 4.5 %collective-permute-start.52 = (bf16[2,8,2048]{2,1,0:T(8,128)(2,1)S(1)}, bf16[2,8,2048]{2,1,0:T(8,128)(2,1)S(1)}, u32[]{:S(2)}, u32[]{:S(2)}) collective-permute-start(bf16[2,8,2048]{2,1,0:T(8,128)(2,1)S(1)} %get-tuple-element.39), channel_id=1, source_target_pairs={{0,8},{4,12},{8,0},{12,4},{16,24},{20,28},{24,16},{28,20},{1,9},{5... | collective-permute-start | bytes 196616 | tf_op jit(solution)/shard_map/ppermute | solution.py:172
  127.7 4.3 %collective-permute-start.53 = (bf16[2,8,2048]{2,1,0:T(8,128)(2,1)S(1)}, bf16[2,8,2048]{2,1,0:T(8,128)(2,1)S(1)}, u32[]{:S(2)}, u32[]{:S(2)}) collective-permute-start(bf16[2,8,2048]{2,1,0:T(8,128)(2,1)S(1)} %get-tuple-element.40), channel_id=1, source_target_pairs={{0,16},{4,20},{8,24},{12,28},{16,0},{20,4},{24,8},{28,12},{1,17},{... | collective-permute-start | bytes 196616 | tf_op jit(solution)/shard_map/ppermute | solution.py:172
  128.0 5.2 %collective-permute-start.54 = (bf16[2,8,2048]{2,1,0:T(8,128)(2,1)S(1)}, bf16[2,8,2048]{2,1,0:T(8,128)(2,1)S(1)}, u32[]{:S(2)}, u32[]{:S(2)}) collective-permute-start(bf16[2,8,2048]{2,1,0:T(8,128)(2,1)S(1)} %get-tuple-element.41), channel_id=1, source_target_pairs={{0,24},{4,28},{8,16},{12,20},{16,8},{20,12},{24,0},{28,4},{1,25},{... | collective-permute-start | bytes 196616 | tf_op jit(solution)/shard_map/ppermute | solution.py:172
  (9 other events, 41.0 us)

commit v4 on v2

--- a/solution.py
+++ b/solution.py
@@ -34,45 +34,95 @@
 
 PART = 128
 GROUP = 4
-
-
-def attend_kernel(lengths, query, key_new, value_new, k_cache, v_cache, out, keys, values, wide, sems):
-    rows, span = keys.shape[:2]
+EARLY = 4
+FETCH_ROOM = 38 * 2**20
+ATTEND_ROOM = 44 * 2**20
+
+
+def by_length(length, span, act):
+    for case in range(1, span // PART + 1):
+        pl.when((length + PART - 1) // PART == case)(functools.partial(act, case * PART))
+
+
+def cache_copies(lengths, k_cache, v_cache, keys, values, sems, first):
+    pairs = ((k_cache, keys), (v_cache, values))
+
+    def copy(cache, at, count):
+        source, target = pairs[cache]
+        some = pl.ds(0, count)
+        return pltpu.make_async_copy(
+            source.at[first + at, some], target.at[at, some], sems.at[at, cache]
+        )
+
+    def start(cache, at):
+        by_length(
+            lengths[first + at], keys.shape[1], lambda count: copy(cache, at, count).start()
+        )
+
+    def wait(cache, at):
+        by_length(
+            lengths[first + at], keys.shape[1], lambda count: copy(cache, at, count).wait()
+        )
+
+    def clear(at):
+        for part in range(1, values.shape[1] // PART):
+
+            @pl.when(lengths[first + at] <= part * PART)
+            def _():
+                values[at, part * PART : (part + 1) * PART] = jnp.zeros(
+                    (PART, values.shape[2]), values.dtype
+                )
+
+    return start, wait, clear
+
+
+def fetch_kernel(lengths, k_cache, v_cache, keys, values, sems):
+    rows = keys.shape[0]
+    start, wait, clear = cache_copies(lengths, k_cache, v_cache, keys, values, sems, 0)
+    for act in (start, wait):
+        for cache in range(2):
+            for at in range(rows):
+                act(cache, at)
+        if act is start:
+            for at in range(rows):
+                clear(at)
+
+
+def fetch(lengths, k_cache, v_cache):
+    vmem = pl.BlockSpec(memory_space=pltpu.VMEM)
+    anywhere = pl.BlockSpec(memory_space=pl.ANY)
+    shape = jax.ShapeDtypeStruct((EARLY,) + k_cache.shape[1:], k_cache.dtype)
+    return pl.pallas_call(
+        fetch_kernel,
+        in_specs=[pl.BlockSpec(memory_space=pltpu.SMEM), anywhere, anywhere],
+        out_specs=[vmem, vmem],
+        out_shape=[shape, shape],
+        scratch_shapes=[pltpu.SemaphoreType.DMA((EARLY, 2))],
+        compiler_params=pltpu.CompilerParams(vmem_limit_bytes=FETCH_ROOM),
+        cost_estimate=pl.CostEstimate(
+            flops=0, bytes_accessed=4 * EARLY * shape.shape[1] * shape.shape[2], transcendentals=0
+        ),
+    )(lengths, k_cache, v_cache)
+
+
+def attend_kernel(
+    lengths, query, key_new, value_new, early_keys, early_values, k_cache, v_cache, out,
+    keys, values, wide, sems,
+):
+    rows = query.shape[0]
+    span = keys.shape[1]
+    early = early_keys.shape[0]
     share = HQ // KVH
-    parts = span // PART
     scale = 1.0 / math.sqrt(HD)
-
-    def copies(row, count):
-        some = pl.ds(0, count)
-        return (
-            pltpu.make_async_copy(k_cache.at[row, some], keys.at[row, some], sems.at[row, 0]),
-            pltpu.make_async_copy(v_cache.at[row, some], values.at[row, some], sems.at[row, 1]),
-        )
-
-    def by_length(length, act):
-        for case in range(1, parts + 1):
-            pl.when((length + PART - 1) // PART == case)(functools.partial(act, case * PART))
-
-    def fetch(row, count):
-        for copy in copies(row, count):
-            copy.start()
-
-    def arrive(row, count):
-        for copy in copies(row, count):
-            copy.wait()
-
-    def clear(row, part):
-        values[row, part * PART : (part + 1) * PART] = jnp.zeros(
-            (PART, values.shape[2]), values.dtype
-        )
-
-    def score(row, wide, count):
+    start, wait, clear = cache_copies(lengths, k_cache, v_cache, keys, values, sems, early)
+
+    def score(row, row_keys, wide):
         for group in range(KVH):
             heads = pl.ds(group * share, share)
             wide[heads, group * HD : (group + 1) * HD] = query[row, heads]
         scores = lax.dot_general(
             wide[...],
-            keys[row, :count],
+            row_keys,
             (((1,), (1,)), ((), ())),
             preferred_element_type=jnp.float32,
         )
@@ -90,41 +140,47 @@
         weights = (probs * unit).astype(jnp.bfloat16)
         return weights, (pnew * unit).astype(jnp.bfloat16).astype(jnp.float32)
 
-    def mix(row, weights, wnew, count):
-        mixed = jnp.dot(weights, values[row, :count], preferred_element_type=jnp.float32)
+    def mix(row, weights, wnew, row_values):
+        mixed = jnp.dot(weights, row_values, preferred_element_type=jnp.float32)
         for group in range(KVH):
             heads = slice(group * share, (group + 1) * share)
             own = mixed[heads, group * HD : (group + 1) * HD]
             own = own + wnew[heads] * value_new[row, group : group + 1]
             out[row, heads] = own.astype(out.dtype)
 
-    def group(row, count):
-        each = [row + at for at in range(GROUP)]
-        for one in each:
-            by_length(lengths[one], functools.partial(arrive, one))
-            for part in range(1, count // PART):
-                pl.when(lengths[one] <= part * PART)(functools.partial(clear, one, part))
-        scores = [score(one, wide.at[at], count) for at, one in enumerate(each)]
-        weighed = [weigh(one, of_one) for one, of_one in zip(each, scores)]
-        for one, (weights, wnew) in zip(each, weighed):
-            mix(one, weights, wnew, count)
-
-    @pl.loop(0, rows)
-    def _(row):
-        by_length(lengths[row], functools.partial(fetch, row))
-
+    def group(first, base, late, count):
+        some_keys, some_values = (keys, values) if late else (early_keys, early_values)
+        each = range(GROUP)
+        if late:
+            for at in each:
+                wait(0, base + at)
+        scores = [
+            score(first + at, some_keys[base + at, :count], wide.at[at]) for at in each
+        ]
+        weighed = [weigh(first + at, scores[at]) for at in each]
+        if late:
+            for at in each:
+                wait(1, base + at)
+        for at, (weights, wnew) in zip(each, weighed):
+            mix(first + at, weights, wnew, some_values[base + at, :count])
+
+    for base in range(0, rows - early, GROUP):
+        for cache in range(2):
+            for at in range(GROUP):
+                start(cache, base + at)
     wide[...] = jnp.zeros_like(wide)
-
-    @pl.loop(0, rows // GROUP)
-    def _(index):
-        row = index * GROUP
-        longest = lengths[row]
+    for at in range(rows - early):
+        clear(at)
+    for first in range(0, rows, GROUP):
+        longest = lengths[first]
         for at in range(1, GROUP):
-            longest = jnp.maximum(longest, lengths[row + at])
-        by_length(longest, functools.partial(group, row))
-
-
-def attend_local(owned, k_cache, v_cache, lengths):
+            longest = jnp.maximum(longest, lengths[first + at])
+        late = first >= early
+        base = first - early if late else first
+        by_length(longest, span, functools.partial(group, first, base, late))
+
+
+def attend_local(owned, early, k_cache, v_cache, lengths):
     rows = owned.shape[0]
     query = owned[:, : HQ * HD].reshape(rows, HQ, HD).astype(jnp.float32)
     key_new = owned[:, HQ * HD : (HQ + KVH) * HD].reshape(rows, KVH, HD).astype(jnp.float32)
@@ -137,29 +193,22 @@
     anywhere = pl.BlockSpec(memory_space=pl.ANY)
     mixed = pl.pallas_call(
         attend_kernel,
-        in_specs=[
-            pl.BlockSpec(memory_space=pltpu.SMEM),
-            vmem,
-            vmem,
-            vmem,
-            anywhere,
-            anywhere,
-        ],
+        in_specs=[pl.BlockSpec(memory_space=pltpu.SMEM)] + [vmem] * 5 + [anywhere] * 2,
         out_specs=vmem,
         out_shape=jax.ShapeDtypeStruct((rows, HQ, HD), jnp.bfloat16),
         scratch_shapes=[
-            pltpu.VMEM((rows, span, width), jnp.bfloat16),
-            pltpu.VMEM((rows, span, width), jnp.bfloat16),
+            pltpu.VMEM((rows - EARLY, span, width), jnp.bfloat16),
+            pltpu.VMEM((rows - EARLY, span, width), jnp.bfloat16),
             pltpu.VMEM((GROUP, HQ, width), jnp.bfloat16),
-            pltpu.SemaphoreType.DMA((rows, 2)),
+            pltpu.SemaphoreType.DMA((rows - EARLY, 2)),
         ],
-        compiler_params=pltpu.CompilerParams(vmem_limit_bytes=ROOM),
+        compiler_params=pltpu.CompilerParams(vmem_limit_bytes=ATTEND_ROOM),
         cost_estimate=pl.CostEstimate(
             flops=4 * rows * span * width * HQ,
             bytes_accessed=2 * rows * span * width,
             transcendentals=rows * span * HQ,
         ),
-    )(lengths, query, key_new, value_new, k_cache, v_cache)
+    )(lengths, query, key_new, value_new, *early, k_cache, v_cache)
     return mixed.reshape(rows, HQ * HD)
 
 
@@ -173,8 +222,11 @@
         pieces = lax.all_gather(block, "gx", axis=0)
         count, rows, width = pieces.shape
         return pieces.reshape(count, 2, rows // 2, width).transpose(1, 0, 2, 3)
-    mine = [block] + [swap(block, "gx", chip) for chip in (2, 4, 6)]
-    theirs = [swap(piece, "gx", 1) for piece in mine]
+    other = swap(block, "gx", 1)
+    later = lax.optimization_barrier((block, other))[0]
+    mine = [swap(block, "gx", 2), swap(block, "gx", 4), swap(later, "gx", 6)]
+    theirs = [other] + [swap(piece, "gx", 1) for piece in mine]
+    mine = [block] + mine
     pieces = [piece for pair in zip(mine, theirs) for piece in pair]
     halves = [piece.reshape(2, 1, -1, block.shape[1]) for piece in pieces]
     return jnp.concatenate(halves, axis=1)
@@ -224,7 +276,7 @@
     )(far, near, weights)
 
 
-def project(rows, weights, scale):
+def project(rows, weights, scale, beside=None):
     width, columns = weights.shape
     here = lax.axis_index("gy")
 
@@ -250,15 +302,16 @@
     go_left, far, near = lax.optimization_barrier((go_left, far, near))
     left = left[:, 0] + send(go_left, 1)
     if first == columns:
-        return [left[1] + send(pack(left[0]), 2)]
+        return [left[1] + send(pack(left[0]), 2)], beside and beside(go_left)
     right = multiply(far, near, weights, first, columns - first)
     right = right.reshape(shape + (columns - first,))
     go_far = pack(right[0, 1])
     across, go_near = lax.optimization_barrier((pack(left[0]), pack(right[1, 1])))
+    others = beside and beside(across)
     left = left[1] + send(across, 2)
     across = pack(right[0, 0] + send(go_far, 1))
     right = right[1, 0] + send(go_near, 1) + send(across, 2)
-    return [left, right]
+    return [left, right], others
 
 
 def collect(columns):
@@ -303,11 +356,14 @@
     normed = (
         widened * lax.rsqrt(jnp.mean(widened * widened, axis=-1, keepdims=True) + eps) * norm_gain
     ).astype(jnp.bfloat16)
-    qkv = project(normed, w_qkv, 32.0)
-    owned = deliver(qkv)
-    attended = attend_local(owned, k_cache, v_cache, lengths)
+    def caches(ready):
+        return fetch(lax.optimization_barrier((lengths, ready))[0], k_cache, v_cache)
+
+    qkv, early = project(normed, w_qkv, 32.0, caches)
+    attended = attend_local(deliver(qkv), early, k_cache, v_cache, lengths)
     scaled, unit = level(attended)
-    out = deliver(project(scaled, w_out, 8.0))
+    out, _ = project(scaled, w_out, 8.0)
+    out = deliver([jnp.concatenate(out, axis=-1)])
     return (out.astype(jnp.float32) * unit).astype(jnp.bfloat16)
 
 

time: 138 us -> 144 us (1.043)
  starting transfers between devices: 61.4 us -> 51.6 us
  local copies, waits for them, and re-layouts: 1.76 us -> 9.33 us
  waiting for transfers between devices: 42.9 us -> 49.6 us
  Pallas kernels: 24.7 us -> 27 us
    ppermute x60 -> x56, starting transfers between devices: 61.4 us -> 51.6 us  [swap(): return lax.ppermute(block, axis, [(i, i ^ bit) for i in range(count)])]
    unnamed x31 -> x39, local copies, waits for them, and re-layouts: 0.39 us -> 8 us
    ppermute x60 -> x56, waiting for transfers between devices: 42.9 us -> 49.6 us  [swap(): return lax.ppermute(block, axis, [(i, i ^ bit) for i in range(count)])]
    pallas_call x0 -> x1, Pallas kernels: none -> 2.62 us  [fetch(): pl.pallas_call(fetch_kernel, in_specs=[pl.BlockSpec(memory_space=pltpu.SM...]
  transfers between devices with their start and end apart: 60 -> 56, of which waited for: 27 -> 29; matrix products, arithmetic and copies ran while one was open for 1% -> 1% of each run, Pallas kernels for 8% -> 9%
where the time goes in v4:
time: 144 us
  starting transfers between devices  51.6 us (36%)
  waiting for transfers between devices  49.6 us (34%)
  Pallas kernels  27 us (19%)
  local copies, waits for them, and re-layouts  9.33 us (6%)
  other arithmetic  6.02 us (4%)
    ppermute x56, starting transfers between devices, swap(): return lax.ppermute(block, axis, [(i, i ^ bit) for i in range(count)])  51.6 us
    ppermute x56, waiting for transfers between devices, swap(): return lax.ppermute(block, axis, [(i, i ^ bit) for i in range(count)])  49.6 us
    pallas_call x4, Pallas kernels, multiply(): pl.pallas_call(functools.partial(multiply_kernel, start), in_specs=[vmem,...  20.3 us
    unnamed x39, local copies, waits for them, and re-layouts  8 us
    pallas_call x1, Pallas kernels, attend_local(): pl.pallas_call(attend_kernel, in_specs=[pl.BlockSpec(memory_space=pltpu.S...  4.04 us
  transfers between devices with their start and end apart: 56, of which 29 were waited for; matrix products, arithmetic and copies ran while one was open for 1% of the time, Pallas kernels for 9%

profile of v4, /device:TPU:0, one launch (start us, length us, event | category | flops | bytes accessed | tf_op | source)
XLA Modules:
  0.0 144.5 jit_solution(350852122246630862)
XLA Ops:
  2.3 3.1 %collective-permute-start.9 = (bf16[8,4096]{1,0:T(8,128)(2,1)S(1)}, bf16[8,4096]{1,0:T(8,128)(2,1)S(1)}, u32[]{:S(2)}, u32[]{:S(2)}) collective-permute-start(bf16[8,4096]{1,0:T(8,128)(2,1)S(1)} %get-tuple-element.61), channel_id=1, source_target_pairs={{0,1},{1,0},{2,3},{3,2},{4,5},{5,4},{6,7},{7,6},{8,9},{9,8},{10,11... | collective-permute-start | bytes 196616 | tf_op jit(solution)/shard_map/ppermute | solution.py:217
  5.4 2.5 %collective-permute-start.1 = (bf16[8,4096]{1,0:T(8,128)(2,1)S(1)}, bf16[8,4096]{1,0:T(8,128)(2,1)S(1)}, u32[]{:S(2)}, u32[]{:S(2)}) collective-permute-start(bf16[8,4096]{1,0:T(8,128)(2,1)S(1)} %get-tuple-element.62), channel_id=1, source_target_pairs={{0,3},{1,2},{2,1},{3,0},{4,7},{5,6},{6,5},{7,4},{8,11},{9,10},{10,... | collective-permute-start | bytes 196616 | tf_op jit(solution)/shard_map/ppermute | solution.py:217
  8.9 1.6 %collective-permute-start.13 = (bf16[16,4096]{1,0:T(8,128)(2,1)S(1)}, bf16[16,4096]{1,0:T(8,128)(2,1)S(1)}, u32[]{:S(2)}, u32[]{:S(2)}) collective-permute-start(bf16[16,4096]{1,0:T(8,128)(2,1)S(1)} %pad_maximum_fusion.4), channel_id=1, source_target_pairs={{0,16},{4,20},{8,24},{12,28},{16,0},{20,4},{24,8},{28,12},{1,17},{... | collective-permute-start | bytes 393224 | tf_op jit(solution)/shard_map/ppermute | solution.py:217
  10.4 1.5 %collective-permute-start.11 = (bf16[16,4096]{1,0:T(8,128)(2,1)S(1)}, bf16[16,4096]{1,0:T(8,128)(2,1)S(1)}, u32[]{:S(2)}, u32[]{:S(2)}) collective-permute-start(bf16[16,4096]{1,0:T(8,128)(2,1)S(1)} %pad_maximum_fusion.4), channel_id=1, source_target_pairs={{0,8},{4,12},{8,0},{12,4},{16,24},{20,28},{24,16},{28,20},{1,9},{5... | collective-permute-start | bytes 393224 | tf_op jit(solution)/shard_map/ppermute | solution.py:217
  11.9 2.4 %collective-permute-done = bf16[8,4096]{1,0:T(8,128)(2,1)S(1)} collective-permute-done((bf16[8,4096]{1,0:T(8,128)(2,1)S(1)}, bf16[8,4096]{1,0:T(8,128)(2,1)S(1)}, u32[]{:S(2)}, u32[]{:S(2)}) %collective-permute-start) | collective-permute-done | bytes 65568 | tf_op jit(solution)/shard_map/ppermute | solution.py:217
  14.4 1.6 %collective-permute-start.5 = (bf16[16,4096]{1,0:T(8,128)(2,1)S(1)}, bf16[16,4096]{1,0:T(8,128)(2,1)S(1)}, u32[]{:S(2)}, u32[]{:S(2)}) collective-permute-start(bf16[16,4096]{1,0:T(8,128)(2,1)S(1)} %constant_dynamic-update-slice_fusion), channel_id=1, source_target_pairs={{0,16},{4,20},{8,24},{12,28},{16,0},{20,4},{24,8},{28,12},{1,17},{... | collective-permute-start | bytes 393224 | tf_op jit(solution)/shard_map/ppermute | solution.py:217
  16.0 1.5 %collective-permute-start.3 = (bf16[16,4096]{1,0:T(8,128)(2,1)S(1)}, bf16[16,4096]{1,0:T(8,128)(2,1)S(1)}, u32[]{:S(2)}, u32[]{:S(2)}) collective-permute-start(bf16[16,4096]{1,0:T(8,128)(2,1)S(1)} %constant_dynamic-update-slice_fusion), channel_id=1, source_target_pairs={{0,8},{4,12},{8,0},{12,4},{16,24},{20,28},{24,16},{28,20},{1,9},{5... | collective-permute-start | bytes 393224 | tf_op jit(solution)/shard_map/ppermute | solution.py:217
  17.6 1.3 collective-permute-done.2
  19.4 2.5 %collective-permute-start.7 = (bf16[16,4096]{1,0:T(8,128)(2,1)S(1)}, bf16[16,4096]{1,0:T(8,128)(2,1)S(1)}, u32[]{:S(2)}, u32[]{:S(2)}) collective-permute-start(bf16[16,4096]{1,0:T(8,128)(2,1)S(1)} %constant_dynamic-update-slice_fusion), channel_id=1, source_target_pairs={{0,24},{4,28},{8,16},{12,20},{16,8},{20,12},{24,0},{28,4},{1,25},{... | collective-permute-start | bytes 393224 | tf_op jit(solution)/shard_map/ppermute | solution.py:217
  23.5 2.6 %collective-permute-done.15 = bf16[16,4096]{1,0:T(8,128)(2,1)S(1)} collective-permute-done((bf16[16,4096]{1,0:T(8,128)(2,1)S(1)}, bf16[16,4096]{1,0:T(8,128)(2,1)S(1)}, u32[]{:S(2)}, u32[]{:S(2)}) %collective-permute-start.15) | collective-permute-done | bytes 131104 | tf_op jit(solution)/shard_map/ppermute | solution.py:217
  26.2 2.0 %collective-permute-done.7 = bf16[16,4096]{1,0:T(8,128)(2,1)S(1)} collective-permute-done((bf16[16,4096]{1,0:T(8,128)(2,1)S(1)}, bf16[16,4096]{1,0:T(8,128)(2,1)S(1)}, u32[]{:S(2)}, u32[]{:S(2)}) %collective-permute-start.7) | collective-permute-done | bytes 131104 | tf_op jit(solution)/shard_map/ppermute | solution.py:217
  29.5 4.9 %shard_map.73 = f32[256,1024]{1,0:T(8,128)S(1)} custom-call(bf16[128,4096]{1,0:T(8,128)(2,1)S(1)} %bitcast.244, bf16[128,4096]{1,0:T(8,128)(2,1)S(1)} %bitcast.246, bf16[4096,2304]{1,0:T(8,128)(2,1)} %weights.5), custom_call_target="tpu_custom_call" | custom-call | flops 2147483648 | bytes 8388608 | tf_op jit(solution)/shard_map/pallas_call | solution.py:261
  34.6 5.6 %shard_map.74 = f32[256,1280]{1,0:T(8,128)S(1)} custom-call(bf16[128,4096]{1,0:T(8,128)(2,1)S(1)} %bitcast.245, bf16[128,4096]{1,0:T(8,128)(2,1)S(1)} %bitcast.247, bf16[4096,2304]{1,0:T(8,128)(2,1)} %weights.5), custom_call_target="tpu_custom_call" | custom-call | flops 2684354560 | bytes 10485760 | tf_op jit(solution)/shard_map/pallas_call | solution.py:261
  40.3 2.1 %collective-permute-start.24 = (f16[8,8,1280]{2,1,0:T(8,128)(2,1)S(1)}, f16[8,8,1280]{2,1,0:T(8,128)(2,1)S(1)}, u32[]{:S(2)}, u32[]{:S(2)}) collective-permute-start(f16[8,8,1280]{2,1,0:T(8,128)(2,1)S(1)} %get-tuple-element.44), channel_id=1, source_target_pairs={{0,1},{1,0},{2,3},{3,2},{4,5},{5,4},{6,7},{7,6},{8,9},{9,8},{10,11... | collective-permute-start | bytes 491528 | tf_op jit(solution)/shard_map/ppermute | solution.py:217
  43.1 1.3 collective-permute-start.18
  44.4 4.0 %collective-permute-done.24 = f16[8,8,1280]{2,1,0:T(8,128)(2,1)S(1)} collective-permute-done((f16[8,8,1280]{2,1,0:T(8,128)(2,1)S(1)}, f16[8,8,1280]{2,1,0:T(8,128)(2,1)S(1)}, u32[]{:S(2)}, u32[]{:S(2)}) %collective-permute-start.24) | collective-permute-done | bytes 163872 | tf_op jit(solution)/shard_map/ppermute | solution.py:217
  48.4 2.1 %collective-permute-start.25 = (f16[8,8,1280]{2,1,0:T(8,128)(2,1)S(1)}, f16[8,8,1280]{2,1,0:T(8,128)(2,1)S(1)}, u32[]{:S(2)}, u32[]{:S(2)}) collective-permute-start(f16[8,8,1280]{2,1,0:T(8,128)(2,1)S(1)} %fusion.14), channel_id=1, source_target_pairs={{0,2},{1,3},{2,0},{3,1},{4,6},{5,7},{6,4},{7,5},{8,10},{9,11},{10,... | collective-permute-start | bytes 491528 | tf_op jit(solution)/shard_map/ppermute | solution.py:217
  50.9 2.6 %shard_map.75 = (bf16[4,512,1024]{2,1,0:T(8,128)(2,1)S(1)}, bf16[4,512,1024]{2,1,0:T(8,128)(2,1)S(1)}) custom-call(s32[8]{0:T(128)S(1)} %copy-done.4, bf16[8,512,1024]{2,1,0:T(8,128)(2,1)} %k_cache.3, bf16[8,512,1024]{2,1,0:T(8,128)(2,1)} %v_cache.3), custom_call_target="tpu_custom_call" | custom-call | bytes 8388608 | tf_op jit(solution)/shard_map/pallas_call | solution.py:95
  53.6 2.0 %copy-done = bf16[4,512,1024]{2,1,0:T(8,128)(2,1)} copy-done((bf16[4,512,1024]{2,1,0:T(8,128)(2,1)}, bf16[4,512,1024]{2,1,0:T(8,128)(2,1)S(1)}, u32[]{:S(2)}) %copy-start) | copy-done | bytes 4194328
  55.6 2.0 %copy-done.2 = bf16[4,512,1024]{2,1,0:T(8,128)(2,1)} copy-done((bf16[4,512,1024]{2,1,0:T(8,128)(2,1)}, bf16[4,512,1024]{2,1,0:T(8,128)(2,1)S(1)}, u32[]{:S(2)}) %copy-start.2) | copy-done | bytes 4194328
  59.4 1.8 %collective-permute-start.20 = (bf16[2,8,1024]{2,1,0:T(8,128)(2,1)S(1)}, bf16[2,8,1024]{2,1,0:T(8,128)(2,1)S(1)}, u32[]{:S(2)}, u32[]{:S(2)}) collective-permute-start(bf16[2,8,1024]{2,1,0:T(8,128)(2,1)S(1)} %get-tuple-element.73), channel_id=1, source_target_pairs={{0,16},{4,20},{8,24},{12,28},{16,0},{20,4},{24,8},{28,12},{1,17},{... | collective-permute-start | bytes 98312 | tf_op jit(solution)/shard_map/ppermute | solution.py:217
  61.6 1.8 %collective-permute-done.21 = bf16[2,8,1024]{2,1,0:T(8,128)(2,1)S(1)} collective-permute-done((bf16[2,8,1024]{2,1,0:T(8,128)(2,1)S(1)}, bf16[2,8,1024]{2,1,0:T(8,128)(2,1)S(1)}, u32[]{:S(2)}, u32[]{:S(2)}) %collective-permute-start.21) | collective-permute-done | bytes 32800 | tf_op jit(solution)/shard_map/ppermute | solution.py:217
  63.7 1.5 %collective-permute-start.26 = (bf16[2,8,1280]{2,1,0:T(8,128)(2,1)S(1)}, bf16[2,8,1280]{2,1,0:T(8,128)(2,1)S(1)}, u32[]{:S(2)}, u32[]{:S(2)}) collective-permute-start(bf16[2,8,1280]{2,1,0:T(8,128)(2,1)S(1)} %get-tuple-element.66), channel_id=1, source_target_pairs={{0,8},{4,12},{8,0},{12,4},{16,24},{20,28},{24,16},{28,20},{1,9},{5... | collective-permute-start | bytes 122888 | tf_op jit(solution)/shard_map/ppermute | solution.py:217
  65.2 1.5 %collective-permute-start.28 = (bf16[2,8,1280]{2,1,0:T(8,128)(2,1)S(1)}, bf16[2,8,1280]{2,1,0:T(8,128)(2,1)S(1)}, u32[]{:S(2)}, u32[]{:S(2)}) collective-permute-start(bf16[2,8,1280]{2,1,0:T(8,128)(2,1)S(1)} %get-tuple-element.67), channel_id=1, source_target_pairs={{0,24},{4,28},{8,16},{12,20},{16,8},{20,12},{24,0},{28,4},{1,25},{... | collective-permute-start | bytes 122888 | tf_op jit(solution)/shard_map/ppermute | solution.py:217
  67.8 2.3 %collective-permute-done.28 = bf16[2,8,1280]{2,1,0:T(8,128)(2,1)S(1)} collective-permute-done((bf16[2,8,1280]{2,1,0:T(8,128)(2,1)S(1)}, bf16[2,8,1280]{2,1,0:T(8,128)(2,1)S(1)}, u32[]{:S(2)}, u32[]{:S(2)}) %collective-permute-start.28) | collective-permute-done | bytes 40992 | tf_op jit(solution)/shard_map/ppermute | solution.py:217
  73.5 1.4 copy-done.1
  74.9 2.2 %copy-done.3 = bf16[4,512,1024]{2,1,0:T(8,128)(2,1)S(1)} copy-done((bf16[4,512,1024]{2,1,0:T(8,128)(2,1)S(1)}, bf16[4,512,1024]{2,1,0:T(8,128)(2,1)}, u32[]{:S(2)}) %copy-start.3) | copy-done | bytes 4194328
  77.1 4.0 %shard_map.76 = bf16[8,128,128]{2,1,0:T(8,128)(2,1)S(1)} custom-call(s32[8]{0:T(128)S(1)} %copy-done.4, bf16[8,128,128]{2,1,0:T(8,128)(2,1)S(1)} %pad_maximum_fusion.1.query, bf16[8,8,128]{2,1,0:T(8,128)(2,1)S(1)} %pad_maximum_fusion.9.key_new, f32[8,8,128]{2,1,0:T(8,128)S(1)} %get-tuple-element.96.value_new, bf16[4,512,1024]{2,1,0:T(8,128)(2,1)S(1)} %copy-done.1, ...), custom_call_target="tpu_custom_call" | custom-call | flops 2147483648 | bytes 8388608 | tf_op jit(solution)/shard_map/pallas_call | solution.py:194
  82.2 4.2 %collective-permute-start.31 = (bf16[8,4096]{1,0:T(8,128)(2,1)S(1)}, bf16[8,4096]{1,0:T(8,128)(2,1)S(1)}, u32[]{:S(2)}, u32[]{:S(2)}) collective-permute-start(bf16[8,4096]{1,0:T(8,128)(2,1)S(1)} %get-tuple-element.58), channel_id=1, source_target_pairs={{0,3},{1,2},{2,1},{3,0},{4,7},{5,6},{6,5},{7,4},{8,11},{9,10},{10,... | collective-permute-start | bytes 196616 | tf_op jit(solution)/shard_map/ppermute | solution.py:217
  89.4 2.9 %collective-permute-done.30 = bf16[8,4096]{1,0:T(8,128)(2,1)S(1)} collective-permute-done((bf16[8,4096]{1,0:T(8,128)(2,1)S(1)}, bf16[8,4096]{1,0:T(8,128)(2,1)S(1)}, u32[]{:S(2)}, u32[]{:S(2)}) %collective-permute-start.30) | collective-permute-done | bytes 65568 | tf_op jit(solution)/shard_map/ppermute | solution.py:217
  92.4 1.3 collective-permute-start.35
  93.7 1.5 %collective-permute-start.33 = (bf16[16,4096]{1,0:T(8,128)(2,1)S(1)}, bf16[16,4096]{1,0:T(8,128)(2,1)S(1)}, u32[]{:S(2)}, u32[]{:S(2)}) collective-permute-start(bf16[16,4096]{1,0:T(8,128)(2,1)S(1)} %constant_dynamic-update-slice_fusion.2), channel_id=1, source_target_pairs={{0,8},{4,12},{8,0},{12,4},{16,24},{20,28},{24,16},{28,20},{1,9},{5... | collective-permute-start | bytes 393224 | tf_op jit(solution)/shard_map/ppermute | solution.py:217
  95.3 1.3 collective-permute-done.32
  97.4 2.2 %collective-permute-start.37 = (bf16[16,4096]{1,0:T(8,128)(2,1)S(1)}, bf16[16,4096]{1,0:T(8,128)(2,1)S(1)}, u32[]{:S(2)}, u32[]{:S(2)}) collective-permute-start(bf16[16,4096]{1,0:T(8,128)(2,1)S(1)} %constant_dynamic-update-slice_fusion.2), channel_id=1, source_target_pairs={{0,24},{4,28},{8,16},{12,20},{16,8},{20,12},{24,0},{28,4},{1,25},{... | collective-permute-start | bytes 393224 | tf_op jit(solution)/shard_map/ppermute | solution.py:217
  101.2 2.6 %collective-permute-done.45 = bf16[16,4096]{1,0:T(8,128)(2,1)S(1)} collective-permute-done((bf16[16,4096]{1,0:T(8,128)(2,1)S(1)}, bf16[16,4096]{1,0:T(8,128)(2,1)S(1)}, u32[]{:S(2)}, u32[]{:S(2)}) %collective-permute-start.45) | collective-permute-done | bytes 131104 | tf_op jit(solution)/shard_map/ppermute | solution.py:217
  103.9 2.0 %collective-permute-done.37 = bf16[16,4096]{1,0:T(8,128)(2,1)S(1)} collective-permute-done((bf16[16,4096]{1,0:T(8,128)(2,1)S(1)}, bf16[16,4096]{1,0:T(8,128)(2,1)S(1)}, u32[]{:S(2)}, u32[]{:S(2)}) %collective-permute-start.37) | collective-permute-done | bytes 131104 | tf_op jit(solution)/shard_map/ppermute | solution.py:217
  107.3 4.9 %shard_map.77 = f32[256,1024]{1,0:T(8,128)S(1)} custom-call(bf16[128,4096]{1,0:T(8,128)(2,1)S(1)} %bitcast.240, bf16[128,4096]{1,0:T(8,128)(2,1)S(1)} %bitcast.242, bf16[4096,2048]{1,0:T(8,128)(2,1)} %weights.7), custom_call_target="tpu_custom_call" | custom-call | flops 2147483648 | bytes 8388608 | tf_op jit(solution)/shard_map/pallas_call | solution.py:261
  112.3 4.9 %shard_map.78 = f32[256,1024]{1,0:T(8,128)S(1)} custom-call(bf16[128,4096]{1,0:T(8,128)(2,1)S(1)} %bitcast.241, bf16[128,4096]{1,0:T(8,128)(2,1)S(1)} %bitcast.243, bf16[4096,2048]{1,0:T(8,128)(2,1)} %weights.7), custom_call_target="tpu_custom_call" | custom-call | flops 2147483648 | bytes 8388608 | tf_op jit(solution)/shard_map/pallas_call | solution.py:261
  117.3 2.1 %collective-permute-start.50 = (f16[8,8,1024]{2,1,0:T(8,128)(2,1)S(1)}, f16[8,8,1024]{2,1,0:T(8,128)(2,1)S(1)}, u32[]{:S(2)}, u32[]{:S(2)}) collective-permute-start(f16[8,8,1024]{2,1,0:T(8,128)(2,1)S(1)} %get-tuple-element.46), channel_id=1, source_target_pairs={{0,1},{1,0},{2,3},{3,2},{4,5},{5,4},{6,7},{7,6},{8,9},{9,8},{10,11... | collective-permute-start | bytes 393224 | tf_op jit(solution)/shard_map/ppermute | solution.py:217
  119.4 1.8 %collective-permute-done.47 = f16[2,8,8,1024]{3,2,1,0:T(8,128)(2,1)S(1)} collective-permute-done((f16[2,8,8,1024]{3,2,1,0:T(8,128)(2,1)S(1)}, f16[2,8,8,1024]{3,2,1,0:T(8,128)(2,1)S(1)}, u32[]{:S(2)}, u32[]{:S(2)}) %collective-permute-start.47) | collective-permute-done | bytes 262176 | tf_op jit(solution)/shard_map/ppermute | solution.py:217
  121.3 2.1 %collective-permute-done.50 = f16[8,8,1024]{2,1,0:T(8,128)(2,1)S(1)} collective-permute-done((f16[8,8,1024]{2,1,0:T(8,128)(2,1)S(1)}, f16[8,8,1024]{2,1,0:T(8,128)(2,1)S(1)}, u32[]{:S(2)}, u32[]{:S(2)}) %collective-permute-start.50) | collective-permute-done | bytes 131104 | tf_op jit(solution)/shard_map/ppermute | solution.py:217
  123.5 1.5 %collective-permute-start.51 = (f16[8,8,1024]{2,1,0:T(8,128)(2,1)S(1)}, f16[8,8,1024]{2,1,0:T(8,128)(2,1)S(1)}, u32[]{:S(2)}, u32[]{:S(2)}) collective-permute-start(f16[8,8,1024]{2,1,0:T(8,128)(2,1)S(1)} %fusion.28), channel_id=1, source_target_pairs={{0,2},{1,3},{2,0},{3,1},{4,6},{5,7},{6,4},{7,5},{8,10},{9,11},{10,... | collective-permute-start | bytes 393224 | tf_op jit(solution)/shard_map/ppermute | solution.py:217
  126.0 6.7 %collective-permute-done.48 = f16[8,8,1024]{2,1,0:T(8,128)(2,1)S(1)} collective-permute-done((f16[8,8,1024]{2,1,0:T(8,128)(2,1)S(1)}, f16[8,8,1024]{2,1,0:T(8,128)(2,1)S(1)}, u32[]{:S(2)}, u32[]{:S(2)}) %collective-permute-start.48) | collective-permute-done | bytes 131104 | tf_op jit(solution)/shard_map/ppermute | solution.py:217
  132.7 2.2 %collective-permute-done.51 = f16[8,8,1024]{2,1,0:T(8,128)(2,1)S(1)} collective-permute-done((f16[8,8,1024]{2,1,0:T(8,128)(2,1)S(1)}, f16[8,8,1024]{2,1,0:T(8,128)(2,1)S(1)}, u32[]{:S(2)}, u32[]{:S(2)}) %collective-permute-start.51) | collective-permute-done | bytes 131104 | tf_op jit(solution)/shard_map/ppermute | solution.py:217
  136.4 2.1 %collective-permute-start.54 = (bf16[2,8,2048]{2,1,0:T(8,128)(2,1)S(1)}, bf16[2,8,2048]{2,1,0:T(8,128)(2,1)S(1)}, u32[]{:S(2)}, u32[]{:S(2)}) collective-permute-start(bf16[2,8,2048]{2,1,0:T(8,128)(2,1)S(1)} %get-tuple-element.55), channel_id=1, source_target_pairs={{0,24},{4,28},{8,16},{12,20},{16,8},{20,12},{24,0},{28,4},{1,25},{... | collective-permute-start | bytes 196616 | tf_op jit(solution)/shard_map/ppermute | solution.py:217
  138.5 1.2 collective-permute-done.52
  140.3 1.3 collective-permute-done.54
  141.7 1.3 collective-permute-done.55
  (183 shorter events, 27.3 us)
Async XLA Ops:
  2.3 6.5 %collective-permute-start.9 = (bf16[8,4096]{1,0:T(8,128)(2,1)S(1)}, bf16[8,4096]{1,0:T(8,128)(2,1)S(1)}, u32[]{:S(2)}, u32[]{:S(2)}) collective-permute-start(bf16[8,4096]{1,0:T(8,128)(2,1)S(1)} %get-tuple-element.61), channel_id=1, source_target_pairs={{0,1},{1,0},{2,3},{3,2},{4,5},{5,4},{6,7},{7,6},{8,9},{9,8},{10,11... | collective-permute-start | bytes 196616 | tf_op jit(solution)/shard_map/ppermute | solution.py:217
  5.4 8.9 %collective-permute-start.1 = (bf16[8,4096]{1,0:T(8,128)(2,1)S(1)}, bf16[8,4096]{1,0:T(8,128)(2,1)S(1)}, u32[]{:S(2)}, u32[]{:S(2)}) collective-permute-start(bf16[8,4096]{1,0:T(8,128)(2,1)S(1)} %get-tuple-element.62), channel_id=1, source_target_pairs={{0,3},{1,2},{2,1},{3,0},{4,7},{5,6},{6,5},{7,4},{8,11},{9,10},{10,... | collective-permute-start | bytes 196616 | tf_op jit(solution)/shard_map/ppermute | solution.py:217
  7.9 6.4 %collective-permute-start = (bf16[8,4096]{1,0:T(8,128)(2,1)S(1)}, bf16[8,4096]{1,0:T(8,128)(2,1)S(1)}, u32[]{:S(2)}, u32[]{:S(2)}) collective-permute-start(bf16[8,4096]{1,0:T(8,128)(2,1)S(1)} %get-tuple-element.63), channel_id=1, source_target_pairs={{0,2},{1,3},{2,0},{3,1},{4,6},{5,7},{6,4},{7,5},{8,10},{9,11},{10,... | collective-permute-start | bytes 196616 | tf_op jit(solution)/shard_map/ppermute | solution.py:217
  8.9 13.2 %collective-permute-start.13 = (bf16[16,4096]{1,0:T(8,128)(2,1)S(1)}, bf16[16,4096]{1,0:T(8,128)(2,1)S(1)}, u32[]{:S(2)}, u32[]{:S(2)}) collective-permute-start(bf16[16,4096]{1,0:T(8,128)(2,1)S(1)} %pad_maximum_fusion.4), channel_id=1, source_target_pairs={{0,16},{4,20},{8,24},{12,28},{16,0},{20,4},{24,8},{28,12},{1,17},{... | collective-permute-start | bytes 393224 | tf_op jit(solution)/shard_map/ppermute | solution.py:217
  10.4 9.0 %collective-permute-start.11 = (bf16[16,4096]{1,0:T(8,128)(2,1)S(1)}, bf16[16,4096]{1,0:T(8,128)(2,1)S(1)}, u32[]{:S(2)}, u32[]{:S(2)}) collective-permute-start(bf16[16,4096]{1,0:T(8,128)(2,1)S(1)} %pad_maximum_fusion.4), channel_id=1, source_target_pairs={{0,8},{4,12},{8,0},{12,4},{16,24},{20,28},{24,16},{28,20},{1,9},{5... | collective-permute-start | bytes 393224 | tf_op jit(solution)/shard_map/ppermute | solution.py:217
  11.9 5.6 %collective-permute-start.10 = (bf16[16,4096]{1,0:T(8,128)(2,1)S(1)}, bf16[16,4096]{1,0:T(8,128)(2,1)S(1)}, u32[]{:S(2)}, u32[]{:S(2)}) collective-permute-start(bf16[16,4096]{1,0:T(8,128)(2,1)S(1)} %pad_maximum_fusion.4), channel_id=1, source_target_pairs={{0,4},{4,0},{8,12},{12,8},{16,20},{20,16},{24,28},{28,24},{1,5},{5... | collective-permute-start | bytes 393224 | tf_op jit(solution)/shard_map/ppermute | solution.py:217
  14.4 8.2 %collective-permute-start.5 = (bf16[16,4096]{1,0:T(8,128)(2,1)S(1)}, bf16[16,4096]{1,0:T(8,128)(2,1)S(1)}, u32[]{:S(2)}, u32[]{:S(2)}) collective-permute-start(bf16[16,4096]{1,0:T(8,128)(2,1)S(1)} %constant_dynamic-update-slice_fusion), channel_id=1, source_target_pairs={{0,16},{4,20},{8,24},{12,28},{16,0},{20,4},{24,8},{28,12},{1,17},{... | collective-permute-start | bytes 393224 | tf_op jit(solution)/shard_map/ppermute | solution.py:217
  16.0 6.0 %collective-permute-start.3 = (bf16[16,4096]{1,0:T(8,128)(2,1)S(1)}, bf16[16,4096]{1,0:T(8,128)(2,1)S(1)}, u32[]{:S(2)}, u32[]{:S(2)}) collective-permute-start(bf16[16,4096]{1,0:T(8,128)(2,1)S(1)} %constant_dynamic-update-slice_fusion), channel_id=1, source_target_pairs={{0,8},{4,12},{8,0},{12,4},{16,24},{20,28},{24,16},{28,20},{1,9},{5... | collective-permute-start | bytes 393224 | tf_op jit(solution)/shard_map/ppermute | solution.py:217
  18.9 7.2 %collective-permute-start.15 = (bf16[16,4096]{1,0:T(8,128)(2,1)S(1)}, bf16[16,4096]{1,0:T(8,128)(2,1)S(1)}, u32[]{:S(2)}, u32[]{:S(2)}) collective-permute-start(bf16[16,4096]{1,0:T(8,128)(2,1)S(1)} %pad_maximum_fusion.4), channel_id=1, source_target_pairs={{0,24},{4,28},{8,16},{12,20},{16,8},{20,12},{24,0},{28,4},{1,25},{... | collective-permute-start | bytes 393224 | tf_op jit(solution)/shard_map/ppermute | solution.py:217
  19.4 8.8 %collective-permute-start.7 = (bf16[16,4096]{1,0:T(8,128)(2,1)S(1)}, bf16[16,4096]{1,0:T(8,128)(2,1)S(1)}, u32[]{:S(2)}, u32[]{:S(2)}) collective-permute-start(bf16[16,4096]{1,0:T(8,128)(2,1)S(1)} %constant_dynamic-update-slice_fusion), channel_id=1, source_target_pairs={{0,24},{4,28},{8,16},{12,20},{16,8},{20,12},{24,0},{28,4},{1,25},{... | collective-permute-start | bytes 393224 | tf_op jit(solution)/shard_map/ppermute | solution.py:217
  22.1 6.2 %collective-permute-start.4 = (bf16[16,4096]{1,0:T(8,128)(2,1)S(1)}, bf16[16,4096]{1,0:T(8,128)(2,1)S(1)}, u32[]{:S(2)}, u32[]{:S(2)}) collective-permute-start(bf16[16,4096]{1,0:T(8,128)(2,1)S(1)} %collective-permute-done.3), channel_id=1, source_target_pairs={{0,4},{4,0},{8,12},{12,8},{16,20},{20,16},{24,28},{28,24},{1,5},{5... | collective-permute-start | bytes 393224 | tf_op jit(solution)/shard_map/ppermute | solution.py:217
  22.6 5.6 %collective-permute-start.14 = (bf16[16,4096]{1,0:T(8,128)(2,1)S(1)}, bf16[16,4096]{1,0:T(8,128)(2,1)S(1)}, u32[]{:S(2)}, u32[]{:S(2)}) collective-permute-start(bf16[16,4096]{1,0:T(8,128)(2,1)S(1)} %collective-permute-done.13), channel_id=1, source_target_pairs={{0,4},{4,0},{8,12},{12,8},{16,20},{20,16},{24,28},{28,24},{1,5},{5... | collective-permute-start | bytes 393224 | tf_op jit(solution)/shard_map/ppermute | solution.py:217
  23.4 4.9 %collective-permute-start.6 = (bf16[16,4096]{1,0:T(8,128)(2,1)S(1)}, bf16[16,4096]{1,0:T(8,128)(2,1)S(1)}, u32[]{:S(2)}, u32[]{:S(2)}) collective-permute-start(bf16[16,4096]{1,0:T(8,128)(2,1)S(1)} %collective-permute-done.5), channel_id=1, source_target_pairs={{0,4},{4,0},{8,12},{12,8},{16,20},{20,16},{24,28},{28,24},{1,5},{5... | collective-permute-start | bytes 393224 | tf_op jit(solution)/shard_map/ppermute | solution.py:217
  26.2 2.2 %collective-permute-start.16 = (bf16[16,4096]{1,0:T(8,128)(2,1)S(1)}, bf16[16,4096]{1,0:T(8,128)(2,1)S(1)}, u32[]{:S(2)}, u32[]{:S(2)}) collective-permute-start(bf16[16,4096]{1,0:T(8,128)(2,1)S(1)} %collective-permute-done.15), channel_id=1, source_target_pairs={{0,4},{4,0},{8,12},{12,8},{16,20},{20,16},{24,28},{28,24},{1,5},{5... | collective-permute-start | bytes 393224 | tf_op jit(solution)/shard_map/ppermute | solution.py:217
  34.5 8.4 %collective-permute-start.17 = (f16[2,8,8,1024]{3,2,1,0:T(8,128)(2,1)S(1)}, f16[2,8,8,1024]{3,2,1,0:T(8,128)(2,1)S(1)}, u32[]{:S(2)}, u32[]{:S(2)}) collective-permute-start(f16[2,8,8,1024]{3,2,1,0:T(8,128)(2,1)S(1)} %fusion.19), channel_id=1, source_target_pairs={{0,1},{1,0},{2,3},{3,2},{4,5},{5,4},{6,7},{7,6},{8,9},{9,8},{10,11... | collective-permute-start | bytes 786440 | tf_op jit(solution)/shard_map/ppermute | solution.py:217
  40.3 8.1 %collective-permute-start.24 = (f16[8,8,1280]{2,1,0:T(8,128)(2,1)S(1)}, f16[8,8,1280]{2,1,0:T(8,128)(2,1)S(1)}, u32[]{:S(2)}, u32[]{:S(2)}) collective-permute-start(f16[8,8,1280]{2,1,0:T(8,128)(2,1)S(1)} %get-tuple-element.44), channel_id=1, source_target_pairs={{0,1},{1,0},{2,3},{3,2},{4,5},{5,4},{6,7},{7,6},{8,9},{9,8},{10,11... | collective-permute-start | bytes 491528 | tf_op jit(solution)/shard_map/ppermute | solution.py:217
  43.1 14.5 %collective-permute-start.18 = (f16[8,8,1024]{2,1,0:T(8,128)(2,1)S(1)}, f16[8,8,1024]{2,1,0:T(8,128)(2,1)S(1)}, u32[]{:S(2)}, u32[]{:S(2)}) collective-permute-start(f16[8,8,1024]{2,1,0:T(8,128)(2,1)S(1)} %fusion.41), channel_id=1, source_target_pairs={{0,2},{1,3},{2,0},{3,1},{4,6},{5,7},{6,4},{7,5},{8,10},{9,11},{10,... | collective-permute-start | bytes 393224 | tf_op jit(solution)/shard_map/ppermute | solution.py:217
  48.4 12.8 %collective-permute-start.25 = (f16[8,8,1280]{2,1,0:T(8,128)(2,1)S(1)}, f16[8,8,1280]{2,1,0:T(8,128)(2,1)S(1)}, u32[]{:S(2)}, u32[]{:S(2)}) collective-permute-start(f16[8,8,1280]{2,1,0:T(8,128)(2,1)S(1)} %fusion.14), channel_id=1, source_target_pairs={{0,2},{1,3},{2,0},{3,1},{4,6},{5,7},{6,4},{7,5},{8,10},{9,11},{10,... | collective-permute-start | bytes 491528 | tf_op jit(solution)/shard_map/ppermute | solution.py:217
  50.6 10.6 %collective-permute-start.23 = (f16[8,8,1280]{2,1,0:T(8,128)(2,1)S(1)}, f16[8,8,1280]{2,1,0:T(8,128)(2,1)S(1)}, u32[]{:S(2)}, u32[]{:S(2)}) collective-permute-start(f16[8,8,1280]{2,1,0:T(8,128)(2,1)S(1)} %get-tuple-element.28), channel_id=1, source_target_pairs={{0,1},{1,0},{2,3},{3,2},{4,5},{5,4},{6,7},{7,6},{8,9},{9,8},{10,11... | collective-permute-start | bytes 491528 | tf_op jit(solution)/shard_map/ppermute | solution.py:217
  57.6 4.0 %collective-permute-start.19 = (bf16[2,8,1024]{2,1,0:T(8,128)(2,1)S(1)}, bf16[2,8,1024]{2,1,0:T(8,128)(2,1)S(1)}, u32[]{:S(2)}, u32[]{:S(2)}) collective-permute-start(bf16[2,8,1024]{2,1,0:T(8,128)(2,1)S(1)} %get-tuple-element.71), channel_id=1, source_target_pairs={{0,8},{4,12},{8,0},{12,4},{16,24},{20,28},{24,16},{28,20},{1,9},{5... | collective-permute-start | bytes 98312 | tf_op jit(solution)/shard_map/ppermute | solution.py:217
  58.5 4.9 %collective-permute-start.21 = (bf16[2,8,1024]{2,1,0:T(8,128)(2,1)S(1)}, bf16[2,8,1024]{2,1,0:T(8,128)(2,1)S(1)}, u32[]{:S(2)}, u32[]{:S(2)}) collective-permute-start(bf16[2,8,1024]{2,1,0:T(8,128)(2,1)S(1)} %get-tuple-element.72), channel_id=1, source_target_pairs={{0,24},{4,28},{8,16},{12,20},{16,8},{20,12},{24,0},{28,4},{1,25},{... | collective-permute-start | bytes 98312 | tf_op jit(solution)/shard_map/ppermute | solution.py:217
  59.4 4.3 %collective-permute-start.20 = (bf16[2,8,1024]{2,1,0:T(8,128)(2,1)S(1)}, bf16[2,8,1024]{2,1,0:T(8,128)(2,1)S(1)}, u32[]{:S(2)}, u32[]{:S(2)}) collective-permute-start(bf16[2,8,1024]{2,1,0:T(8,128)(2,1)S(1)} %get-tuple-element.73), channel_id=1, source_target_pairs={{0,16},{4,20},{8,24},{12,28},{16,0},{20,4},{24,8},{28,12},{1,17},{... | collective-permute-start | bytes 98312 | tf_op jit(solution)/shard_map/ppermute | solution.py:217
  63.6 7.2 %collective-permute-start.22 = (bf16[4,8,1024]{2,1,0:T(8,128)(2,1)S(1)}, bf16[4,8,1024]{2,1,0:T(8,128)(2,1)S(1)}, u32[]{:S(2)}, u32[]{:S(2)}) collective-permute-start(bf16[4,8,1024]{2,1,0:T(8,128)(2,1)S(1)} %pad_maximum_fusion.8), channel_id=1, source_target_pairs={{0,4},{4,0},{8,12},{12,8},{16,20},{20,16},{24,28},{28,24},{1,5},{5... | collective-permute-start | bytes 196616 | tf_op jit(solution)/shard_map/ppermute | solution.py:217
  63.7 4.1 %collective-permute-start.26 = (bf16[2,8,1280]{2,1,0:T(8,128)(2,1)S(1)}, bf16[2,8,1280]{2,1,0:T(8,128)(2,1)S(1)}, u32[]{:S(2)}, u32[]{:S(2)}) collective-permute-start(bf16[2,8,1280]{2,1,0:T(8,128)(2,1)S(1)} %get-tuple-element.66), channel_id=1, source_target_pairs={{0,8},{4,12},{8,0},{12,4},{16,24},{20,28},{24,16},{28,20},{1,9},{5... | collective-permute-start | bytes 122888 | tf_op jit(solution)/shard_map/ppermute | solution.py:217
  65.2 4.9 %collective-permute-start.28 = (bf16[2,8,1280]{2,1,0:T(8,128)(2,1)S(1)}, bf16[2,8,1280]{2,1,0:T(8,128)(2,1)S(1)}, u32[]{:S(2)}, u32[]{:S(2)}) collective-permute-start(bf16[2,8,1280]{2,1,0:T(8,128)(2,1)S(1)} %get-tuple-element.67), channel_id=1, source_target_pairs={{0,24},{4,28},{8,16},{12,20},{16,8},{20,12},{24,0},{28,4},{1,25},{... | collective-permute-start | bytes 122888 | tf_op jit(solution)/shard_map/ppermute | solution.py:217
  66.7 4.0 %collective-permute-start.27 = (bf16[2,8,1280]{2,1,0:T(8,128)(2,1)S(1)}, bf16[2,8,1280]{2,1,0:T(8,128)(2,1)S(1)}, u32[]{:S(2)}, u32[]{:S(2)}) collective-permute-start(bf16[2,8,1280]{2,1,0:T(8,128)(2,1)S(1)} %get-tuple-element.68), channel_id=1, source_target_pairs={{0,16},{4,20},{8,24},{12,28},{16,0},{20,4},{24,8},{28,12},{1,17},{... | collective-permute-start | bytes 122888 | tf_op jit(solution)/shard_map/ppermute | solution.py:217
  81.7 5.2 %collective-permute-start.39 = (bf16[8,4096]{1,0:T(8,128)(2,1)S(1)}, bf16[8,4096]{1,0:T(8,128)(2,1)S(1)}, u32[]{:S(2)}, u32[]{:S(2)}) collective-permute-start(bf16[8,4096]{1,0:T(8,128)(2,1)S(1)} %get-tuple-element.57), channel_id=1, source_target_pairs={{0,1},{1,0},{2,3},{3,2},{4,5},{5,4},{6,7},{7,6},{8,9},{9,8},{10,11... | collective-permute-start | bytes 196616 | tf_op jit(solution)/shard_map/ppermute | solution.py:217
  82.2 10.1 %collective-permute-start.31 = (bf16[8,4096]{1,0:T(8,128)(2,1)S(1)}, bf16[8,4096]{1,0:T(8,128)(2,1)S(1)}, u32[]{:S(2)}, u32[]{:S(2)}) collective-permute-start(bf16[8,4096]{1,0:T(8,128)(2,1)S(1)} %get-tuple-element.58), channel_id=1, source_target_pairs={{0,3},{1,2},{2,1},{3,0},{4,7},{5,6},{6,5},{7,4},{8,11},{9,10},{10,... | collective-permute-start | bytes 196616 | tf_op jit(solution)/shard_map/ppermute | solution.py:217
  86.5 5.9 %collective-permute-start.30 = (bf16[8,4096]{1,0:T(8,128)(2,1)S(1)}, bf16[8,4096]{1,0:T(8,128)(2,1)S(1)}, u32[]{:S(2)}, u32[]{:S(2)}) collective-permute-start(bf16[8,4096]{1,0:T(8,128)(2,1)S(1)} %get-tuple-element.59), channel_id=1, source_target_pairs={{0,2},{1,3},{2,0},{3,1},{4,6},{5,7},{6,4},{7,5},{8,10},{9,11},{10,... | collective-permute-start | bytes 196616 | tf_op jit(solution)/shard_map/ppermute | solution.py:217
  87.0 12.8 %collective-permute-start.43 = (bf16[16,4096]{1,0:T(8,128)(2,1)S(1)}, bf16[16,4096]{1,0:T(8,128)(2,1)S(1)}, u32[]{:S(2)}, u32[]{:S(2)}) collective-permute-start(bf16[16,4096]{1,0:T(8,128)(2,1)S(1)} %pad_maximum_fusion.6), channel_id=1, source_target_pairs={{0,16},{4,20},{8,24},{12,28},{16,0},{20,4},{24,8},{28,12},{1,17},{... | collective-permute-start | bytes 393224 | tf_op jit(solution)/shard_map/ppermute | solution.py:217
  88.2 9.2 %collective-permute-start.41 = (bf16[16,4096]{1,0:T(8,128)(2,1)S(1)}, bf16[16,4096]{1,0:T(8,128)(2,1)S(1)}, u32[]{:S(2)}, u32[]{:S(2)}) collective-permute-start(bf16[16,4096]{1,0:T(8,128)(2,1)S(1)} %pad_maximum_fusion.6), channel_id=1, source_target_pairs={{0,8},{4,12},{8,0},{12,4},{16,24},{20,28},{24,16},{28,20},{1,9},{5... | collective-permute-start | bytes 393224 | tf_op jit(solution)/shard_map/ppermute | solution.py:217
  89.4 5.8 %collective-permute-start.40 = (bf16[16,4096]{1,0:T(8,128)(2,1)S(1)}, bf16[16,4096]{1,0:T(8,128)(2,1)S(1)}, u32[]{:S(2)}, u32[]{:S(2)}) collective-permute-start(bf16[16,4096]{1,0:T(8,128)(2,1)S(1)} %pad_maximum_fusion.6), channel_id=1, source_target_pairs={{0,4},{4,0},{8,12},{12,8},{16,20},{20,16},{24,28},{28,24},{1,5},{5... | collective-permute-start | bytes 393224 | tf_op jit(solution)/shard_map/ppermute | solution.py:217
  92.4 8.0 %collective-permute-start.35 = (bf16[16,4096]{1,0:T(8,128)(2,1)S(1)}, bf16[16,4096]{1,0:T(8,128)(2,1)S(1)}, u32[]{:S(2)}, u32[]{:S(2)}) collective-permute-start(bf16[16,4096]{1,0:T(8,128)(2,1)S(1)} %constant_dynamic-update-slice_fusion.2), channel_id=1, source_target_pairs={{0,16},{4,20},{8,24},{12,28},{16,0},{20,4},{24,8},{28,12},{1,17},{... | collective-permute-start | bytes 393224 | tf_op jit(solution)/shard_map/ppermute | solution.py:217
  93.7 6.0 %collective-permute-start.33 = (bf16[16,4096]{1,0:T(8,128)(2,1)S(1)}, bf16[16,4096]{1,0:T(8,128)(2,1)S(1)}, u32[]{:S(2)}, u32[]{:S(2)}) collective-permute-start(bf16[16,4096]{1,0:T(8,128)(2,1)S(1)} %constant_dynamic-update-slice_fusion.2), channel_id=1, source_target_pairs={{0,8},{4,12},{8,0},{12,4},{16,24},{20,28},{24,16},{28,20},{1,9},{5... | collective-permute-start | bytes 393224 | tf_op jit(solution)/shard_map/ppermute | solution.py:217
  96.6 7.2 %collective-permute-start.45 = (bf16[16,4096]{1,0:T(8,128)(2,1)S(1)}, bf16[16,4096]{1,0:T(8,128)(2,1)S(1)}, u32[]{:S(2)}, u32[]{:S(2)}) collective-permute-start(bf16[16,4096]{1,0:T(8,128)(2,1)S(1)} %pad_maximum_fusion.6), channel_id=1, source_target_pairs={{0,24},{4,28},{8,16},{12,20},{16,8},{20,12},{24,0},{28,4},{1,25},{... | collective-permute-start | bytes 393224 | tf_op jit(solution)/shard_map/ppermute | solution.py:217
  97.4 8.5 %collective-permute-start.37 = (bf16[16,4096]{1,0:T(8,128)(2,1)S(1)}, bf16[16,4096]{1,0:T(8,128)(2,1)S(1)}, u32[]{:S(2)}, u32[]{:S(2)}) collective-permute-start(bf16[16,4096]{1,0:T(8,128)(2,1)S(1)} %constant_dynamic-update-slice_fusion.2), channel_id=1, source_target_pairs={{0,24},{4,28},{8,16},{12,20},{16,8},{20,12},{24,0},{28,4},{1,25},{... | collective-permute-start | bytes 393224 | tf_op jit(solution)/shard_map/ppermute | solution.py:217
  99.8 6.2 %collective-permute-start.34 = (bf16[16,4096]{1,0:T(8,128)(2,1)S(1)}, bf16[16,4096]{1,0:T(8,128)(2,1)S(1)}, u32[]{:S(2)}, u32[]{:S(2)}) collective-permute-start(bf16[16,4096]{1,0:T(8,128)(2,1)S(1)} %collective-permute-done.33), channel_id=1, source_target_pairs={{0,4},{4,0},{8,12},{12,8},{16,20},{20,16},{24,28},{28,24},{1,5},{5... | collective-permute-start | bytes 393224 | tf_op jit(solution)/shard_map/ppermute | solution.py:217
  100.3 5.6 %collective-permute-start.44 = (bf16[16,4096]{1,0:T(8,128)(2,1)S(1)}, bf16[16,4096]{1,0:T(8,128)(2,1)S(1)}, u32[]{:S(2)}, u32[]{:S(2)}) collective-permute-start(bf16[16,4096]{1,0:T(8,128)(2,1)S(1)} %collective-permute-done.43), channel_id=1, source_target_pairs={{0,4},{4,0},{8,12},{12,8},{16,20},{20,16},{24,28},{28,24},{1,5},{5... | collective-permute-start | bytes 393224 | tf_op jit(solution)/shard_map/ppermute | solution.py:217
  101.1 4.9 %collective-permute-start.36 = (bf16[16,4096]{1,0:T(8,128)(2,1)S(1)}, bf16[16,4096]{1,0:T(8,128)(2,1)S(1)}, u32[]{:S(2)}, u32[]{:S(2)}) collective-permute-start(bf16[16,4096]{1,0:T(8,128)(2,1)S(1)} %collective-permute-done.35), channel_id=1, source_target_pairs={{0,4},{4,0},{8,12},{12,8},{16,20},{20,16},{24,28},{28,24},{1,5},{5... | collective-permute-start | bytes 393224 | tf_op jit(solution)/shard_map/ppermute | solution.py:217
  103.9 2.2 %collective-permute-start.46 = (bf16[16,4096]{1,0:T(8,128)(2,1)S(1)}, bf16[16,4096]{1,0:T(8,128)(2,1)S(1)}, u32[]{:S(2)}, u32[]{:S(2)}) collective-permute-start(bf16[16,4096]{1,0:T(8,128)(2,1)S(1)} %collective-permute-done.45), channel_id=1, source_target_pairs={{0,4},{4,0},{8,12},{12,8},{16,20},{20,16},{24,28},{28,24},{1,5},{5... | collective-permute-start | bytes 393224 | tf_op jit(solution)/shard_map/ppermute | solution.py:217
  112.2 8.9 %collective-permute-start.47 = (f16[2,8,8,1024]{3,2,1,0:T(8,128)(2,1)S(1)}, f16[2,8,8,1024]{3,2,1,0:T(8,128)(2,1)S(1)}, u32[]{:S(2)}, u32[]{:S(2)}) collective-permute-start(f16[2,8,8,1024]{3,2,1,0:T(8,128)(2,1)S(1)} %fusion.20), channel_id=1, source_target_pairs={{0,1},{1,0},{2,3},{3,2},{4,5},{5,4},{6,7},{7,6},{8,9},{9,8},{10,11... | collective-permute-start | bytes 786440 | tf_op jit(solution)/shard_map/ppermute | solution.py:217
  117.3 6.2 %collective-permute-start.50 = (f16[8,8,1024]{2,1,0:T(8,128)(2,1)S(1)}, f16[8,8,1024]{2,1,0:T(8,128)(2,1)S(1)}, u32[]{:S(2)}, u32[]{:S(2)}) collective-permute-start(f16[8,8,1024]{2,1,0:T(8,128)(2,1)S(1)} %get-tuple-element.46), channel_id=1, source_target_pairs={{0,1},{1,0},{2,3},{3,2},{4,5},{5,4},{6,7},{7,6},{8,9},{9,8},{10,11... | collective-permute-start | bytes 393224 | tf_op jit(solution)/shard_map/ppermute | solution.py:217
  121.3 11.4 %collective-permute-start.48 = (f16[8,8,1024]{2,1,0:T(8,128)(2,1)S(1)}, f16[8,8,1024]{2,1,0:T(8,128)(2,1)S(1)}, u32[]{:S(2)}, u32[]{:S(2)}) collective-permute-start(f16[8,8,1024]{2,1,0:T(8,128)(2,1)S(1)} %fusion.42), channel_id=1, source_target_pairs={{0,2},{1,3},{2,0},{3,1},{4,6},{5,7},{6,4},{7,5},{8,10},{9,11},{10,... | collective-permute-start | bytes 393224 | tf_op jit(solution)/shard_map/ppermute | solution.py:217
  123.5 11.4 %collective-permute-start.51 = (f16[8,8,1024]{2,1,0:T(8,128)(2,1)S(1)}, f16[8,8,1024]{2,1,0:T(8,128)(2,1)S(1)}, u32[]{:S(2)}, u32[]{:S(2)}) collective-permute-start(f16[8,8,1024]{2,1,0:T(8,128)(2,1)S(1)} %fusion.28), channel_id=1, source_target_pairs={{0,2},{1,3},{2,0},{3,1},{4,6},{5,7},{6,4},{7,5},{8,10},{9,11},{10,... | collective-permute-start | bytes 393224 | tf_op jit(solution)/shard_map/ppermute | solution.py:217
  125.1 9.8 %collective-permute-start.49 = (f16[8,8,1024]{2,1,0:T(8,128)(2,1)S(1)}, f16[8,8,1024]{2,1,0:T(8,128)(2,1)S(1)}, u32[]{:S(2)}, u32[]{:S(2)}) collective-permute-start(f16[8,8,1024]{2,1,0:T(8,128)(2,1)S(1)} %get-tuple-element.38), channel_id=1, source_target_pairs={{0,1},{1,0},{2,3},{3,2},{4,5},{5,4},{6,7},{7,6},{8,9},{9,8},{10,11... | collective-permute-start | bytes 393224 | tf_op jit(solution)/shard_map/ppermute | solution.py:217
  135.0 4.8 %collective-permute-start.52 = (bf16[2,8,2048]{2,1,0:T(8,128)(2,1)S(1)}, bf16[2,8,2048]{2,1,0:T(8,128)(2,1)S(1)}, u32[]{:S(2)}, u32[]{:S(2)}) collective-permute-start(bf16[2,8,2048]{2,1,0:T(8,128)(2,1)S(1)} %get-tuple-element.53), channel_id=1, source_target_pairs={{0,8},{4,12},{8,0},{12,4},{16,24},{20,28},{24,16},{28,20},{1,9},{5... | collective-permute-start | bytes 196616 | tf_op jit(solution)/shard_map/ppermute | solution.py:217
  135.6 4.7 %collective-permute-start.53 = (bf16[2,8,2048]{2,1,0:T(8,128)(2,1)S(1)}, bf16[2,8,2048]{2,1,0:T(8,128)(2,1)S(1)}, u32[]{:S(2)}, u32[]{:S(2)}) collective-permute-start(bf16[2,8,2048]{2,1,0:T(8,128)(2,1)S(1)} %get-tuple-element.54), channel_id=1, source_target_pairs={{0,16},{4,20},{8,24},{12,28},{16,0},{20,4},{24,8},{28,12},{1,17},{... | collective-permute-start | bytes 196616 | tf_op jit(solution)/shard_map/ppermute | solution.py:217
  136.4 5.2 %collective-permute-start.54 = (bf16[2,8,2048]{2,1,0:T(8,128)(2,1)S(1)}, bf16[2,8,2048]{2,1,0:T(8,128)(2,1)S(1)}, u32[]{:S(2)}, u32[]{:S(2)}) collective-permute-start(bf16[2,8,2048]{2,1,0:T(8,128)(2,1)S(1)} %get-tuple-element.55), channel_id=1, source_target_pairs={{0,24},{4,28},{8,16},{12,20},{16,8},{20,12},{24,0},{28,4},{1,25},{... | collective-permute-start | bytes 196616 | tf_op jit(solution)/shard_map/ppermute | solution.py:217
  (13 other events, 35.9 us)

commit v5 on v3

--- a/solution.py
+++ b/solution.py
@@ -67,13 +67,18 @@
     def score(row, wide, count):
         for group in range(KVH):
             heads = pl.ds(group * share, share)
-            wide[heads, group * HD : (group + 1) * HD] = query[row, heads]
-        scores = lax.dot_general(
-            wide[...],
-            keys[row, :count],
-            (((1,), (1,)), ((), ())),
-            preferred_element_type=jnp.float32,
-        )
+            side = group % 2 * HD
+            wide[heads, side : side + HD] = query[row, heads]
+        scores = [
+            lax.dot_general(
+                wide[2 * share * pair : 2 * share * (pair + 1)],
+                keys[row, :count, 2 * HD * pair : 2 * HD * (pair + 1)],
+                (((1,), (1,)), ((), ())),
+                preferred_element_type=jnp.float32,
+            )
+            for pair in range(KVH // 2)
+        ]
+        scores = jnp.concatenate(scores, axis=0)
         position = lax.broadcasted_iota(jnp.int32, scores.shape, 1)
         return jnp.where(position < lengths[row], scores * scale, -jnp.inf)
 
@@ -89,12 +94,18 @@
         return weights, (pnew * unit).astype(jnp.bfloat16).astype(jnp.float32)
 
     def mix(row, weights, wnew, count):
-        mixed = jnp.dot(weights, values[row, :count], preferred_element_type=jnp.float32)
-        for group in range(KVH):
-            heads = slice(group * share, (group + 1) * share)
-            own = mixed[heads, group * HD : (group + 1) * HD]
-            own = own + wnew[heads] * value_new[row, group : group + 1]
-            out[row, heads] = own.astype(out.dtype)
+        for pair in range(KVH // 2):
+            mixed = jnp.dot(
+                weights[2 * share * pair : 2 * share * (pair + 1)],
+                values[row, :count, 2 * HD * pair : 2 * HD * (pair + 1)],
+                preferred_element_type=jnp.float32,
+            )
+            for side in range(2):
+                group = 2 * pair + side
+                heads = slice(group * share, (group + 1) * share)
+                own = mixed[side * share : (side + 1) * share, side * HD : (side + 1) * HD]
+                own = own + wnew[heads] * value_new[row, group : group + 1]
+                out[row, heads] = own.astype(out.dtype)
 
     def group(row, count):
         each = [row + at for at in range(GROUP)]
@@ -154,7 +165,7 @@
         scratch_shapes=[
             pltpu.VMEM((rows, span, width), jnp.bfloat16),
             pltpu.VMEM((rows, span, width), jnp.bfloat16),
-            pltpu.VMEM((GROUP, HQ, width), jnp.bfloat16),
+            pltpu.VMEM((GROUP, HQ, 2 * HD), jnp.bfloat16),
             pltpu.SemaphoreType.DMA((rows, 2)),
         ],
         compiler_params=pltpu.CompilerParams(vmem_limit_bytes=ROOM),
@@ -302,39 +313,11 @@
     return (rows * scale).astype(jnp.bfloat16), unit
 
 
-def norm_kernel(hidden_hbm, gain_hbm, out, hidden, gain, sems):
-    copies = (
-        pltpu.make_async_copy(hidden_hbm, hidden, sems.at[0]),
-        pltpu.make_async_copy(gain_hbm, gain, sems.at[1]),
-    )
-    for copy in copies:
-        copy.start()
-    for copy in copies:
-        copy.wait()
-    widened = hidden[...].astype(jnp.float32)
-    mean = jnp.mean(widened * widened, axis=-1, keepdims=True)
-    out[...] = (widened * lax.rsqrt(mean + eps) * gain[...]).astype(out.dtype)
-
-
-def norm(hidden_in, norm_gain):
-    anywhere = pl.BlockSpec(memory_space=pl.ANY)
-    gain = norm_gain.reshape(1, -1)
-    return pl.pallas_call(
-        norm_kernel,
-        in_specs=[anywhere, anywhere],
-        out_specs=pl.BlockSpec(memory_space=pltpu.VMEM),
-        out_shape=jax.ShapeDtypeStruct(hidden_in.shape, jnp.bfloat16),
-        scratch_shapes=[
-            pltpu.VMEM(hidden_in.shape, hidden_in.dtype),
-            pltpu.VMEM(gain.shape, gain.dtype),
-            pltpu.SemaphoreType.DMA((2,)),
-        ],
-        compiler_params=pltpu.CompilerParams(vmem_limit_bytes=62 * 2**20),
-    )(hidden_in, gain)
-
-
 def on_device(hidden_in, norm_gain, w_qkv, k_cache, v_cache, lengths, w_out):
-    normed = norm(hidden_in, norm_gain)
+    widened = hidden_in.astype(jnp.float32)
+    normed = (
+        widened * lax.rsqrt(jnp.mean(widened * widened, axis=-1, keepdims=True) + eps) * norm_gain
+    ).astype(jnp.bfloat16)
     qkv = project(normed, w_qkv, 32.0)
     owned = deliver(qkv)
     attended = attend_local(owned, k_cache, v_cache, lengths)

time: 136 us -> 135 us (level)
  starting transfers between devices: 52.4 us -> 49 us
  waiting for transfers between devices: 48.9 us -> 51.6 us
  Pallas kernels: 27.6 us -> 25.3 us
  other arithmetic: 3.7 us -> 5.99 us
    ppermute x56, starting transfers between devices: 52.4 us -> 49 us  [swap(): return lax.ppermute(block, axis, [(i, i ^ bit) for i in range(count)])]
    ppermute x56, waiting for transfers between devices: 48.9 us -> 51.6 us  [swap(): return lax.ppermute(block, axis, [(i, i ^ bit) for i in range(count)])]
    pallas_call x1 -> x0, Pallas kernels: 1.98 us -> none  [norm(): pl.pallas_call(norm_kernel, in_specs=[anywhere, anywhere], out_specs=pl.B...]
  transfers between devices with their start and end apart: 56 -> 56, of which waited for: 29 -> 28; matrix products, arithmetic and copies ran while one was open for 1% -> 1% of each run, Pallas kernels for 8% -> 8%
where the time goes in v5:
time: 135 us; the launch traced here: 134 us
  waiting for transfers between devices  51.6 us (38%)
  starting transfers between devices  49 us (36%)
  Pallas kernels  25.3 us (19%)
  other arithmetic  5.99 us (4%)
  local copies, waits for them, and re-layouts  1.72 us (1%)
    ppermute x56, waiting for transfers between devices, swap(): return lax.ppermute(block, axis, [(i, i ^ bit) for i in range(count)])  51.6 us
    ppermute x56, starting transfers between devices, swap(): return lax.ppermute(block, axis, [(i, i ^ bit) for i in range(count)])  49 us
    pallas_call x4, Pallas kernels, multiply(): pl.pallas_call(functools.partial(multiply_kernel, start), in_specs=[vmem,...  20.3 us
    pallas_call x1, Pallas kernels, attend_local(): pl.pallas_call(attend_kernel, in_specs=[pl.BlockSpec(memory_space=pltpu.S...  4.98 us
  transfers between devices with their start and end apart: 56, of which 28 were waited for; matrix products, arithmetic and copies ran while one was open for 1% of the time, Pallas kernels for 8%

profile of v5, /device:TPU:0, one launch (start us, length us, event | category | flops | bytes accessed | tf_op | source)
XLA Modules:
  0.0 134.4 jit_solution(15615507270202767750)
XLA Ops:
  0.0 1.2 fusion
  1.2 1.1 fusion.2
  2.3 3.1 %collective-permute-start.9 = (bf16[8,4096]{1,0:T(8,128)(2,1)S(1)}, bf16[8,4096]{1,0:T(8,128)(2,1)S(1)}, u32[]{:S(2)}, u32[]{:S(2)}) collective-permute-start(bf16[8,4096]{1,0:T(8,128)(2,1)S(1)} %get-tuple-element.47), channel_id=1, source_target_pairs={{0,1},{1,0},{2,3},{3,2},{4,5},{5,4},{6,7},{7,6},{8,9},{9,8},{10,11... | collective-permute-start | bytes 196616 | tf_op jit(solution)/shard_map/ppermute | solution.py:183
  5.4 2.6 %collective-permute-start = (bf16[8,4096]{1,0:T(8,128)(2,1)S(1)}, bf16[8,4096]{1,0:T(8,128)(2,1)S(1)}, u32[]{:S(2)}, u32[]{:S(2)}) collective-permute-start(bf16[8,4096]{1,0:T(8,128)(2,1)S(1)} %get-tuple-element.49), channel_id=1, source_target_pairs={{0,2},{1,3},{2,0},{3,1},{4,6},{5,7},{6,4},{7,5},{8,10},{9,11},{10,... | collective-permute-start | bytes 196616 | tf_op jit(solution)/shard_map/ppermute | solution.py:183
  8.9 1.8 %collective-permute-start.11 = (bf16[16,4096]{1,0:T(8,128)(2,1)S(1)}, bf16[16,4096]{1,0:T(8,128)(2,1)S(1)}, u32[]{:S(2)}, u32[]{:S(2)}) collective-permute-start(bf16[16,4096]{1,0:T(8,128)(2,1)S(1)} %pad_maximum_fusion.4), channel_id=1, source_target_pairs={{0,8},{4,12},{8,0},{12,4},{16,24},{20,28},{24,16},{28,20},{1,9},{5... | collective-permute-start | bytes 393224 | tf_op jit(solution)/shard_map/ppermute | solution.py:183
  10.7 1.5 %collective-permute-start.13 = (bf16[16,4096]{1,0:T(8,128)(2,1)S(1)}, bf16[16,4096]{1,0:T(8,128)(2,1)S(1)}, u32[]{:S(2)}, u32[]{:S(2)}) collective-permute-start(bf16[16,4096]{1,0:T(8,128)(2,1)S(1)} %pad_maximum_fusion.4), channel_id=1, source_target_pairs={{0,16},{4,20},{8,24},{12,28},{16,0},{20,4},{24,8},{28,12},{1,17},{... | collective-permute-start | bytes 393224 | tf_op jit(solution)/shard_map/ppermute | solution.py:183
  12.7 2.4 %collective-permute-start.15 = (bf16[16,4096]{1,0:T(8,128)(2,1)S(1)}, bf16[16,4096]{1,0:T(8,128)(2,1)S(1)}, u32[]{:S(2)}, u32[]{:S(2)}) collective-permute-start(bf16[16,4096]{1,0:T(8,128)(2,1)S(1)} %pad_maximum_fusion.4), channel_id=1, source_target_pairs={{0,24},{4,28},{8,16},{12,20},{16,8},{20,12},{24,0},{28,4},{1,25},{... | collective-permute-start | bytes 393224 | tf_op jit(solution)/shard_map/ppermute | solution.py:183
  15.9 1.5 %collective-permute-start.5 = (bf16[16,4096]{1,0:T(8,128)(2,1)S(1)}, bf16[16,4096]{1,0:T(8,128)(2,1)S(1)}, u32[]{:S(2)}, u32[]{:S(2)}) collective-permute-start(bf16[16,4096]{1,0:T(8,128)(2,1)S(1)} %constant_dynamic-update-slice_fusion), channel_id=1, source_target_pairs={{0,16},{4,20},{8,24},{12,28},{16,0},{20,4},{24,8},{28,12},{1,17},{... | collective-permute-start | bytes 393224 | tf_op jit(solution)/shard_map/ppermute | solution.py:183
  17.4 1.6 %collective-permute-start.7 = (bf16[16,4096]{1,0:T(8,128)(2,1)S(1)}, bf16[16,4096]{1,0:T(8,128)(2,1)S(1)}, u32[]{:S(2)}, u32[]{:S(2)}) collective-permute-start(bf16[16,4096]{1,0:T(8,128)(2,1)S(1)} %constant_dynamic-update-slice_fusion), channel_id=1, source_target_pairs={{0,24},{4,28},{8,16},{12,20},{16,8},{20,12},{24,0},{28,4},{1,25},{... | collective-permute-start | bytes 393224 | tf_op jit(solution)/shard_map/ppermute | solution.py:183
  19.0 2.7 %collective-permute-done.3 = bf16[16,4096]{1,0:T(8,128)(2,1)S(1)} collective-permute-done((bf16[16,4096]{1,0:T(8,128)(2,1)S(1)}, bf16[16,4096]{1,0:T(8,128)(2,1)S(1)}, u32[]{:S(2)}, u32[]{:S(2)}) %collective-permute-start.3) | collective-permute-done | bytes 131104 | tf_op jit(solution)/shard_map/ppermute | solution.py:183
  22.4 2.3 %collective-permute-done.5 = bf16[16,4096]{1,0:T(8,128)(2,1)S(1)} collective-permute-done((bf16[16,4096]{1,0:T(8,128)(2,1)S(1)}, bf16[16,4096]{1,0:T(8,128)(2,1)S(1)}, u32[]{:S(2)}, u32[]{:S(2)}) %collective-permute-start.5) | collective-permute-done | bytes 131104 | tf_op jit(solution)/shard_map/ppermute | solution.py:183
  26.6 4.9 %shard_map.73 = f32[256,1024]{1,0:T(8,128)S(1)} custom-call(bf16[128,4096]{1,0:T(8,128)(2,1)S(1)} %bitcast.244, bf16[128,4096]{1,0:T(8,128)(2,1)S(1)} %bitcast.246, bf16[4096,2304]{1,0:T(8,128)(2,1)} %weights.5), custom_call_target="tpu_custom_call" | custom-call | flops 2147483648 | bytes 8388608 | tf_op jit(solution)/shard_map/pallas_call | solution.py:224
  32.3 5.6 %shard_map.74 = f32[256,1280]{1,0:T(8,128)S(1)} custom-call(bf16[128,4096]{1,0:T(8,128)(2,1)S(1)} %bitcast.245, bf16[128,4096]{1,0:T(8,128)(2,1)S(1)} %bitcast.247, bf16[4096,2304]{1,0:T(8,128)(2,1)} %weights.5), custom_call_target="tpu_custom_call" | custom-call | flops 2684354560 | bytes 10485760 | tf_op jit(solution)/shard_map/pallas_call | solution.py:224
  38.0 1.4 %collective-permute-start.24 = (f16[8,8,1280]{2,1,0:T(8,128)(2,1)S(1)}, f16[8,8,1280]{2,1,0:T(8,128)(2,1)S(1)}, u32[]{:S(2)}, u32[]{:S(2)}) collective-permute-start(f16[8,8,1280]{2,1,0:T(8,128)(2,1)S(1)} %get-tuple-element.30), channel_id=1, source_target_pairs={{0,1},{1,0},{2,3},{3,2},{4,5},{5,4},{6,7},{7,6},{8,9},{9,8},{10,11... | collective-permute-start | bytes 491528 | tf_op jit(solution)/shard_map/ppermute | solution.py:183
  40.1 2.5 %collective-permute-start.18 = (f16[8,8,1024]{2,1,0:T(8,128)(2,1)S(1)}, f16[8,8,1024]{2,1,0:T(8,128)(2,1)S(1)}, u32[]{:S(2)}, u32[]{:S(2)}) collective-permute-start(f16[8,8,1024]{2,1,0:T(8,128)(2,1)S(1)} %fusion.41), channel_id=1, source_target_pairs={{0,2},{1,3},{2,0},{3,1},{4,6},{5,7},{6,4},{7,5},{8,10},{9,11},{10,... | collective-permute-start | bytes 393224 | tf_op jit(solution)/shard_map/ppermute | solution.py:183
  42.6 4.2 %collective-permute-done.24 = f16[8,8,1280]{2,1,0:T(8,128)(2,1)S(1)} collective-permute-done((f16[8,8,1280]{2,1,0:T(8,128)(2,1)S(1)}, f16[8,8,1280]{2,1,0:T(8,128)(2,1)S(1)}, u32[]{:S(2)}, u32[]{:S(2)}) %collective-permute-start.24) | collective-permute-done | bytes 163872 | tf_op jit(solution)/shard_map/ppermute | solution.py:183
  46.9 1.8 %collective-permute-start.25 = (f16[8,8,1280]{2,1,0:T(8,128)(2,1)S(1)}, f16[8,8,1280]{2,1,0:T(8,128)(2,1)S(1)}, u32[]{:S(2)}, u32[]{:S(2)}) collective-permute-start(f16[8,8,1280]{2,1,0:T(8,128)(2,1)S(1)} %fusion.14), channel_id=1, source_target_pairs={{0,2},{1,3},{2,0},{3,1},{4,6},{5,7},{6,4},{7,5},{8,10},{9,11},{10,... | collective-permute-start | bytes 491528 | tf_op jit(solution)/shard_map/ppermute | solution.py:183
  48.8 1.4 %collective-permute-start.19 = (bf16[2,8,1024]{2,1,0:T(8,128)(2,1)S(1)}, bf16[2,8,1024]{2,1,0:T(8,128)(2,1)S(1)}, u32[]{:S(2)}, u32[]{:S(2)}) collective-permute-start(bf16[2,8,1024]{2,1,0:T(8,128)(2,1)S(1)} %get-tuple-element.57), channel_id=1, source_target_pairs={{0,8},{4,12},{8,0},{12,4},{16,24},{20,28},{24,16},{28,20},{1,9},{5... | collective-permute-start | bytes 98312 | tf_op jit(solution)/shard_map/ppermute | solution.py:183
  51.1 1.3 collective-permute-start.21
  52.4 4.3 %collective-permute-done.25 = f16[8,8,1280]{2,1,0:T(8,128)(2,1)S(1)} collective-permute-done((f16[8,8,1280]{2,1,0:T(8,128)(2,1)S(1)}, f16[8,8,1280]{2,1,0:T(8,128)(2,1)S(1)}, u32[]{:S(2)}, u32[]{:S(2)}) %collective-permute-start.25) | collective-permute-done | bytes 163872 | tf_op jit(solution)/shard_map/ppermute | solution.py:183
  57.4 1.4 %collective-permute-start.26 = (bf16[2,8,1280]{2,1,0:T(8,128)(2,1)S(1)}, bf16[2,8,1280]{2,1,0:T(8,128)(2,1)S(1)}, u32[]{:S(2)}, u32[]{:S(2)}) collective-permute-start(bf16[2,8,1280]{2,1,0:T(8,128)(2,1)S(1)} %get-tuple-element.52), channel_id=1, source_target_pairs={{0,8},{4,12},{8,0},{12,4},{16,24},{20,28},{24,16},{28,20},{1,9},{5... | collective-permute-start | bytes 122888 | tf_op jit(solution)/shard_map/ppermute | solution.py:183
  59.7 1.3 collective-permute-start.28
  61.4 1.5 %collective-permute-done.27 = bf16[2,8,1280]{2,1,0:T(8,128)(2,1)S(1)} collective-permute-done((bf16[2,8,1280]{2,1,0:T(8,128)(2,1)S(1)}, bf16[2,8,1280]{2,1,0:T(8,128)(2,1)S(1)}, u32[]{:S(2)}, u32[]{:S(2)}) %collective-permute-start.27) | collective-permute-done | bytes 40992 | tf_op jit(solution)/shard_map/ppermute | solution.py:183
  62.9 1.7 %collective-permute-done.28 = bf16[2,8,1280]{2,1,0:T(8,128)(2,1)S(1)} collective-permute-done((bf16[2,8,1280]{2,1,0:T(8,128)(2,1)S(1)}, bf16[2,8,1280]{2,1,0:T(8,128)(2,1)S(1)}, u32[]{:S(2)}, u32[]{:S(2)}) %collective-permute-start.28) | collective-permute-done | bytes 40992 | tf_op jit(solution)/shard_map/ppermute | solution.py:183
  64.7 1.2 collective-permute-done.29
  67.3 5.0 %shard_map.75 = bf16[8,128,128]{2,1,0:T(8,128)(2,1)S(1)} custom-call(s32[8]{0:T(128)S(1)} %copy-done, bf16[8,128,128]{2,1,0:T(8,128)(2,1)S(1)} %pad_maximum_fusion.1.query, bf16[8,8,128]{2,1,0:T(8,128)(2,1)S(1)} %pad_maximum_fusion.9.key_new, f32[8,8,128]{2,1,0:T(8,128)S(1)} %get-tuple-element.82.value_new, bf16[8,512,1024]{2,1,0:T(8,128)(2,1)} %k_cache.1, ...), custom_call_target="tpu_custom_call" | custom-call | flops 2147483648 | bytes 8388608 | tf_op jit(solution)/shard_map/pallas_call | solution.py:153
  72.9 1.5 %collective-permute-start.39 = (bf16[8,4096]{1,0:T(8,128)(2,1)S(1)}, bf16[8,4096]{1,0:T(8,128)(2,1)S(1)}, u32[]{:S(2)}, u32[]{:S(2)}) collective-permute-start(bf16[8,4096]{1,0:T(8,128)(2,1)S(1)} %get-tuple-element.43), channel_id=1, source_target_pairs={{0,1},{1,0},{2,3},{3,2},{4,5},{5,4},{6,7},{7,6},{8,9},{9,8},{10,11... | collective-permute-start | bytes 196616 | tf_op jit(solution)/shard_map/ppermute | solution.py:183
  74.5 1.1 collective-permute-start.30
  75.6 1.8 %collective-permute-start.31 = (bf16[8,4096]{1,0:T(8,128)(2,1)S(1)}, bf16[8,4096]{1,0:T(8,128)(2,1)S(1)}, u32[]{:S(2)}, u32[]{:S(2)}) collective-permute-start(bf16[8,4096]{1,0:T(8,128)(2,1)S(1)} %get-tuple-element.44), channel_id=1, source_target_pairs={{0,3},{1,2},{2,1},{3,0},{4,7},{5,6},{6,5},{7,4},{8,11},{9,10},{10,... | collective-permute-start | bytes 196616 | tf_op jit(solution)/shard_map/ppermute | solution.py:183
  77.4 2.2 %collective-permute-start.40 = (bf16[16,4096]{1,0:T(8,128)(2,1)S(1)}, bf16[16,4096]{1,0:T(8,128)(2,1)S(1)}, u32[]{:S(2)}, u32[]{:S(2)}) collective-permute-start(bf16[16,4096]{1,0:T(8,128)(2,1)S(1)} %pad_maximum_fusion.6), channel_id=1, source_target_pairs={{0,4},{4,0},{8,12},{12,8},{16,20},{20,16},{24,28},{28,24},{1,5},{5... | collective-permute-start | bytes 393224 | tf_op jit(solution)/shard_map/ppermute | solution.py:183
  79.8 2.3 %collective-permute-done.30 = bf16[8,4096]{1,0:T(8,128)(2,1)S(1)} collective-permute-done((bf16[8,4096]{1,0:T(8,128)(2,1)S(1)}, bf16[8,4096]{1,0:T(8,128)(2,1)S(1)}, u32[]{:S(2)}, u32[]{:S(2)}) %collective-permute-start.30) | collective-permute-done | bytes 65568 | tf_op jit(solution)/shard_map/ppermute | solution.py:183
  82.2 0.9 collective-permute-start.45
  83.6 2.3 %collective-permute-done.41 = bf16[16,4096]{1,0:T(8,128)(2,1)S(1)} collective-permute-done((bf16[16,4096]{1,0:T(8,128)(2,1)S(1)}, bf16[16,4096]{1,0:T(8,128)(2,1)S(1)}, u32[]{:S(2)}, u32[]{:S(2)}) %collective-permute-start.41) | collective-permute-done | bytes 131104 | tf_op jit(solution)/shard_map/ppermute | solution.py:183
  87.2 4.3 %collective-permute-done.33 = bf16[16,4096]{1,0:T(8,128)(2,1)S(1)} collective-permute-done((bf16[16,4096]{1,0:T(8,128)(2,1)S(1)}, bf16[16,4096]{1,0:T(8,128)(2,1)S(1)}, u32[]{:S(2)}, u32[]{:S(2)}) %collective-permute-start.33) | collective-permute-done | bytes 131104 | tf_op jit(solution)/shard_map/ppermute | solution.py:183
  92.8 2.3 %collective-permute-done.37 = bf16[16,4096]{1,0:T(8,128)(2,1)S(1)} collective-permute-done((bf16[16,4096]{1,0:T(8,128)(2,1)S(1)}, bf16[16,4096]{1,0:T(8,128)(2,1)S(1)}, u32[]{:S(2)}, u32[]{:S(2)}) %collective-permute-start.37) | collective-permute-done | bytes 131104 | tf_op jit(solution)/shard_map/ppermute | solution.py:183
  96.6 4.9 %shard_map.76 = f32[256,1024]{1,0:T(8,128)S(1)} custom-call(bf16[128,4096]{1,0:T(8,128)(2,1)S(1)} %bitcast.240, bf16[128,4096]{1,0:T(8,128)(2,1)S(1)} %bitcast.242, bf16[4096,2048]{1,0:T(8,128)(2,1)} %weights.7), custom_call_target="tpu_custom_call" | custom-call | flops 2147483648 | bytes 8388608 | tf_op jit(solution)/shard_map/pallas_call | solution.py:224
  101.7 4.9 %shard_map.77 = f32[256,1024]{1,0:T(8,128)S(1)} custom-call(bf16[128,4096]{1,0:T(8,128)(2,1)S(1)} %bitcast.241, bf16[128,4096]{1,0:T(8,128)(2,1)S(1)} %bitcast.243, bf16[4096,2048]{1,0:T(8,128)(2,1)} %weights.7), custom_call_target="tpu_custom_call" | custom-call | flops 2147483648 | bytes 8388608 | tf_op jit(solution)/shard_map/pallas_call | solution.py:224
  106.6 2.1 %collective-permute-start.50 = (f16[8,8,1024]{2,1,0:T(8,128)(2,1)S(1)}, f16[8,8,1024]{2,1,0:T(8,128)(2,1)S(1)}, u32[]{:S(2)}, u32[]{:S(2)}) collective-permute-start(f16[8,8,1024]{2,1,0:T(8,128)(2,1)S(1)} %get-tuple-element.32), channel_id=1, source_target_pairs={{0,1},{1,0},{2,3},{3,2},{4,5},{5,4},{6,7},{7,6},{8,9},{9,8},{10,11... | collective-permute-start | bytes 393224 | tf_op jit(solution)/shard_map/ppermute | solution.py:183
  108.7 2.0 %collective-permute-done.47 = f16[2,8,8,1024]{3,2,1,0:T(8,128)(2,1)S(1)} collective-permute-done((f16[2,8,8,1024]{3,2,1,0:T(8,128)(2,1)S(1)}, f16[2,8,8,1024]{3,2,1,0:T(8,128)(2,1)S(1)}, u32[]{:S(2)}, u32[]{:S(2)}) %collective-permute-start.47) | collective-permute-done | bytes 262176 | tf_op jit(solution)/shard_map/ppermute | solution.py:183
  110.9 2.1 %collective-permute-done.50 = f16[8,8,1024]{2,1,0:T(8,128)(2,1)S(1)} collective-permute-done((f16[8,8,1024]{2,1,0:T(8,128)(2,1)S(1)}, f16[8,8,1024]{2,1,0:T(8,128)(2,1)S(1)}, u32[]{:S(2)}, u32[]{:S(2)}) %collective-permute-start.50) | collective-permute-done | bytes 131104 | tf_op jit(solution)/shard_map/ppermute | solution.py:183
  113.1 1.4 %collective-permute-start.51 = (f16[8,8,1024]{2,1,0:T(8,128)(2,1)S(1)}, f16[8,8,1024]{2,1,0:T(8,128)(2,1)S(1)}, u32[]{:S(2)}, u32[]{:S(2)}) collective-permute-start(f16[8,8,1024]{2,1,0:T(8,128)(2,1)S(1)} %fusion.28), channel_id=1, source_target_pairs={{0,2},{1,3},{2,0},{3,1},{4,6},{5,7},{6,4},{7,5},{8,10},{9,11},{10,... | collective-permute-start | bytes 393224 | tf_op jit(solution)/shard_map/ppermute | solution.py:183
  115.3 7.0 %collective-permute-done.48 = f16[8,8,1024]{2,1,0:T(8,128)(2,1)S(1)} collective-permute-done((f16[8,8,1024]{2,1,0:T(8,128)(2,1)S(1)}, f16[8,8,1024]{2,1,0:T(8,128)(2,1)S(1)}, u32[]{:S(2)}, u32[]{:S(2)}) %collective-permute-start.48) | collective-permute-done | bytes 131104 | tf_op jit(solution)/shard_map/ppermute | solution.py:183
  122.3 2.3 %collective-permute-done.51 = f16[8,8,1024]{2,1,0:T(8,128)(2,1)S(1)} collective-permute-done((f16[8,8,1024]{2,1,0:T(8,128)(2,1)S(1)}, f16[8,8,1024]{2,1,0:T(8,128)(2,1)S(1)}, u32[]{:S(2)}, u32[]{:S(2)}) %collective-permute-start.51) | collective-permute-done | bytes 131104 | tf_op jit(solution)/shard_map/ppermute | solution.py:183
  125.5 0.9 collective-permute-start.53
  126.4 1.9 %collective-permute-start.54 = (bf16[2,8,2048]{2,1,0:T(8,128)(2,1)S(1)}, bf16[2,8,2048]{2,1,0:T(8,128)(2,1)S(1)}, u32[]{:S(2)}, u32[]{:S(2)}) collective-permute-start(bf16[2,8,2048]{2,1,0:T(8,128)(2,1)S(1)} %get-tuple-element.41), channel_id=1, source_target_pairs={{0,24},{4,28},{8,16},{12,20},{16,8},{20,12},{24,0},{28,4},{1,25},{... | collective-permute-start | bytes 196616 | tf_op jit(solution)/shard_map/ppermute | solution.py:183
  128.3 1.5 %collective-permute-done.52 = bf16[2,8,2048]{2,1,0:T(8,128)(2,1)S(1)} collective-permute-done((bf16[2,8,2048]{2,1,0:T(8,128)(2,1)S(1)}, bf16[2,8,2048]{2,1,0:T(8,128)(2,1)S(1)}, u32[]{:S(2)}, u32[]{:S(2)}) %collective-permute-start.52) | collective-permute-done | bytes 65568 | tf_op jit(solution)/shard_map/ppermute | solution.py:183
  129.9 1.6 %collective-permute-done.54 = bf16[2,8,2048]{2,1,0:T(8,128)(2,1)S(1)} collective-permute-done((bf16[2,8,2048]{2,1,0:T(8,128)(2,1)S(1)}, bf16[2,8,2048]{2,1,0:T(8,128)(2,1)S(1)}, u32[]{:S(2)}, u32[]{:S(2)}) %collective-permute-start.54) | collective-permute-done | bytes 65568 | tf_op jit(solution)/shard_map/ppermute | solution.py:183
  131.6 1.3 collective-permute-done.55
  (174 shorter events, 19.7 us)
Async XLA Ops:
  2.3 6.5 %collective-permute-start.9 = (bf16[8,4096]{1,0:T(8,128)(2,1)S(1)}, bf16[8,4096]{1,0:T(8,128)(2,1)S(1)}, u32[]{:S(2)}, u32[]{:S(2)}) collective-permute-start(bf16[8,4096]{1,0:T(8,128)(2,1)S(1)} %get-tuple-element.47), channel_id=1, source_target_pairs={{0,1},{1,0},{2,3},{3,2},{4,5},{5,4},{6,7},{7,6},{8,9},{9,8},{10,11... | collective-permute-start | bytes 196616 | tf_op jit(solution)/shard_map/ppermute | solution.py:183
  5.4 7.3 %collective-permute-start = (bf16[8,4096]{1,0:T(8,128)(2,1)S(1)}, bf16[8,4096]{1,0:T(8,128)(2,1)S(1)}, u32[]{:S(2)}, u32[]{:S(2)}) collective-permute-start(bf16[8,4096]{1,0:T(8,128)(2,1)S(1)} %get-tuple-element.49), channel_id=1, source_target_pairs={{0,2},{1,3},{2,0},{3,1},{4,6},{5,7},{6,4},{7,5},{8,10},{9,11},{10,... | collective-permute-start | bytes 196616 | tf_op jit(solution)/shard_map/ppermute | solution.py:183
  8.0 7.1 %collective-permute-start.1 = (bf16[8,4096]{1,0:T(8,128)(2,1)S(1)}, bf16[8,4096]{1,0:T(8,128)(2,1)S(1)}, u32[]{:S(2)}, u32[]{:S(2)}) collective-permute-start(bf16[8,4096]{1,0:T(8,128)(2,1)S(1)} %get-tuple-element.48), channel_id=1, source_target_pairs={{0,3},{1,2},{2,1},{3,0},{4,7},{5,6},{6,5},{7,4},{8,11},{9,10},{10,... | collective-permute-start | bytes 196616 | tf_op jit(solution)/shard_map/ppermute | solution.py:183
  8.9 6.4 %collective-permute-start.10 = (bf16[16,4096]{1,0:T(8,128)(2,1)S(1)}, bf16[16,4096]{1,0:T(8,128)(2,1)S(1)}, u32[]{:S(2)}, u32[]{:S(2)}) collective-permute-start(bf16[16,4096]{1,0:T(8,128)(2,1)S(1)} %pad_maximum_fusion.4), channel_id=1, source_target_pairs={{0,4},{4,0},{8,12},{12,8},{16,20},{20,16},{24,28},{28,24},{1,5},{5... | collective-permute-start | bytes 393224 | tf_op jit(solution)/shard_map/ppermute | solution.py:183
  8.9 7.0 %collective-permute-start.11 = (bf16[16,4096]{1,0:T(8,128)(2,1)S(1)}, bf16[16,4096]{1,0:T(8,128)(2,1)S(1)}, u32[]{:S(2)}, u32[]{:S(2)}) collective-permute-start(bf16[16,4096]{1,0:T(8,128)(2,1)S(1)} %pad_maximum_fusion.4), channel_id=1, source_target_pairs={{0,8},{4,12},{8,0},{12,4},{16,24},{20,28},{24,16},{28,20},{1,9},{5... | collective-permute-start | bytes 393224 | tf_op jit(solution)/shard_map/ppermute | solution.py:183
  10.7 11.0 %collective-permute-start.13 = (bf16[16,4096]{1,0:T(8,128)(2,1)S(1)}, bf16[16,4096]{1,0:T(8,128)(2,1)S(1)}, u32[]{:S(2)}, u32[]{:S(2)}) collective-permute-start(bf16[16,4096]{1,0:T(8,128)(2,1)S(1)} %pad_maximum_fusion.4), channel_id=1, source_target_pairs={{0,16},{4,20},{8,24},{12,28},{16,0},{20,4},{24,8},{28,12},{1,17},{... | collective-permute-start | bytes 393224 | tf_op jit(solution)/shard_map/ppermute | solution.py:183
  12.7 9.6 %collective-permute-start.15 = (bf16[16,4096]{1,0:T(8,128)(2,1)S(1)}, bf16[16,4096]{1,0:T(8,128)(2,1)S(1)}, u32[]{:S(2)}, u32[]{:S(2)}) collective-permute-start(bf16[16,4096]{1,0:T(8,128)(2,1)S(1)} %pad_maximum_fusion.4), channel_id=1, source_target_pairs={{0,24},{4,28},{8,16},{12,20},{16,8},{20,12},{24,0},{28,4},{1,25},{... | collective-permute-start | bytes 393224 | tf_op jit(solution)/shard_map/ppermute | solution.py:183
  15.3 6.4 %collective-permute-start.3 = (bf16[16,4096]{1,0:T(8,128)(2,1)S(1)}, bf16[16,4096]{1,0:T(8,128)(2,1)S(1)}, u32[]{:S(2)}, u32[]{:S(2)}) collective-permute-start(bf16[16,4096]{1,0:T(8,128)(2,1)S(1)} %constant_dynamic-update-slice_fusion), channel_id=1, source_target_pairs={{0,8},{4,12},{8,0},{12,4},{16,24},{20,28},{24,16},{28,20},{1,9},{5... | collective-permute-start | bytes 393224 | tf_op jit(solution)/shard_map/ppermute | solution.py:183
  15.9 8.8 %collective-permute-start.5 = (bf16[16,4096]{1,0:T(8,128)(2,1)S(1)}, bf16[16,4096]{1,0:T(8,128)(2,1)S(1)}, u32[]{:S(2)}, u32[]{:S(2)}) collective-permute-start(bf16[16,4096]{1,0:T(8,128)(2,1)S(1)} %constant_dynamic-update-slice_fusion), channel_id=1, source_target_pairs={{0,16},{4,20},{8,24},{12,28},{16,0},{20,4},{24,8},{28,12},{1,17},{... | collective-permute-start | bytes 393224 | tf_op jit(solution)/shard_map/ppermute | solution.py:183
  17.4 7.3 %collective-permute-start.7 = (bf16[16,4096]{1,0:T(8,128)(2,1)S(1)}, bf16[16,4096]{1,0:T(8,128)(2,1)S(1)}, u32[]{:S(2)}, u32[]{:S(2)}) collective-permute-start(bf16[16,4096]{1,0:T(8,128)(2,1)S(1)} %constant_dynamic-update-slice_fusion), channel_id=1, source_target_pairs={{0,24},{4,28},{8,16},{12,20},{16,8},{20,12},{24,0},{28,4},{1,25},{... | collective-permute-start | bytes 393224 | tf_op jit(solution)/shard_map/ppermute | solution.py:183
  21.7 3.5 %collective-permute-start.12 = (bf16[16,4096]{1,0:T(8,128)(2,1)S(1)}, bf16[16,4096]{1,0:T(8,128)(2,1)S(1)}, u32[]{:S(2)}, u32[]{:S(2)}) collective-permute-start(bf16[16,4096]{1,0:T(8,128)(2,1)S(1)} %collective-permute-done.11), channel_id=1, source_target_pairs={{0,4},{4,0},{8,12},{12,8},{16,20},{20,16},{24,28},{28,24},{1,5},{5... | collective-permute-start | bytes 393224 | tf_op jit(solution)/shard_map/ppermute | solution.py:183
  21.8 3.6 %collective-permute-start.4 = (bf16[16,4096]{1,0:T(8,128)(2,1)S(1)}, bf16[16,4096]{1,0:T(8,128)(2,1)S(1)}, u32[]{:S(2)}, u32[]{:S(2)}) collective-permute-start(bf16[16,4096]{1,0:T(8,128)(2,1)S(1)} %collective-permute-done.3), channel_id=1, source_target_pairs={{0,4},{4,0},{8,12},{12,8},{16,20},{20,16},{24,28},{28,24},{1,5},{5... | collective-permute-start | bytes 393224 | tf_op jit(solution)/shard_map/ppermute | solution.py:183
  22.3 3.0 %collective-permute-start.14 = (bf16[16,4096]{1,0:T(8,128)(2,1)S(1)}, bf16[16,4096]{1,0:T(8,128)(2,1)S(1)}, u32[]{:S(2)}, u32[]{:S(2)}) collective-permute-start(bf16[16,4096]{1,0:T(8,128)(2,1)S(1)} %collective-permute-done.13), channel_id=1, source_target_pairs={{0,4},{4,0},{8,12},{12,8},{16,20},{20,16},{24,28},{28,24},{1,5},{5... | collective-permute-start | bytes 393224 | tf_op jit(solution)/shard_map/ppermute | solution.py:183
  31.6 8.5 %collective-permute-start.17 = (f16[2,8,8,1024]{3,2,1,0:T(8,128)(2,1)S(1)}, f16[2,8,8,1024]{3,2,1,0:T(8,128)(2,1)S(1)}, u32[]{:S(2)}, u32[]{:S(2)}) collective-permute-start(f16[2,8,8,1024]{3,2,1,0:T(8,128)(2,1)S(1)} %fusion.19), channel_id=1, source_target_pairs={{0,1},{1,0},{2,3},{3,2},{4,5},{5,4},{6,7},{7,6},{8,9},{9,8},{10,11... | collective-permute-start | bytes 786440 | tf_op jit(solution)/shard_map/ppermute | solution.py:183
  38.0 8.9 %collective-permute-start.24 = (f16[8,8,1280]{2,1,0:T(8,128)(2,1)S(1)}, f16[8,8,1280]{2,1,0:T(8,128)(2,1)S(1)}, u32[]{:S(2)}, u32[]{:S(2)}) collective-permute-start(f16[8,8,1280]{2,1,0:T(8,128)(2,1)S(1)} %get-tuple-element.30), channel_id=1, source_target_pairs={{0,1},{1,0},{2,3},{3,2},{4,5},{5,4},{6,7},{7,6},{8,9},{9,8},{10,11... | collective-permute-start | bytes 491528 | tf_op jit(solution)/shard_map/ppermute | solution.py:183
  40.1 8.6 %collective-permute-start.18 = (f16[8,8,1024]{2,1,0:T(8,128)(2,1)S(1)}, f16[8,8,1024]{2,1,0:T(8,128)(2,1)S(1)}, u32[]{:S(2)}, u32[]{:S(2)}) collective-permute-start(f16[8,8,1024]{2,1,0:T(8,128)(2,1)S(1)} %fusion.41), channel_id=1, source_target_pairs={{0,2},{1,3},{2,0},{3,1},{4,6},{5,7},{6,4},{7,5},{8,10},{9,11},{10,... | collective-permute-start | bytes 393224 | tf_op jit(solution)/shard_map/ppermute | solution.py:183
  46.9 9.8 %collective-permute-start.25 = (f16[8,8,1280]{2,1,0:T(8,128)(2,1)S(1)}, f16[8,8,1280]{2,1,0:T(8,128)(2,1)S(1)}, u32[]{:S(2)}, u32[]{:S(2)}) collective-permute-start(f16[8,8,1280]{2,1,0:T(8,128)(2,1)S(1)} %fusion.14), channel_id=1, source_target_pairs={{0,2},{1,3},{2,0},{3,1},{4,6},{5,7},{6,4},{7,5},{8,10},{9,11},{10,... | collective-permute-start | bytes 491528 | tf_op jit(solution)/shard_map/ppermute | solution.py:183
  48.7 8.5 %collective-permute-start.23 = (f16[8,8,1280]{2,1,0:T(8,128)(2,1)S(1)}, f16[8,8,1280]{2,1,0:T(8,128)(2,1)S(1)}, u32[]{:S(2)}, u32[]{:S(2)}) collective-permute-start(f16[8,8,1280]{2,1,0:T(8,128)(2,1)S(1)} %get-tuple-element.19), channel_id=1, source_target_pairs={{0,1},{1,0},{2,3},{3,2},{4,5},{5,4},{6,7},{7,6},{8,9},{9,8},{10,11... | collective-permute-start | bytes 491528 | tf_op jit(solution)/shard_map/ppermute | solution.py:183
  48.8 10.9 %collective-permute-start.19 = (bf16[2,8,1024]{2,1,0:T(8,128)(2,1)S(1)}, bf16[2,8,1024]{2,1,0:T(8,128)(2,1)S(1)}, u32[]{:S(2)}, u32[]{:S(2)}) collective-permute-start(bf16[2,8,1024]{2,1,0:T(8,128)(2,1)S(1)} %get-tuple-element.57), channel_id=1, source_target_pairs={{0,8},{4,12},{8,0},{12,4},{16,24},{20,28},{24,16},{28,20},{1,9},{5... | collective-permute-start | bytes 98312 | tf_op jit(solution)/shard_map/ppermute | solution.py:183
  50.3 10.7 %collective-permute-start.20 = (bf16[2,8,1024]{2,1,0:T(8,128)(2,1)S(1)}, bf16[2,8,1024]{2,1,0:T(8,128)(2,1)S(1)}, u32[]{:S(2)}, u32[]{:S(2)}) collective-permute-start(bf16[2,8,1024]{2,1,0:T(8,128)(2,1)S(1)} %get-tuple-element.59), channel_id=1, source_target_pairs={{0,16},{4,20},{8,24},{12,28},{16,0},{20,4},{24,8},{28,12},{1,17},{... | collective-permute-start | bytes 98312 | tf_op jit(solution)/shard_map/ppermute | solution.py:183
  51.1 9.8 %collective-permute-start.21 = (bf16[2,8,1024]{2,1,0:T(8,128)(2,1)S(1)}, bf16[2,8,1024]{2,1,0:T(8,128)(2,1)S(1)}, u32[]{:S(2)}, u32[]{:S(2)}) collective-permute-start(bf16[2,8,1024]{2,1,0:T(8,128)(2,1)S(1)} %get-tuple-element.58), channel_id=1, source_target_pairs={{0,24},{4,28},{8,16},{12,20},{16,8},{20,12},{24,0},{28,4},{1,25},{... | collective-permute-start | bytes 98312 | tf_op jit(solution)/shard_map/ppermute | solution.py:183
  57.4 4.1 %collective-permute-start.26 = (bf16[2,8,1280]{2,1,0:T(8,128)(2,1)S(1)}, bf16[2,8,1280]{2,1,0:T(8,128)(2,1)S(1)}, u32[]{:S(2)}, u32[]{:S(2)}) collective-permute-start(bf16[2,8,1280]{2,1,0:T(8,128)(2,1)S(1)} %get-tuple-element.52), channel_id=1, source_target_pairs={{0,8},{4,12},{8,0},{12,4},{16,24},{20,28},{24,16},{28,20},{1,9},{5... | collective-permute-start | bytes 122888 | tf_op jit(solution)/shard_map/ppermute | solution.py:183
  58.8 4.1 %collective-permute-start.27 = (bf16[2,8,1280]{2,1,0:T(8,128)(2,1)S(1)}, bf16[2,8,1280]{2,1,0:T(8,128)(2,1)S(1)}, u32[]{:S(2)}, u32[]{:S(2)}) collective-permute-start(bf16[2,8,1280]{2,1,0:T(8,128)(2,1)S(1)} %get-tuple-element.54), channel_id=1, source_target_pairs={{0,16},{4,20},{8,24},{12,28},{16,0},{20,4},{24,8},{28,12},{1,17},{... | collective-permute-start | bytes 122888 | tf_op jit(solution)/shard_map/ppermute | solution.py:183
  59.7 4.9 %collective-permute-start.28 = (bf16[2,8,1280]{2,1,0:T(8,128)(2,1)S(1)}, bf16[2,8,1280]{2,1,0:T(8,128)(2,1)S(1)}, u32[]{:S(2)}, u32[]{:S(2)}) collective-permute-start(bf16[2,8,1280]{2,1,0:T(8,128)(2,1)S(1)} %get-tuple-element.53), channel_id=1, source_target_pairs={{0,24},{4,28},{8,16},{12,20},{16,8},{20,12},{24,0},{28,4},{1,25},{... | collective-permute-start | bytes 122888 | tf_op jit(solution)/shard_map/ppermute | solution.py:183
  61.0 3.7 %collective-permute-start.22 = (bf16[4,8,1024]{2,1,0:T(8,128)(2,1)S(1)}, bf16[4,8,1024]{2,1,0:T(8,128)(2,1)S(1)}, u32[]{:S(2)}, u32[]{:S(2)}) collective-permute-start(bf16[4,8,1024]{2,1,0:T(8,128)(2,1)S(1)} %pad_maximum_fusion.8), channel_id=1, source_target_pairs={{0,4},{4,0},{8,12},{12,8},{16,20},{20,16},{24,28},{28,24},{1,5},{5... | collective-permute-start | bytes 196616 | tf_op jit(solution)/shard_map/ppermute | solution.py:183
  72.9 4.5 %collective-permute-start.39 = (bf16[8,4096]{1,0:T(8,128)(2,1)S(1)}, bf16[8,4096]{1,0:T(8,128)(2,1)S(1)}, u32[]{:S(2)}, u32[]{:S(2)}) collective-permute-start(bf16[8,4096]{1,0:T(8,128)(2,1)S(1)} %get-tuple-element.43), channel_id=1, source_target_pairs={{0,1},{1,0},{2,3},{3,2},{4,5},{5,4},{6,7},{7,6},{8,9},{9,8},{10,11... | collective-permute-start | bytes 196616 | tf_op jit(solution)/shard_map/ppermute | solution.py:183
  74.5 7.7 %collective-permute-start.30 = (bf16[8,4096]{1,0:T(8,128)(2,1)S(1)}, bf16[8,4096]{1,0:T(8,128)(2,1)S(1)}, u32[]{:S(2)}, u32[]{:S(2)}) collective-permute-start(bf16[8,4096]{1,0:T(8,128)(2,1)S(1)} %get-tuple-element.45), channel_id=1, source_target_pairs={{0,2},{1,3},{2,0},{3,1},{4,6},{5,7},{6,4},{7,5},{8,10},{9,11},{10,... | collective-permute-start | bytes 196616 | tf_op jit(solution)/shard_map/ppermute | solution.py:183
  75.6 7.5 %collective-permute-start.31 = (bf16[8,4096]{1,0:T(8,128)(2,1)S(1)}, bf16[8,4096]{1,0:T(8,128)(2,1)S(1)}, u32[]{:S(2)}, u32[]{:S(2)}) collective-permute-start(bf16[8,4096]{1,0:T(8,128)(2,1)S(1)} %get-tuple-element.44), channel_id=1, source_target_pairs={{0,3},{1,2},{2,1},{3,0},{4,7},{5,6},{6,5},{7,4},{8,11},{9,10},{10,... | collective-permute-start | bytes 196616 | tf_op jit(solution)/shard_map/ppermute | solution.py:183
  77.4 5.9 %collective-permute-start.40 = (bf16[16,4096]{1,0:T(8,128)(2,1)S(1)}, bf16[16,4096]{1,0:T(8,128)(2,1)S(1)}, u32[]{:S(2)}, u32[]{:S(2)}) collective-permute-start(bf16[16,4096]{1,0:T(8,128)(2,1)S(1)} %pad_maximum_fusion.6), channel_id=1, source_target_pairs={{0,4},{4,0},{8,12},{12,8},{16,20},{20,16},{24,28},{28,24},{1,5},{5... | collective-permute-start | bytes 393224 | tf_op jit(solution)/shard_map/ppermute | solution.py:183
  79.6 6.4 %collective-permute-start.41 = (bf16[16,4096]{1,0:T(8,128)(2,1)S(1)}, bf16[16,4096]{1,0:T(8,128)(2,1)S(1)}, u32[]{:S(2)}, u32[]{:S(2)}) collective-permute-start(bf16[16,4096]{1,0:T(8,128)(2,1)S(1)} %pad_maximum_fusion.6), channel_id=1, source_target_pairs={{0,8},{4,12},{8,0},{12,4},{16,24},{20,28},{24,16},{28,20},{1,9},{5... | collective-permute-start | bytes 393224 | tf_op jit(solution)/shard_map/ppermute | solution.py:183
  79.8 11.7 %collective-permute-start.43 = (bf16[16,4096]{1,0:T(8,128)(2,1)S(1)}, bf16[16,4096]{1,0:T(8,128)(2,1)S(1)}, u32[]{:S(2)}, u32[]{:S(2)}) collective-permute-start(bf16[16,4096]{1,0:T(8,128)(2,1)S(1)} %pad_maximum_fusion.6), channel_id=1, source_target_pairs={{0,16},{4,20},{8,24},{12,28},{16,0},{20,4},{24,8},{28,12},{1,17},{... | collective-permute-start | bytes 393224 | tf_op jit(solution)/shard_map/ppermute | solution.py:183
  82.2 10.0 %collective-permute-start.45 = (bf16[16,4096]{1,0:T(8,128)(2,1)S(1)}, bf16[16,4096]{1,0:T(8,128)(2,1)S(1)}, u32[]{:S(2)}, u32[]{:S(2)}) collective-permute-start(bf16[16,4096]{1,0:T(8,128)(2,1)S(1)} %pad_maximum_fusion.6), channel_id=1, source_target_pairs={{0,24},{4,28},{8,16},{12,20},{16,8},{20,12},{24,0},{28,4},{1,25},{... | collective-permute-start | bytes 393224 | tf_op jit(solution)/shard_map/ppermute | solution.py:183
  83.1 3.6 %collective-permute-start.32 = (bf16[16,4096]{1,0:T(8,128)(2,1)S(1)}, bf16[16,4096]{1,0:T(8,128)(2,1)S(1)}, u32[]{:S(2)}, u32[]{:S(2)}) collective-permute-start(bf16[16,4096]{1,0:T(8,128)(2,1)S(1)} %constant_dynamic-update-slice_fusion.2), channel_id=1, source_target_pairs={{0,4},{4,0},{8,12},{12,8},{16,20},{20,16},{24,28},{28,24},{1,5},{5... | collective-permute-start | bytes 393224 | tf_op jit(solution)/shard_map/ppermute | solution.py:183
  83.3 8.2 %collective-permute-start.33 = (bf16[16,4096]{1,0:T(8,128)(2,1)S(1)}, bf16[16,4096]{1,0:T(8,128)(2,1)S(1)}, u32[]{:S(2)}, u32[]{:S(2)}) collective-permute-start(bf16[16,4096]{1,0:T(8,128)(2,1)S(1)} %constant_dynamic-update-slice_fusion.2), channel_id=1, source_target_pairs={{0,8},{4,12},{8,0},{12,4},{16,24},{20,28},{24,16},{28,20},{1,9},{5... | collective-permute-start | bytes 393224 | tf_op jit(solution)/shard_map/ppermute | solution.py:183
  85.9 6.9 %collective-permute-start.35 = (bf16[16,4096]{1,0:T(8,128)(2,1)S(1)}, bf16[16,4096]{1,0:T(8,128)(2,1)S(1)}, u32[]{:S(2)}, u32[]{:S(2)}) collective-permute-start(bf16[16,4096]{1,0:T(8,128)(2,1)S(1)} %constant_dynamic-update-slice_fusion.2), channel_id=1, source_target_pairs={{0,16},{4,20},{8,24},{12,28},{16,0},{20,4},{24,8},{28,12},{1,17},{... | collective-permute-start | bytes 393224 | tf_op jit(solution)/shard_map/ppermute | solution.py:183
  86.7 8.4 %collective-permute-start.37 = (bf16[16,4096]{1,0:T(8,128)(2,1)S(1)}, bf16[16,4096]{1,0:T(8,128)(2,1)S(1)}, u32[]{:S(2)}, u32[]{:S(2)}) collective-permute-start(bf16[16,4096]{1,0:T(8,128)(2,1)S(1)} %constant_dynamic-update-slice_fusion.2), channel_id=1, source_target_pairs={{0,24},{4,28},{8,16},{12,20},{16,8},{20,12},{24,0},{28,4},{1,25},{... | collective-permute-start | bytes 393224 | tf_op jit(solution)/shard_map/ppermute | solution.py:183
  91.5 3.6 %collective-permute-start.42 = (bf16[16,4096]{1,0:T(8,128)(2,1)S(1)}, bf16[16,4096]{1,0:T(8,128)(2,1)S(1)}, u32[]{:S(2)}, u32[]{:S(2)}) collective-permute-start(bf16[16,4096]{1,0:T(8,128)(2,1)S(1)} %collective-permute-done.41), channel_id=1, source_target_pairs={{0,4},{4,0},{8,12},{12,8},{16,20},{20,16},{24,28},{28,24},{1,5},{5... | collective-permute-start | bytes 393224 | tf_op jit(solution)/shard_map/ppermute | solution.py:183
  91.6 4.1 %collective-permute-start.34 = (bf16[16,4096]{1,0:T(8,128)(2,1)S(1)}, bf16[16,4096]{1,0:T(8,128)(2,1)S(1)}, u32[]{:S(2)}, u32[]{:S(2)}) collective-permute-start(bf16[16,4096]{1,0:T(8,128)(2,1)S(1)} %collective-permute-done.33), channel_id=1, source_target_pairs={{0,4},{4,0},{8,12},{12,8},{16,20},{20,16},{24,28},{28,24},{1,5},{5... | collective-permute-start | bytes 393224 | tf_op jit(solution)/shard_map/ppermute | solution.py:183
  92.1 3.5 %collective-permute-start.44 = (bf16[16,4096]{1,0:T(8,128)(2,1)S(1)}, bf16[16,4096]{1,0:T(8,128)(2,1)S(1)}, u32[]{:S(2)}, u32[]{:S(2)}) collective-permute-start(bf16[16,4096]{1,0:T(8,128)(2,1)S(1)} %collective-permute-done.43), channel_id=1, source_target_pairs={{0,4},{4,0},{8,12},{12,8},{16,20},{20,16},{24,28},{28,24},{1,5},{5... | collective-permute-start | bytes 393224 | tf_op jit(solution)/shard_map/ppermute | solution.py:183
  92.8 3.7 %collective-permute-start.46 = (bf16[16,4096]{1,0:T(8,128)(2,1)S(1)}, bf16[16,4096]{1,0:T(8,128)(2,1)S(1)}, u32[]{:S(2)}, u32[]{:S(2)}) collective-permute-start(bf16[16,4096]{1,0:T(8,128)(2,1)S(1)} %collective-permute-done.45), channel_id=1, source_target_pairs={{0,4},{4,0},{8,12},{12,8},{16,20},{20,16},{24,28},{28,24},{1,5},{5... | collective-permute-start | bytes 393224 | tf_op jit(solution)/shard_map/ppermute | solution.py:183
  101.6 9.1 %collective-permute-start.47 = (f16[2,8,8,1024]{3,2,1,0:T(8,128)(2,1)S(1)}, f16[2,8,8,1024]{3,2,1,0:T(8,128)(2,1)S(1)}, u32[]{:S(2)}, u32[]{:S(2)}) collective-permute-start(f16[2,8,8,1024]{3,2,1,0:T(8,128)(2,1)S(1)} %fusion.20), channel_id=1, source_target_pairs={{0,1},{1,0},{2,3},{3,2},{4,5},{5,4},{6,7},{7,6},{8,9},{9,8},{10,11... | collective-permute-start | bytes 786440 | tf_op jit(solution)/shard_map/ppermute | solution.py:183
  106.6 6.4 %collective-permute-start.50 = (f16[8,8,1024]{2,1,0:T(8,128)(2,1)S(1)}, f16[8,8,1024]{2,1,0:T(8,128)(2,1)S(1)}, u32[]{:S(2)}, u32[]{:S(2)}) collective-permute-start(f16[8,8,1024]{2,1,0:T(8,128)(2,1)S(1)} %get-tuple-element.32), channel_id=1, source_target_pairs={{0,1},{1,0},{2,3},{3,2},{4,5},{5,4},{6,7},{7,6},{8,9},{9,8},{10,11... | collective-permute-start | bytes 393224 | tf_op jit(solution)/shard_map/ppermute | solution.py:183
  110.8 11.4 %collective-permute-start.48 = (f16[8,8,1024]{2,1,0:T(8,128)(2,1)S(1)}, f16[8,8,1024]{2,1,0:T(8,128)(2,1)S(1)}, u32[]{:S(2)}, u32[]{:S(2)}) collective-permute-start(f16[8,8,1024]{2,1,0:T(8,128)(2,1)S(1)} %fusion.42), channel_id=1, source_target_pairs={{0,2},{1,3},{2,0},{3,1},{4,6},{5,7},{6,4},{7,5},{8,10},{9,11},{10,... | collective-permute-start | bytes 393224 | tf_op jit(solution)/shard_map/ppermute | solution.py:183
  113.1 11.6 %collective-permute-start.51 = (f16[8,8,1024]{2,1,0:T(8,128)(2,1)S(1)}, f16[8,8,1024]{2,1,0:T(8,128)(2,1)S(1)}, u32[]{:S(2)}, u32[]{:S(2)}) collective-permute-start(f16[8,8,1024]{2,1,0:T(8,128)(2,1)S(1)} %fusion.28), channel_id=1, source_target_pairs={{0,2},{1,3},{2,0},{3,1},{4,6},{5,7},{6,4},{7,5},{8,10},{9,11},{10,... | collective-permute-start | bytes 393224 | tf_op jit(solution)/shard_map/ppermute | solution.py:183
  114.5 10.1 %collective-permute-start.49 = (f16[8,8,1024]{2,1,0:T(8,128)(2,1)S(1)}, f16[8,8,1024]{2,1,0:T(8,128)(2,1)S(1)}, u32[]{:S(2)}, u32[]{:S(2)}) collective-permute-start(f16[8,8,1024]{2,1,0:T(8,128)(2,1)S(1)} %get-tuple-element.24), channel_id=1, source_target_pairs={{0,1},{1,0},{2,3},{3,2},{4,5},{5,4},{6,7},{7,6},{8,9},{9,8},{10,11... | collective-permute-start | bytes 393224 | tf_op jit(solution)/shard_map/ppermute | solution.py:183
  124.7 5.0 %collective-permute-start.52 = (bf16[2,8,2048]{2,1,0:T(8,128)(2,1)S(1)}, bf16[2,8,2048]{2,1,0:T(8,128)(2,1)S(1)}, u32[]{:S(2)}, u32[]{:S(2)}) collective-permute-start(bf16[2,8,2048]{2,1,0:T(8,128)(2,1)S(1)} %get-tuple-element.39), channel_id=1, source_target_pairs={{0,8},{4,12},{8,0},{12,4},{16,24},{20,28},{24,16},{28,20},{1,9},{5... | collective-permute-start | bytes 196616 | tf_op jit(solution)/shard_map/ppermute | solution.py:183
  125.5 4.4 %collective-permute-start.53 = (bf16[2,8,2048]{2,1,0:T(8,128)(2,1)S(1)}, bf16[2,8,2048]{2,1,0:T(8,128)(2,1)S(1)}, u32[]{:S(2)}, u32[]{:S(2)}) collective-permute-start(bf16[2,8,2048]{2,1,0:T(8,128)(2,1)S(1)} %get-tuple-element.40), channel_id=1, source_target_pairs={{0,16},{4,20},{8,24},{12,28},{16,0},{20,4},{24,8},{28,12},{1,17},{... | collective-permute-start | bytes 196616 | tf_op jit(solution)/shard_map/ppermute | solution.py:183
  126.4 5.2 %collective-permute-start.54 = (bf16[2,8,2048]{2,1,0:T(8,128)(2,1)S(1)}, bf16[2,8,2048]{2,1,0:T(8,128)(2,1)S(1)}, u32[]{:S(2)}, u32[]{:S(2)}) collective-permute-start(bf16[2,8,2048]{2,1,0:T(8,128)(2,1)S(1)} %get-tuple-element.41), channel_id=1, source_target_pairs={{0,24},{4,28},{8,16},{12,20},{16,8},{20,12},{24,0},{28,4},{1,25},{... | collective-permute-start | bytes 196616 | tf_op jit(solution)/shard_map/ppermute | solution.py:183
  (9 other events, 41.6 us)

commit v6 on v5

--- a/solution.py
+++ b/solution.py
@@ -33,7 +33,7 @@
 
 
 PART = 128
-GROUP = 4
+GROUP = 2
 
 
 def attend_kernel(lengths, query, key_new, value_new, k_cache, v_cache, out, keys, values, wide, sems):
@@ -292,9 +292,11 @@
 def deliver(parts):
     owned = jnp.concatenate([collect(part) for part in parts], axis=-1)
     count, rows, width = owned.shape
-    if count == 8:
-        owned = owned[jnp.arange(count) ^ lax.axis_index("gx")]
-    return owned.transpose(1, 0, 2).reshape(rows, count * width)
+    if count != 8:
+        return owned.transpose(1, 0, 2).reshape(rows, count * width)
+    me = lax.axis_index("gx")
+    blocks = [lax.dynamic_index_in_dim(owned, at ^ me, keepdims=False) for at in range(count)]
+    return jnp.concatenate(blocks, axis=1)
 
 
 def level(rows):

time: 135 us -> 135 us (level)
  waiting for transfers between devices: 51.6 us -> 47.3 us
  starting transfers between devices: 49 us -> 52.7 us
  Pallas kernels: 25.3 us -> 27.2 us
    ppermute x56, waiting for transfers between devices: 51.6 us -> 47.3 us  [swap(): return lax.ppermute(block, axis, [(i, i ^ bit) for i in range(count)])]
    ppermute x56, starting transfers between devices: 49 us -> 52.7 us  [swap(): return lax.ppermute(block, axis, [(i, i ^ bit) for i in range(count)])]
    pallas_call x1, Pallas kernels: 4.98 us -> 6.91 us  [attend_local(): pl.pallas_call(attend_kernel, in_specs=[pl.BlockSpec(memory_space=pltpu.S...]
  transfers between devices with their start and end apart: 56 -> 56, of which waited for: 28 -> 29; matrix products, arithmetic and copies ran while one was open for 1% -> 1% of each run, Pallas kernels for 8% -> 8%
where the time goes in v6:
time: 135 us
  starting transfers between devices  52.7 us (39%)
  waiting for transfers between devices  47.3 us (35%)
  Pallas kernels  27.2 us (20%)
  other arithmetic  6.07 us (4%)
    ppermute x56, starting transfers between devices, swap(): return lax.ppermute(block, axis, [(i, i ^ bit) for i in range(count)])  52.7 us
    ppermute x56, waiting for transfers between devices, swap(): return lax.ppermute(block, axis, [(i, i ^ bit) for i in range(count)])  47.3 us
    pallas_call x4, Pallas kernels, multiply(): pl.pallas_call(functools.partial(multiply_kernel, start), in_specs=[vmem,...  20.3 us
    pallas_call x1, Pallas kernels, attend_local(): pl.pallas_call(attend_kernel, in_specs=[pl.BlockSpec(memory_space=pltpu.S...  6.91 us
  transfers between devices with their start and end apart: 56, of which 29 were waited for; matrix products, arithmetic and copies ran while one was open for 1% of the time, Pallas kernels for 8%

profile of v6, /device:TPU:0, one launch (start us, length us, event | category | flops | bytes accessed | tf_op | source)
XLA Modules:
  0.0 135.0 jit_solution(14374154204681758971)
XLA Ops:
  0.0 1.2 fusion
  1.2 1.1 fusion.2
  2.3 3.1 %collective-permute-start.9 = (bf16[8,4096]{1,0:T(8,128)(2,1)S(1)}, bf16[8,4096]{1,0:T(8,128)(2,1)S(1)}, u32[]{:S(2)}, u32[]{:S(2)}) collective-permute-start(bf16[8,4096]{1,0:T(8,128)(2,1)S(1)} %get-tuple-element.47), channel_id=1, source_target_pairs={{0,1},{1,0},{2,3},{3,2},{4,5},{5,4},{6,7},{7,6},{8,9},{9,8},{10,11... | collective-permute-start | bytes 196616 | tf_op jit(solution)/shard_map/ppermute | solution.py:183
  5.4 2.6 %collective-permute-start = (bf16[8,4096]{1,0:T(8,128)(2,1)S(1)}, bf16[8,4096]{1,0:T(8,128)(2,1)S(1)}, u32[]{:S(2)}, u32[]{:S(2)}) collective-permute-start(bf16[8,4096]{1,0:T(8,128)(2,1)S(1)} %get-tuple-element.49), channel_id=1, source_target_pairs={{0,2},{1,3},{2,0},{3,1},{4,6},{5,7},{6,4},{7,5},{8,10},{9,11},{10,... | collective-permute-start | bytes 196616 | tf_op jit(solution)/shard_map/ppermute | solution.py:183
  9.0 1.8 %collective-permute-start.11 = (bf16[16,4096]{1,0:T(8,128)(2,1)S(1)}, bf16[16,4096]{1,0:T(8,128)(2,1)S(1)}, u32[]{:S(2)}, u32[]{:S(2)}) collective-permute-start(bf16[16,4096]{1,0:T(8,128)(2,1)S(1)} %pad_maximum_fusion.3), channel_id=1, source_target_pairs={{0,8},{4,12},{8,0},{12,4},{16,24},{20,28},{24,16},{28,20},{1,9},{5... | collective-permute-start | bytes 393224 | tf_op jit(solution)/shard_map/ppermute | solution.py:183
  10.7 1.5 %collective-permute-start.13 = (bf16[16,4096]{1,0:T(8,128)(2,1)S(1)}, bf16[16,4096]{1,0:T(8,128)(2,1)S(1)}, u32[]{:S(2)}, u32[]{:S(2)}) collective-permute-start(bf16[16,4096]{1,0:T(8,128)(2,1)S(1)} %pad_maximum_fusion.3), channel_id=1, source_target_pairs={{0,16},{4,20},{8,24},{12,28},{16,0},{20,4},{24,8},{28,12},{1,17},{... | collective-permute-start | bytes 393224 | tf_op jit(solution)/shard_map/ppermute | solution.py:183
  12.7 2.4 %collective-permute-start.15 = (bf16[16,4096]{1,0:T(8,128)(2,1)S(1)}, bf16[16,4096]{1,0:T(8,128)(2,1)S(1)}, u32[]{:S(2)}, u32[]{:S(2)}) collective-permute-start(bf16[16,4096]{1,0:T(8,128)(2,1)S(1)} %pad_maximum_fusion.3), channel_id=1, source_target_pairs={{0,24},{4,28},{8,16},{12,20},{16,8},{20,12},{24,0},{28,4},{1,25},{... | collective-permute-start | bytes 393224 | tf_op jit(solution)/shard_map/ppermute | solution.py:183
  15.9 1.5 %collective-permute-start.5 = (bf16[16,4096]{1,0:T(8,128)(2,1)S(1)}, bf16[16,4096]{1,0:T(8,128)(2,1)S(1)}, u32[]{:S(2)}, u32[]{:S(2)}) collective-permute-start(bf16[16,4096]{1,0:T(8,128)(2,1)S(1)} %constant_dynamic-update-slice_fusion), channel_id=1, source_target_pairs={{0,16},{4,20},{8,24},{12,28},{16,0},{20,4},{24,8},{28,12},{1,17},{... | collective-permute-start | bytes 393224 | tf_op jit(solution)/shard_map/ppermute | solution.py:183
  17.4 1.6 %collective-permute-start.7 = (bf16[16,4096]{1,0:T(8,128)(2,1)S(1)}, bf16[16,4096]{1,0:T(8,128)(2,1)S(1)}, u32[]{:S(2)}, u32[]{:S(2)}) collective-permute-start(bf16[16,4096]{1,0:T(8,128)(2,1)S(1)} %constant_dynamic-update-slice_fusion), channel_id=1, source_target_pairs={{0,24},{4,28},{8,16},{12,20},{16,8},{20,12},{24,0},{28,4},{1,25},{... | collective-permute-start | bytes 393224 | tf_op jit(solution)/shard_map/ppermute | solution.py:183
  19.0 2.7 %collective-permute-done.3 = bf16[16,4096]{1,0:T(8,128)(2,1)S(1)} collective-permute-done((bf16[16,4096]{1,0:T(8,128)(2,1)S(1)}, bf16[16,4096]{1,0:T(8,128)(2,1)S(1)}, u32[]{:S(2)}, u32[]{:S(2)}) %collective-permute-start.3) | collective-permute-done | bytes 131104 | tf_op jit(solution)/shard_map/ppermute | solution.py:183
  22.4 2.3 %collective-permute-done.5 = bf16[16,4096]{1,0:T(8,128)(2,1)S(1)} collective-permute-done((bf16[16,4096]{1,0:T(8,128)(2,1)S(1)}, bf16[16,4096]{1,0:T(8,128)(2,1)S(1)}, u32[]{:S(2)}, u32[]{:S(2)}) %collective-permute-start.5) | collective-permute-done | bytes 131104 | tf_op jit(solution)/shard_map/ppermute | solution.py:183
  26.6 4.9 %shard_map.73 = f32[256,1024]{1,0:T(8,128)S(1)} custom-call(bf16[128,4096]{1,0:T(8,128)(2,1)S(1)} %bitcast.269, bf16[128,4096]{1,0:T(8,128)(2,1)S(1)} %bitcast.271, bf16[4096,2304]{1,0:T(8,128)(2,1)} %weights.5), custom_call_target="tpu_custom_call" | custom-call | flops 2147483648 | bytes 8388608 | tf_op jit(solution)/shard_map/pallas_call | solution.py:224
  32.3 5.6 %shard_map.74 = f32[256,1280]{1,0:T(8,128)S(1)} custom-call(bf16[128,4096]{1,0:T(8,128)(2,1)S(1)} %bitcast.270, bf16[128,4096]{1,0:T(8,128)(2,1)S(1)} %bitcast.272, bf16[4096,2304]{1,0:T(8,128)(2,1)} %weights.5), custom_call_target="tpu_custom_call" | custom-call | flops 2684354560 | bytes 10485760 | tf_op jit(solution)/shard_map/pallas_call | solution.py:224
  38.0 1.4 %collective-permute-start.24 = (f16[8,8,1280]{2,1,0:T(8,128)(2,1)S(1)}, f16[8,8,1280]{2,1,0:T(8,128)(2,1)S(1)}, u32[]{:S(2)}, u32[]{:S(2)}) collective-permute-start(f16[8,8,1280]{2,1,0:T(8,128)(2,1)S(1)} %get-tuple-element.32), channel_id=1, source_target_pairs={{0,1},{1,0},{2,3},{3,2},{4,5},{5,4},{6,7},{7,6},{8,9},{9,8},{10,11... | collective-permute-start | bytes 491528 | tf_op jit(solution)/shard_map/ppermute | solution.py:183
  40.2 2.5 %collective-permute-start.18 = (f16[8,8,1024]{2,1,0:T(8,128)(2,1)S(1)}, f16[8,8,1024]{2,1,0:T(8,128)(2,1)S(1)}, u32[]{:S(2)}, u32[]{:S(2)}) collective-permute-start(f16[8,8,1024]{2,1,0:T(8,128)(2,1)S(1)} %fusion.41), channel_id=1, source_target_pairs={{0,2},{1,3},{2,0},{3,1},{4,6},{5,7},{6,4},{7,5},{8,10},{9,11},{10,... | collective-permute-start | bytes 393224 | tf_op jit(solution)/shard_map/ppermute | solution.py:183
  42.7 4.2 %collective-permute-done.24 = f16[8,8,1280]{2,1,0:T(8,128)(2,1)S(1)} collective-permute-done((f16[8,8,1280]{2,1,0:T(8,128)(2,1)S(1)}, f16[8,8,1280]{2,1,0:T(8,128)(2,1)S(1)}, u32[]{:S(2)}, u32[]{:S(2)}) %collective-permute-start.24) | collective-permute-done | bytes 163872 | tf_op jit(solution)/shard_map/ppermute | solution.py:183
  47.0 1.8 %collective-permute-start.25 = (f16[8,8,1280]{2,1,0:T(8,128)(2,1)S(1)}, f16[8,8,1280]{2,1,0:T(8,128)(2,1)S(1)}, u32[]{:S(2)}, u32[]{:S(2)}) collective-permute-start(f16[8,8,1280]{2,1,0:T(8,128)(2,1)S(1)} %fusion.14), channel_id=1, source_target_pairs={{0,2},{1,3},{2,0},{3,1},{4,6},{5,7},{6,4},{7,5},{8,10},{9,11},{10,... | collective-permute-start | bytes 491528 | tf_op jit(solution)/shard_map/ppermute | solution.py:183
  48.8 1.4 %collective-permute-start.19 = (bf16[2,8,1024]{2,1,0:T(8,128)(2,1)S(1)}, bf16[2,8,1024]{2,1,0:T(8,128)(2,1)S(1)}, u32[]{:S(2)}, u32[]{:S(2)}) collective-permute-start(bf16[2,8,1024]{2,1,0:T(8,128)(2,1)S(1)} %get-tuple-element.57), channel_id=1, source_target_pairs={{0,8},{4,12},{8,0},{12,4},{16,24},{20,28},{24,16},{28,20},{1,9},{5... | collective-permute-start | bytes 98312 | tf_op jit(solution)/shard_map/ppermute | solution.py:183
  51.1 1.3 collective-permute-start.21
  52.4 4.3 %collective-permute-done.25 = f16[8,8,1280]{2,1,0:T(8,128)(2,1)S(1)} collective-permute-done((f16[8,8,1280]{2,1,0:T(8,128)(2,1)S(1)}, f16[8,8,1280]{2,1,0:T(8,128)(2,1)S(1)}, u32[]{:S(2)}, u32[]{:S(2)}) %collective-permute-start.25) | collective-permute-done | bytes 163872 | tf_op jit(solution)/shard_map/ppermute | solution.py:183
  57.4 1.4 %collective-permute-start.26 = (bf16[2,8,1280]{2,1,0:T(8,128)(2,1)S(1)}, bf16[2,8,1280]{2,1,0:T(8,128)(2,1)S(1)}, u32[]{:S(2)}, u32[]{:S(2)}) collective-permute-start(bf16[2,8,1280]{2,1,0:T(8,128)(2,1)S(1)} %get-tuple-element.52), channel_id=1, source_target_pairs={{0,8},{4,12},{8,0},{12,4},{16,24},{20,28},{24,16},{28,20},{1,9},{5... | collective-permute-start | bytes 122888 | tf_op jit(solution)/shard_map/ppermute | solution.py:183
  59.7 1.3 collective-permute-start.28
  61.5 1.4 %collective-permute-done.27 = bf16[2,8,1280]{2,1,0:T(8,128)(2,1)S(1)} collective-permute-done((bf16[2,8,1280]{2,1,0:T(8,128)(2,1)S(1)}, bf16[2,8,1280]{2,1,0:T(8,128)(2,1)S(1)}, u32[]{:S(2)}, u32[]{:S(2)}) %collective-permute-start.27) | collective-permute-done | bytes 40992 | tf_op jit(solution)/shard_map/ppermute | solution.py:183
  62.9 1.7 %collective-permute-done.28 = bf16[2,8,1280]{2,1,0:T(8,128)(2,1)S(1)} collective-permute-done((bf16[2,8,1280]{2,1,0:T(8,128)(2,1)S(1)}, bf16[2,8,1280]{2,1,0:T(8,128)(2,1)S(1)}, u32[]{:S(2)}, u32[]{:S(2)}) %collective-permute-start.28) | collective-permute-done | bytes 40992 | tf_op jit(solution)/shard_map/ppermute | solution.py:183
  64.7 1.2 collective-permute-done.29
  66.9 6.9 %shard_map.75 = bf16[8,128,128]{2,1,0:T(8,128)(2,1)S(1)} custom-call(s32[8]{0:T(128)S(1)} %copy-done, bf16[8,128,128]{2,1,0:T(8,128)(2,1)S(1)} %pad_maximum_fusion.query, bf16[8,8,128]{2,1,0:T(8,128)(2,1)S(1)} %pad_maximum_fusion.8.key_new, f32[8,8,128]{2,1,0:T(8,128)S(1)} %get-tuple-element.84.value_new, bf16[8,512,1024]{2,1,0:T(8,128)(2,1)} %k_cache.1, ...), custom_call_target="tpu_custom_call" | custom-call | flops 2147483648 | bytes 8388608 | tf_op jit(solution)/shard_map/pallas_call | solution.py:153
  74.5 3.7 %collective-permute-start.30 = (bf16[8,4096]{1,0:T(8,128)(2,1)S(1)}, bf16[8,4096]{1,0:T(8,128)(2,1)S(1)}, u32[]{:S(2)}, u32[]{:S(2)}) collective-permute-start(bf16[8,4096]{1,0:T(8,128)(2,1)S(1)} %get-tuple-element.45), channel_id=1, source_target_pairs={{0,2},{1,3},{2,0},{3,1},{4,6},{5,7},{6,4},{7,5},{8,10},{9,11},{10,... | collective-permute-start | bytes 196616 | tf_op jit(solution)/shard_map/ppermute | solution.py:183
  79.0 2.4 %collective-permute-start.41 = (bf16[16,4096]{1,0:T(8,128)(2,1)S(1)}, bf16[16,4096]{1,0:T(8,128)(2,1)S(1)}, u32[]{:S(2)}, u32[]{:S(2)}) collective-permute-start(bf16[16,4096]{1,0:T(8,128)(2,1)S(1)} %pad_maximum_fusion.5), channel_id=1, source_target_pairs={{0,8},{4,12},{8,0},{12,4},{16,24},{20,28},{24,16},{28,20},{1,9},{5... | collective-permute-start | bytes 393224 | tf_op jit(solution)/shard_map/ppermute | solution.py:183
  81.8 1.1 collective-permute-start.45
  82.9 1.3 collective-permute-done.31
  85.5 1.0 collective-permute-start.35
  86.6 2.6 %collective-permute-start.37 = (bf16[16,4096]{1,0:T(8,128)(2,1)S(1)}, bf16[16,4096]{1,0:T(8,128)(2,1)S(1)}, u32[]{:S(2)}, u32[]{:S(2)}) collective-permute-start(bf16[16,4096]{1,0:T(8,128)(2,1)S(1)} %constant_dynamic-update-slice_fusion.10), channel_id=1, source_target_pairs={{0,24},{4,28},{8,16},{12,20},{16,8},{20,12},{24,0},{28,4},{1,25},{... | collective-permute-start | bytes 393224 | tf_op jit(solution)/shard_map/ppermute | solution.py:183
  89.2 2.7 %collective-permute-done.33 = bf16[16,4096]{1,0:T(8,128)(2,1)S(1)} collective-permute-done((bf16[16,4096]{1,0:T(8,128)(2,1)S(1)}, bf16[16,4096]{1,0:T(8,128)(2,1)S(1)}, u32[]{:S(2)}, u32[]{:S(2)}) %collective-permute-start.33) | collective-permute-done | bytes 131104 | tf_op jit(solution)/shard_map/ppermute | solution.py:183
  92.5 2.8 %collective-permute-done.35 = bf16[16,4096]{1,0:T(8,128)(2,1)S(1)} collective-permute-done((bf16[16,4096]{1,0:T(8,128)(2,1)S(1)}, bf16[16,4096]{1,0:T(8,128)(2,1)S(1)}, u32[]{:S(2)}, u32[]{:S(2)}) %collective-permute-start.35) | collective-permute-done | bytes 131104 | tf_op jit(solution)/shard_map/ppermute | solution.py:183
  97.2 4.9 %shard_map.76 = f32[256,1024]{1,0:T(8,128)S(1)} custom-call(bf16[128,4096]{1,0:T(8,128)(2,1)S(1)} %bitcast.265, bf16[128,4096]{1,0:T(8,128)(2,1)S(1)} %bitcast.267, bf16[4096,2048]{1,0:T(8,128)(2,1)} %weights.7), custom_call_target="tpu_custom_call" | custom-call | flops 2147483648 | bytes 8388608 | tf_op jit(solution)/shard_map/pallas_call | solution.py:224
  102.3 4.9 %shard_map.77 = f32[256,1024]{1,0:T(8,128)S(1)} custom-call(bf16[128,4096]{1,0:T(8,128)(2,1)S(1)} %bitcast.266, bf16[128,4096]{1,0:T(8,128)(2,1)S(1)} %bitcast.268, bf16[4096,2048]{1,0:T(8,128)(2,1)} %weights.7), custom_call_target="tpu_custom_call" | custom-call | flops 2147483648 | bytes 8388608 | tf_op jit(solution)/shard_map/pallas_call | solution.py:224
  107.2 2.1 %collective-permute-start.50 = (f16[8,8,1024]{2,1,0:T(8,128)(2,1)S(1)}, f16[8,8,1024]{2,1,0:T(8,128)(2,1)S(1)}, u32[]{:S(2)}, u32[]{:S(2)}) collective-permute-start(f16[8,8,1024]{2,1,0:T(8,128)(2,1)S(1)} %get-tuple-element.34), channel_id=1, source_target_pairs={{0,1},{1,0},{2,3},{3,2},{4,5},{5,4},{6,7},{7,6},{8,9},{9,8},{10,11... | collective-permute-start | bytes 393224 | tf_op jit(solution)/shard_map/ppermute | solution.py:183
  109.3 1.8 %collective-permute-done.47 = f16[2,8,8,1024]{3,2,1,0:T(8,128)(2,1)S(1)} collective-permute-done((f16[2,8,8,1024]{3,2,1,0:T(8,128)(2,1)S(1)}, f16[2,8,8,1024]{3,2,1,0:T(8,128)(2,1)S(1)}, u32[]{:S(2)}, u32[]{:S(2)}) %collective-permute-start.47) | collective-permute-done | bytes 262176 | tf_op jit(solution)/shard_map/ppermute | solution.py:183
  111.7 1.8 %collective-permute-done.50 = f16[8,8,1024]{2,1,0:T(8,128)(2,1)S(1)} collective-permute-done((f16[8,8,1024]{2,1,0:T(8,128)(2,1)S(1)}, f16[8,8,1024]{2,1,0:T(8,128)(2,1)S(1)}, u32[]{:S(2)}, u32[]{:S(2)}) %collective-permute-start.50) | collective-permute-done | bytes 131104 | tf_op jit(solution)/shard_map/ppermute | solution.py:183
  113.5 2.7 %collective-permute-start.51 = (f16[8,8,1024]{2,1,0:T(8,128)(2,1)S(1)}, f16[8,8,1024]{2,1,0:T(8,128)(2,1)S(1)}, u32[]{:S(2)}, u32[]{:S(2)}) collective-permute-start(f16[8,8,1024]{2,1,0:T(8,128)(2,1)S(1)} %fusion.28), channel_id=1, source_target_pairs={{0,2},{1,3},{2,0},{3,1},{4,6},{5,7},{6,4},{7,5},{8,10},{9,11},{10,... | collective-permute-start | bytes 393224 | tf_op jit(solution)/shard_map/ppermute | solution.py:183
  116.2 7.0 %collective-permute-done.48 = f16[8,8,1024]{2,1,0:T(8,128)(2,1)S(1)} collective-permute-done((f16[8,8,1024]{2,1,0:T(8,128)(2,1)S(1)}, f16[8,8,1024]{2,1,0:T(8,128)(2,1)S(1)}, u32[]{:S(2)}, u32[]{:S(2)}) %collective-permute-start.48) | collective-permute-done | bytes 131104 | tf_op jit(solution)/shard_map/ppermute | solution.py:183
  123.2 1.8 %collective-permute-done.51 = f16[8,8,1024]{2,1,0:T(8,128)(2,1)S(1)} collective-permute-done((f16[8,8,1024]{2,1,0:T(8,128)(2,1)S(1)}, f16[8,8,1024]{2,1,0:T(8,128)(2,1)S(1)}, u32[]{:S(2)}, u32[]{:S(2)}) %collective-permute-start.51) | collective-permute-done | bytes 131104 | tf_op jit(solution)/shard_map/ppermute | solution.py:183
  125.2 1.7 %collective-permute-start.52 = (bf16[2,8,2048]{2,1,0:T(8,128)(2,1)S(1)}, bf16[2,8,2048]{2,1,0:T(8,128)(2,1)S(1)}, u32[]{:S(2)}, u32[]{:S(2)}) collective-permute-start(bf16[2,8,2048]{2,1,0:T(8,128)(2,1)S(1)} %get-tuple-element.39), channel_id=1, source_target_pairs={{0,8},{4,12},{8,0},{12,4},{16,24},{20,28},{24,16},{28,20},{1,9},{5... | collective-permute-start | bytes 196616 | tf_op jit(solution)/shard_map/ppermute | solution.py:183
  127.4 1.4 %collective-permute-start.54 = (bf16[2,8,2048]{2,1,0:T(8,128)(2,1)S(1)}, bf16[2,8,2048]{2,1,0:T(8,128)(2,1)S(1)}, u32[]{:S(2)}, u32[]{:S(2)}) collective-permute-start(bf16[2,8,2048]{2,1,0:T(8,128)(2,1)S(1)} %get-tuple-element.41), channel_id=1, source_target_pairs={{0,24},{4,28},{8,16},{12,20},{16,8},{20,12},{24,0},{28,4},{1,25},{... | collective-permute-start | bytes 196616 | tf_op jit(solution)/shard_map/ppermute | solution.py:183
  128.7 1.4 %collective-permute-done.52 = bf16[2,8,2048]{2,1,0:T(8,128)(2,1)S(1)} collective-permute-done((bf16[2,8,2048]{2,1,0:T(8,128)(2,1)S(1)}, bf16[2,8,2048]{2,1,0:T(8,128)(2,1)S(1)}, u32[]{:S(2)}, u32[]{:S(2)}) %collective-permute-start.52) | collective-permute-done | bytes 65568 | tf_op jit(solution)/shard_map/ppermute | solution.py:183
  130.1 1.0 collective-permute-done.53
  131.1 1.4 %collective-permute-done.54 = bf16[2,8,2048]{2,1,0:T(8,128)(2,1)S(1)} collective-permute-done((bf16[2,8,2048]{2,1,0:T(8,128)(2,1)S(1)}, bf16[2,8,2048]{2,1,0:T(8,128)(2,1)S(1)}, u32[]{:S(2)}, u32[]{:S(2)}) %collective-permute-start.54) | collective-permute-done | bytes 65568 | tf_op jit(solution)/shard_map/ppermute | solution.py:183
  132.7 1.3 collective-permute-done.55
  (184 shorter events, 18.2 us)
Async XLA Ops:
  2.3 6.5 %collective-permute-start.9 = (bf16[8,4096]{1,0:T(8,128)(2,1)S(1)}, bf16[8,4096]{1,0:T(8,128)(2,1)S(1)}, u32[]{:S(2)}, u32[]{:S(2)}) collective-permute-start(bf16[8,4096]{1,0:T(8,128)(2,1)S(1)} %get-tuple-element.47), channel_id=1, source_target_pairs={{0,1},{1,0},{2,3},{3,2},{4,5},{5,4},{6,7},{7,6},{8,9},{9,8},{10,11... | collective-permute-start | bytes 196616 | tf_op jit(solution)/shard_map/ppermute | solution.py:183
  5.4 7.3 %collective-permute-start = (bf16[8,4096]{1,0:T(8,128)(2,1)S(1)}, bf16[8,4096]{1,0:T(8,128)(2,1)S(1)}, u32[]{:S(2)}, u32[]{:S(2)}) collective-permute-start(bf16[8,4096]{1,0:T(8,128)(2,1)S(1)} %get-tuple-element.49), channel_id=1, source_target_pairs={{0,2},{1,3},{2,0},{3,1},{4,6},{5,7},{6,4},{7,5},{8,10},{9,11},{10,... | collective-permute-start | bytes 196616 | tf_op jit(solution)/shard_map/ppermute | solution.py:183
  8.0 7.1 %collective-permute-start.1 = (bf16[8,4096]{1,0:T(8,128)(2,1)S(1)}, bf16[8,4096]{1,0:T(8,128)(2,1)S(1)}, u32[]{:S(2)}, u32[]{:S(2)}) collective-permute-start(bf16[8,4096]{1,0:T(8,128)(2,1)S(1)} %get-tuple-element.48), channel_id=1, source_target_pairs={{0,3},{1,2},{2,1},{3,0},{4,7},{5,6},{6,5},{7,4},{8,11},{9,10},{10,... | collective-permute-start | bytes 196616 | tf_op jit(solution)/shard_map/ppermute | solution.py:183
  8.9 6.4 %collective-permute-start.10 = (bf16[16,4096]{1,0:T(8,128)(2,1)S(1)}, bf16[16,4096]{1,0:T(8,128)(2,1)S(1)}, u32[]{:S(2)}, u32[]{:S(2)}) collective-permute-start(bf16[16,4096]{1,0:T(8,128)(2,1)S(1)} %pad_maximum_fusion.3), channel_id=1, source_target_pairs={{0,4},{4,0},{8,12},{12,8},{16,20},{20,16},{24,28},{28,24},{1,5},{5... | collective-permute-start | bytes 393224 | tf_op jit(solution)/shard_map/ppermute | solution.py:183
  9.0 7.0 %collective-permute-start.11 = (bf16[16,4096]{1,0:T(8,128)(2,1)S(1)}, bf16[16,4096]{1,0:T(8,128)(2,1)S(1)}, u32[]{:S(2)}, u32[]{:S(2)}) collective-permute-start(bf16[16,4096]{1,0:T(8,128)(2,1)S(1)} %pad_maximum_fusion.3), channel_id=1, source_target_pairs={{0,8},{4,12},{8,0},{12,4},{16,24},{20,28},{24,16},{28,20},{1,9},{5... | collective-permute-start | bytes 393224 | tf_op jit(solution)/shard_map/ppermute | solution.py:183
  10.7 11.0 %collective-permute-start.13 = (bf16[16,4096]{1,0:T(8,128)(2,1)S(1)}, bf16[16,4096]{1,0:T(8,128)(2,1)S(1)}, u32[]{:S(2)}, u32[]{:S(2)}) collective-permute-start(bf16[16,4096]{1,0:T(8,128)(2,1)S(1)} %pad_maximum_fusion.3), channel_id=1, source_target_pairs={{0,16},{4,20},{8,24},{12,28},{16,0},{20,4},{24,8},{28,12},{1,17},{... | collective-permute-start | bytes 393224 | tf_op jit(solution)/shard_map/ppermute | solution.py:183
  12.7 9.6 %collective-permute-start.15 = (bf16[16,4096]{1,0:T(8,128)(2,1)S(1)}, bf16[16,4096]{1,0:T(8,128)(2,1)S(1)}, u32[]{:S(2)}, u32[]{:S(2)}) collective-permute-start(bf16[16,4096]{1,0:T(8,128)(2,1)S(1)} %pad_maximum_fusion.3), channel_id=1, source_target_pairs={{0,24},{4,28},{8,16},{12,20},{16,8},{20,12},{24,0},{28,4},{1,25},{... | collective-permute-start | bytes 393224 | tf_op jit(solution)/shard_map/ppermute | solution.py:183
  15.2 2.2 %collective-permute-start.2 = (bf16[16,4096]{1,0:T(8,128)(2,1)S(1)}, bf16[16,4096]{1,0:T(8,128)(2,1)S(1)}, u32[]{:S(2)}, u32[]{:S(2)}) collective-permute-start(bf16[16,4096]{1,0:T(8,128)(2,1)S(1)} %constant_dynamic-update-slice_fusion), channel_id=1, source_target_pairs={{0,4},{4,0},{8,12},{12,8},{16,20},{20,16},{24,28},{28,24},{1,5},{5... | collective-permute-start | bytes 393224 | tf_op jit(solution)/shard_map/ppermute | solution.py:183
  15.3 6.4 %collective-permute-start.3 = (bf16[16,4096]{1,0:T(8,128)(2,1)S(1)}, bf16[16,4096]{1,0:T(8,128)(2,1)S(1)}, u32[]{:S(2)}, u32[]{:S(2)}) collective-permute-start(bf16[16,4096]{1,0:T(8,128)(2,1)S(1)} %constant_dynamic-update-slice_fusion), channel_id=1, source_target_pairs={{0,8},{4,12},{8,0},{12,4},{16,24},{20,28},{24,16},{28,20},{1,9},{5... | collective-permute-start | bytes 393224 | tf_op jit(solution)/shard_map/ppermute | solution.py:183
  15.9 8.8 %collective-permute-start.5 = (bf16[16,4096]{1,0:T(8,128)(2,1)S(1)}, bf16[16,4096]{1,0:T(8,128)(2,1)S(1)}, u32[]{:S(2)}, u32[]{:S(2)}) collective-permute-start(bf16[16,4096]{1,0:T(8,128)(2,1)S(1)} %constant_dynamic-update-slice_fusion), channel_id=1, source_target_pairs={{0,16},{4,20},{8,24},{12,28},{16,0},{20,4},{24,8},{28,12},{1,17},{... | collective-permute-start | bytes 393224 | tf_op jit(solution)/shard_map/ppermute | solution.py:183
  17.4 7.3 %collective-permute-start.7 = (bf16[16,4096]{1,0:T(8,128)(2,1)S(1)}, bf16[16,4096]{1,0:T(8,128)(2,1)S(1)}, u32[]{:S(2)}, u32[]{:S(2)}) collective-permute-start(bf16[16,4096]{1,0:T(8,128)(2,1)S(1)} %constant_dynamic-update-slice_fusion), channel_id=1, source_target_pairs={{0,24},{4,28},{8,16},{12,20},{16,8},{20,12},{24,0},{28,4},{1,25},{... | collective-permute-start | bytes 393224 | tf_op jit(solution)/shard_map/ppermute | solution.py:183
  21.7 3.5 %collective-permute-start.12 = (bf16[16,4096]{1,0:T(8,128)(2,1)S(1)}, bf16[16,4096]{1,0:T(8,128)(2,1)S(1)}, u32[]{:S(2)}, u32[]{:S(2)}) collective-permute-start(bf16[16,4096]{1,0:T(8,128)(2,1)S(1)} %collective-permute-done.11), channel_id=1, source_target_pairs={{0,4},{4,0},{8,12},{12,8},{16,20},{20,16},{24,28},{28,24},{1,5},{5... | collective-permute-start | bytes 393224 | tf_op jit(solution)/shard_map/ppermute | solution.py:183
  21.8 3.6 %collective-permute-start.4 = (bf16[16,4096]{1,0:T(8,128)(2,1)S(1)}, bf16[16,4096]{1,0:T(8,128)(2,1)S(1)}, u32[]{:S(2)}, u32[]{:S(2)}) collective-permute-start(bf16[16,4096]{1,0:T(8,128)(2,1)S(1)} %collective-permute-done.3), channel_id=1, source_target_pairs={{0,4},{4,0},{8,12},{12,8},{16,20},{20,16},{24,28},{28,24},{1,5},{5... | collective-permute-start | bytes 393224 | tf_op jit(solution)/shard_map/ppermute | solution.py:183
  22.3 3.0 %collective-permute-start.14 = (bf16[16,4096]{1,0:T(8,128)(2,1)S(1)}, bf16[16,4096]{1,0:T(8,128)(2,1)S(1)}, u32[]{:S(2)}, u32[]{:S(2)}) collective-permute-start(bf16[16,4096]{1,0:T(8,128)(2,1)S(1)} %collective-permute-done.13), channel_id=1, source_target_pairs={{0,4},{4,0},{8,12},{12,8},{16,20},{20,16},{24,28},{28,24},{1,5},{5... | collective-permute-start | bytes 393224 | tf_op jit(solution)/shard_map/ppermute | solution.py:183
  31.6 8.5 %collective-permute-start.17 = (f16[2,8,8,1024]{3,2,1,0:T(8,128)(2,1)S(1)}, f16[2,8,8,1024]{3,2,1,0:T(8,128)(2,1)S(1)}, u32[]{:S(2)}, u32[]{:S(2)}) collective-permute-start(f16[2,8,8,1024]{3,2,1,0:T(8,128)(2,1)S(1)} %fusion.19), channel_id=1, source_target_pairs={{0,1},{1,0},{2,3},{3,2},{4,5},{5,4},{6,7},{7,6},{8,9},{9,8},{10,11... | collective-permute-start | bytes 786440 | tf_op jit(solution)/shard_map/ppermute | solution.py:183
  38.0 8.9 %collective-permute-start.24 = (f16[8,8,1280]{2,1,0:T(8,128)(2,1)S(1)}, f16[8,8,1280]{2,1,0:T(8,128)(2,1)S(1)}, u32[]{:S(2)}, u32[]{:S(2)}) collective-permute-start(f16[8,8,1280]{2,1,0:T(8,128)(2,1)S(1)} %get-tuple-element.32), channel_id=1, source_target_pairs={{0,1},{1,0},{2,3},{3,2},{4,5},{5,4},{6,7},{7,6},{8,9},{9,8},{10,11... | collective-permute-start | bytes 491528 | tf_op jit(solution)/shard_map/ppermute | solution.py:183
  40.2 8.6 %collective-permute-start.18 = (f16[8,8,1024]{2,1,0:T(8,128)(2,1)S(1)}, f16[8,8,1024]{2,1,0:T(8,128)(2,1)S(1)}, u32[]{:S(2)}, u32[]{:S(2)}) collective-permute-start(f16[8,8,1024]{2,1,0:T(8,128)(2,1)S(1)} %fusion.41), channel_id=1, source_target_pairs={{0,2},{1,3},{2,0},{3,1},{4,6},{5,7},{6,4},{7,5},{8,10},{9,11},{10,... | collective-permute-start | bytes 393224 | tf_op jit(solution)/shard_map/ppermute | solution.py:183
  47.0 9.7 %collective-permute-start.25 = (f16[8,8,1280]{2,1,0:T(8,128)(2,1)S(1)}, f16[8,8,1280]{2,1,0:T(8,128)(2,1)S(1)}, u32[]{:S(2)}, u32[]{:S(2)}) collective-permute-start(f16[8,8,1280]{2,1,0:T(8,128)(2,1)S(1)} %fusion.14), channel_id=1, source_target_pairs={{0,2},{1,3},{2,0},{3,1},{4,6},{5,7},{6,4},{7,5},{8,10},{9,11},{10,... | collective-permute-start | bytes 491528 | tf_op jit(solution)/shard_map/ppermute | solution.py:183
  48.8 8.5 %collective-permute-start.23 = (f16[8,8,1280]{2,1,0:T(8,128)(2,1)S(1)}, f16[8,8,1280]{2,1,0:T(8,128)(2,1)S(1)}, u32[]{:S(2)}, u32[]{:S(2)}) collective-permute-start(f16[8,8,1280]{2,1,0:T(8,128)(2,1)S(1)} %get-tuple-element.19), channel_id=1, source_target_pairs={{0,1},{1,0},{2,3},{3,2},{4,5},{5,4},{6,7},{7,6},{8,9},{9,8},{10,11... | collective-permute-start | bytes 491528 | tf_op jit(solution)/shard_map/ppermute | solution.py:183
  48.8 10.8 %collective-permute-start.19 = (bf16[2,8,1024]{2,1,0:T(8,128)(2,1)S(1)}, bf16[2,8,1024]{2,1,0:T(8,128)(2,1)S(1)}, u32[]{:S(2)}, u32[]{:S(2)}) collective-permute-start(bf16[2,8,1024]{2,1,0:T(8,128)(2,1)S(1)} %get-tuple-element.57), channel_id=1, source_target_pairs={{0,8},{4,12},{8,0},{12,4},{16,24},{20,28},{24,16},{28,20},{1,9},{5... | collective-permute-start | bytes 98312 | tf_op jit(solution)/shard_map/ppermute | solution.py:183
  50.3 10.7 %collective-permute-start.20 = (bf16[2,8,1024]{2,1,0:T(8,128)(2,1)S(1)}, bf16[2,8,1024]{2,1,0:T(8,128)(2,1)S(1)}, u32[]{:S(2)}, u32[]{:S(2)}) collective-permute-start(bf16[2,8,1024]{2,1,0:T(8,128)(2,1)S(1)} %get-tuple-element.59), channel_id=1, source_target_pairs={{0,16},{4,20},{8,24},{12,28},{16,0},{20,4},{24,8},{28,12},{1,17},{... | collective-permute-start | bytes 98312 | tf_op jit(solution)/shard_map/ppermute | solution.py:183
  51.1 9.9 %collective-permute-start.21 = (bf16[2,8,1024]{2,1,0:T(8,128)(2,1)S(1)}, bf16[2,8,1024]{2,1,0:T(8,128)(2,1)S(1)}, u32[]{:S(2)}, u32[]{:S(2)}) collective-permute-start(bf16[2,8,1024]{2,1,0:T(8,128)(2,1)S(1)} %get-tuple-element.58), channel_id=1, source_target_pairs={{0,24},{4,28},{8,16},{12,20},{16,8},{20,12},{24,0},{28,4},{1,25},{... | collective-permute-start | bytes 98312 | tf_op jit(solution)/shard_map/ppermute | solution.py:183
  57.4 4.1 %collective-permute-start.26 = (bf16[2,8,1280]{2,1,0:T(8,128)(2,1)S(1)}, bf16[2,8,1280]{2,1,0:T(8,128)(2,1)S(1)}, u32[]{:S(2)}, u32[]{:S(2)}) collective-permute-start(bf16[2,8,1280]{2,1,0:T(8,128)(2,1)S(1)} %get-tuple-element.52), channel_id=1, source_target_pairs={{0,8},{4,12},{8,0},{12,4},{16,24},{20,28},{24,16},{28,20},{1,9},{5... | collective-permute-start | bytes 122888 | tf_op jit(solution)/shard_map/ppermute | solution.py:183
  58.8 4.1 %collective-permute-start.27 = (bf16[2,8,1280]{2,1,0:T(8,128)(2,1)S(1)}, bf16[2,8,1280]{2,1,0:T(8,128)(2,1)S(1)}, u32[]{:S(2)}, u32[]{:S(2)}) collective-permute-start(bf16[2,8,1280]{2,1,0:T(8,128)(2,1)S(1)} %get-tuple-element.54), channel_id=1, source_target_pairs={{0,16},{4,20},{8,24},{12,28},{16,0},{20,4},{24,8},{28,12},{1,17},{... | collective-permute-start | bytes 122888 | tf_op jit(solution)/shard_map/ppermute | solution.py:183
  59.7 4.9 %collective-permute-start.28 = (bf16[2,8,1280]{2,1,0:T(8,128)(2,1)S(1)}, bf16[2,8,1280]{2,1,0:T(8,128)(2,1)S(1)}, u32[]{:S(2)}, u32[]{:S(2)}) collective-permute-start(bf16[2,8,1280]{2,1,0:T(8,128)(2,1)S(1)} %get-tuple-element.53), channel_id=1, source_target_pairs={{0,24},{4,28},{8,16},{12,20},{16,8},{20,12},{24,0},{28,4},{1,25},{... | collective-permute-start | bytes 122888 | tf_op jit(solution)/shard_map/ppermute | solution.py:183
  61.0 3.7 %collective-permute-start.22 = (bf16[4,8,1024]{2,1,0:T(8,128)(2,1)S(1)}, bf16[4,8,1024]{2,1,0:T(8,128)(2,1)S(1)}, u32[]{:S(2)}, u32[]{:S(2)}) collective-permute-start(bf16[4,8,1024]{2,1,0:T(8,128)(2,1)S(1)} %pad_maximum_fusion.7), channel_id=1, source_target_pairs={{0,4},{4,0},{8,12},{12,8},{16,20},{20,16},{24,28},{28,24},{1,5},{5... | collective-permute-start | bytes 196616 | tf_op jit(solution)/shard_map/ppermute | solution.py:183
  74.4 4.5 %collective-permute-start.39 = (bf16[8,4096]{1,0:T(8,128)(2,1)S(1)}, bf16[8,4096]{1,0:T(8,128)(2,1)S(1)}, u32[]{:S(2)}, u32[]{:S(2)}) collective-permute-start(bf16[8,4096]{1,0:T(8,128)(2,1)S(1)} %get-tuple-element.43), channel_id=1, source_target_pairs={{0,1},{1,0},{2,3},{3,2},{4,5},{5,4},{6,7},{7,6},{8,9},{9,8},{10,11... | collective-permute-start | bytes 196616 | tf_op jit(solution)/shard_map/ppermute | solution.py:183
  74.5 7.3 %collective-permute-start.30 = (bf16[8,4096]{1,0:T(8,128)(2,1)S(1)}, bf16[8,4096]{1,0:T(8,128)(2,1)S(1)}, u32[]{:S(2)}, u32[]{:S(2)}) collective-permute-start(bf16[8,4096]{1,0:T(8,128)(2,1)S(1)} %get-tuple-element.45), channel_id=1, source_target_pairs={{0,2},{1,3},{2,0},{3,1},{4,6},{5,7},{6,4},{7,5},{8,10},{9,11},{10,... | collective-permute-start | bytes 196616 | tf_op jit(solution)/shard_map/ppermute | solution.py:183
  78.2 6.1 %collective-permute-start.31 = (bf16[8,4096]{1,0:T(8,128)(2,1)S(1)}, bf16[8,4096]{1,0:T(8,128)(2,1)S(1)}, u32[]{:S(2)}, u32[]{:S(2)}) collective-permute-start(bf16[8,4096]{1,0:T(8,128)(2,1)S(1)} %get-tuple-element.44), channel_id=1, source_target_pairs={{0,3},{1,2},{2,1},{3,0},{4,7},{5,6},{6,5},{7,4},{8,11},{9,10},{10,... | collective-permute-start | bytes 196616 | tf_op jit(solution)/shard_map/ppermute | solution.py:183
  78.9 5.4 %collective-permute-start.40 = (bf16[16,4096]{1,0:T(8,128)(2,1)S(1)}, bf16[16,4096]{1,0:T(8,128)(2,1)S(1)}, u32[]{:S(2)}, u32[]{:S(2)}) collective-permute-start(bf16[16,4096]{1,0:T(8,128)(2,1)S(1)} %pad_maximum_fusion.5), channel_id=1, source_target_pairs={{0,4},{4,0},{8,12},{12,8},{16,20},{20,16},{24,28},{28,24},{1,5},{5... | collective-permute-start | bytes 393224 | tf_op jit(solution)/shard_map/ppermute | solution.py:183
  79.0 6.5 %collective-permute-start.41 = (bf16[16,4096]{1,0:T(8,128)(2,1)S(1)}, bf16[16,4096]{1,0:T(8,128)(2,1)S(1)}, u32[]{:S(2)}, u32[]{:S(2)}) collective-permute-start(bf16[16,4096]{1,0:T(8,128)(2,1)S(1)} %pad_maximum_fusion.5), channel_id=1, source_target_pairs={{0,8},{4,12},{8,0},{12,4},{16,24},{20,28},{24,16},{28,20},{1,9},{5... | collective-permute-start | bytes 393224 | tf_op jit(solution)/shard_map/ppermute | solution.py:183
  81.3 10.5 %collective-permute-start.43 = (bf16[16,4096]{1,0:T(8,128)(2,1)S(1)}, bf16[16,4096]{1,0:T(8,128)(2,1)S(1)}, u32[]{:S(2)}, u32[]{:S(2)}) collective-permute-start(bf16[16,4096]{1,0:T(8,128)(2,1)S(1)} %pad_maximum_fusion.5), channel_id=1, source_target_pairs={{0,16},{4,20},{8,24},{12,28},{16,0},{20,4},{24,8},{28,12},{1,17},{... | collective-permute-start | bytes 393224 | tf_op jit(solution)/shard_map/ppermute | solution.py:183
  81.8 10.6 %collective-permute-start.45 = (bf16[16,4096]{1,0:T(8,128)(2,1)S(1)}, bf16[16,4096]{1,0:T(8,128)(2,1)S(1)}, u32[]{:S(2)}, u32[]{:S(2)}) collective-permute-start(bf16[16,4096]{1,0:T(8,128)(2,1)S(1)} %pad_maximum_fusion.5), channel_id=1, source_target_pairs={{0,24},{4,28},{8,16},{12,20},{16,8},{20,12},{24,0},{28,4},{1,25},{... | collective-permute-start | bytes 393224 | tf_op jit(solution)/shard_map/ppermute | solution.py:183
  84.2 2.3 %collective-permute-start.32 = (bf16[16,4096]{1,0:T(8,128)(2,1)S(1)}, bf16[16,4096]{1,0:T(8,128)(2,1)S(1)}, u32[]{:S(2)}, u32[]{:S(2)}) collective-permute-start(bf16[16,4096]{1,0:T(8,128)(2,1)S(1)} %constant_dynamic-update-slice_fusion.10), channel_id=1, source_target_pairs={{0,4},{4,0},{8,12},{12,8},{16,20},{20,16},{24,28},{28,24},{1,5},{5... | collective-permute-start | bytes 393224 | tf_op jit(solution)/shard_map/ppermute | solution.py:183
  84.3 7.5 %collective-permute-start.33 = (bf16[16,4096]{1,0:T(8,128)(2,1)S(1)}, bf16[16,4096]{1,0:T(8,128)(2,1)S(1)}, u32[]{:S(2)}, u32[]{:S(2)}) collective-permute-start(bf16[16,4096]{1,0:T(8,128)(2,1)S(1)} %constant_dynamic-update-slice_fusion.10), channel_id=1, source_target_pairs={{0,8},{4,12},{8,0},{12,4},{16,24},{20,28},{24,16},{28,20},{1,9},{5... | collective-permute-start | bytes 393224 | tf_op jit(solution)/shard_map/ppermute | solution.py:183
  85.5 9.8 %collective-permute-start.35 = (bf16[16,4096]{1,0:T(8,128)(2,1)S(1)}, bf16[16,4096]{1,0:T(8,128)(2,1)S(1)}, u32[]{:S(2)}, u32[]{:S(2)}) collective-permute-start(bf16[16,4096]{1,0:T(8,128)(2,1)S(1)} %constant_dynamic-update-slice_fusion.10), channel_id=1, source_target_pairs={{0,16},{4,20},{8,24},{12,28},{16,0},{20,4},{24,8},{28,12},{1,17},{... | collective-permute-start | bytes 393224 | tf_op jit(solution)/shard_map/ppermute | solution.py:183
  86.6 8.8 %collective-permute-start.37 = (bf16[16,4096]{1,0:T(8,128)(2,1)S(1)}, bf16[16,4096]{1,0:T(8,128)(2,1)S(1)}, u32[]{:S(2)}, u32[]{:S(2)}) collective-permute-start(bf16[16,4096]{1,0:T(8,128)(2,1)S(1)} %constant_dynamic-update-slice_fusion.10), channel_id=1, source_target_pairs={{0,24},{4,28},{8,16},{12,20},{16,8},{20,12},{24,0},{28,4},{1,25},{... | collective-permute-start | bytes 393224 | tf_op jit(solution)/shard_map/ppermute | solution.py:183
  91.8 4.0 %collective-permute-start.42 = (bf16[16,4096]{1,0:T(8,128)(2,1)S(1)}, bf16[16,4096]{1,0:T(8,128)(2,1)S(1)}, u32[]{:S(2)}, u32[]{:S(2)}) collective-permute-start(bf16[16,4096]{1,0:T(8,128)(2,1)S(1)} %collective-permute-done.41), channel_id=1, source_target_pairs={{0,4},{4,0},{8,12},{12,8},{16,20},{20,16},{24,28},{28,24},{1,5},{5... | collective-permute-start | bytes 393224 | tf_op jit(solution)/shard_map/ppermute | solution.py:183
  91.9 4.1 %collective-permute-start.34 = (bf16[16,4096]{1,0:T(8,128)(2,1)S(1)}, bf16[16,4096]{1,0:T(8,128)(2,1)S(1)}, u32[]{:S(2)}, u32[]{:S(2)}) collective-permute-start(bf16[16,4096]{1,0:T(8,128)(2,1)S(1)} %collective-permute-done.33), channel_id=1, source_target_pairs={{0,4},{4,0},{8,12},{12,8},{16,20},{20,16},{24,28},{28,24},{1,5},{5... | collective-permute-start | bytes 393224 | tf_op jit(solution)/shard_map/ppermute | solution.py:183
  92.4 3.5 %collective-permute-start.44 = (bf16[16,4096]{1,0:T(8,128)(2,1)S(1)}, bf16[16,4096]{1,0:T(8,128)(2,1)S(1)}, u32[]{:S(2)}, u32[]{:S(2)}) collective-permute-start(bf16[16,4096]{1,0:T(8,128)(2,1)S(1)} %collective-permute-done.43), channel_id=1, source_target_pairs={{0,4},{4,0},{8,12},{12,8},{16,20},{20,16},{24,28},{28,24},{1,5},{5... | collective-permute-start | bytes 393224 | tf_op jit(solution)/shard_map/ppermute | solution.py:183
  102.2 8.9 %collective-permute-start.47 = (f16[2,8,8,1024]{3,2,1,0:T(8,128)(2,1)S(1)}, f16[2,8,8,1024]{3,2,1,0:T(8,128)(2,1)S(1)}, u32[]{:S(2)}, u32[]{:S(2)}) collective-permute-start(f16[2,8,8,1024]{3,2,1,0:T(8,128)(2,1)S(1)} %fusion.20), channel_id=1, source_target_pairs={{0,1},{1,0},{2,3},{3,2},{4,5},{5,4},{6,7},{7,6},{8,9},{9,8},{10,11... | collective-permute-start | bytes 786440 | tf_op jit(solution)/shard_map/ppermute | solution.py:183
  107.2 6.2 %collective-permute-start.50 = (f16[8,8,1024]{2,1,0:T(8,128)(2,1)S(1)}, f16[8,8,1024]{2,1,0:T(8,128)(2,1)S(1)}, u32[]{:S(2)}, u32[]{:S(2)}) collective-permute-start(f16[8,8,1024]{2,1,0:T(8,128)(2,1)S(1)} %get-tuple-element.34), channel_id=1, source_target_pairs={{0,1},{1,0},{2,3},{3,2},{4,5},{5,4},{6,7},{7,6},{8,9},{9,8},{10,11... | collective-permute-start | bytes 393224 | tf_op jit(solution)/shard_map/ppermute | solution.py:183
  111.2 11.9 %collective-permute-start.48 = (f16[8,8,1024]{2,1,0:T(8,128)(2,1)S(1)}, f16[8,8,1024]{2,1,0:T(8,128)(2,1)S(1)}, u32[]{:S(2)}, u32[]{:S(2)}) collective-permute-start(f16[8,8,1024]{2,1,0:T(8,128)(2,1)S(1)} %fusion.42), channel_id=1, source_target_pairs={{0,2},{1,3},{2,0},{3,1},{4,6},{5,7},{6,4},{7,5},{8,10},{9,11},{10,... | collective-permute-start | bytes 393224 | tf_op jit(solution)/shard_map/ppermute | solution.py:183
  113.5 11.5 %collective-permute-start.51 = (f16[8,8,1024]{2,1,0:T(8,128)(2,1)S(1)}, f16[8,8,1024]{2,1,0:T(8,128)(2,1)S(1)}, u32[]{:S(2)}, u32[]{:S(2)}) collective-permute-start(f16[8,8,1024]{2,1,0:T(8,128)(2,1)S(1)} %fusion.28), channel_id=1, source_target_pairs={{0,2},{1,3},{2,0},{3,1},{4,6},{5,7},{6,4},{7,5},{8,10},{9,11},{10,... | collective-permute-start | bytes 393224 | tf_op jit(solution)/shard_map/ppermute | solution.py:183
  116.2 8.9 %collective-permute-start.49 = (f16[8,8,1024]{2,1,0:T(8,128)(2,1)S(1)}, f16[8,8,1024]{2,1,0:T(8,128)(2,1)S(1)}, u32[]{:S(2)}, u32[]{:S(2)}) collective-permute-start(f16[8,8,1024]{2,1,0:T(8,128)(2,1)S(1)} %get-tuple-element.24), channel_id=1, source_target_pairs={{0,1},{1,0},{2,3},{3,2},{4,5},{5,4},{6,7},{7,6},{8,9},{9,8},{10,11... | collective-permute-start | bytes 393224 | tf_op jit(solution)/shard_map/ppermute | solution.py:183
  125.2 4.9 %collective-permute-start.52 = (bf16[2,8,2048]{2,1,0:T(8,128)(2,1)S(1)}, bf16[2,8,2048]{2,1,0:T(8,128)(2,1)S(1)}, u32[]{:S(2)}, u32[]{:S(2)}) collective-permute-start(bf16[2,8,2048]{2,1,0:T(8,128)(2,1)S(1)} %get-tuple-element.39), channel_id=1, source_target_pairs={{0,8},{4,12},{8,0},{12,4},{16,24},{20,28},{24,16},{28,20},{1,9},{5... | collective-permute-start | bytes 196616 | tf_op jit(solution)/shard_map/ppermute | solution.py:183
  126.9 4.3 %collective-permute-start.53 = (bf16[2,8,2048]{2,1,0:T(8,128)(2,1)S(1)}, bf16[2,8,2048]{2,1,0:T(8,128)(2,1)S(1)}, u32[]{:S(2)}, u32[]{:S(2)}) collective-permute-start(bf16[2,8,2048]{2,1,0:T(8,128)(2,1)S(1)} %get-tuple-element.40), channel_id=1, source_target_pairs={{0,16},{4,20},{8,24},{12,28},{16,0},{20,4},{24,8},{28,12},{1,17},{... | collective-permute-start | bytes 196616 | tf_op jit(solution)/shard_map/ppermute | solution.py:183
  127.4 5.2 %collective-permute-start.54 = (bf16[2,8,2048]{2,1,0:T(8,128)(2,1)S(1)}, bf16[2,8,2048]{2,1,0:T(8,128)(2,1)S(1)}, u32[]{:S(2)}, u32[]{:S(2)}) collective-permute-start(bf16[2,8,2048]{2,1,0:T(8,128)(2,1)S(1)} %get-tuple-element.41), channel_id=1, source_target_pairs={{0,24},{4,28},{8,16},{12,20},{16,8},{20,12},{24,0},{28,4},{1,25},{... | collective-permute-start | bytes 196616 | tf_op jit(solution)/shard_map/ppermute | solution.py:183
  (9 other events, 40.6 us)

commit v7 on v6

--- a/solution.py
+++ b/solution.py
@@ -33,7 +33,7 @@
 
 
 PART = 128
-GROUP = 2
+GROUP = 4
 
 
 def attend_kernel(lengths, query, key_new, value_new, k_cache, v_cache, out, keys, values, wide, sems):
@@ -205,21 +205,24 @@
             sems.at[part],
         )
 
+    def product(part):
+        copy(part).wait()
+        some = pl.ds(part * depth, depth)
+        rows = jnp.concatenate([far[:, some], near[:, some]], axis=0)
+        return jnp.dot(rows, held[part], preferred_element_type=jnp.float32)
+
     for part in range(parts):
         copy(part).start()
-    out[...] = jnp.zeros_like(out)
-
-    @pl.loop(0, parts)
+    out[...] = product(0)
+
+    @pl.loop(1, parts)
     def _(part):
-        copy(part).wait()
-        some = pl.ds(pl.multiple_of(part * depth, depth), depth)
-        rows = jnp.concatenate([far[:, some], near[:, some]], axis=0)
-        out[...] += jnp.dot(rows, held[part], preferred_element_type=jnp.float32)
+        out[...] += product(part)
 
 
 def multiply(far, near, weights, start, columns):
     half, width = far.shape
-    depth = 512
+    depth = 1024
     vmem = pl.BlockSpec(memory_space=pltpu.VMEM)
     return pl.pallas_call(
         functools.partial(multiply_kernel, start),

time: 135 us -> 134 us (level)
  starting transfers between devices: 52.7 us -> 58.3 us
  waiting for transfers between devices: 47.3 us -> 43.4 us
  Pallas kernels: 27.2 us -> 24.9 us
    ppermute x56, starting transfers between devices: 52.7 us -> 58.3 us  [swap(): return lax.ppermute(block, axis, [(i, i ^ bit) for i in range(count)])]
    ppermute x56, waiting for transfers between devices: 47.3 us -> 43.4 us  [swap(): return lax.ppermute(block, axis, [(i, i ^ bit) for i in range(count)])]
    pallas_call x1, Pallas kernels: 6.91 us -> 5.27 us  [attend_local(): pl.pallas_call(attend_kernel, in_specs=[pl.BlockSpec(memory_space=pltpu.S...]
  transfers between devices with their start and end apart: 56 -> 56, of which waited for: 29 -> 27; matrix products, arithmetic and copies ran while one was open for 1% -> 1% of each run, Pallas kernels for 8% -> 8%
where the time goes in v7:
time: 134 us
  starting transfers between devices  58.3 us (44%)
  waiting for transfers between devices  43.4 us (32%)
  Pallas kernels  24.9 us (19%)
  other arithmetic  6.07 us (5%)
    ppermute x56, starting transfers between devices, swap(): return lax.ppermute(block, axis, [(i, i ^ bit) for i in range(count)])  58.3 us
    ppermute x56, waiting for transfers between devices, swap(): return lax.ppermute(block, axis, [(i, i ^ bit) for i in range(count)])  43.4 us
    pallas_call x4, Pallas kernels, multiply(): pl.pallas_call(functools.partial(multiply_kernel, start), in_specs=[vmem,...  19.6 us
    pallas_call x1, Pallas kernels, attend_local(): pl.pallas_call(attend_kernel, in_specs=[pl.BlockSpec(memory_space=pltpu.S...  5.27 us
  transfers between devices with their start and end apart: 56, of which 27 were waited for; matrix products, arithmetic and copies ran while one was open for 1% of the time, Pallas kernels for 8%

profile of v7, /device:TPU:0, one launch (start us, length us, event | category | flops | bytes accessed | tf_op | source)
XLA Modules:
  0.0 134.3 jit_solution(9895897169844894714)
XLA Ops:
  0.0 1.2 fusion
  1.2 1.1 fusion.2
  2.3 3.1 %collective-permute-start.9 = (bf16[8,4096]{1,0:T(8,128)(2,1)S(1)}, bf16[8,4096]{1,0:T(8,128)(2,1)S(1)}, u32[]{:S(2)}, u32[]{:S(2)}) collective-permute-start(bf16[8,4096]{1,0:T(8,128)(2,1)S(1)} %get-tuple-element.47), channel_id=1, source_target_pairs={{0,1},{1,0},{2,3},{3,2},{4,5},{5,4},{6,7},{7,6},{8,9},{9,8},{10,11... | collective-permute-start | bytes 196616 | tf_op jit(solution)/shard_map/ppermute | solution.py:183
  5.4 2.6 %collective-permute-start = (bf16[8,4096]{1,0:T(8,128)(2,1)S(1)}, bf16[8,4096]{1,0:T(8,128)(2,1)S(1)}, u32[]{:S(2)}, u32[]{:S(2)}) collective-permute-start(bf16[8,4096]{1,0:T(8,128)(2,1)S(1)} %get-tuple-element.49), channel_id=1, source_target_pairs={{0,2},{1,3},{2,0},{3,1},{4,6},{5,7},{6,4},{7,5},{8,10},{9,11},{10,... | collective-permute-start | bytes 196616 | tf_op jit(solution)/shard_map/ppermute | solution.py:183
  9.0 1.8 %collective-permute-start.11 = (bf16[16,4096]{1,0:T(8,128)(2,1)S(1)}, bf16[16,4096]{1,0:T(8,128)(2,1)S(1)}, u32[]{:S(2)}, u32[]{:S(2)}) collective-permute-start(bf16[16,4096]{1,0:T(8,128)(2,1)S(1)} %pad_maximum_fusion.3), channel_id=1, source_target_pairs={{0,8},{4,12},{8,0},{12,4},{16,24},{20,28},{24,16},{28,20},{1,9},{5... | collective-permute-start | bytes 393224 | tf_op jit(solution)/shard_map/ppermute | solution.py:183
  10.7 1.5 %collective-permute-start.13 = (bf16[16,4096]{1,0:T(8,128)(2,1)S(1)}, bf16[16,4096]{1,0:T(8,128)(2,1)S(1)}, u32[]{:S(2)}, u32[]{:S(2)}) collective-permute-start(bf16[16,4096]{1,0:T(8,128)(2,1)S(1)} %pad_maximum_fusion.3), channel_id=1, source_target_pairs={{0,16},{4,20},{8,24},{12,28},{16,0},{20,4},{24,8},{28,12},{1,17},{... | collective-permute-start | bytes 393224 | tf_op jit(solution)/shard_map/ppermute | solution.py:183
  12.7 2.4 %collective-permute-start.15 = (bf16[16,4096]{1,0:T(8,128)(2,1)S(1)}, bf16[16,4096]{1,0:T(8,128)(2,1)S(1)}, u32[]{:S(2)}, u32[]{:S(2)}) collective-permute-start(bf16[16,4096]{1,0:T(8,128)(2,1)S(1)} %pad_maximum_fusion.3), channel_id=1, source_target_pairs={{0,24},{4,28},{8,16},{12,20},{16,8},{20,12},{24,0},{28,4},{1,25},{... | collective-permute-start | bytes 393224 | tf_op jit(solution)/shard_map/ppermute | solution.py:183
  15.9 1.5 %collective-permute-start.5 = (bf16[16,4096]{1,0:T(8,128)(2,1)S(1)}, bf16[16,4096]{1,0:T(8,128)(2,1)S(1)}, u32[]{:S(2)}, u32[]{:S(2)}) collective-permute-start(bf16[16,4096]{1,0:T(8,128)(2,1)S(1)} %constant_dynamic-update-slice_fusion), channel_id=1, source_target_pairs={{0,16},{4,20},{8,24},{12,28},{16,0},{20,4},{24,8},{28,12},{1,17},{... | collective-permute-start | bytes 393224 | tf_op jit(solution)/shard_map/ppermute | solution.py:183
  17.4 1.6 %collective-permute-start.7 = (bf16[16,4096]{1,0:T(8,128)(2,1)S(1)}, bf16[16,4096]{1,0:T(8,128)(2,1)S(1)}, u32[]{:S(2)}, u32[]{:S(2)}) collective-permute-start(bf16[16,4096]{1,0:T(8,128)(2,1)S(1)} %constant_dynamic-update-slice_fusion), channel_id=1, source_target_pairs={{0,24},{4,28},{8,16},{12,20},{16,8},{20,12},{24,0},{28,4},{1,25},{... | collective-permute-start | bytes 393224 | tf_op jit(solution)/shard_map/ppermute | solution.py:183
  19.0 2.7 %collective-permute-done.3 = bf16[16,4096]{1,0:T(8,128)(2,1)S(1)} collective-permute-done((bf16[16,4096]{1,0:T(8,128)(2,1)S(1)}, bf16[16,4096]{1,0:T(8,128)(2,1)S(1)}, u32[]{:S(2)}, u32[]{:S(2)}) %collective-permute-start.3) | collective-permute-done | bytes 131104 | tf_op jit(solution)/shard_map/ppermute | solution.py:183
  22.4 2.3 %collective-permute-done.5 = bf16[16,4096]{1,0:T(8,128)(2,1)S(1)} collective-permute-done((bf16[16,4096]{1,0:T(8,128)(2,1)S(1)}, bf16[16,4096]{1,0:T(8,128)(2,1)S(1)}, u32[]{:S(2)}, u32[]{:S(2)}) %collective-permute-start.5) | collective-permute-done | bytes 131104 | tf_op jit(solution)/shard_map/ppermute | solution.py:183
  26.6 4.8 %shard_map.73 = f32[256,1024]{1,0:T(8,128)S(1)} custom-call(bf16[128,4096]{1,0:T(8,128)(2,1)S(1)} %bitcast.269, bf16[128,4096]{1,0:T(8,128)(2,1)S(1)} %bitcast.271, bf16[4096,2304]{1,0:T(8,128)(2,1)} %weights.5), custom_call_target="tpu_custom_call" | custom-call | flops 2147483648 | bytes 8388608 | tf_op jit(solution)/shard_map/pallas_call | solution.py:227
  32.3 5.4 %shard_map.74 = f32[256,1280]{1,0:T(8,128)S(1)} custom-call(bf16[128,4096]{1,0:T(8,128)(2,1)S(1)} %bitcast.270, bf16[128,4096]{1,0:T(8,128)(2,1)S(1)} %bitcast.272, bf16[4096,2304]{1,0:T(8,128)(2,1)} %weights.5), custom_call_target="tpu_custom_call" | custom-call | flops 2684354560 | bytes 10485760 | tf_op jit(solution)/shard_map/pallas_call | solution.py:227
  37.8 1.4 %collective-permute-start.24 = (f16[8,8,1280]{2,1,0:T(8,128)(2,1)S(1)}, f16[8,8,1280]{2,1,0:T(8,128)(2,1)S(1)}, u32[]{:S(2)}, u32[]{:S(2)}) collective-permute-start(f16[8,8,1280]{2,1,0:T(8,128)(2,1)S(1)} %get-tuple-element.32), channel_id=1, source_target_pairs={{0,1},{1,0},{2,3},{3,2},{4,5},{5,4},{6,7},{7,6},{8,9},{9,8},{10,11... | collective-permute-start | bytes 491528 | tf_op jit(solution)/shard_map/ppermute | solution.py:183
  40.1 2.5 %collective-permute-start.18 = (f16[8,8,1024]{2,1,0:T(8,128)(2,1)S(1)}, f16[8,8,1024]{2,1,0:T(8,128)(2,1)S(1)}, u32[]{:S(2)}, u32[]{:S(2)}) collective-permute-start(f16[8,8,1024]{2,1,0:T(8,128)(2,1)S(1)} %fusion.41), channel_id=1, source_target_pairs={{0,2},{1,3},{2,0},{3,1},{4,6},{5,7},{6,4},{7,5},{8,10},{9,11},{10,... | collective-permute-start | bytes 393224 | tf_op jit(solution)/shard_map/ppermute | solution.py:183
  42.6 4.0 %collective-permute-done.24 = f16[8,8,1280]{2,1,0:T(8,128)(2,1)S(1)} collective-permute-done((f16[8,8,1280]{2,1,0:T(8,128)(2,1)S(1)}, f16[8,8,1280]{2,1,0:T(8,128)(2,1)S(1)}, u32[]{:S(2)}, u32[]{:S(2)}) %collective-permute-start.24) | collective-permute-done | bytes 163872 | tf_op jit(solution)/shard_map/ppermute | solution.py:183
  46.7 1.8 %collective-permute-start.25 = (f16[8,8,1280]{2,1,0:T(8,128)(2,1)S(1)}, f16[8,8,1280]{2,1,0:T(8,128)(2,1)S(1)}, u32[]{:S(2)}, u32[]{:S(2)}) collective-permute-start(f16[8,8,1280]{2,1,0:T(8,128)(2,1)S(1)} %fusion.14), channel_id=1, source_target_pairs={{0,2},{1,3},{2,0},{3,1},{4,6},{5,7},{6,4},{7,5},{8,10},{9,11},{10,... | collective-permute-start | bytes 491528 | tf_op jit(solution)/shard_map/ppermute | solution.py:183
  48.6 1.4 %collective-permute-start.19 = (bf16[2,8,1024]{2,1,0:T(8,128)(2,1)S(1)}, bf16[2,8,1024]{2,1,0:T(8,128)(2,1)S(1)}, u32[]{:S(2)}, u32[]{:S(2)}) collective-permute-start(bf16[2,8,1024]{2,1,0:T(8,128)(2,1)S(1)} %get-tuple-element.57), channel_id=1, source_target_pairs={{0,8},{4,12},{8,0},{12,4},{16,24},{20,28},{24,16},{28,20},{1,9},{5... | collective-permute-start | bytes 98312 | tf_op jit(solution)/shard_map/ppermute | solution.py:183
  50.9 1.3 collective-permute-start.21
  52.2 4.3 %collective-permute-done.25 = f16[8,8,1280]{2,1,0:T(8,128)(2,1)S(1)} collective-permute-done((f16[8,8,1280]{2,1,0:T(8,128)(2,1)S(1)}, f16[8,8,1280]{2,1,0:T(8,128)(2,1)S(1)}, u32[]{:S(2)}, u32[]{:S(2)}) %collective-permute-start.25) | collective-permute-done | bytes 163872 | tf_op jit(solution)/shard_map/ppermute | solution.py:183
  57.2 1.4 %collective-permute-start.26 = (bf16[2,8,1280]{2,1,0:T(8,128)(2,1)S(1)}, bf16[2,8,1280]{2,1,0:T(8,128)(2,1)S(1)}, u32[]{:S(2)}, u32[]{:S(2)}) collective-permute-start(bf16[2,8,1280]{2,1,0:T(8,128)(2,1)S(1)} %get-tuple-element.52), channel_id=1, source_target_pairs={{0,8},{4,12},{8,0},{12,4},{16,24},{20,28},{24,16},{28,20},{1,9},{5... | collective-permute-start | bytes 122888 | tf_op jit(solution)/shard_map/ppermute | solution.py:183
  59.4 1.3 collective-permute-start.28
  61.2 1.4 %collective-permute-done.27 = bf16[2,8,1280]{2,1,0:T(8,128)(2,1)S(1)} collective-permute-done((bf16[2,8,1280]{2,1,0:T(8,128)(2,1)S(1)}, bf16[2,8,1280]{2,1,0:T(8,128)(2,1)S(1)}, u32[]{:S(2)}, u32[]{:S(2)}) %collective-permute-start.27) | collective-permute-done | bytes 40992 | tf_op jit(solution)/shard_map/ppermute | solution.py:183
  62.6 1.7 %collective-permute-done.28 = bf16[2,8,1280]{2,1,0:T(8,128)(2,1)S(1)} collective-permute-done((bf16[2,8,1280]{2,1,0:T(8,128)(2,1)S(1)}, bf16[2,8,1280]{2,1,0:T(8,128)(2,1)S(1)}, u32[]{:S(2)}, u32[]{:S(2)}) %collective-permute-start.28) | collective-permute-done | bytes 40992 | tf_op jit(solution)/shard_map/ppermute | solution.py:183
  64.5 1.2 collective-permute-done.29
  66.6 5.3 %shard_map.75 = bf16[8,128,128]{2,1,0:T(8,128)(2,1)S(1)} custom-call(s32[8]{0:T(128)S(1)} %copy-done, bf16[8,128,128]{2,1,0:T(8,128)(2,1)S(1)} %pad_maximum_fusion.query, bf16[8,8,128]{2,1,0:T(8,128)(2,1)S(1)} %pad_maximum_fusion.8.key_new, f32[8,8,128]{2,1,0:T(8,128)S(1)} %get-tuple-element.84.value_new, bf16[8,512,1024]{2,1,0:T(8,128)(2,1)} %k_cache.1, ...), custom_call_target="tpu_custom_call" | custom-call | flops 2147483648 | bytes 8388608 | tf_op jit(solution)/shard_map/pallas_call | solution.py:153
  73.0 3.5 %collective-permute-start.30 = (bf16[8,4096]{1,0:T(8,128)(2,1)S(1)}, bf16[8,4096]{1,0:T(8,128)(2,1)S(1)}, u32[]{:S(2)}, u32[]{:S(2)}) collective-permute-start(bf16[8,4096]{1,0:T(8,128)(2,1)S(1)} %get-tuple-element.45), channel_id=1, source_target_pairs={{0,2},{1,3},{2,0},{3,1},{4,6},{5,7},{6,4},{7,5},{8,10},{9,11},{10,... | collective-permute-start | bytes 196616 | tf_op jit(solution)/shard_map/ppermute | solution.py:183
  77.6 1.4 %collective-permute-start.41 = (bf16[16,4096]{1,0:T(8,128)(2,1)S(1)}, bf16[16,4096]{1,0:T(8,128)(2,1)S(1)}, u32[]{:S(2)}, u32[]{:S(2)}) collective-permute-start(bf16[16,4096]{1,0:T(8,128)(2,1)S(1)} %pad_maximum_fusion.5), channel_id=1, source_target_pairs={{0,8},{4,12},{8,0},{12,4},{16,24},{20,28},{24,16},{28,20},{1,9},{5... | collective-permute-start | bytes 393224 | tf_op jit(solution)/shard_map/ppermute | solution.py:183
  79.0 1.5 %collective-permute-start.43 = (bf16[16,4096]{1,0:T(8,128)(2,1)S(1)}, bf16[16,4096]{1,0:T(8,128)(2,1)S(1)}, u32[]{:S(2)}, u32[]{:S(2)}) collective-permute-start(bf16[16,4096]{1,0:T(8,128)(2,1)S(1)} %pad_maximum_fusion.5), channel_id=1, source_target_pairs={{0,16},{4,20},{8,24},{12,28},{16,0},{20,4},{24,8},{28,12},{1,17},{... | collective-permute-start | bytes 393224 | tf_op jit(solution)/shard_map/ppermute | solution.py:183
  80.9 2.5 %collective-permute-start.45 = (bf16[16,4096]{1,0:T(8,128)(2,1)S(1)}, bf16[16,4096]{1,0:T(8,128)(2,1)S(1)}, u32[]{:S(2)}, u32[]{:S(2)}) collective-permute-start(bf16[16,4096]{1,0:T(8,128)(2,1)S(1)} %pad_maximum_fusion.5), channel_id=1, source_target_pairs={{0,24},{4,28},{8,16},{12,20},{16,8},{20,12},{24,0},{28,4},{1,25},{... | collective-permute-start | bytes 393224 | tf_op jit(solution)/shard_map/ppermute | solution.py:183
  84.1 2.6 %collective-permute-start.35 = (bf16[16,4096]{1,0:T(8,128)(2,1)S(1)}, bf16[16,4096]{1,0:T(8,128)(2,1)S(1)}, u32[]{:S(2)}, u32[]{:S(2)}) collective-permute-start(bf16[16,4096]{1,0:T(8,128)(2,1)S(1)} %constant_dynamic-update-slice_fusion.10), channel_id=1, source_target_pairs={{0,16},{4,20},{8,24},{12,28},{16,0},{20,4},{24,8},{28,12},{1,17},{... | collective-permute-start | bytes 393224 | tf_op jit(solution)/shard_map/ppermute | solution.py:183
  87.3 2.6 %collective-permute-done.33 = bf16[16,4096]{1,0:T(8,128)(2,1)S(1)} collective-permute-done((bf16[16,4096]{1,0:T(8,128)(2,1)S(1)}, bf16[16,4096]{1,0:T(8,128)(2,1)S(1)}, u32[]{:S(2)}, u32[]{:S(2)}) %collective-permute-start.33) | collective-permute-done | bytes 131104 | tf_op jit(solution)/shard_map/ppermute | solution.py:183
  90.6 2.7 %collective-permute-done.35 = bf16[16,4096]{1,0:T(8,128)(2,1)S(1)} collective-permute-done((bf16[16,4096]{1,0:T(8,128)(2,1)S(1)}, bf16[16,4096]{1,0:T(8,128)(2,1)S(1)}, u32[]{:S(2)}, u32[]{:S(2)}) %collective-permute-start.35) | collective-permute-done | bytes 131104 | tf_op jit(solution)/shard_map/ppermute | solution.py:183
  95.2 4.7 %shard_map.76 = f32[256,1024]{1,0:T(8,128)S(1)} custom-call(bf16[128,4096]{1,0:T(8,128)(2,1)S(1)} %bitcast.265, bf16[128,4096]{1,0:T(8,128)(2,1)S(1)} %bitcast.267, bf16[4096,2048]{1,0:T(8,128)(2,1)} %weights.7), custom_call_target="tpu_custom_call" | custom-call | flops 2147483648 | bytes 8388608 | tf_op jit(solution)/shard_map/pallas_call | solution.py:227
  100.0 0.9 collective-permute-start.47
  100.9 4.7 %shard_map.77 = f32[256,1024]{1,0:T(8,128)S(1)} custom-call(bf16[128,4096]{1,0:T(8,128)(2,1)S(1)} %bitcast.266, bf16[128,4096]{1,0:T(8,128)(2,1)S(1)} %bitcast.268, bf16[4096,2048]{1,0:T(8,128)(2,1)} %weights.7), custom_call_target="tpu_custom_call" | custom-call | flops 2147483648 | bytes 8388608 | tf_op jit(solution)/shard_map/pallas_call | solution.py:227
  105.6 1.3 collective-permute-start.50
  106.9 1.8 %collective-permute-done.47 = f16[2,8,8,1024]{3,2,1,0:T(8,128)(2,1)S(1)} collective-permute-done((f16[2,8,8,1024]{3,2,1,0:T(8,128)(2,1)S(1)}, f16[2,8,8,1024]{3,2,1,0:T(8,128)(2,1)S(1)}, u32[]{:S(2)}, u32[]{:S(2)}) %collective-permute-start.47) | collective-permute-done | bytes 262176 | tf_op jit(solution)/shard_map/ppermute | solution.py:183
  108.7 3.0 %collective-permute-start.48 = (f16[8,8,1024]{2,1,0:T(8,128)(2,1)S(1)}, f16[8,8,1024]{2,1,0:T(8,128)(2,1)S(1)}, u32[]{:S(2)}, u32[]{:S(2)}) collective-permute-start(f16[8,8,1024]{2,1,0:T(8,128)(2,1)S(1)} %fusion.42), channel_id=1, source_target_pairs={{0,2},{1,3},{2,0},{3,1},{4,6},{5,7},{6,4},{7,5},{8,10},{9,11},{10,... | collective-permute-start | bytes 393224 | tf_op jit(solution)/shard_map/ppermute | solution.py:183
  111.8 4.4 %collective-permute-start.51 = (f16[8,8,1024]{2,1,0:T(8,128)(2,1)S(1)}, f16[8,8,1024]{2,1,0:T(8,128)(2,1)S(1)}, u32[]{:S(2)}, u32[]{:S(2)}) collective-permute-start(f16[8,8,1024]{2,1,0:T(8,128)(2,1)S(1)} %fusion.28), channel_id=1, source_target_pairs={{0,2},{1,3},{2,0},{3,1},{4,6},{5,7},{6,4},{7,5},{8,10},{9,11},{10,... | collective-permute-start | bytes 393224 | tf_op jit(solution)/shard_map/ppermute | solution.py:183
  116.2 5.4 %collective-permute-done.48 = f16[8,8,1024]{2,1,0:T(8,128)(2,1)S(1)} collective-permute-done((f16[8,8,1024]{2,1,0:T(8,128)(2,1)S(1)}, f16[8,8,1024]{2,1,0:T(8,128)(2,1)S(1)}, u32[]{:S(2)}, u32[]{:S(2)}) %collective-permute-start.48) | collective-permute-done | bytes 131104 | tf_op jit(solution)/shard_map/ppermute | solution.py:183
  121.6 2.0 %collective-permute-done.51 = f16[8,8,1024]{2,1,0:T(8,128)(2,1)S(1)} collective-permute-done((f16[8,8,1024]{2,1,0:T(8,128)(2,1)S(1)}, f16[8,8,1024]{2,1,0:T(8,128)(2,1)S(1)}, u32[]{:S(2)}, u32[]{:S(2)}) %collective-permute-start.51) | collective-permute-done | bytes 131104 | tf_op jit(solution)/shard_map/ppermute | solution.py:183
  124.2 1.5 %collective-permute-start.52 = (bf16[2,8,2048]{2,1,0:T(8,128)(2,1)S(1)}, bf16[2,8,2048]{2,1,0:T(8,128)(2,1)S(1)}, u32[]{:S(2)}, u32[]{:S(2)}) collective-permute-start(bf16[2,8,2048]{2,1,0:T(8,128)(2,1)S(1)} %get-tuple-element.39), channel_id=1, source_target_pairs={{0,8},{4,12},{8,0},{12,4},{16,24},{20,28},{24,16},{28,20},{1,9},{5... | collective-permute-start | bytes 196616 | tf_op jit(solution)/shard_map/ppermute | solution.py:183
  125.7 0.9 collective-permute-start.53
  126.6 1.2 collective-permute-start.54
  127.8 1.5 %collective-permute-done.52 = bf16[2,8,2048]{2,1,0:T(8,128)(2,1)S(1)} collective-permute-done((bf16[2,8,2048]{2,1,0:T(8,128)(2,1)S(1)}, bf16[2,8,2048]{2,1,0:T(8,128)(2,1)S(1)}, u32[]{:S(2)}, u32[]{:S(2)}) %collective-permute-start.52) | collective-permute-done | bytes 65568 | tf_op jit(solution)/shard_map/ppermute | solution.py:183
  130.0 1.8 %collective-permute-done.54 = bf16[2,8,2048]{2,1,0:T(8,128)(2,1)S(1)} collective-permute-done((bf16[2,8,2048]{2,1,0:T(8,128)(2,1)S(1)}, bf16[2,8,2048]{2,1,0:T(8,128)(2,1)S(1)}, u32[]{:S(2)}, u32[]{:S(2)}) %collective-permute-start.54) | collective-permute-done | bytes 65568 | tf_op jit(solution)/shard_map/ppermute | solution.py:183
  131.9 1.3 collective-permute-done.55
  (184 shorter events, 19.3 us)
Async XLA Ops:
  2.3 6.5 %collective-permute-start.9 = (bf16[8,4096]{1,0:T(8,128)(2,1)S(1)}, bf16[8,4096]{1,0:T(8,128)(2,1)S(1)}, u32[]{:S(2)}, u32[]{:S(2)}) collective-permute-start(bf16[8,4096]{1,0:T(8,128)(2,1)S(1)} %get-tuple-element.47), channel_id=1, source_target_pairs={{0,1},{1,0},{2,3},{3,2},{4,5},{5,4},{6,7},{7,6},{8,9},{9,8},{10,11... | collective-permute-start | bytes 196616 | tf_op jit(solution)/shard_map/ppermute | solution.py:183
  5.4 7.3 %collective-permute-start = (bf16[8,4096]{1,0:T(8,128)(2,1)S(1)}, bf16[8,4096]{1,0:T(8,128)(2,1)S(1)}, u32[]{:S(2)}, u32[]{:S(2)}) collective-permute-start(bf16[8,4096]{1,0:T(8,128)(2,1)S(1)} %get-tuple-element.49), channel_id=1, source_target_pairs={{0,2},{1,3},{2,0},{3,1},{4,6},{5,7},{6,4},{7,5},{8,10},{9,11},{10,... | collective-permute-start | bytes 196616 | tf_op jit(solution)/shard_map/ppermute | solution.py:183
  8.0 7.1 %collective-permute-start.1 = (bf16[8,4096]{1,0:T(8,128)(2,1)S(1)}, bf16[8,4096]{1,0:T(8,128)(2,1)S(1)}, u32[]{:S(2)}, u32[]{:S(2)}) collective-permute-start(bf16[8,4096]{1,0:T(8,128)(2,1)S(1)} %get-tuple-element.48), channel_id=1, source_target_pairs={{0,3},{1,2},{2,1},{3,0},{4,7},{5,6},{6,5},{7,4},{8,11},{9,10},{10,... | collective-permute-start | bytes 196616 | tf_op jit(solution)/shard_map/ppermute | solution.py:183
  8.9 6.4 %collective-permute-start.10 = (bf16[16,4096]{1,0:T(8,128)(2,1)S(1)}, bf16[16,4096]{1,0:T(8,128)(2,1)S(1)}, u32[]{:S(2)}, u32[]{:S(2)}) collective-permute-start(bf16[16,4096]{1,0:T(8,128)(2,1)S(1)} %pad_maximum_fusion.3), channel_id=1, source_target_pairs={{0,4},{4,0},{8,12},{12,8},{16,20},{20,16},{24,28},{28,24},{1,5},{5... | collective-permute-start | bytes 393224 | tf_op jit(solution)/shard_map/ppermute | solution.py:183
  9.0 7.0 %collective-permute-start.11 = (bf16[16,4096]{1,0:T(8,128)(2,1)S(1)}, bf16[16,4096]{1,0:T(8,128)(2,1)S(1)}, u32[]{:S(2)}, u32[]{:S(2)}) collective-permute-start(bf16[16,4096]{1,0:T(8,128)(2,1)S(1)} %pad_maximum_fusion.3), channel_id=1, source_target_pairs={{0,8},{4,12},{8,0},{12,4},{16,24},{20,28},{24,16},{28,20},{1,9},{5... | collective-permute-start | bytes 393224 | tf_op jit(solution)/shard_map/ppermute | solution.py:183
  10.7 11.0 %collective-permute-start.13 = (bf16[16,4096]{1,0:T(8,128)(2,1)S(1)}, bf16[16,4096]{1,0:T(8,128)(2,1)S(1)}, u32[]{:S(2)}, u32[]{:S(2)}) collective-permute-start(bf16[16,4096]{1,0:T(8,128)(2,1)S(1)} %pad_maximum_fusion.3), channel_id=1, source_target_pairs={{0,16},{4,20},{8,24},{12,28},{16,0},{20,4},{24,8},{28,12},{1,17},{... | collective-permute-start | bytes 393224 | tf_op jit(solution)/shard_map/ppermute | solution.py:183
  12.7 9.6 %collective-permute-start.15 = (bf16[16,4096]{1,0:T(8,128)(2,1)S(1)}, bf16[16,4096]{1,0:T(8,128)(2,1)S(1)}, u32[]{:S(2)}, u32[]{:S(2)}) collective-permute-start(bf16[16,4096]{1,0:T(8,128)(2,1)S(1)} %pad_maximum_fusion.3), channel_id=1, source_target_pairs={{0,24},{4,28},{8,16},{12,20},{16,8},{20,12},{24,0},{28,4},{1,25},{... | collective-permute-start | bytes 393224 | tf_op jit(solution)/shard_map/ppermute | solution.py:183
  15.2 2.2 %collective-permute-start.2 = (bf16[16,4096]{1,0:T(8,128)(2,1)S(1)}, bf16[16,4096]{1,0:T(8,128)(2,1)S(1)}, u32[]{:S(2)}, u32[]{:S(2)}) collective-permute-start(bf16[16,4096]{1,0:T(8,128)(2,1)S(1)} %constant_dynamic-update-slice_fusion), channel_id=1, source_target_pairs={{0,4},{4,0},{8,12},{12,8},{16,20},{20,16},{24,28},{28,24},{1,5},{5... | collective-permute-start | bytes 393224 | tf_op jit(solution)/shard_map/ppermute | solution.py:183
  15.3 6.4 %collective-permute-start.3 = (bf16[16,4096]{1,0:T(8,128)(2,1)S(1)}, bf16[16,4096]{1,0:T(8,128)(2,1)S(1)}, u32[]{:S(2)}, u32[]{:S(2)}) collective-permute-start(bf16[16,4096]{1,0:T(8,128)(2,1)S(1)} %constant_dynamic-update-slice_fusion), channel_id=1, source_target_pairs={{0,8},{4,12},{8,0},{12,4},{16,24},{20,28},{24,16},{28,20},{1,9},{5... | collective-permute-start | bytes 393224 | tf_op jit(solution)/shard_map/ppermute | solution.py:183
  15.9 8.8 %collective-permute-start.5 = (bf16[16,4096]{1,0:T(8,128)(2,1)S(1)}, bf16[16,4096]{1,0:T(8,128)(2,1)S(1)}, u32[]{:S(2)}, u32[]{:S(2)}) collective-permute-start(bf16[16,4096]{1,0:T(8,128)(2,1)S(1)} %constant_dynamic-update-slice_fusion), channel_id=1, source_target_pairs={{0,16},{4,20},{8,24},{12,28},{16,0},{20,4},{24,8},{28,12},{1,17},{... | collective-permute-start | bytes 393224 | tf_op jit(solution)/shard_map/ppermute | solution.py:183
  17.4 7.3 %collective-permute-start.7 = (bf16[16,4096]{1,0:T(8,128)(2,1)S(1)}, bf16[16,4096]{1,0:T(8,128)(2,1)S(1)}, u32[]{:S(2)}, u32[]{:S(2)}) collective-permute-start(bf16[16,4096]{1,0:T(8,128)(2,1)S(1)} %constant_dynamic-update-slice_fusion), channel_id=1, source_target_pairs={{0,24},{4,28},{8,16},{12,20},{16,8},{20,12},{24,0},{28,4},{1,25},{... | collective-permute-start | bytes 393224 | tf_op jit(solution)/shard_map/ppermute | solution.py:183
  21.7 3.5 %collective-permute-start.12 = (bf16[16,4096]{1,0:T(8,128)(2,1)S(1)}, bf16[16,4096]{1,0:T(8,128)(2,1)S(1)}, u32[]{:S(2)}, u32[]{:S(2)}) collective-permute-start(bf16[16,4096]{1,0:T(8,128)(2,1)S(1)} %collective-permute-done.11), channel_id=1, source_target_pairs={{0,4},{4,0},{8,12},{12,8},{16,20},{20,16},{24,28},{28,24},{1,5},{5... | collective-permute-start | bytes 393224 | tf_op jit(solution)/shard_map/ppermute | solution.py:183
  21.8 3.6 %collective-permute-start.4 = (bf16[16,4096]{1,0:T(8,128)(2,1)S(1)}, bf16[16,4096]{1,0:T(8,128)(2,1)S(1)}, u32[]{:S(2)}, u32[]{:S(2)}) collective-permute-start(bf16[16,4096]{1,0:T(8,128)(2,1)S(1)} %collective-permute-done.3), channel_id=1, source_target_pairs={{0,4},{4,0},{8,12},{12,8},{16,20},{20,16},{24,28},{28,24},{1,5},{5... | collective-permute-start | bytes 393224 | tf_op jit(solution)/shard_map/ppermute | solution.py:183
  22.3 3.0 %collective-permute-start.14 = (bf16[16,4096]{1,0:T(8,128)(2,1)S(1)}, bf16[16,4096]{1,0:T(8,128)(2,1)S(1)}, u32[]{:S(2)}, u32[]{:S(2)}) collective-permute-start(bf16[16,4096]{1,0:T(8,128)(2,1)S(1)} %collective-permute-done.13), channel_id=1, source_target_pairs={{0,4},{4,0},{8,12},{12,8},{16,20},{20,16},{24,28},{28,24},{1,5},{5... | collective-permute-start | bytes 393224 | tf_op jit(solution)/shard_map/ppermute | solution.py:183
  31.5 8.5 %collective-permute-start.17 = (f16[2,8,8,1024]{3,2,1,0:T(8,128)(2,1)S(1)}, f16[2,8,8,1024]{3,2,1,0:T(8,128)(2,1)S(1)}, u32[]{:S(2)}, u32[]{:S(2)}) collective-permute-start(f16[2,8,8,1024]{3,2,1,0:T(8,128)(2,1)S(1)} %fusion.19), channel_id=1, source_target_pairs={{0,1},{1,0},{2,3},{3,2},{4,5},{5,4},{6,7},{7,6},{8,9},{9,8},{10,11... | collective-permute-start | bytes 786440 | tf_op jit(solution)/shard_map/ppermute | solution.py:183
  37.8 8.9 %collective-permute-start.24 = (f16[8,8,1280]{2,1,0:T(8,128)(2,1)S(1)}, f16[8,8,1280]{2,1,0:T(8,128)(2,1)S(1)}, u32[]{:S(2)}, u32[]{:S(2)}) collective-permute-start(f16[8,8,1280]{2,1,0:T(8,128)(2,1)S(1)} %get-tuple-element.32), channel_id=1, source_target_pairs={{0,1},{1,0},{2,3},{3,2},{4,5},{5,4},{6,7},{7,6},{8,9},{9,8},{10,11... | collective-permute-start | bytes 491528 | tf_op jit(solution)/shard_map/ppermute | solution.py:183
  40.1 8.4 %collective-permute-start.18 = (f16[8,8,1024]{2,1,0:T(8,128)(2,1)S(1)}, f16[8,8,1024]{2,1,0:T(8,128)(2,1)S(1)}, u32[]{:S(2)}, u32[]{:S(2)}) collective-permute-start(f16[8,8,1024]{2,1,0:T(8,128)(2,1)S(1)} %fusion.41), channel_id=1, source_target_pairs={{0,2},{1,3},{2,0},{3,1},{4,6},{5,7},{6,4},{7,5},{8,10},{9,11},{10,... | collective-permute-start | bytes 393224 | tf_op jit(solution)/shard_map/ppermute | solution.py:183
  46.7 9.7 %collective-permute-start.25 = (f16[8,8,1280]{2,1,0:T(8,128)(2,1)S(1)}, f16[8,8,1280]{2,1,0:T(8,128)(2,1)S(1)}, u32[]{:S(2)}, u32[]{:S(2)}) collective-permute-start(f16[8,8,1280]{2,1,0:T(8,128)(2,1)S(1)} %fusion.14), channel_id=1, source_target_pairs={{0,2},{1,3},{2,0},{3,1},{4,6},{5,7},{6,4},{7,5},{8,10},{9,11},{10,... | collective-permute-start | bytes 491528 | tf_op jit(solution)/shard_map/ppermute | solution.py:183
  48.5 8.5 %collective-permute-start.23 = (f16[8,8,1280]{2,1,0:T(8,128)(2,1)S(1)}, f16[8,8,1280]{2,1,0:T(8,128)(2,1)S(1)}, u32[]{:S(2)}, u32[]{:S(2)}) collective-permute-start(f16[8,8,1280]{2,1,0:T(8,128)(2,1)S(1)} %get-tuple-element.19), channel_id=1, source_target_pairs={{0,1},{1,0},{2,3},{3,2},{4,5},{5,4},{6,7},{7,6},{8,9},{9,8},{10,11... | collective-permute-start | bytes 491528 | tf_op jit(solution)/shard_map/ppermute | solution.py:183
  48.6 10.8 %collective-permute-start.19 = (bf16[2,8,1024]{2,1,0:T(8,128)(2,1)S(1)}, bf16[2,8,1024]{2,1,0:T(8,128)(2,1)S(1)}, u32[]{:S(2)}, u32[]{:S(2)}) collective-permute-start(bf16[2,8,1024]{2,1,0:T(8,128)(2,1)S(1)} %get-tuple-element.57), channel_id=1, source_target_pairs={{0,8},{4,12},{8,0},{12,4},{16,24},{20,28},{24,16},{28,20},{1,9},{5... | collective-permute-start | bytes 98312 | tf_op jit(solution)/shard_map/ppermute | solution.py:183
  50.0 10.7 %collective-permute-start.20 = (bf16[2,8,1024]{2,1,0:T(8,128)(2,1)S(1)}, bf16[2,8,1024]{2,1,0:T(8,128)(2,1)S(1)}, u32[]{:S(2)}, u32[]{:S(2)}) collective-permute-start(bf16[2,8,1024]{2,1,0:T(8,128)(2,1)S(1)} %get-tuple-element.59), channel_id=1, source_target_pairs={{0,16},{4,20},{8,24},{12,28},{16,0},{20,4},{24,8},{28,12},{1,17},{... | collective-permute-start | bytes 98312 | tf_op jit(solution)/shard_map/ppermute | solution.py:183
  50.9 9.9 %collective-permute-start.21 = (bf16[2,8,1024]{2,1,0:T(8,128)(2,1)S(1)}, bf16[2,8,1024]{2,1,0:T(8,128)(2,1)S(1)}, u32[]{:S(2)}, u32[]{:S(2)}) collective-permute-start(bf16[2,8,1024]{2,1,0:T(8,128)(2,1)S(1)} %get-tuple-element.58), channel_id=1, source_target_pairs={{0,24},{4,28},{8,16},{12,20},{16,8},{20,12},{24,0},{28,4},{1,25},{... | collective-permute-start | bytes 98312 | tf_op jit(solution)/shard_map/ppermute | solution.py:183
  57.2 4.1 %collective-permute-start.26 = (bf16[2,8,1280]{2,1,0:T(8,128)(2,1)S(1)}, bf16[2,8,1280]{2,1,0:T(8,128)(2,1)S(1)}, u32[]{:S(2)}, u32[]{:S(2)}) collective-permute-start(bf16[2,8,1280]{2,1,0:T(8,128)(2,1)S(1)} %get-tuple-element.52), channel_id=1, source_target_pairs={{0,8},{4,12},{8,0},{12,4},{16,24},{20,28},{24,16},{28,20},{1,9},{5... | collective-permute-start | bytes 122888 | tf_op jit(solution)/shard_map/ppermute | solution.py:183
  58.6 4.0 %collective-permute-start.27 = (bf16[2,8,1280]{2,1,0:T(8,128)(2,1)S(1)}, bf16[2,8,1280]{2,1,0:T(8,128)(2,1)S(1)}, u32[]{:S(2)}, u32[]{:S(2)}) collective-permute-start(bf16[2,8,1280]{2,1,0:T(8,128)(2,1)S(1)} %get-tuple-element.54), channel_id=1, source_target_pairs={{0,16},{4,20},{8,24},{12,28},{16,0},{20,4},{24,8},{28,12},{1,17},{... | collective-permute-start | bytes 122888 | tf_op jit(solution)/shard_map/ppermute | solution.py:183
  59.4 4.9 %collective-permute-start.28 = (bf16[2,8,1280]{2,1,0:T(8,128)(2,1)S(1)}, bf16[2,8,1280]{2,1,0:T(8,128)(2,1)S(1)}, u32[]{:S(2)}, u32[]{:S(2)}) collective-permute-start(bf16[2,8,1280]{2,1,0:T(8,128)(2,1)S(1)} %get-tuple-element.53), channel_id=1, source_target_pairs={{0,24},{4,28},{8,16},{12,20},{16,8},{20,12},{24,0},{28,4},{1,25},{... | collective-permute-start | bytes 122888 | tf_op jit(solution)/shard_map/ppermute | solution.py:183
  60.8 3.7 %collective-permute-start.22 = (bf16[4,8,1024]{2,1,0:T(8,128)(2,1)S(1)}, bf16[4,8,1024]{2,1,0:T(8,128)(2,1)S(1)}, u32[]{:S(2)}, u32[]{:S(2)}) collective-permute-start(bf16[4,8,1024]{2,1,0:T(8,128)(2,1)S(1)} %pad_maximum_fusion.7), channel_id=1, source_target_pairs={{0,4},{4,0},{8,12},{12,8},{16,20},{20,16},{24,28},{28,24},{1,5},{5... | collective-permute-start | bytes 196616 | tf_op jit(solution)/shard_map/ppermute | solution.py:183
  72.5 5.0 %collective-permute-start.39 = (bf16[8,4096]{1,0:T(8,128)(2,1)S(1)}, bf16[8,4096]{1,0:T(8,128)(2,1)S(1)}, u32[]{:S(2)}, u32[]{:S(2)}) collective-permute-start(bf16[8,4096]{1,0:T(8,128)(2,1)S(1)} %get-tuple-element.43), channel_id=1, source_target_pairs={{0,1},{1,0},{2,3},{3,2},{4,5},{5,4},{6,7},{7,6},{8,9},{9,8},{10,11... | collective-permute-start | bytes 196616 | tf_op jit(solution)/shard_map/ppermute | solution.py:183
  73.0 7.9 %collective-permute-start.30 = (bf16[8,4096]{1,0:T(8,128)(2,1)S(1)}, bf16[8,4096]{1,0:T(8,128)(2,1)S(1)}, u32[]{:S(2)}, u32[]{:S(2)}) collective-permute-start(bf16[8,4096]{1,0:T(8,128)(2,1)S(1)} %get-tuple-element.45), channel_id=1, source_target_pairs={{0,2},{1,3},{2,0},{3,1},{4,6},{5,7},{6,4},{7,5},{8,10},{9,11},{10,... | collective-permute-start | bytes 196616 | tf_op jit(solution)/shard_map/ppermute | solution.py:183
  76.5 6.9 %collective-permute-start.31 = (bf16[8,4096]{1,0:T(8,128)(2,1)S(1)}, bf16[8,4096]{1,0:T(8,128)(2,1)S(1)}, u32[]{:S(2)}, u32[]{:S(2)}) collective-permute-start(bf16[8,4096]{1,0:T(8,128)(2,1)S(1)} %get-tuple-element.44), channel_id=1, source_target_pairs={{0,3},{1,2},{2,1},{3,0},{4,7},{5,6},{6,5},{7,4},{8,11},{9,10},{10,... | collective-permute-start | bytes 196616 | tf_op jit(solution)/shard_map/ppermute | solution.py:183
  77.6 6.0 %collective-permute-start.40 = (bf16[16,4096]{1,0:T(8,128)(2,1)S(1)}, bf16[16,4096]{1,0:T(8,128)(2,1)S(1)}, u32[]{:S(2)}, u32[]{:S(2)}) collective-permute-start(bf16[16,4096]{1,0:T(8,128)(2,1)S(1)} %pad_maximum_fusion.5), channel_id=1, source_target_pairs={{0,4},{4,0},{8,12},{12,8},{16,20},{20,16},{24,28},{28,24},{1,5},{5... | collective-permute-start | bytes 393224 | tf_op jit(solution)/shard_map/ppermute | solution.py:183
  77.6 6.4 %collective-permute-start.41 = (bf16[16,4096]{1,0:T(8,128)(2,1)S(1)}, bf16[16,4096]{1,0:T(8,128)(2,1)S(1)}, u32[]{:S(2)}, u32[]{:S(2)}) collective-permute-start(bf16[16,4096]{1,0:T(8,128)(2,1)S(1)} %pad_maximum_fusion.5), channel_id=1, source_target_pairs={{0,8},{4,12},{8,0},{12,4},{16,24},{20,28},{24,16},{28,20},{1,9},{5... | collective-permute-start | bytes 393224 | tf_op jit(solution)/shard_map/ppermute | solution.py:183
  79.0 10.9 %collective-permute-start.43 = (bf16[16,4096]{1,0:T(8,128)(2,1)S(1)}, bf16[16,4096]{1,0:T(8,128)(2,1)S(1)}, u32[]{:S(2)}, u32[]{:S(2)}) collective-permute-start(bf16[16,4096]{1,0:T(8,128)(2,1)S(1)} %pad_maximum_fusion.5), channel_id=1, source_target_pairs={{0,16},{4,20},{8,24},{12,28},{16,0},{20,4},{24,8},{28,12},{1,17},{... | collective-permute-start | bytes 393224 | tf_op jit(solution)/shard_map/ppermute | solution.py:183
  80.9 9.7 %collective-permute-start.45 = (bf16[16,4096]{1,0:T(8,128)(2,1)S(1)}, bf16[16,4096]{1,0:T(8,128)(2,1)S(1)}, u32[]{:S(2)}, u32[]{:S(2)}) collective-permute-start(bf16[16,4096]{1,0:T(8,128)(2,1)S(1)} %pad_maximum_fusion.5), channel_id=1, source_target_pairs={{0,24},{4,28},{8,16},{12,20},{16,8},{20,12},{24,0},{28,4},{1,25},{... | collective-permute-start | bytes 393224 | tf_op jit(solution)/shard_map/ppermute | solution.py:183
  83.4 3.2 %collective-permute-start.32 = (bf16[16,4096]{1,0:T(8,128)(2,1)S(1)}, bf16[16,4096]{1,0:T(8,128)(2,1)S(1)}, u32[]{:S(2)}, u32[]{:S(2)}) collective-permute-start(bf16[16,4096]{1,0:T(8,128)(2,1)S(1)} %constant_dynamic-update-slice_fusion.10), channel_id=1, source_target_pairs={{0,4},{4,0},{8,12},{12,8},{16,20},{20,16},{24,28},{28,24},{1,5},{5... | collective-permute-start | bytes 393224 | tf_op jit(solution)/shard_map/ppermute | solution.py:183
  83.6 6.4 %collective-permute-start.33 = (bf16[16,4096]{1,0:T(8,128)(2,1)S(1)}, bf16[16,4096]{1,0:T(8,128)(2,1)S(1)}, u32[]{:S(2)}, u32[]{:S(2)}) collective-permute-start(bf16[16,4096]{1,0:T(8,128)(2,1)S(1)} %constant_dynamic-update-slice_fusion.10), channel_id=1, source_target_pairs={{0,8},{4,12},{8,0},{12,4},{16,24},{20,28},{24,16},{28,20},{1,9},{5... | collective-permute-start | bytes 393224 | tf_op jit(solution)/shard_map/ppermute | solution.py:183
  84.1 9.2 %collective-permute-start.35 = (bf16[16,4096]{1,0:T(8,128)(2,1)S(1)}, bf16[16,4096]{1,0:T(8,128)(2,1)S(1)}, u32[]{:S(2)}, u32[]{:S(2)}) collective-permute-start(bf16[16,4096]{1,0:T(8,128)(2,1)S(1)} %constant_dynamic-update-slice_fusion.10), channel_id=1, source_target_pairs={{0,16},{4,20},{8,24},{12,28},{16,0},{20,4},{24,8},{28,12},{1,17},{... | collective-permute-start | bytes 393224 | tf_op jit(solution)/shard_map/ppermute | solution.py:183
  86.7 6.7 %collective-permute-start.37 = (bf16[16,4096]{1,0:T(8,128)(2,1)S(1)}, bf16[16,4096]{1,0:T(8,128)(2,1)S(1)}, u32[]{:S(2)}, u32[]{:S(2)}) collective-permute-start(bf16[16,4096]{1,0:T(8,128)(2,1)S(1)} %constant_dynamic-update-slice_fusion.10), channel_id=1, source_target_pairs={{0,24},{4,28},{8,16},{12,20},{16,8},{20,12},{24,0},{28,4},{1,25},{... | collective-permute-start | bytes 393224 | tf_op jit(solution)/shard_map/ppermute | solution.py:183
  89.9 3.9 %collective-permute-start.42 = (bf16[16,4096]{1,0:T(8,128)(2,1)S(1)}, bf16[16,4096]{1,0:T(8,128)(2,1)S(1)}, u32[]{:S(2)}, u32[]{:S(2)}) collective-permute-start(bf16[16,4096]{1,0:T(8,128)(2,1)S(1)} %collective-permute-done.41), channel_id=1, source_target_pairs={{0,4},{4,0},{8,12},{12,8},{16,20},{20,16},{24,28},{28,24},{1,5},{5... | collective-permute-start | bytes 393224 | tf_op jit(solution)/shard_map/ppermute | solution.py:183
  89.9 4.1 %collective-permute-start.34 = (bf16[16,4096]{1,0:T(8,128)(2,1)S(1)}, bf16[16,4096]{1,0:T(8,128)(2,1)S(1)}, u32[]{:S(2)}, u32[]{:S(2)}) collective-permute-start(bf16[16,4096]{1,0:T(8,128)(2,1)S(1)} %collective-permute-done.33), channel_id=1, source_target_pairs={{0,4},{4,0},{8,12},{12,8},{16,20},{20,16},{24,28},{28,24},{1,5},{5... | collective-permute-start | bytes 393224 | tf_op jit(solution)/shard_map/ppermute | solution.py:183
  90.5 3.5 %collective-permute-start.44 = (bf16[16,4096]{1,0:T(8,128)(2,1)S(1)}, bf16[16,4096]{1,0:T(8,128)(2,1)S(1)}, u32[]{:S(2)}, u32[]{:S(2)}) collective-permute-start(bf16[16,4096]{1,0:T(8,128)(2,1)S(1)} %collective-permute-done.43), channel_id=1, source_target_pairs={{0,4},{4,0},{8,12},{12,8},{16,20},{20,16},{24,28},{28,24},{1,5},{5... | collective-permute-start | bytes 393224 | tf_op jit(solution)/shard_map/ppermute | solution.py:183
  100.0 8.7 %collective-permute-start.47 = (f16[2,8,8,1024]{3,2,1,0:T(8,128)(2,1)S(1)}, f16[2,8,8,1024]{3,2,1,0:T(8,128)(2,1)S(1)}, u32[]{:S(2)}, u32[]{:S(2)}) collective-permute-start(f16[2,8,8,1024]{3,2,1,0:T(8,128)(2,1)S(1)} %fusion.20), channel_id=1, source_target_pairs={{0,1},{1,0},{2,3},{3,2},{4,5},{5,4},{6,7},{7,6},{8,9},{9,8},{10,11... | collective-permute-start | bytes 786440 | tf_op jit(solution)/shard_map/ppermute | solution.py:183
  105.6 6.1 %collective-permute-start.50 = (f16[8,8,1024]{2,1,0:T(8,128)(2,1)S(1)}, f16[8,8,1024]{2,1,0:T(8,128)(2,1)S(1)}, u32[]{:S(2)}, u32[]{:S(2)}) collective-permute-start(f16[8,8,1024]{2,1,0:T(8,128)(2,1)S(1)} %get-tuple-element.34), channel_id=1, source_target_pairs={{0,1},{1,0},{2,3},{3,2},{4,5},{5,4},{6,7},{7,6},{8,9},{9,8},{10,11... | collective-permute-start | bytes 393224 | tf_op jit(solution)/shard_map/ppermute | solution.py:183
  108.7 12.8 %collective-permute-start.48 = (f16[8,8,1024]{2,1,0:T(8,128)(2,1)S(1)}, f16[8,8,1024]{2,1,0:T(8,128)(2,1)S(1)}, u32[]{:S(2)}, u32[]{:S(2)}) collective-permute-start(f16[8,8,1024]{2,1,0:T(8,128)(2,1)S(1)} %fusion.42), channel_id=1, source_target_pairs={{0,2},{1,3},{2,0},{3,1},{4,6},{5,7},{6,4},{7,5},{8,10},{9,11},{10,... | collective-permute-start | bytes 393224 | tf_op jit(solution)/shard_map/ppermute | solution.py:183
  111.8 11.8 %collective-permute-start.51 = (f16[8,8,1024]{2,1,0:T(8,128)(2,1)S(1)}, f16[8,8,1024]{2,1,0:T(8,128)(2,1)S(1)}, u32[]{:S(2)}, u32[]{:S(2)}) collective-permute-start(f16[8,8,1024]{2,1,0:T(8,128)(2,1)S(1)} %fusion.28), channel_id=1, source_target_pairs={{0,2},{1,3},{2,0},{3,1},{4,6},{5,7},{6,4},{7,5},{8,10},{9,11},{10,... | collective-permute-start | bytes 393224 | tf_op jit(solution)/shard_map/ppermute | solution.py:183
  116.1 8.0 %collective-permute-start.49 = (f16[8,8,1024]{2,1,0:T(8,128)(2,1)S(1)}, f16[8,8,1024]{2,1,0:T(8,128)(2,1)S(1)}, u32[]{:S(2)}, u32[]{:S(2)}) collective-permute-start(f16[8,8,1024]{2,1,0:T(8,128)(2,1)S(1)} %get-tuple-element.24), channel_id=1, source_target_pairs={{0,1},{1,0},{2,3},{3,2},{4,5},{5,4},{6,7},{7,6},{8,9},{9,8},{10,11... | collective-permute-start | bytes 393224 | tf_op jit(solution)/shard_map/ppermute | solution.py:183
  124.2 5.0 %collective-permute-start.52 = (bf16[2,8,2048]{2,1,0:T(8,128)(2,1)S(1)}, bf16[2,8,2048]{2,1,0:T(8,128)(2,1)S(1)}, u32[]{:S(2)}, u32[]{:S(2)}) collective-permute-start(bf16[2,8,2048]{2,1,0:T(8,128)(2,1)S(1)} %get-tuple-element.39), channel_id=1, source_target_pairs={{0,8},{4,12},{8,0},{12,4},{16,24},{20,28},{24,16},{28,20},{1,9},{5... | collective-permute-start | bytes 196616 | tf_op jit(solution)/shard_map/ppermute | solution.py:183
  125.7 4.3 %collective-permute-start.53 = (bf16[2,8,2048]{2,1,0:T(8,128)(2,1)S(1)}, bf16[2,8,2048]{2,1,0:T(8,128)(2,1)S(1)}, u32[]{:S(2)}, u32[]{:S(2)}) collective-permute-start(bf16[2,8,2048]{2,1,0:T(8,128)(2,1)S(1)} %get-tuple-element.40), channel_id=1, source_target_pairs={{0,16},{4,20},{8,24},{12,28},{16,0},{20,4},{24,8},{28,12},{1,17},{... | collective-permute-start | bytes 196616 | tf_op jit(solution)/shard_map/ppermute | solution.py:183
  126.6 5.2 %collective-permute-start.54 = (bf16[2,8,2048]{2,1,0:T(8,128)(2,1)S(1)}, bf16[2,8,2048]{2,1,0:T(8,128)(2,1)S(1)}, u32[]{:S(2)}, u32[]{:S(2)}) collective-permute-start(bf16[2,8,2048]{2,1,0:T(8,128)(2,1)S(1)} %get-tuple-element.41), channel_id=1, source_target_pairs={{0,24},{4,28},{8,16},{12,20},{16,8},{20,12},{24,0},{28,4},{1,25},{... | collective-permute-start | bytes 196616 | tf_op jit(solution)/shard_map/ppermute | solution.py:183
  (9 other events, 40.6 us)

commit v8 on v7

--- a/solution.py
+++ b/solution.py
@@ -15,7 +15,7 @@
 
 eps = 1e-05
 theta = 500000.0
-ROOM = 50 * 2**20
+ROOM = 47 * 2**20
 
 
 def rotate(values, position, head_size):
@@ -33,6 +33,7 @@
 
 
 PART = 128
+DEPTH = 1024
 GROUP = 4
 
 
@@ -183,20 +184,23 @@
     return lax.ppermute(block, axis, [(i, i ^ bit) for i in range(count)])
 
 
-def all_rows(block):
+def all_rows(block, also=None):
     if lax.axis_size("gx") != 8:
         pieces = lax.all_gather(block, "gx", axis=0)
         count, rows, width = pieces.shape
-        return pieces.reshape(count, 2, rows // 2, width).transpose(1, 0, 2, 3)
+        return pieces.reshape(count, 2, rows // 2, width).transpose(1, 0, 2, 3), also
     mine = [block] + [swap(block, "gx", chip) for chip in (2, 4, 6)]
+    if also is not None:
+        mine[1], also = lax.optimization_barrier((mine[1], also))
     theirs = [swap(piece, "gx", 1) for piece in mine]
     pieces = [piece for pair in zip(mine, theirs) for piece in pair]
     halves = [piece.reshape(2, 1, -1, block.shape[1]) for piece in pieces]
-    return jnp.concatenate(halves, axis=1)
-
-
-def multiply_kernel(start, far, near, weights, out, held, sems):
+    return jnp.concatenate(halves, axis=1), also
+
+
+def multiply_kernel(start, far, near, head, weights, out, held, sems):
     parts, depth, columns = held.shape
+    ready = 1 if head.shape[0] == depth else 0
 
     def copy(part):
         return pltpu.make_async_copy(
@@ -205,28 +209,32 @@
             sems.at[part],
         )
 
-    def product(part):
-        copy(part).wait()
+    def product(part, block):
         some = pl.ds(part * depth, depth)
         rows = jnp.concatenate([far[:, some], near[:, some]], axis=0)
-        return jnp.dot(rows, held[part], preferred_element_type=jnp.float32)
-
-    for part in range(parts):
+        return jnp.dot(rows, block, preferred_element_type=jnp.float32)
+
+    for part in range(ready, parts):
         copy(part).start()
-    out[...] = product(0)
+    if ready:
+        out[...] = product(0, head[...])
+    else:
+        copy(0).wait()
+        out[...] = product(0, held[0])
 
     @pl.loop(1, parts)
     def _(part):
-        out[...] += product(part)
-
-
-def multiply(far, near, weights, start, columns):
+        copy(part).wait()
+        out[...] += product(part, held[part])
+
+
+def multiply(far, near, head, weights, start, columns):
     half, width = far.shape
-    depth = 1024
+    depth = DEPTH
     vmem = pl.BlockSpec(memory_space=pltpu.VMEM)
     return pl.pallas_call(
         functools.partial(multiply_kernel, start),
-        in_specs=[vmem, vmem, pl.BlockSpec(memory_space=pl.ANY)],
+        in_specs=[vmem, vmem, vmem, pl.BlockSpec(memory_space=pl.ANY)],
         out_specs=vmem,
         out_shape=jax.ShapeDtypeStruct((2 * half, columns), jnp.float32),
         scratch_shapes=[
@@ -239,7 +247,7 @@
             bytes_accessed=2 * width * columns,
             transcendentals=0,
         ),
-    )(far, near, weights)
+    )(far, near, head, weights)
 
 
 def project(rows, weights, scale):
@@ -257,19 +265,21 @@
 
     near, far, last = (swap(features(here ^ bit), "gy", bit) for bit in (1, 2, 3))
     near = jnp.concatenate([features(here), near])
-    far = all_rows(jnp.concatenate([far, last]))
-    near = all_rows(near)
+    first = columns // 512 * 256 if columns % 256 == 0 else columns
+    head = weights[:DEPTH, :first]
+    none = jnp.zeros((16, 128), weights.dtype)
+    far = all_rows(jnp.concatenate([far, last]))[0]
+    near, head = all_rows(near, head)
     shape = (2, 2) + far.shape[1:3]
     far = far.reshape(-1, width)
     near = near.reshape(-1, width)
-    first = columns // 512 * 256 if columns % 256 == 0 else columns
-    left = multiply(far, near, weights, 0, first).reshape(shape + (first,))
+    left = multiply(far, near, head, weights, 0, first).reshape(shape + (first,))
     go_left = pack(left[:, 1])
     go_left, far, near = lax.optimization_barrier((go_left, far, near))
     left = left[:, 0] + send(go_left, 1)
     if first == columns:
         return [left[1] + send(pack(left[0]), 2)]
-    right = multiply(far, near, weights, first, columns - first)
+    right = multiply(far, near, none, weights, first, columns - first)
     right = right.reshape(shape + (columns - first,))
     go_far = pack(right[0, 1])
     across, go_near = lax.optimization_barrier((pack(left[0]), pack(right[1, 1])))

time: 134 us -> 137 us (1.022)
  starting transfers between devices: 58.3 us -> 52.5 us
  waiting for transfers between devices: 43.4 us -> 49.1 us
  local copies, waits for them, and re-layouts: 0.68 us -> 4.22 us
  Pallas kernels: 24.9 us -> 23.4 us
    ppermute x56, starting transfers between devices: 58.3 us -> 52.5 us  [swap(): return lax.ppermute(block, axis, [(i, i ^ bit) for i in range(count)])]
    ppermute x56, waiting for transfers between devices: 43.4 us -> 49.1 us  [swap(): return lax.ppermute(block, axis, [(i, i ^ bit) for i in range(count)])]
    slice x0 -> x2, local copies, waits for them, and re-layouts: none -> 3.53 us  [project(): head = weights[:DEPTH, :first]]
  transfers between devices with their start and end apart: 56 -> 56, of which waited for: 27 -> 27; matrix products, arithmetic and copies ran while one was open for 1% -> 4% of each run, Pallas kernels for 8% -> 7%
where the time goes in v8:
time: 137 us; the launch traced here: 136 us
  starting transfers between devices  52.5 us (38%)
  waiting for transfers between devices  49.1 us (36%)
  Pallas kernels  23.4 us (17%)
  other arithmetic  6.01 us (4%)
  local copies, waits for them, and re-layouts  4.22 us (3%)
    ppermute x56, starting transfers between devices, swap(): return lax.ppermute(block, axis, [(i, i ^ bit) for i in range(count)])  52.5 us
    ppermute x56, waiting for transfers between devices, swap(): return lax.ppermute(block, axis, [(i, i ^ bit) for i in range(count)])  49.1 us
    pallas_call x4, Pallas kernels, multiply(): pl.pallas_call(functools.partial(multiply_kernel, start), in_specs=[vmem,...  18.3 us
    pallas_call x1, Pallas kernels, attend_local(): pl.pallas_call(attend_kernel, in_specs=[pl.BlockSpec(memory_space=pltpu.S...  5.18 us
    slice x2, local copies, waits for them, and re-layouts, project(): head = weights[:DEPTH, :first]  3.53 us
  transfers between devices with their start and end apart: 56, of which 27 were waited for; matrix products, arithmetic and copies ran while one was open for 4% of the time, Pallas kernels for 7%

profile of v8, /device:TPU:0, one launch (start us, length us, event | category | flops | bytes accessed | tf_op | source)
XLA Modules:
  0.0 136.2 jit_solution(13572078379559593193)
XLA Ops:
  0.0 1.2 fusion
  1.2 1.1 fusion.2
  2.3 3.1 %collective-permute-start.9 = (bf16[8,4096]{1,0:T(8,128)(2,1)S(1)}, bf16[8,4096]{1,0:T(8,128)(2,1)S(1)}, u32[]{:S(2)}, u32[]{:S(2)}) collective-permute-start(bf16[8,4096]{1,0:T(8,128)(2,1)S(1)} %get-tuple-element.55), channel_id=1, source_target_pairs={{0,1},{1,0},{2,3},{3,2},{4,5},{5,4},{6,7},{7,6},{8,9},{9,8},{10,11... | collective-permute-start | bytes 196616 | tf_op jit(solution)/shard_map/ppermute | solution.py:184
  5.4 2.6 %collective-permute-start = (bf16[8,4096]{1,0:T(8,128)(2,1)S(1)}, bf16[8,4096]{1,0:T(8,128)(2,1)S(1)}, u32[]{:S(2)}, u32[]{:S(2)}) collective-permute-start(bf16[8,4096]{1,0:T(8,128)(2,1)S(1)} %get-tuple-element.57), channel_id=1, source_target_pairs={{0,2},{1,3},{2,0},{3,1},{4,6},{5,7},{6,4},{7,5},{8,10},{9,11},{10,... | collective-permute-start | bytes 196616 | tf_op jit(solution)/shard_map/ppermute | solution.py:184
  8.8 1.8 %slice.183.head = bf16[1024,1024]{1,0:T(8,128)(2,1)S(1)} slice(bf16[4096,2304]{1,0:T(8,128)(2,1)} %weights.5), slice={[0:1024], [0:1024]} | slice | bytes 4194304 | tf_op jit(solution)/shard_map/slice | solution.py:269
  10.8 1.8 %collective-permute-start.11 = (bf16[16,4096]{1,0:T(8,128)(2,1)S(1)}, bf16[16,4096]{1,0:T(8,128)(2,1)S(1)}, u32[]{:S(2)}, u32[]{:S(2)}) collective-permute-start(bf16[16,4096]{1,0:T(8,128)(2,1)S(1)} %pad_maximum_fusion.3), channel_id=1, source_target_pairs={{0,8},{4,12},{8,0},{12,4},{16,24},{20,28},{24,16},{28,20},{1,9},{5... | collective-permute-start | bytes 393224 | tf_op jit(solution)/shard_map/ppermute | solution.py:184
  12.5 1.5 %collective-permute-start.13 = (bf16[16,4096]{1,0:T(8,128)(2,1)S(1)}, bf16[16,4096]{1,0:T(8,128)(2,1)S(1)}, u32[]{:S(2)}, u32[]{:S(2)}) collective-permute-start(bf16[16,4096]{1,0:T(8,128)(2,1)S(1)} %pad_maximum_fusion.3), channel_id=1, source_target_pairs={{0,16},{4,20},{8,24},{12,28},{16,0},{20,4},{24,8},{28,12},{1,17},{... | collective-permute-start | bytes 393224 | tf_op jit(solution)/shard_map/ppermute | solution.py:184
  14.1 1.1 collective-permute-start.15
  15.3 1.5 %collective-permute-done.11 = bf16[16,4096]{1,0:T(8,128)(2,1)S(1)} collective-permute-done((bf16[16,4096]{1,0:T(8,128)(2,1)S(1)}, bf16[16,4096]{1,0:T(8,128)(2,1)S(1)}, u32[]{:S(2)}, u32[]{:S(2)}) %collective-permute-start.11) | collective-permute-done | bytes 131104 | tf_op jit(solution)/shard_map/ppermute | solution.py:184
  16.8 2.0 %collective-permute-start.3 = (bf16[16,4096]{1,0:T(8,128)(2,1)S(1)}, bf16[16,4096]{1,0:T(8,128)(2,1)S(1)}, u32[]{:S(2)}, u32[]{:S(2)}) collective-permute-start(bf16[16,4096]{1,0:T(8,128)(2,1)S(1)} %constant_dynamic-update-slice_fusion), channel_id=1, source_target_pairs={{0,8},{4,12},{8,0},{12,4},{16,24},{20,28},{24,16},{28,20},{1,9},{5... | collective-permute-start | bytes 393224 | tf_op jit(solution)/shard_map/ppermute | solution.py:184
  18.8 1.5 %collective-permute-start.5 = (bf16[16,4096]{1,0:T(8,128)(2,1)S(1)}, bf16[16,4096]{1,0:T(8,128)(2,1)S(1)}, u32[]{:S(2)}, u32[]{:S(2)}) collective-permute-start(bf16[16,4096]{1,0:T(8,128)(2,1)S(1)} %constant_dynamic-update-slice_fusion), channel_id=1, source_target_pairs={{0,16},{4,20},{8,24},{12,28},{16,0},{20,4},{24,8},{28,12},{1,17},{... | collective-permute-start | bytes 393224 | tf_op jit(solution)/shard_map/ppermute | solution.py:184
  20.5 2.5 %collective-permute-done.3 = bf16[16,4096]{1,0:T(8,128)(2,1)S(1)} collective-permute-done((bf16[16,4096]{1,0:T(8,128)(2,1)S(1)}, bf16[16,4096]{1,0:T(8,128)(2,1)S(1)}, u32[]{:S(2)}, u32[]{:S(2)}) %collective-permute-start.3) | collective-permute-done | bytes 131104 | tf_op jit(solution)/shard_map/ppermute | solution.py:184
  23.7 2.9 %collective-permute-done.5 = bf16[16,4096]{1,0:T(8,128)(2,1)S(1)} collective-permute-done((bf16[16,4096]{1,0:T(8,128)(2,1)S(1)}, bf16[16,4096]{1,0:T(8,128)(2,1)S(1)}, u32[]{:S(2)}, u32[]{:S(2)}) %collective-permute-start.5) | collective-permute-done | bytes 131104 | tf_op jit(solution)/shard_map/ppermute | solution.py:184
  28.5 4.3 %shard_map.73 = f32[256,1024]{1,0:T(8,128)S(1)} custom-call(bf16[128,4096]{1,0:T(8,128)(2,1)S(1)} %bitcast.265, bf16[128,4096]{1,0:T(8,128)(2,1)S(1)} %bitcast.267, bf16[1024,1024]{1,0:T(8,128)(2,1)S(1)} %slice.183.head, bf16[4096,2304]{1,0:T(8,128)(2,1)} %weights.5), custom_call_target="tpu_custom_call" | custom-call | flops 2147483648 | bytes 8388608 | tf_op jit(solution)/shard_map/pallas_call | solution.py:235
  33.6 5.2 %shard_map.74 = f32[256,1280]{1,0:T(8,128)S(1)} custom-call(bf16[128,4096]{1,0:T(8,128)(2,1)S(1)} %bitcast.266, bf16[128,4096]{1,0:T(8,128)(2,1)S(1)} %bitcast.268, bf16[16,128]{1,0:T(8,128)(2,1)S(1)} %broadcast_57_head.2.head, bf16[4096,2304]{1,0:T(8,128)(2,1)} %weights.5), custom_call_target="tpu_custom_call" | custom-call | flops 2684354560 | bytes 10485760 | tf_op jit(solution)/shard_map/pallas_call | solution.py:235
  38.9 1.4 %collective-permute-start.24 = (f16[8,8,1280]{2,1,0:T(8,128)(2,1)S(1)}, f16[8,8,1280]{2,1,0:T(8,128)(2,1)S(1)}, u32[]{:S(2)}, u32[]{:S(2)}) collective-permute-start(f16[8,8,1280]{2,1,0:T(8,128)(2,1)S(1)} %get-tuple-element.40), channel_id=1, source_target_pairs={{0,1},{1,0},{2,3},{3,2},{4,5},{5,4},{6,7},{7,6},{8,9},{9,8},{10,11... | collective-permute-start | bytes 491528 | tf_op jit(solution)/shard_map/ppermute | solution.py:184
  41.4 2.5 %collective-permute-start.18 = (f16[8,8,1024]{2,1,0:T(8,128)(2,1)S(1)}, f16[8,8,1024]{2,1,0:T(8,128)(2,1)S(1)}, u32[]{:S(2)}, u32[]{:S(2)}) collective-permute-start(f16[8,8,1024]{2,1,0:T(8,128)(2,1)S(1)} %fusion.41), channel_id=1, source_target_pairs={{0,2},{1,3},{2,0},{3,1},{4,6},{5,7},{6,4},{7,5},{8,10},{9,11},{10,... | collective-permute-start | bytes 393224 | tf_op jit(solution)/shard_map/ppermute | solution.py:184
  43.9 3.7 %collective-permute-done.24 = f16[8,8,1280]{2,1,0:T(8,128)(2,1)S(1)} collective-permute-done((f16[8,8,1280]{2,1,0:T(8,128)(2,1)S(1)}, f16[8,8,1280]{2,1,0:T(8,128)(2,1)S(1)}, u32[]{:S(2)}, u32[]{:S(2)}) %collective-permute-start.24) | collective-permute-done | bytes 163872 | tf_op jit(solution)/shard_map/ppermute | solution.py:184
  47.7 1.9 %collective-permute-start.25 = (f16[8,8,1280]{2,1,0:T(8,128)(2,1)S(1)}, f16[8,8,1280]{2,1,0:T(8,128)(2,1)S(1)}, u32[]{:S(2)}, u32[]{:S(2)}) collective-permute-start(f16[8,8,1280]{2,1,0:T(8,128)(2,1)S(1)} %fusion.14), channel_id=1, source_target_pairs={{0,2},{1,3},{2,0},{3,1},{4,6},{5,7},{6,4},{7,5},{8,10},{9,11},{10,... | collective-permute-start | bytes 491528 | tf_op jit(solution)/shard_map/ppermute | solution.py:184
  50.6 1.2 collective-permute-start.20
  51.7 1.5 %collective-permute-start.21 = (bf16[2,8,1024]{2,1,0:T(8,128)(2,1)S(1)}, bf16[2,8,1024]{2,1,0:T(8,128)(2,1)S(1)}, u32[]{:S(2)}, u32[]{:S(2)}) collective-permute-start(bf16[2,8,1024]{2,1,0:T(8,128)(2,1)S(1)} %get-tuple-element.66), channel_id=1, source_target_pairs={{0,24},{4,28},{8,16},{12,20},{16,8},{20,12},{24,0},{28,4},{1,25},{... | collective-permute-start | bytes 98312 | tf_op jit(solution)/shard_map/ppermute | solution.py:184
  53.3 4.3 %collective-permute-done.25 = f16[8,8,1280]{2,1,0:T(8,128)(2,1)S(1)} collective-permute-done((f16[8,8,1280]{2,1,0:T(8,128)(2,1)S(1)}, f16[8,8,1280]{2,1,0:T(8,128)(2,1)S(1)}, u32[]{:S(2)}, u32[]{:S(2)}) %collective-permute-start.25) | collective-permute-done | bytes 163872 | tf_op jit(solution)/shard_map/ppermute | solution.py:184
  60.3 1.5 %collective-permute-start.28 = (bf16[2,8,1280]{2,1,0:T(8,128)(2,1)S(1)}, bf16[2,8,1280]{2,1,0:T(8,128)(2,1)S(1)}, u32[]{:S(2)}, u32[]{:S(2)}) collective-permute-start(bf16[2,8,1280]{2,1,0:T(8,128)(2,1)S(1)} %get-tuple-element.61), channel_id=1, source_target_pairs={{0,24},{4,28},{8,16},{12,20},{16,8},{20,12},{24,0},{28,4},{1,25},{... | collective-permute-start | bytes 122888 | tf_op jit(solution)/shard_map/ppermute | solution.py:184
  63.4 1.8 %collective-permute-done.28 = bf16[2,8,1280]{2,1,0:T(8,128)(2,1)S(1)} collective-permute-done((bf16[2,8,1280]{2,1,0:T(8,128)(2,1)S(1)}, bf16[2,8,1280]{2,1,0:T(8,128)(2,1)S(1)}, u32[]{:S(2)}, u32[]{:S(2)}) %collective-permute-start.28) | collective-permute-done | bytes 40992 | tf_op jit(solution)/shard_map/ppermute | solution.py:184
  65.3 1.2 collective-permute-done.29
  67.5 5.2 %shard_map.75 = bf16[8,128,128]{2,1,0:T(8,128)(2,1)S(1)} custom-call(s32[8]{0:T(128)S(1)} %copy-done, bf16[8,128,128]{2,1,0:T(8,128)(2,1)S(1)} %pad_maximum_fusion.query, bf16[8,8,128]{2,1,0:T(8,128)(2,1)S(1)} %pad_maximum_fusion.8.key_new, f32[8,8,128]{2,1,0:T(8,128)S(1)} %get-tuple-element.92.value_new, bf16[8,512,1024]{2,1,0:T(8,128)(2,1)} %k_cache.1, ...), custom_call_target="tpu_custom_call" | custom-call | flops 2147483648 | bytes 8388608 | tf_op jit(solution)/shard_map/pallas_call | solution.py:154
  73.4 1.8 %slice.221.head = bf16[1024,1024]{1,0:T(8,128)(2,1)S(1)} slice(bf16[4096,2048]{1,0:T(8,128)(2,1)} %weights.7), slice={[0:1024], [0:1024]} | slice | bytes 4194304 | tf_op jit(solution)/shard_map/slice | solution.py:269
  75.1 4.8 %collective-permute-start.30 = (bf16[8,4096]{1,0:T(8,128)(2,1)S(1)}, bf16[8,4096]{1,0:T(8,128)(2,1)S(1)}, u32[]{:S(2)}, u32[]{:S(2)}) collective-permute-start(bf16[8,4096]{1,0:T(8,128)(2,1)S(1)} %get-tuple-element.53), channel_id=1, source_target_pairs={{0,2},{1,3},{2,0},{3,1},{4,6},{5,7},{6,4},{7,5},{8,10},{9,11},{10,... | collective-permute-start | bytes 196616 | tf_op jit(solution)/shard_map/ppermute | solution.py:184
  80.0 1.2 collective-permute-start.41
  81.2 1.2 collective-permute-start.40
  83.3 3.1 %collective-permute-start.45 = (bf16[16,4096]{1,0:T(8,128)(2,1)S(1)}, bf16[16,4096]{1,0:T(8,128)(2,1)S(1)}, u32[]{:S(2)}, u32[]{:S(2)}) collective-permute-start(bf16[16,4096]{1,0:T(8,128)(2,1)S(1)} %pad_maximum_fusion.5), channel_id=1, source_target_pairs={{0,24},{4,28},{8,16},{12,20},{16,8},{20,12},{24,0},{28,4},{1,25},{... | collective-permute-start | bytes 393224 | tf_op jit(solution)/shard_map/ppermute | solution.py:184
  87.2 1.5 %collective-permute-start.35 = (bf16[16,4096]{1,0:T(8,128)(2,1)S(1)}, bf16[16,4096]{1,0:T(8,128)(2,1)S(1)}, u32[]{:S(2)}, u32[]{:S(2)}) collective-permute-start(bf16[16,4096]{1,0:T(8,128)(2,1)S(1)} %constant_dynamic-update-slice_fusion.10), channel_id=1, source_target_pairs={{0,16},{4,20},{8,24},{12,28},{16,0},{20,4},{24,8},{28,12},{1,17},{... | collective-permute-start | bytes 393224 | tf_op jit(solution)/shard_map/ppermute | solution.py:184
  88.8 1.4 %collective-permute-start.37 = (bf16[16,4096]{1,0:T(8,128)(2,1)S(1)}, bf16[16,4096]{1,0:T(8,128)(2,1)S(1)}, u32[]{:S(2)}, u32[]{:S(2)}) collective-permute-start(bf16[16,4096]{1,0:T(8,128)(2,1)S(1)} %constant_dynamic-update-slice_fusion.10), channel_id=1, source_target_pairs={{0,24},{4,28},{8,16},{12,20},{16,8},{20,12},{24,0},{28,4},{1,25},{... | collective-permute-start | bytes 393224 | tf_op jit(solution)/shard_map/ppermute | solution.py:184
  90.2 3.6 %collective-permute-done.33 = bf16[16,4096]{1,0:T(8,128)(2,1)S(1)} collective-permute-done((bf16[16,4096]{1,0:T(8,128)(2,1)S(1)}, bf16[16,4096]{1,0:T(8,128)(2,1)S(1)}, u32[]{:S(2)}, u32[]{:S(2)}) %collective-permute-start.33) | collective-permute-done | bytes 131104 | tf_op jit(solution)/shard_map/ppermute | solution.py:184
  95.3 1.4 %collective-permute-done.37 = bf16[16,4096]{1,0:T(8,128)(2,1)S(1)} collective-permute-done((bf16[16,4096]{1,0:T(8,128)(2,1)S(1)}, bf16[16,4096]{1,0:T(8,128)(2,1)S(1)}, u32[]{:S(2)}, u32[]{:S(2)}) %collective-permute-start.37) | collective-permute-done | bytes 131104 | tf_op jit(solution)/shard_map/ppermute | solution.py:184
  98.3 4.3 %shard_map.76 = f32[256,1024]{1,0:T(8,128)S(1)} custom-call(bf16[128,4096]{1,0:T(8,128)(2,1)S(1)} %bitcast.269, bf16[128,4096]{1,0:T(8,128)(2,1)S(1)} %bitcast.271, bf16[1024,1024]{1,0:T(8,128)(2,1)S(1)} %slice.221.head, bf16[4096,2048]{1,0:T(8,128)(2,1)} %weights.7), custom_call_target="tpu_custom_call" | custom-call | flops 2147483648 | bytes 8388608 | tf_op jit(solution)/shard_map/pallas_call | solution.py:235
  103.7 4.5 %shard_map.77 = f32[256,1024]{1,0:T(8,128)S(1)} custom-call(bf16[128,4096]{1,0:T(8,128)(2,1)S(1)} %bitcast.270, bf16[128,4096]{1,0:T(8,128)(2,1)S(1)} %bitcast.272, bf16[16,128]{1,0:T(8,128)(2,1)S(1)} %broadcast_57_head.2.head, bf16[4096,2048]{1,0:T(8,128)(2,1)} %weights.7), custom_call_target="tpu_custom_call" | custom-call | flops 2147483648 | bytes 8388608 | tf_op jit(solution)/shard_map/pallas_call | solution.py:235
  108.2 1.2 collective-permute-start.50
  109.4 2.3 %collective-permute-done.47 = f16[2,8,8,1024]{3,2,1,0:T(8,128)(2,1)S(1)} collective-permute-done((f16[2,8,8,1024]{3,2,1,0:T(8,128)(2,1)S(1)}, f16[2,8,8,1024]{3,2,1,0:T(8,128)(2,1)S(1)}, u32[]{:S(2)}, u32[]{:S(2)}) %collective-permute-start.47) | collective-permute-done | bytes 262176 | tf_op jit(solution)/shard_map/ppermute | solution.py:184
  112.0 2.1 %collective-permute-done.50 = f16[8,8,1024]{2,1,0:T(8,128)(2,1)S(1)} collective-permute-done((f16[8,8,1024]{2,1,0:T(8,128)(2,1)S(1)}, f16[8,8,1024]{2,1,0:T(8,128)(2,1)S(1)}, u32[]{:S(2)}, u32[]{:S(2)}) %collective-permute-start.50) | collective-permute-done | bytes 131104 | tf_op jit(solution)/shard_map/ppermute | solution.py:184
  114.1 1.0 collective-permute-start.51
  115.2 1.3 collective-permute-start.49
  116.5 6.7 %collective-permute-done.48 = f16[8,8,1024]{2,1,0:T(8,128)(2,1)S(1)} collective-permute-done((f16[8,8,1024]{2,1,0:T(8,128)(2,1)S(1)}, f16[8,8,1024]{2,1,0:T(8,128)(2,1)S(1)}, u32[]{:S(2)}, u32[]{:S(2)}) %collective-permute-start.48) | collective-permute-done | bytes 131104 | tf_op jit(solution)/shard_map/ppermute | solution.py:184
  123.2 2.5 %collective-permute-done.51 = f16[8,8,1024]{2,1,0:T(8,128)(2,1)S(1)} collective-permute-done((f16[8,8,1024]{2,1,0:T(8,128)(2,1)S(1)}, f16[8,8,1024]{2,1,0:T(8,128)(2,1)S(1)}, u32[]{:S(2)}, u32[]{:S(2)}) %collective-permute-start.51) | collective-permute-done | bytes 131104 | tf_op jit(solution)/shard_map/ppermute | solution.py:184
  125.8 1.9 %collective-permute-start.52 = (bf16[2,8,2048]{2,1,0:T(8,128)(2,1)S(1)}, bf16[2,8,2048]{2,1,0:T(8,128)(2,1)S(1)}, u32[]{:S(2)}, u32[]{:S(2)}) collective-permute-start(bf16[2,8,2048]{2,1,0:T(8,128)(2,1)S(1)} %get-tuple-element.47), channel_id=1, source_target_pairs={{0,8},{4,12},{8,0},{12,4},{16,24},{20,28},{24,16},{28,20},{1,9},{5... | collective-permute-start | bytes 196616 | tf_op jit(solution)/shard_map/ppermute | solution.py:184
  130.2 2.5 %collective-permute-done.53 = bf16[2,8,2048]{2,1,0:T(8,128)(2,1)S(1)} collective-permute-done((bf16[2,8,2048]{2,1,0:T(8,128)(2,1)S(1)}, bf16[2,8,2048]{2,1,0:T(8,128)(2,1)S(1)}, u32[]{:S(2)}, u32[]{:S(2)}) %collective-permute-start.53) | collective-permute-done | bytes 65568 | tf_op jit(solution)/shard_map/ppermute | solution.py:184
  132.7 1.1 collective-permute-done.54
  133.9 1.3 collective-permute-done.55
  (187 shorter events, 21.9 us)
Async XLA Ops:
  2.3 8.3 %collective-permute-start.9 = (bf16[8,4096]{1,0:T(8,128)(2,1)S(1)}, bf16[8,4096]{1,0:T(8,128)(2,1)S(1)}, u32[]{:S(2)}, u32[]{:S(2)}) collective-permute-start(bf16[8,4096]{1,0:T(8,128)(2,1)S(1)} %get-tuple-element.55), channel_id=1, source_target_pairs={{0,1},{1,0},{2,3},{3,2},{4,5},{5,4},{6,7},{7,6},{8,9},{9,8},{10,11... | collective-permute-start | bytes 196616 | tf_op jit(solution)/shard_map/ppermute | solution.py:184
  5.4 8.6 %collective-permute-start = (bf16[8,4096]{1,0:T(8,128)(2,1)S(1)}, bf16[8,4096]{1,0:T(8,128)(2,1)S(1)}, u32[]{:S(2)}, u32[]{:S(2)}) collective-permute-start(bf16[8,4096]{1,0:T(8,128)(2,1)S(1)} %get-tuple-element.57), channel_id=1, source_target_pairs={{0,2},{1,3},{2,0},{3,1},{4,6},{5,7},{6,4},{7,5},{8,10},{9,11},{10,... | collective-permute-start | bytes 196616 | tf_op jit(solution)/shard_map/ppermute | solution.py:184
  8.0 7.1 %collective-permute-start.1 = (bf16[8,4096]{1,0:T(8,128)(2,1)S(1)}, bf16[8,4096]{1,0:T(8,128)(2,1)S(1)}, u32[]{:S(2)}, u32[]{:S(2)}) collective-permute-start(bf16[8,4096]{1,0:T(8,128)(2,1)S(1)} %get-tuple-element.56), channel_id=1, source_target_pairs={{0,3},{1,2},{2,1},{3,0},{4,7},{5,6},{6,5},{7,4},{8,11},{9,10},{10,... | collective-permute-start | bytes 196616 | tf_op jit(solution)/shard_map/ppermute | solution.py:184
  10.7 8.2 %collective-permute-start.10 = (bf16[16,4096]{1,0:T(8,128)(2,1)S(1)}, bf16[16,4096]{1,0:T(8,128)(2,1)S(1)}, u32[]{:S(2)}, u32[]{:S(2)}) collective-permute-start(bf16[16,4096]{1,0:T(8,128)(2,1)S(1)} %pad_maximum_fusion.3), channel_id=1, source_target_pairs={{0,4},{4,0},{8,12},{12,8},{16,20},{20,16},{24,28},{28,24},{1,5},{5... | collective-permute-start | bytes 393224 | tf_op jit(solution)/shard_map/ppermute | solution.py:184
  10.8 6.0 %collective-permute-start.11 = (bf16[16,4096]{1,0:T(8,128)(2,1)S(1)}, bf16[16,4096]{1,0:T(8,128)(2,1)S(1)}, u32[]{:S(2)}, u32[]{:S(2)}) collective-permute-start(bf16[16,4096]{1,0:T(8,128)(2,1)S(1)} %pad_maximum_fusion.3), channel_id=1, source_target_pairs={{0,8},{4,12},{8,0},{12,4},{16,24},{20,28},{24,16},{28,20},{1,9},{5... | collective-permute-start | bytes 393224 | tf_op jit(solution)/shard_map/ppermute | solution.py:184
  12.5 10.5 %collective-permute-start.13 = (bf16[16,4096]{1,0:T(8,128)(2,1)S(1)}, bf16[16,4096]{1,0:T(8,128)(2,1)S(1)}, u32[]{:S(2)}, u32[]{:S(2)}) collective-permute-start(bf16[16,4096]{1,0:T(8,128)(2,1)S(1)} %pad_maximum_fusion.3), channel_id=1, source_target_pairs={{0,16},{4,20},{8,24},{12,28},{16,0},{20,4},{24,8},{28,12},{1,17},{... | collective-permute-start | bytes 393224 | tf_op jit(solution)/shard_map/ppermute | solution.py:184
  14.1 9.5 %collective-permute-start.15 = (bf16[16,4096]{1,0:T(8,128)(2,1)S(1)}, bf16[16,4096]{1,0:T(8,128)(2,1)S(1)}, u32[]{:S(2)}, u32[]{:S(2)}) collective-permute-start(bf16[16,4096]{1,0:T(8,128)(2,1)S(1)} %pad_maximum_fusion.3), channel_id=1, source_target_pairs={{0,24},{4,28},{8,16},{12,20},{16,8},{20,12},{24,0},{28,4},{1,25},{... | collective-permute-start | bytes 393224 | tf_op jit(solution)/shard_map/ppermute | solution.py:184
  15.2 5.2 %collective-permute-start.2 = (bf16[16,4096]{1,0:T(8,128)(2,1)S(1)}, bf16[16,4096]{1,0:T(8,128)(2,1)S(1)}, u32[]{:S(2)}, u32[]{:S(2)}) collective-permute-start(bf16[16,4096]{1,0:T(8,128)(2,1)S(1)} %constant_dynamic-update-slice_fusion), channel_id=1, source_target_pairs={{0,4},{4,0},{8,12},{12,8},{16,20},{20,16},{24,28},{28,24},{1,5},{5... | collective-permute-start | bytes 393224 | tf_op jit(solution)/shard_map/ppermute | solution.py:184
  16.8 6.2 %collective-permute-start.3 = (bf16[16,4096]{1,0:T(8,128)(2,1)S(1)}, bf16[16,4096]{1,0:T(8,128)(2,1)S(1)}, u32[]{:S(2)}, u32[]{:S(2)}) collective-permute-start(bf16[16,4096]{1,0:T(8,128)(2,1)S(1)} %constant_dynamic-update-slice_fusion), channel_id=1, source_target_pairs={{0,8},{4,12},{8,0},{12,4},{16,24},{20,28},{24,16},{28,20},{1,9},{5... | collective-permute-start | bytes 393224 | tf_op jit(solution)/shard_map/ppermute | solution.py:184
  18.8 7.8 %collective-permute-start.5 = (bf16[16,4096]{1,0:T(8,128)(2,1)S(1)}, bf16[16,4096]{1,0:T(8,128)(2,1)S(1)}, u32[]{:S(2)}, u32[]{:S(2)}) collective-permute-start(bf16[16,4096]{1,0:T(8,128)(2,1)S(1)} %constant_dynamic-update-slice_fusion), channel_id=1, source_target_pairs={{0,16},{4,20},{8,24},{12,28},{16,0},{20,4},{24,8},{28,12},{1,17},{... | collective-permute-start | bytes 393224 | tf_op jit(solution)/shard_map/ppermute | solution.py:184
  20.4 6.2 %collective-permute-start.7 = (bf16[16,4096]{1,0:T(8,128)(2,1)S(1)}, bf16[16,4096]{1,0:T(8,128)(2,1)S(1)}, u32[]{:S(2)}, u32[]{:S(2)}) collective-permute-start(bf16[16,4096]{1,0:T(8,128)(2,1)S(1)} %constant_dynamic-update-slice_fusion), channel_id=1, source_target_pairs={{0,24},{4,28},{8,16},{12,20},{16,8},{20,12},{24,0},{28,4},{1,25},{... | collective-permute-start | bytes 393224 | tf_op jit(solution)/shard_map/ppermute | solution.py:184
  23.0 4.2 %collective-permute-start.12 = (bf16[16,4096]{1,0:T(8,128)(2,1)S(1)}, bf16[16,4096]{1,0:T(8,128)(2,1)S(1)}, u32[]{:S(2)}, u32[]{:S(2)}) collective-permute-start(bf16[16,4096]{1,0:T(8,128)(2,1)S(1)} %collective-permute-done.11), channel_id=1, source_target_pairs={{0,4},{4,0},{8,12},{12,8},{16,20},{20,16},{24,28},{28,24},{1,5},{5... | collective-permute-start | bytes 393224 | tf_op jit(solution)/shard_map/ppermute | solution.py:184
  23.0 4.3 %collective-permute-start.4 = (bf16[16,4096]{1,0:T(8,128)(2,1)S(1)}, bf16[16,4096]{1,0:T(8,128)(2,1)S(1)}, u32[]{:S(2)}, u32[]{:S(2)}) collective-permute-start(bf16[16,4096]{1,0:T(8,128)(2,1)S(1)} %collective-permute-done.3), channel_id=1, source_target_pairs={{0,4},{4,0},{8,12},{12,8},{16,20},{20,16},{24,28},{28,24},{1,5},{5... | collective-permute-start | bytes 393224 | tf_op jit(solution)/shard_map/ppermute | solution.py:184
  23.6 3.7 %collective-permute-start.14 = (bf16[16,4096]{1,0:T(8,128)(2,1)S(1)}, bf16[16,4096]{1,0:T(8,128)(2,1)S(1)}, u32[]{:S(2)}, u32[]{:S(2)}) collective-permute-start(bf16[16,4096]{1,0:T(8,128)(2,1)S(1)} %collective-permute-done.13), channel_id=1, source_target_pairs={{0,4},{4,0},{8,12},{12,8},{16,20},{20,16},{24,28},{28,24},{1,5},{5... | collective-permute-start | bytes 393224 | tf_op jit(solution)/shard_map/ppermute | solution.py:184
  32.8 8.5 %collective-permute-start.17 = (f16[2,8,8,1024]{3,2,1,0:T(8,128)(2,1)S(1)}, f16[2,8,8,1024]{3,2,1,0:T(8,128)(2,1)S(1)}, u32[]{:S(2)}, u32[]{:S(2)}) collective-permute-start(f16[2,8,8,1024]{3,2,1,0:T(8,128)(2,1)S(1)} %fusion.19), channel_id=1, source_target_pairs={{0,1},{1,0},{2,3},{3,2},{4,5},{5,4},{6,7},{7,6},{8,9},{9,8},{10,11... | collective-permute-start | bytes 786440 | tf_op jit(solution)/shard_map/ppermute | solution.py:184
  38.9 8.8 %collective-permute-start.24 = (f16[8,8,1280]{2,1,0:T(8,128)(2,1)S(1)}, f16[8,8,1280]{2,1,0:T(8,128)(2,1)S(1)}, u32[]{:S(2)}, u32[]{:S(2)}) collective-permute-start(f16[8,8,1280]{2,1,0:T(8,128)(2,1)S(1)} %get-tuple-element.40), channel_id=1, source_target_pairs={{0,1},{1,0},{2,3},{3,2},{4,5},{5,4},{6,7},{7,6},{8,9},{9,8},{10,11... | collective-permute-start | bytes 491528 | tf_op jit(solution)/shard_map/ppermute | solution.py:184
  41.4 8.2 %collective-permute-start.18 = (f16[8,8,1024]{2,1,0:T(8,128)(2,1)S(1)}, f16[8,8,1024]{2,1,0:T(8,128)(2,1)S(1)}, u32[]{:S(2)}, u32[]{:S(2)}) collective-permute-start(f16[8,8,1024]{2,1,0:T(8,128)(2,1)S(1)} %fusion.41), channel_id=1, source_target_pairs={{0,2},{1,3},{2,0},{3,1},{4,6},{5,7},{6,4},{7,5},{8,10},{9,11},{10,... | collective-permute-start | bytes 393224 | tf_op jit(solution)/shard_map/ppermute | solution.py:184
  47.7 9.9 %collective-permute-start.25 = (f16[8,8,1280]{2,1,0:T(8,128)(2,1)S(1)}, f16[8,8,1280]{2,1,0:T(8,128)(2,1)S(1)}, u32[]{:S(2)}, u32[]{:S(2)}) collective-permute-start(f16[8,8,1280]{2,1,0:T(8,128)(2,1)S(1)} %fusion.14), channel_id=1, source_target_pairs={{0,2},{1,3},{2,0},{3,1},{4,6},{5,7},{6,4},{7,5},{8,10},{9,11},{10,... | collective-permute-start | bytes 491528 | tf_op jit(solution)/shard_map/ppermute | solution.py:184
  49.6 8.5 %collective-permute-start.23 = (f16[8,8,1280]{2,1,0:T(8,128)(2,1)S(1)}, f16[8,8,1280]{2,1,0:T(8,128)(2,1)S(1)}, u32[]{:S(2)}, u32[]{:S(2)}) collective-permute-start(f16[8,8,1280]{2,1,0:T(8,128)(2,1)S(1)} %get-tuple-element.25), channel_id=1, source_target_pairs={{0,1},{1,0},{2,3},{3,2},{4,5},{5,4},{6,7},{7,6},{8,9},{9,8},{10,11... | collective-permute-start | bytes 491528 | tf_op jit(solution)/shard_map/ppermute | solution.py:184
  49.7 10.6 %collective-permute-start.19 = (bf16[2,8,1024]{2,1,0:T(8,128)(2,1)S(1)}, bf16[2,8,1024]{2,1,0:T(8,128)(2,1)S(1)}, u32[]{:S(2)}, u32[]{:S(2)}) collective-permute-start(bf16[2,8,1024]{2,1,0:T(8,128)(2,1)S(1)} %get-tuple-element.65), channel_id=1, source_target_pairs={{0,8},{4,12},{8,0},{12,4},{16,24},{20,28},{24,16},{28,20},{1,9},{5... | collective-permute-start | bytes 98312 | tf_op jit(solution)/shard_map/ppermute | solution.py:184
  50.6 11.2 %collective-permute-start.20 = (bf16[2,8,1024]{2,1,0:T(8,128)(2,1)S(1)}, bf16[2,8,1024]{2,1,0:T(8,128)(2,1)S(1)}, u32[]{:S(2)}, u32[]{:S(2)}) collective-permute-start(bf16[2,8,1024]{2,1,0:T(8,128)(2,1)S(1)} %get-tuple-element.67), channel_id=1, source_target_pairs={{0,16},{4,20},{8,24},{12,28},{16,0},{20,4},{24,8},{28,12},{1,17},{... | collective-permute-start | bytes 98312 | tf_op jit(solution)/shard_map/ppermute | solution.py:184
  51.7 10.1 %collective-permute-start.21 = (bf16[2,8,1024]{2,1,0:T(8,128)(2,1)S(1)}, bf16[2,8,1024]{2,1,0:T(8,128)(2,1)S(1)}, u32[]{:S(2)}, u32[]{:S(2)}) collective-permute-start(bf16[2,8,1024]{2,1,0:T(8,128)(2,1)S(1)} %get-tuple-element.66), channel_id=1, source_target_pairs={{0,24},{4,28},{8,16},{12,20},{16,8},{20,12},{24,0},{28,4},{1,25},{... | collective-permute-start | bytes 98312 | tf_op jit(solution)/shard_map/ppermute | solution.py:184
  58.2 4.2 %collective-permute-start.26 = (bf16[2,8,1280]{2,1,0:T(8,128)(2,1)S(1)}, bf16[2,8,1280]{2,1,0:T(8,128)(2,1)S(1)}, u32[]{:S(2)}, u32[]{:S(2)}) collective-permute-start(bf16[2,8,1280]{2,1,0:T(8,128)(2,1)S(1)} %get-tuple-element.60), channel_id=1, source_target_pairs={{0,8},{4,12},{8,0},{12,4},{16,24},{20,28},{24,16},{28,20},{1,9},{5... | collective-permute-start | bytes 122888 | tf_op jit(solution)/shard_map/ppermute | solution.py:184
  59.3 4.1 %collective-permute-start.27 = (bf16[2,8,1280]{2,1,0:T(8,128)(2,1)S(1)}, bf16[2,8,1280]{2,1,0:T(8,128)(2,1)S(1)}, u32[]{:S(2)}, u32[]{:S(2)}) collective-permute-start(bf16[2,8,1280]{2,1,0:T(8,128)(2,1)S(1)} %get-tuple-element.62), channel_id=1, source_target_pairs={{0,16},{4,20},{8,24},{12,28},{16,0},{20,4},{24,8},{28,12},{1,17},{... | collective-permute-start | bytes 122888 | tf_op jit(solution)/shard_map/ppermute | solution.py:184
  60.3 4.9 %collective-permute-start.28 = (bf16[2,8,1280]{2,1,0:T(8,128)(2,1)S(1)}, bf16[2,8,1280]{2,1,0:T(8,128)(2,1)S(1)}, u32[]{:S(2)}, u32[]{:S(2)}) collective-permute-start(bf16[2,8,1280]{2,1,0:T(8,128)(2,1)S(1)} %get-tuple-element.61), channel_id=1, source_target_pairs={{0,24},{4,28},{8,16},{12,20},{16,8},{20,12},{24,0},{28,4},{1,25},{... | collective-permute-start | bytes 122888 | tf_op jit(solution)/shard_map/ppermute | solution.py:184
  61.9 3.5 %collective-permute-start.22 = (bf16[4,8,1024]{2,1,0:T(8,128)(2,1)S(1)}, bf16[4,8,1024]{2,1,0:T(8,128)(2,1)S(1)}, u32[]{:S(2)}, u32[]{:S(2)}) collective-permute-start(bf16[4,8,1024]{2,1,0:T(8,128)(2,1)S(1)} %pad_maximum_fusion.7), channel_id=1, source_target_pairs={{0,4},{4,0},{8,12},{12,8},{16,20},{20,16},{24,28},{28,24},{1,5},{5... | collective-permute-start | bytes 196616 | tf_op jit(solution)/shard_map/ppermute | solution.py:184
  73.3 6.7 %collective-permute-start.39 = (bf16[8,4096]{1,0:T(8,128)(2,1)S(1)}, bf16[8,4096]{1,0:T(8,128)(2,1)S(1)}, u32[]{:S(2)}, u32[]{:S(2)}) collective-permute-start(bf16[8,4096]{1,0:T(8,128)(2,1)S(1)} %get-tuple-element.51), channel_id=1, source_target_pairs={{0,1},{1,0},{2,3},{3,2},{4,5},{5,4},{6,7},{7,6},{8,9},{9,8},{10,11... | collective-permute-start | bytes 196616 | tf_op jit(solution)/shard_map/ppermute | solution.py:184
  75.1 8.2 %collective-permute-start.30 = (bf16[8,4096]{1,0:T(8,128)(2,1)S(1)}, bf16[8,4096]{1,0:T(8,128)(2,1)S(1)}, u32[]{:S(2)}, u32[]{:S(2)}) collective-permute-start(bf16[8,4096]{1,0:T(8,128)(2,1)S(1)} %get-tuple-element.53), channel_id=1, source_target_pairs={{0,2},{1,3},{2,0},{3,1},{4,6},{5,7},{6,4},{7,5},{8,10},{9,11},{10,... | collective-permute-start | bytes 196616 | tf_op jit(solution)/shard_map/ppermute | solution.py:184
  80.0 6.4 %collective-permute-start.31 = (bf16[8,4096]{1,0:T(8,128)(2,1)S(1)}, bf16[8,4096]{1,0:T(8,128)(2,1)S(1)}, u32[]{:S(2)}, u32[]{:S(2)}) collective-permute-start(bf16[8,4096]{1,0:T(8,128)(2,1)S(1)} %get-tuple-element.52), channel_id=1, source_target_pairs={{0,3},{1,2},{2,1},{3,0},{4,7},{5,6},{6,5},{7,4},{8,11},{9,10},{10,... | collective-permute-start | bytes 196616 | tf_op jit(solution)/shard_map/ppermute | solution.py:184
  80.0 6.5 %collective-permute-start.41 = (bf16[16,4096]{1,0:T(8,128)(2,1)S(1)}, bf16[16,4096]{1,0:T(8,128)(2,1)S(1)}, u32[]{:S(2)}, u32[]{:S(2)}) collective-permute-start(bf16[16,4096]{1,0:T(8,128)(2,1)S(1)} %pad_maximum_fusion.5), channel_id=1, source_target_pairs={{0,8},{4,12},{8,0},{12,4},{16,24},{20,28},{24,16},{28,20},{1,9},{5... | collective-permute-start | bytes 393224 | tf_op jit(solution)/shard_map/ppermute | solution.py:184
  81.2 6.0 %collective-permute-start.40 = (bf16[16,4096]{1,0:T(8,128)(2,1)S(1)}, bf16[16,4096]{1,0:T(8,128)(2,1)S(1)}, u32[]{:S(2)}, u32[]{:S(2)}) collective-permute-start(bf16[16,4096]{1,0:T(8,128)(2,1)S(1)} %pad_maximum_fusion.5), channel_id=1, source_target_pairs={{0,4},{4,0},{8,12},{12,8},{16,20},{20,16},{24,28},{28,24},{1,5},{5... | collective-permute-start | bytes 393224 | tf_op jit(solution)/shard_map/ppermute | solution.py:184
  82.4 11.5 %collective-permute-start.43 = (bf16[16,4096]{1,0:T(8,128)(2,1)S(1)}, bf16[16,4096]{1,0:T(8,128)(2,1)S(1)}, u32[]{:S(2)}, u32[]{:S(2)}) collective-permute-start(bf16[16,4096]{1,0:T(8,128)(2,1)S(1)} %pad_maximum_fusion.5), channel_id=1, source_target_pairs={{0,16},{4,20},{8,24},{12,28},{16,0},{20,4},{24,8},{28,12},{1,17},{... | collective-permute-start | bytes 393224 | tf_op jit(solution)/shard_map/ppermute | solution.py:184
  83.3 11.1 %collective-permute-start.45 = (bf16[16,4096]{1,0:T(8,128)(2,1)S(1)}, bf16[16,4096]{1,0:T(8,128)(2,1)S(1)}, u32[]{:S(2)}, u32[]{:S(2)}) collective-permute-start(bf16[16,4096]{1,0:T(8,128)(2,1)S(1)} %pad_maximum_fusion.5), channel_id=1, source_target_pairs={{0,24},{4,28},{8,16},{12,20},{16,8},{20,12},{24,0},{28,4},{1,25},{... | collective-permute-start | bytes 393224 | tf_op jit(solution)/shard_map/ppermute | solution.py:184
  86.5 7.3 %collective-permute-start.33 = (bf16[16,4096]{1,0:T(8,128)(2,1)S(1)}, bf16[16,4096]{1,0:T(8,128)(2,1)S(1)}, u32[]{:S(2)}, u32[]{:S(2)}) collective-permute-start(bf16[16,4096]{1,0:T(8,128)(2,1)S(1)} %constant_dynamic-update-slice_fusion.10), channel_id=1, source_target_pairs={{0,8},{4,12},{8,0},{12,4},{16,24},{20,28},{24,16},{28,20},{1,9},{5... | collective-permute-start | bytes 393224 | tf_op jit(solution)/shard_map/ppermute | solution.py:184
  87.2 8.1 %collective-permute-start.35 = (bf16[16,4096]{1,0:T(8,128)(2,1)S(1)}, bf16[16,4096]{1,0:T(8,128)(2,1)S(1)}, u32[]{:S(2)}, u32[]{:S(2)}) collective-permute-start(bf16[16,4096]{1,0:T(8,128)(2,1)S(1)} %constant_dynamic-update-slice_fusion.10), channel_id=1, source_target_pairs={{0,16},{4,20},{8,24},{12,28},{16,0},{20,4},{24,8},{28,12},{1,17},{... | collective-permute-start | bytes 393224 | tf_op jit(solution)/shard_map/ppermute | solution.py:184
  88.8 8.0 %collective-permute-start.37 = (bf16[16,4096]{1,0:T(8,128)(2,1)S(1)}, bf16[16,4096]{1,0:T(8,128)(2,1)S(1)}, u32[]{:S(2)}, u32[]{:S(2)}) collective-permute-start(bf16[16,4096]{1,0:T(8,128)(2,1)S(1)} %constant_dynamic-update-slice_fusion.10), channel_id=1, source_target_pairs={{0,24},{4,28},{8,16},{12,20},{16,8},{20,12},{24,0},{28,4},{1,25},{... | collective-permute-start | bytes 393224 | tf_op jit(solution)/shard_map/ppermute | solution.py:184
  93.9 2.9 %collective-permute-start.42 = (bf16[16,4096]{1,0:T(8,128)(2,1)S(1)}, bf16[16,4096]{1,0:T(8,128)(2,1)S(1)}, u32[]{:S(2)}, u32[]{:S(2)}) collective-permute-start(bf16[16,4096]{1,0:T(8,128)(2,1)S(1)} %collective-permute-done.41), channel_id=1, source_target_pairs={{0,4},{4,0},{8,12},{12,8},{16,20},{20,16},{24,28},{28,24},{1,5},{5... | collective-permute-start | bytes 393224 | tf_op jit(solution)/shard_map/ppermute | solution.py:184
  93.9 3.5 %collective-permute-start.34 = (bf16[16,4096]{1,0:T(8,128)(2,1)S(1)}, bf16[16,4096]{1,0:T(8,128)(2,1)S(1)}, u32[]{:S(2)}, u32[]{:S(2)}) collective-permute-start(bf16[16,4096]{1,0:T(8,128)(2,1)S(1)} %collective-permute-done.33), channel_id=1, source_target_pairs={{0,4},{4,0},{8,12},{12,8},{16,20},{20,16},{24,28},{28,24},{1,5},{5... | collective-permute-start | bytes 393224 | tf_op jit(solution)/shard_map/ppermute | solution.py:184
  94.5 2.9 %collective-permute-start.44 = (bf16[16,4096]{1,0:T(8,128)(2,1)S(1)}, bf16[16,4096]{1,0:T(8,128)(2,1)S(1)}, u32[]{:S(2)}, u32[]{:S(2)}) collective-permute-start(bf16[16,4096]{1,0:T(8,128)(2,1)S(1)} %collective-permute-done.43), channel_id=1, source_target_pairs={{0,4},{4,0},{8,12},{12,8},{16,20},{20,16},{24,28},{28,24},{1,5},{5... | collective-permute-start | bytes 393224 | tf_op jit(solution)/shard_map/ppermute | solution.py:184
  95.3 2.8 %collective-permute-start.46 = (bf16[16,4096]{1,0:T(8,128)(2,1)S(1)}, bf16[16,4096]{1,0:T(8,128)(2,1)S(1)}, u32[]{:S(2)}, u32[]{:S(2)}) collective-permute-start(bf16[16,4096]{1,0:T(8,128)(2,1)S(1)} %collective-permute-done.45), channel_id=1, source_target_pairs={{0,4},{4,0},{8,12},{12,8},{16,20},{20,16},{24,28},{28,24},{1,5},{5... | collective-permute-start | bytes 393224 | tf_op jit(solution)/shard_map/ppermute | solution.py:184
  102.7 9.0 %collective-permute-start.47 = (f16[2,8,8,1024]{3,2,1,0:T(8,128)(2,1)S(1)}, f16[2,8,8,1024]{3,2,1,0:T(8,128)(2,1)S(1)}, u32[]{:S(2)}, u32[]{:S(2)}) collective-permute-start(f16[2,8,8,1024]{3,2,1,0:T(8,128)(2,1)S(1)} %fusion.20), channel_id=1, source_target_pairs={{0,1},{1,0},{2,3},{3,2},{4,5},{5,4},{6,7},{7,6},{8,9},{9,8},{10,11... | collective-permute-start | bytes 786440 | tf_op jit(solution)/shard_map/ppermute | solution.py:184
  108.2 5.9 %collective-permute-start.50 = (f16[8,8,1024]{2,1,0:T(8,128)(2,1)S(1)}, f16[8,8,1024]{2,1,0:T(8,128)(2,1)S(1)}, u32[]{:S(2)}, u32[]{:S(2)}) collective-permute-start(f16[8,8,1024]{2,1,0:T(8,128)(2,1)S(1)} %get-tuple-element.42), channel_id=1, source_target_pairs={{0,1},{1,0},{2,3},{3,2},{4,5},{5,4},{6,7},{7,6},{8,9},{9,8},{10,11... | collective-permute-start | bytes 393224 | tf_op jit(solution)/shard_map/ppermute | solution.py:184
  111.8 11.3 %collective-permute-start.48 = (f16[8,8,1024]{2,1,0:T(8,128)(2,1)S(1)}, f16[8,8,1024]{2,1,0:T(8,128)(2,1)S(1)}, u32[]{:S(2)}, u32[]{:S(2)}) collective-permute-start(f16[8,8,1024]{2,1,0:T(8,128)(2,1)S(1)} %fusion.42), channel_id=1, source_target_pairs={{0,2},{1,3},{2,0},{3,1},{4,6},{5,7},{6,4},{7,5},{8,10},{9,11},{10,... | collective-permute-start | bytes 393224 | tf_op jit(solution)/shard_map/ppermute | solution.py:184
  114.1 11.6 %collective-permute-start.51 = (f16[8,8,1024]{2,1,0:T(8,128)(2,1)S(1)}, f16[8,8,1024]{2,1,0:T(8,128)(2,1)S(1)}, u32[]{:S(2)}, u32[]{:S(2)}) collective-permute-start(f16[8,8,1024]{2,1,0:T(8,128)(2,1)S(1)} %fusion.28), channel_id=1, source_target_pairs={{0,2},{1,3},{2,0},{3,1},{4,6},{5,7},{6,4},{7,5},{8,10},{9,11},{10,... | collective-permute-start | bytes 393224 | tf_op jit(solution)/shard_map/ppermute | solution.py:184
  115.2 10.5 %collective-permute-start.49 = (f16[8,8,1024]{2,1,0:T(8,128)(2,1)S(1)}, f16[8,8,1024]{2,1,0:T(8,128)(2,1)S(1)}, u32[]{:S(2)}, u32[]{:S(2)}) collective-permute-start(f16[8,8,1024]{2,1,0:T(8,128)(2,1)S(1)} %get-tuple-element.32), channel_id=1, source_target_pairs={{0,1},{1,0},{2,3},{3,2},{4,5},{5,4},{6,7},{7,6},{8,9},{9,8},{10,11... | collective-permute-start | bytes 393224 | tf_op jit(solution)/shard_map/ppermute | solution.py:184
  125.8 4.3 %collective-permute-start.52 = (bf16[2,8,2048]{2,1,0:T(8,128)(2,1)S(1)}, bf16[2,8,2048]{2,1,0:T(8,128)(2,1)S(1)}, u32[]{:S(2)}, u32[]{:S(2)}) collective-permute-start(bf16[2,8,2048]{2,1,0:T(8,128)(2,1)S(1)} %get-tuple-element.47), channel_id=1, source_target_pairs={{0,8},{4,12},{8,0},{12,4},{16,24},{20,28},{24,16},{28,20},{1,9},{5... | collective-permute-start | bytes 196616 | tf_op jit(solution)/shard_map/ppermute | solution.py:184
  127.7 5.0 %collective-permute-start.53 = (bf16[2,8,2048]{2,1,0:T(8,128)(2,1)S(1)}, bf16[2,8,2048]{2,1,0:T(8,128)(2,1)S(1)}, u32[]{:S(2)}, u32[]{:S(2)}) collective-permute-start(bf16[2,8,2048]{2,1,0:T(8,128)(2,1)S(1)} %get-tuple-element.48), channel_id=1, source_target_pairs={{0,16},{4,20},{8,24},{12,28},{16,0},{20,4},{24,8},{28,12},{1,17},{... | collective-permute-start | bytes 196616 | tf_op jit(solution)/shard_map/ppermute | solution.py:184
  128.6 5.2 %collective-permute-start.54 = (bf16[2,8,2048]{2,1,0:T(8,128)(2,1)S(1)}, bf16[2,8,2048]{2,1,0:T(8,128)(2,1)S(1)}, u32[]{:S(2)}, u32[]{:S(2)}) collective-permute-start(bf16[2,8,2048]{2,1,0:T(8,128)(2,1)S(1)} %get-tuple-element.49), channel_id=1, source_target_pairs={{0,24},{4,28},{8,16},{12,20},{16,8},{20,12},{24,0},{28,4},{1,25},{... | collective-permute-start | bytes 196616 | tf_op jit(solution)/shard_map/ppermute | solution.py:184
  (9 other events, 13.2 us)

commit v9 on v7

--- a/solution.py
+++ b/solution.py
@@ -195,29 +195,33 @@
     return jnp.concatenate(halves, axis=1)
 
 
-def multiply_kernel(start, far, near, weights, out, held, sems):
-    parts, depth, columns = held.shape
-
-    def copy(part):
+def multiply_kernel(start, depth, far, near, weights, out, held, sems):
+    width, columns = held.shape
+    parts = width // depth
+    half = depth // 2
+
+    def copy(at, count, sem):
+        some = pl.ds(at, count)
         return pltpu.make_async_copy(
-            weights.at[pl.ds(part * depth, depth), pl.ds(start, columns)],
-            held.at[part],
-            sems.at[part],
+            weights.at[some, pl.ds(start, columns)], held.at[some], sems.at[sem]
         )
 
-    def product(part):
-        copy(part).wait()
-        some = pl.ds(part * depth, depth)
+    def product(at, count, sem):
+        copy(at, count, sem).wait()
+        some = pl.ds(at, count)
         rows = jnp.concatenate([far[:, some], near[:, some]], axis=0)
-        return jnp.dot(rows, held[part], preferred_element_type=jnp.float32)
-
-    for part in range(parts):
-        copy(part).start()
-    out[...] = product(0)
+        return jnp.dot(rows, held[some], preferred_element_type=jnp.float32)
+
+    copy(0, half, 0).start()
+    copy(half, half, parts).start()
+    for part in range(1, parts):
+        copy(part * depth, depth, part).start()
+    out[...] = product(0, half, 0)
+    out[...] += product(half, half, parts)
 
     @pl.loop(1, parts)
     def _(part):
-        out[...] += product(part)
+        out[...] += product(pl.multiple_of(part * depth, depth), depth, part)
 
 
 def multiply(far, near, weights, start, columns):
@@ -225,13 +229,13 @@
     depth = 1024
     vmem = pl.BlockSpec(memory_space=pltpu.VMEM)
     return pl.pallas_call(
-        functools.partial(multiply_kernel, start),
+        functools.partial(multiply_kernel, start, depth),
         in_specs=[vmem, vmem, pl.BlockSpec(memory_space=pl.ANY)],
         out_specs=vmem,
         out_shape=jax.ShapeDtypeStruct((2 * half, columns), jnp.float32),
         scratch_shapes=[
-            pltpu.VMEM((width // depth, depth, columns), jnp.bfloat16),
-            pltpu.SemaphoreType.DMA((width // depth,)),
+            pltpu.VMEM((width, columns), jnp.bfloat16),
+            pltpu.SemaphoreType.DMA((width // depth + 1,)),
         ],
         compiler_params=pltpu.CompilerParams(vmem_limit_bytes=ROOM),
         cost_estimate=pl.CostEstimate(

time: 134 us -> 134 us (level)
  Pallas kernels: 24.9 us -> 23.1 us
  transfers between devices with their start and end apart: 56 -> 56, of which waited for: 27 -> 27; matrix products, arithmetic and copies ran while one was open for 1% -> 1% of each run, Pallas kernels for 8% -> 7%
where the time goes in v9:
time: 134 us; the launch traced here: 133 us
  starting transfers between devices  59.2 us (44%)
  waiting for transfers between devices  43.3 us (32%)
  Pallas kernels  23.1 us (17%)
  other arithmetic  6.07 us (5%)
    ppermute x56, starting transfers between devices, swap(): return lax.ppermute(block, axis, [(i, i ^ bit) for i in range(count)])  59.2 us
    ppermute x56, waiting for transfers between devices, swap(): return lax.ppermute(block, axis, [(i, i ^ bit) for i in range(count)])  43.3 us
    pallas_call x4, Pallas kernels, multiply(): pl.pallas_call(functools.partial(multiply_kernel, start, depth), in_specs...  18.9 us
    pallas_call x1, Pallas kernels, attend_local(): pl.pallas_call(attend_kernel, in_specs=[pl.BlockSpec(memory_space=pltpu.S...  4.13 us
  transfers between devices with their start and end apart: 56, of which 27 were waited for; matrix products, arithmetic and copies ran while one was open for 1% of the time, Pallas kernels for 7%

profile of v9, /device:TPU:0, one launch (start us, length us, event | category | flops | bytes accessed | tf_op | source)
XLA Modules:
  0.0 133.3 jit_solution(15862414998939896760)
XLA Ops:
  0.0 1.2 fusion
  1.2 1.1 fusion.2
  2.3 3.1 %collective-permute-start.9 = (bf16[8,4096]{1,0:T(8,128)(2,1)S(1)}, bf16[8,4096]{1,0:T(8,128)(2,1)S(1)}, u32[]{:S(2)}, u32[]{:S(2)}) collective-permute-start(bf16[8,4096]{1,0:T(8,128)(2,1)S(1)} %get-tuple-element.47), channel_id=1, source_target_pairs={{0,1},{1,0},{2,3},{3,2},{4,5},{5,4},{6,7},{7,6},{8,9},{9,8},{10,11... | collective-permute-start | bytes 196616 | tf_op jit(solution)/shard_map/ppermute | solution.py:183
  5.4 2.6 %collective-permute-start = (bf16[8,4096]{1,0:T(8,128)(2,1)S(1)}, bf16[8,4096]{1,0:T(8,128)(2,1)S(1)}, u32[]{:S(2)}, u32[]{:S(2)}) collective-permute-start(bf16[8,4096]{1,0:T(8,128)(2,1)S(1)} %get-tuple-element.49), channel_id=1, source_target_pairs={{0,2},{1,3},{2,0},{3,1},{4,6},{5,7},{6,4},{7,5},{8,10},{9,11},{10,... | collective-permute-start | bytes 196616 | tf_op jit(solution)/shard_map/ppermute | solution.py:183
  9.0 1.8 %collective-permute-start.11 = (bf16[16,4096]{1,0:T(8,128)(2,1)S(1)}, bf16[16,4096]{1,0:T(8,128)(2,1)S(1)}, u32[]{:S(2)}, u32[]{:S(2)}) collective-permute-start(bf16[16,4096]{1,0:T(8,128)(2,1)S(1)} %pad_maximum_fusion.3), channel_id=1, source_target_pairs={{0,8},{4,12},{8,0},{12,4},{16,24},{20,28},{24,16},{28,20},{1,9},{5... | collective-permute-start | bytes 393224 | tf_op jit(solution)/shard_map/ppermute | solution.py:183
  10.7 1.5 %collective-permute-start.13 = (bf16[16,4096]{1,0:T(8,128)(2,1)S(1)}, bf16[16,4096]{1,0:T(8,128)(2,1)S(1)}, u32[]{:S(2)}, u32[]{:S(2)}) collective-permute-start(bf16[16,4096]{1,0:T(8,128)(2,1)S(1)} %pad_maximum_fusion.3), channel_id=1, source_target_pairs={{0,16},{4,20},{8,24},{12,28},{16,0},{20,4},{24,8},{28,12},{1,17},{... | collective-permute-start | bytes 393224 | tf_op jit(solution)/shard_map/ppermute | solution.py:183
  12.7 2.4 %collective-permute-start.15 = (bf16[16,4096]{1,0:T(8,128)(2,1)S(1)}, bf16[16,4096]{1,0:T(8,128)(2,1)S(1)}, u32[]{:S(2)}, u32[]{:S(2)}) collective-permute-start(bf16[16,4096]{1,0:T(8,128)(2,1)S(1)} %pad_maximum_fusion.3), channel_id=1, source_target_pairs={{0,24},{4,28},{8,16},{12,20},{16,8},{20,12},{24,0},{28,4},{1,25},{... | collective-permute-start | bytes 393224 | tf_op jit(solution)/shard_map/ppermute | solution.py:183
  15.9 1.5 %collective-permute-start.5 = (bf16[16,4096]{1,0:T(8,128)(2,1)S(1)}, bf16[16,4096]{1,0:T(8,128)(2,1)S(1)}, u32[]{:S(2)}, u32[]{:S(2)}) collective-permute-start(bf16[16,4096]{1,0:T(8,128)(2,1)S(1)} %constant_dynamic-update-slice_fusion), channel_id=1, source_target_pairs={{0,16},{4,20},{8,24},{12,28},{16,0},{20,4},{24,8},{28,12},{1,17},{... | collective-permute-start | bytes 393224 | tf_op jit(solution)/shard_map/ppermute | solution.py:183
  17.4 1.6 %collective-permute-start.7 = (bf16[16,4096]{1,0:T(8,128)(2,1)S(1)}, bf16[16,4096]{1,0:T(8,128)(2,1)S(1)}, u32[]{:S(2)}, u32[]{:S(2)}) collective-permute-start(bf16[16,4096]{1,0:T(8,128)(2,1)S(1)} %constant_dynamic-update-slice_fusion), channel_id=1, source_target_pairs={{0,24},{4,28},{8,16},{12,20},{16,8},{20,12},{24,0},{28,4},{1,25},{... | collective-permute-start | bytes 393224 | tf_op jit(solution)/shard_map/ppermute | solution.py:183
  19.0 2.7 %collective-permute-done.3 = bf16[16,4096]{1,0:T(8,128)(2,1)S(1)} collective-permute-done((bf16[16,4096]{1,0:T(8,128)(2,1)S(1)}, bf16[16,4096]{1,0:T(8,128)(2,1)S(1)}, u32[]{:S(2)}, u32[]{:S(2)}) %collective-permute-start.3) | collective-permute-done | bytes 131104 | tf_op jit(solution)/shard_map/ppermute | solution.py:183
  22.4 2.3 %collective-permute-done.5 = bf16[16,4096]{1,0:T(8,128)(2,1)S(1)} collective-permute-done((bf16[16,4096]{1,0:T(8,128)(2,1)S(1)}, bf16[16,4096]{1,0:T(8,128)(2,1)S(1)}, u32[]{:S(2)}, u32[]{:S(2)}) %collective-permute-start.5) | collective-permute-done | bytes 131104 | tf_op jit(solution)/shard_map/ppermute | solution.py:183
  26.6 4.6 %shard_map.73 = f32[256,1024]{1,0:T(8,128)S(1)} custom-call(bf16[128,4096]{1,0:T(8,128)(2,1)S(1)} %bitcast.269, bf16[128,4096]{1,0:T(8,128)(2,1)S(1)} %bitcast.271, bf16[4096,2304]{1,0:T(8,128)(2,1)} %weights.5), custom_call_target="tpu_custom_call" | custom-call | flops 2147483648 | bytes 8388608 | tf_op jit(solution)/shard_map/pallas_call | solution.py:231
  32.0 5.3 %shard_map.74 = f32[256,1280]{1,0:T(8,128)S(1)} custom-call(bf16[128,4096]{1,0:T(8,128)(2,1)S(1)} %bitcast.270, bf16[128,4096]{1,0:T(8,128)(2,1)S(1)} %bitcast.272, bf16[4096,2304]{1,0:T(8,128)(2,1)} %weights.5), custom_call_target="tpu_custom_call" | custom-call | flops 2684354560 | bytes 10485760 | tf_op jit(solution)/shard_map/pallas_call | solution.py:231
  37.4 1.4 %collective-permute-start.24 = (f16[8,8,1280]{2,1,0:T(8,128)(2,1)S(1)}, f16[8,8,1280]{2,1,0:T(8,128)(2,1)S(1)}, u32[]{:S(2)}, u32[]{:S(2)}) collective-permute-start(f16[8,8,1280]{2,1,0:T(8,128)(2,1)S(1)} %get-tuple-element.32), channel_id=1, source_target_pairs={{0,1},{1,0},{2,3},{3,2},{4,5},{5,4},{6,7},{7,6},{8,9},{9,8},{10,11... | collective-permute-start | bytes 491528 | tf_op jit(solution)/shard_map/ppermute | solution.py:183
  38.8 0.9 collective-permute-done.17
  39.8 2.5 %collective-permute-start.18 = (f16[8,8,1024]{2,1,0:T(8,128)(2,1)S(1)}, f16[8,8,1024]{2,1,0:T(8,128)(2,1)S(1)}, u32[]{:S(2)}, u32[]{:S(2)}) collective-permute-start(f16[8,8,1024]{2,1,0:T(8,128)(2,1)S(1)} %fusion.41), channel_id=1, source_target_pairs={{0,2},{1,3},{2,0},{3,1},{4,6},{5,7},{6,4},{7,5},{8,10},{9,11},{10,... | collective-permute-start | bytes 393224 | tf_op jit(solution)/shard_map/ppermute | solution.py:183
  42.3 3.9 %collective-permute-done.24 = f16[8,8,1280]{2,1,0:T(8,128)(2,1)S(1)} collective-permute-done((f16[8,8,1280]{2,1,0:T(8,128)(2,1)S(1)}, f16[8,8,1280]{2,1,0:T(8,128)(2,1)S(1)}, u32[]{:S(2)}, u32[]{:S(2)}) %collective-permute-start.24) | collective-permute-done | bytes 163872 | tf_op jit(solution)/shard_map/ppermute | solution.py:183
  46.3 1.8 %collective-permute-start.25 = (f16[8,8,1280]{2,1,0:T(8,128)(2,1)S(1)}, f16[8,8,1280]{2,1,0:T(8,128)(2,1)S(1)}, u32[]{:S(2)}, u32[]{:S(2)}) collective-permute-start(f16[8,8,1280]{2,1,0:T(8,128)(2,1)S(1)} %fusion.14), channel_id=1, source_target_pairs={{0,2},{1,3},{2,0},{3,1},{4,6},{5,7},{6,4},{7,5},{8,10},{9,11},{10,... | collective-permute-start | bytes 491528 | tf_op jit(solution)/shard_map/ppermute | solution.py:183
  48.2 1.4 %collective-permute-start.19 = (bf16[2,8,1024]{2,1,0:T(8,128)(2,1)S(1)}, bf16[2,8,1024]{2,1,0:T(8,128)(2,1)S(1)}, u32[]{:S(2)}, u32[]{:S(2)}) collective-permute-start(bf16[2,8,1024]{2,1,0:T(8,128)(2,1)S(1)} %get-tuple-element.57), channel_id=1, source_target_pairs={{0,8},{4,12},{8,0},{12,4},{16,24},{20,28},{24,16},{28,20},{1,9},{5... | collective-permute-start | bytes 98312 | tf_op jit(solution)/shard_map/ppermute | solution.py:183
  50.5 1.3 collective-permute-start.21
  51.7 4.3 %collective-permute-done.25 = f16[8,8,1280]{2,1,0:T(8,128)(2,1)S(1)} collective-permute-done((f16[8,8,1280]{2,1,0:T(8,128)(2,1)S(1)}, f16[8,8,1280]{2,1,0:T(8,128)(2,1)S(1)}, u32[]{:S(2)}, u32[]{:S(2)}) %collective-permute-start.25) | collective-permute-done | bytes 163872 | tf_op jit(solution)/shard_map/ppermute | solution.py:183
  56.7 1.4 %collective-permute-start.26 = (bf16[2,8,1280]{2,1,0:T(8,128)(2,1)S(1)}, bf16[2,8,1280]{2,1,0:T(8,128)(2,1)S(1)}, u32[]{:S(2)}, u32[]{:S(2)}) collective-permute-start(bf16[2,8,1280]{2,1,0:T(8,128)(2,1)S(1)} %get-tuple-element.52), channel_id=1, source_target_pairs={{0,8},{4,12},{8,0},{12,4},{16,24},{20,28},{24,16},{28,20},{1,9},{5... | collective-permute-start | bytes 122888 | tf_op jit(solution)/shard_map/ppermute | solution.py:183
  58.2 0.9 collective-permute-start.27
  59.1 1.2 collective-permute-start.28
  60.8 1.6 %collective-permute-done.27 = bf16[2,8,1280]{2,1,0:T(8,128)(2,1)S(1)} collective-permute-done((bf16[2,8,1280]{2,1,0:T(8,128)(2,1)S(1)}, bf16[2,8,1280]{2,1,0:T(8,128)(2,1)S(1)}, u32[]{:S(2)}, u32[]{:S(2)}) %collective-permute-start.27) | collective-permute-done | bytes 40992 | tf_op jit(solution)/shard_map/ppermute | solution.py:183
  62.4 1.6 %collective-permute-done.28 = bf16[2,8,1280]{2,1,0:T(8,128)(2,1)S(1)} collective-permute-done((bf16[2,8,1280]{2,1,0:T(8,128)(2,1)S(1)}, bf16[2,8,1280]{2,1,0:T(8,128)(2,1)S(1)}, u32[]{:S(2)}, u32[]{:S(2)}) %collective-permute-start.28) | collective-permute-done | bytes 40992 | tf_op jit(solution)/shard_map/ppermute | solution.py:183
  64.2 1.2 collective-permute-done.29
  66.3 4.1 %shard_map.75 = bf16[8,128,128]{2,1,0:T(8,128)(2,1)S(1)} custom-call(s32[8]{0:T(128)S(1)} %copy-done, bf16[8,128,128]{2,1,0:T(8,128)(2,1)S(1)} %pad_maximum_fusion.query, bf16[8,8,128]{2,1,0:T(8,128)(2,1)S(1)} %pad_maximum_fusion.8.key_new, f32[8,8,128]{2,1,0:T(8,128)S(1)} %get-tuple-element.84.value_new, bf16[8,512,1024]{2,1,0:T(8,128)(2,1)} %k_cache.1, ...), custom_call_target="tpu_custom_call" | custom-call | flops 2147483648 | bytes 8388608 | tf_op jit(solution)/shard_map/pallas_call | solution.py:153
  71.1 1.6 %collective-permute-start.39 = (bf16[8,4096]{1,0:T(8,128)(2,1)S(1)}, bf16[8,4096]{1,0:T(8,128)(2,1)S(1)}, u32[]{:S(2)}, u32[]{:S(2)}) collective-permute-start(bf16[8,4096]{1,0:T(8,128)(2,1)S(1)} %get-tuple-element.43), channel_id=1, source_target_pairs={{0,1},{1,0},{2,3},{3,2},{4,5},{5,4},{6,7},{7,6},{8,9},{9,8},{10,11... | collective-permute-start | bytes 196616 | tf_op jit(solution)/shard_map/ppermute | solution.py:183
  72.6 2.3 %collective-permute-start.30 = (bf16[8,4096]{1,0:T(8,128)(2,1)S(1)}, bf16[8,4096]{1,0:T(8,128)(2,1)S(1)}, u32[]{:S(2)}, u32[]{:S(2)}) collective-permute-start(bf16[8,4096]{1,0:T(8,128)(2,1)S(1)} %get-tuple-element.45), channel_id=1, source_target_pairs={{0,2},{1,3},{2,0},{3,1},{4,6},{5,7},{6,4},{7,5},{8,10},{9,11},{10,... | collective-permute-start | bytes 196616 | tf_op jit(solution)/shard_map/ppermute | solution.py:183
  76.0 3.8 %collective-permute-start.41 = (bf16[16,4096]{1,0:T(8,128)(2,1)S(1)}, bf16[16,4096]{1,0:T(8,128)(2,1)S(1)}, u32[]{:S(2)}, u32[]{:S(2)}) collective-permute-start(bf16[16,4096]{1,0:T(8,128)(2,1)S(1)} %pad_maximum_fusion.5), channel_id=1, source_target_pairs={{0,8},{4,12},{8,0},{12,4},{16,24},{20,28},{24,16},{28,20},{1,9},{5... | collective-permute-start | bytes 393224 | tf_op jit(solution)/shard_map/ppermute | solution.py:183
  79.9 2.2 %collective-permute-start.45 = (bf16[16,4096]{1,0:T(8,128)(2,1)S(1)}, bf16[16,4096]{1,0:T(8,128)(2,1)S(1)}, u32[]{:S(2)}, u32[]{:S(2)}) collective-permute-start(bf16[16,4096]{1,0:T(8,128)(2,1)S(1)} %pad_maximum_fusion.5), channel_id=1, source_target_pairs={{0,24},{4,28},{8,16},{12,20},{16,8},{20,12},{24,0},{28,4},{1,25},{... | collective-permute-start | bytes 393224 | tf_op jit(solution)/shard_map/ppermute | solution.py:183
  82.2 3.1 %collective-permute-start.33 = (bf16[16,4096]{1,0:T(8,128)(2,1)S(1)}, bf16[16,4096]{1,0:T(8,128)(2,1)S(1)}, u32[]{:S(2)}, u32[]{:S(2)}) collective-permute-start(bf16[16,4096]{1,0:T(8,128)(2,1)S(1)} %constant_dynamic-update-slice_fusion.10), channel_id=1, source_target_pairs={{0,8},{4,12},{8,0},{12,4},{16,24},{20,28},{24,16},{28,20},{1,9},{5... | collective-permute-start | bytes 393224 | tf_op jit(solution)/shard_map/ppermute | solution.py:183
  85.5 2.2 %collective-permute-start.37 = (bf16[16,4096]{1,0:T(8,128)(2,1)S(1)}, bf16[16,4096]{1,0:T(8,128)(2,1)S(1)}, u32[]{:S(2)}, u32[]{:S(2)}) collective-permute-start(bf16[16,4096]{1,0:T(8,128)(2,1)S(1)} %constant_dynamic-update-slice_fusion.10), channel_id=1, source_target_pairs={{0,24},{4,28},{8,16},{12,20},{16,8},{20,12},{24,0},{28,4},{1,25},{... | collective-permute-start | bytes 393224 | tf_op jit(solution)/shard_map/ppermute | solution.py:183
  87.7 2.0 %collective-permute-done.33 = bf16[16,4096]{1,0:T(8,128)(2,1)S(1)} collective-permute-done((bf16[16,4096]{1,0:T(8,128)(2,1)S(1)}, bf16[16,4096]{1,0:T(8,128)(2,1)S(1)}, u32[]{:S(2)}, u32[]{:S(2)}) %collective-permute-start.33) | collective-permute-done | bytes 131104 | tf_op jit(solution)/shard_map/ppermute | solution.py:183
  90.4 3.5 %collective-permute-done.35 = bf16[16,4096]{1,0:T(8,128)(2,1)S(1)} collective-permute-done((bf16[16,4096]{1,0:T(8,128)(2,1)S(1)}, bf16[16,4096]{1,0:T(8,128)(2,1)S(1)}, u32[]{:S(2)}, u32[]{:S(2)}) %collective-permute-start.35) | collective-permute-done | bytes 131104 | tf_op jit(solution)/shard_map/ppermute | solution.py:183
  95.7 4.6 %shard_map.76 = f32[256,1024]{1,0:T(8,128)S(1)} custom-call(bf16[128,4096]{1,0:T(8,128)(2,1)S(1)} %bitcast.265, bf16[128,4096]{1,0:T(8,128)(2,1)S(1)} %bitcast.267, bf16[4096,2048]{1,0:T(8,128)(2,1)} %weights.7), custom_call_target="tpu_custom_call" | custom-call | flops 2147483648 | bytes 8388608 | tf_op jit(solution)/shard_map/pallas_call | solution.py:231
  100.9 4.5 %shard_map.77 = f32[256,1024]{1,0:T(8,128)S(1)} custom-call(bf16[128,4096]{1,0:T(8,128)(2,1)S(1)} %bitcast.266, bf16[128,4096]{1,0:T(8,128)(2,1)S(1)} %bitcast.268, bf16[4096,2048]{1,0:T(8,128)(2,1)} %weights.7), custom_call_target="tpu_custom_call" | custom-call | flops 2147483648 | bytes 8388608 | tf_op jit(solution)/shard_map/pallas_call | solution.py:231
  105.5 1.6 %collective-permute-start.50 = (f16[8,8,1024]{2,1,0:T(8,128)(2,1)S(1)}, f16[8,8,1024]{2,1,0:T(8,128)(2,1)S(1)}, u32[]{:S(2)}, u32[]{:S(2)}) collective-permute-start(f16[8,8,1024]{2,1,0:T(8,128)(2,1)S(1)} %get-tuple-element.34), channel_id=1, source_target_pairs={{0,1},{1,0},{2,3},{3,2},{4,5},{5,4},{6,7},{7,6},{8,9},{9,8},{10,11... | collective-permute-start | bytes 393224 | tf_op jit(solution)/shard_map/ppermute | solution.py:183
  107.1 2.4 %collective-permute-done.47 = f16[2,8,8,1024]{3,2,1,0:T(8,128)(2,1)S(1)} collective-permute-done((f16[2,8,8,1024]{3,2,1,0:T(8,128)(2,1)S(1)}, f16[2,8,8,1024]{3,2,1,0:T(8,128)(2,1)S(1)}, u32[]{:S(2)}, u32[]{:S(2)}) %collective-permute-start.47) | collective-permute-done | bytes 262176 | tf_op jit(solution)/shard_map/ppermute | solution.py:183
  109.6 1.7 %collective-permute-start.48 = (f16[8,8,1024]{2,1,0:T(8,128)(2,1)S(1)}, f16[8,8,1024]{2,1,0:T(8,128)(2,1)S(1)}, u32[]{:S(2)}, u32[]{:S(2)}) collective-permute-start(f16[8,8,1024]{2,1,0:T(8,128)(2,1)S(1)} %fusion.42), channel_id=1, source_target_pairs={{0,2},{1,3},{2,0},{3,1},{4,6},{5,7},{6,4},{7,5},{8,10},{9,11},{10,... | collective-permute-start | bytes 393224 | tf_op jit(solution)/shard_map/ppermute | solution.py:183
  111.7 3.9 %collective-permute-start.51 = (f16[8,8,1024]{2,1,0:T(8,128)(2,1)S(1)}, f16[8,8,1024]{2,1,0:T(8,128)(2,1)S(1)}, u32[]{:S(2)}, u32[]{:S(2)}) collective-permute-start(f16[8,8,1024]{2,1,0:T(8,128)(2,1)S(1)} %fusion.28), channel_id=1, source_target_pairs={{0,2},{1,3},{2,0},{3,1},{4,6},{5,7},{6,4},{7,5},{8,10},{9,11},{10,... | collective-permute-start | bytes 393224 | tf_op jit(solution)/shard_map/ppermute | solution.py:183
  115.7 6.0 %collective-permute-done.48 = f16[8,8,1024]{2,1,0:T(8,128)(2,1)S(1)} collective-permute-done((f16[8,8,1024]{2,1,0:T(8,128)(2,1)S(1)}, f16[8,8,1024]{2,1,0:T(8,128)(2,1)S(1)}, u32[]{:S(2)}, u32[]{:S(2)}) %collective-permute-start.48) | collective-permute-done | bytes 131104 | tf_op jit(solution)/shard_map/ppermute | solution.py:183
  121.7 1.6 %collective-permute-done.51 = f16[8,8,1024]{2,1,0:T(8,128)(2,1)S(1)} collective-permute-done((f16[8,8,1024]{2,1,0:T(8,128)(2,1)S(1)}, f16[8,8,1024]{2,1,0:T(8,128)(2,1)S(1)}, u32[]{:S(2)}, u32[]{:S(2)}) %collective-permute-start.51) | collective-permute-done | bytes 131104 | tf_op jit(solution)/shard_map/ppermute | solution.py:183
  124.7 0.9 collective-permute-start.53
  125.7 1.9 %collective-permute-start.54 = (bf16[2,8,2048]{2,1,0:T(8,128)(2,1)S(1)}, bf16[2,8,2048]{2,1,0:T(8,128)(2,1)S(1)}, u32[]{:S(2)}, u32[]{:S(2)}) collective-permute-start(bf16[2,8,2048]{2,1,0:T(8,128)(2,1)S(1)} %get-tuple-element.41), channel_id=1, source_target_pairs={{0,24},{4,28},{8,16},{12,20},{16,8},{20,12},{24,0},{28,4},{1,25},{... | collective-permute-start | bytes 196616 | tf_op jit(solution)/shard_map/ppermute | solution.py:183
  129.0 1.8 %collective-permute-done.54 = bf16[2,8,2048]{2,1,0:T(8,128)(2,1)S(1)} collective-permute-done((bf16[2,8,2048]{2,1,0:T(8,128)(2,1)S(1)}, bf16[2,8,2048]{2,1,0:T(8,128)(2,1)S(1)}, u32[]{:S(2)}, u32[]{:S(2)}) %collective-permute-start.54) | collective-permute-done | bytes 65568 | tf_op jit(solution)/shard_map/ppermute | solution.py:183
  130.9 1.3 %collective-permute-done.55 = bf16[4,8,2048]{2,1,0:T(8,128)(2,1)S(1)} collective-permute-done((bf16[4,8,2048]{2,1,0:T(8,128)(2,1)S(1)}, bf16[4,8,2048]{2,1,0:T(8,128)(2,1)S(1)}, u32[]{:S(2)}, u32[]{:S(2)}) %collective-permute-start.55) | collective-permute-done | bytes 131104 | tf_op jit(solution)/shard_map/ppermute | solution.py:183
  (184 shorter events, 18.2 us)
Async XLA Ops:
  2.3 6.5 %collective-permute-start.9 = (bf16[8,4096]{1,0:T(8,128)(2,1)S(1)}, bf16[8,4096]{1,0:T(8,128)(2,1)S(1)}, u32[]{:S(2)}, u32[]{:S(2)}) collective-permute-start(bf16[8,4096]{1,0:T(8,128)(2,1)S(1)} %get-tuple-element.47), channel_id=1, source_target_pairs={{0,1},{1,0},{2,3},{3,2},{4,5},{5,4},{6,7},{7,6},{8,9},{9,8},{10,11... | collective-permute-start | bytes 196616 | tf_op jit(solution)/shard_map/ppermute | solution.py:183
  5.4 7.3 %collective-permute-start = (bf16[8,4096]{1,0:T(8,128)(2,1)S(1)}, bf16[8,4096]{1,0:T(8,128)(2,1)S(1)}, u32[]{:S(2)}, u32[]{:S(2)}) collective-permute-start(bf16[8,4096]{1,0:T(8,128)(2,1)S(1)} %get-tuple-element.49), channel_id=1, source_target_pairs={{0,2},{1,3},{2,0},{3,1},{4,6},{5,7},{6,4},{7,5},{8,10},{9,11},{10,... | collective-permute-start | bytes 196616 | tf_op jit(solution)/shard_map/ppermute | solution.py:183
  8.0 7.1 %collective-permute-start.1 = (bf16[8,4096]{1,0:T(8,128)(2,1)S(1)}, bf16[8,4096]{1,0:T(8,128)(2,1)S(1)}, u32[]{:S(2)}, u32[]{:S(2)}) collective-permute-start(bf16[8,4096]{1,0:T(8,128)(2,1)S(1)} %get-tuple-element.48), channel_id=1, source_target_pairs={{0,3},{1,2},{2,1},{3,0},{4,7},{5,6},{6,5},{7,4},{8,11},{9,10},{10,... | collective-permute-start | bytes 196616 | tf_op jit(solution)/shard_map/ppermute | solution.py:183
  8.9 6.4 %collective-permute-start.10 = (bf16[16,4096]{1,0:T(8,128)(2,1)S(1)}, bf16[16,4096]{1,0:T(8,128)(2,1)S(1)}, u32[]{:S(2)}, u32[]{:S(2)}) collective-permute-start(bf16[16,4096]{1,0:T(8,128)(2,1)S(1)} %pad_maximum_fusion.3), channel_id=1, source_target_pairs={{0,4},{4,0},{8,12},{12,8},{16,20},{20,16},{24,28},{28,24},{1,5},{5... | collective-permute-start | bytes 393224 | tf_op jit(solution)/shard_map/ppermute | solution.py:183
  9.0 7.0 %collective-permute-start.11 = (bf16[16,4096]{1,0:T(8,128)(2,1)S(1)}, bf16[16,4096]{1,0:T(8,128)(2,1)S(1)}, u32[]{:S(2)}, u32[]{:S(2)}) collective-permute-start(bf16[16,4096]{1,0:T(8,128)(2,1)S(1)} %pad_maximum_fusion.3), channel_id=1, source_target_pairs={{0,8},{4,12},{8,0},{12,4},{16,24},{20,28},{24,16},{28,20},{1,9},{5... | collective-permute-start | bytes 393224 | tf_op jit(solution)/shard_map/ppermute | solution.py:183
  10.7 11.0 %collective-permute-start.13 = (bf16[16,4096]{1,0:T(8,128)(2,1)S(1)}, bf16[16,4096]{1,0:T(8,128)(2,1)S(1)}, u32[]{:S(2)}, u32[]{:S(2)}) collective-permute-start(bf16[16,4096]{1,0:T(8,128)(2,1)S(1)} %pad_maximum_fusion.3), channel_id=1, source_target_pairs={{0,16},{4,20},{8,24},{12,28},{16,0},{20,4},{24,8},{28,12},{1,17},{... | collective-permute-start | bytes 393224 | tf_op jit(solution)/shard_map/ppermute | solution.py:183
  12.7 9.6 %collective-permute-start.15 = (bf16[16,4096]{1,0:T(8,128)(2,1)S(1)}, bf16[16,4096]{1,0:T(8,128)(2,1)S(1)}, u32[]{:S(2)}, u32[]{:S(2)}) collective-permute-start(bf16[16,4096]{1,0:T(8,128)(2,1)S(1)} %pad_maximum_fusion.3), channel_id=1, source_target_pairs={{0,24},{4,28},{8,16},{12,20},{16,8},{20,12},{24,0},{28,4},{1,25},{... | collective-permute-start | bytes 393224 | tf_op jit(solution)/shard_map/ppermute | solution.py:183
  15.2 2.2 %collective-permute-start.2 = (bf16[16,4096]{1,0:T(8,128)(2,1)S(1)}, bf16[16,4096]{1,0:T(8,128)(2,1)S(1)}, u32[]{:S(2)}, u32[]{:S(2)}) collective-permute-start(bf16[16,4096]{1,0:T(8,128)(2,1)S(1)} %constant_dynamic-update-slice_fusion), channel_id=1, source_target_pairs={{0,4},{4,0},{8,12},{12,8},{16,20},{20,16},{24,28},{28,24},{1,5},{5... | collective-permute-start | bytes 393224 | tf_op jit(solution)/shard_map/ppermute | solution.py:183
  15.3 6.4 %collective-permute-start.3 = (bf16[16,4096]{1,0:T(8,128)(2,1)S(1)}, bf16[16,4096]{1,0:T(8,128)(2,1)S(1)}, u32[]{:S(2)}, u32[]{:S(2)}) collective-permute-start(bf16[16,4096]{1,0:T(8,128)(2,1)S(1)} %constant_dynamic-update-slice_fusion), channel_id=1, source_target_pairs={{0,8},{4,12},{8,0},{12,4},{16,24},{20,28},{24,16},{28,20},{1,9},{5... | collective-permute-start | bytes 393224 | tf_op jit(solution)/shard_map/ppermute | solution.py:183
  15.9 8.8 %collective-permute-start.5 = (bf16[16,4096]{1,0:T(8,128)(2,1)S(1)}, bf16[16,4096]{1,0:T(8,128)(2,1)S(1)}, u32[]{:S(2)}, u32[]{:S(2)}) collective-permute-start(bf16[16,4096]{1,0:T(8,128)(2,1)S(1)} %constant_dynamic-update-slice_fusion), channel_id=1, source_target_pairs={{0,16},{4,20},{8,24},{12,28},{16,0},{20,4},{24,8},{28,12},{1,17},{... | collective-permute-start | bytes 393224 | tf_op jit(solution)/shard_map/ppermute | solution.py:183
  17.4 7.3 %collective-permute-start.7 = (bf16[16,4096]{1,0:T(8,128)(2,1)S(1)}, bf16[16,4096]{1,0:T(8,128)(2,1)S(1)}, u32[]{:S(2)}, u32[]{:S(2)}) collective-permute-start(bf16[16,4096]{1,0:T(8,128)(2,1)S(1)} %constant_dynamic-update-slice_fusion), channel_id=1, source_target_pairs={{0,24},{4,28},{8,16},{12,20},{16,8},{20,12},{24,0},{28,4},{1,25},{... | collective-permute-start | bytes 393224 | tf_op jit(solution)/shard_map/ppermute | solution.py:183
  21.7 3.5 %collective-permute-start.12 = (bf16[16,4096]{1,0:T(8,128)(2,1)S(1)}, bf16[16,4096]{1,0:T(8,128)(2,1)S(1)}, u32[]{:S(2)}, u32[]{:S(2)}) collective-permute-start(bf16[16,4096]{1,0:T(8,128)(2,1)S(1)} %collective-permute-done.11), channel_id=1, source_target_pairs={{0,4},{4,0},{8,12},{12,8},{16,20},{20,16},{24,28},{28,24},{1,5},{5... | collective-permute-start | bytes 393224 | tf_op jit(solution)/shard_map/ppermute | solution.py:183
  21.8 3.6 %collective-permute-start.4 = (bf16[16,4096]{1,0:T(8,128)(2,1)S(1)}, bf16[16,4096]{1,0:T(8,128)(2,1)S(1)}, u32[]{:S(2)}, u32[]{:S(2)}) collective-permute-start(bf16[16,4096]{1,0:T(8,128)(2,1)S(1)} %collective-permute-done.3), channel_id=1, source_target_pairs={{0,4},{4,0},{8,12},{12,8},{16,20},{20,16},{24,28},{28,24},{1,5},{5... | collective-permute-start | bytes 393224 | tf_op jit(solution)/shard_map/ppermute | solution.py:183
  22.3 3.0 %collective-permute-start.14 = (bf16[16,4096]{1,0:T(8,128)(2,1)S(1)}, bf16[16,4096]{1,0:T(8,128)(2,1)S(1)}, u32[]{:S(2)}, u32[]{:S(2)}) collective-permute-start(bf16[16,4096]{1,0:T(8,128)(2,1)S(1)} %collective-permute-done.13), channel_id=1, source_target_pairs={{0,4},{4,0},{8,12},{12,8},{16,20},{20,16},{24,28},{28,24},{1,5},{5... | collective-permute-start | bytes 393224 | tf_op jit(solution)/shard_map/ppermute | solution.py:183
  31.2 8.5 %collective-permute-start.17 = (f16[2,8,8,1024]{3,2,1,0:T(8,128)(2,1)S(1)}, f16[2,8,8,1024]{3,2,1,0:T(8,128)(2,1)S(1)}, u32[]{:S(2)}, u32[]{:S(2)}) collective-permute-start(f16[2,8,8,1024]{3,2,1,0:T(8,128)(2,1)S(1)} %fusion.19), channel_id=1, source_target_pairs={{0,1},{1,0},{2,3},{3,2},{4,5},{5,4},{6,7},{7,6},{8,9},{9,8},{10,11... | collective-permute-start | bytes 786440 | tf_op jit(solution)/shard_map/ppermute | solution.py:183
  37.4 8.9 %collective-permute-start.24 = (f16[8,8,1280]{2,1,0:T(8,128)(2,1)S(1)}, f16[8,8,1280]{2,1,0:T(8,128)(2,1)S(1)}, u32[]{:S(2)}, u32[]{:S(2)}) collective-permute-start(f16[8,8,1280]{2,1,0:T(8,128)(2,1)S(1)} %get-tuple-element.32), channel_id=1, source_target_pairs={{0,1},{1,0},{2,3},{3,2},{4,5},{5,4},{6,7},{7,6},{8,9},{9,8},{10,11... | collective-permute-start | bytes 491528 | tf_op jit(solution)/shard_map/ppermute | solution.py:183
  39.8 8.3 %collective-permute-start.18 = (f16[8,8,1024]{2,1,0:T(8,128)(2,1)S(1)}, f16[8,8,1024]{2,1,0:T(8,128)(2,1)S(1)}, u32[]{:S(2)}, u32[]{:S(2)}) collective-permute-start(f16[8,8,1024]{2,1,0:T(8,128)(2,1)S(1)} %fusion.41), channel_id=1, source_target_pairs={{0,2},{1,3},{2,0},{3,1},{4,6},{5,7},{6,4},{7,5},{8,10},{9,11},{10,... | collective-permute-start | bytes 393224 | tf_op jit(solution)/shard_map/ppermute | solution.py:183
  46.3 9.7 %collective-permute-start.25 = (f16[8,8,1280]{2,1,0:T(8,128)(2,1)S(1)}, f16[8,8,1280]{2,1,0:T(8,128)(2,1)S(1)}, u32[]{:S(2)}, u32[]{:S(2)}) collective-permute-start(f16[8,8,1280]{2,1,0:T(8,128)(2,1)S(1)} %fusion.14), channel_id=1, source_target_pairs={{0,2},{1,3},{2,0},{3,1},{4,6},{5,7},{6,4},{7,5},{8,10},{9,11},{10,... | collective-permute-start | bytes 491528 | tf_op jit(solution)/shard_map/ppermute | solution.py:183
  48.1 8.5 %collective-permute-start.23 = (f16[8,8,1280]{2,1,0:T(8,128)(2,1)S(1)}, f16[8,8,1280]{2,1,0:T(8,128)(2,1)S(1)}, u32[]{:S(2)}, u32[]{:S(2)}) collective-permute-start(f16[8,8,1280]{2,1,0:T(8,128)(2,1)S(1)} %get-tuple-element.19), channel_id=1, source_target_pairs={{0,1},{1,0},{2,3},{3,2},{4,5},{5,4},{6,7},{7,6},{8,9},{9,8},{10,11... | collective-permute-start | bytes 491528 | tf_op jit(solution)/shard_map/ppermute | solution.py:183
  48.2 10.9 %collective-permute-start.19 = (bf16[2,8,1024]{2,1,0:T(8,128)(2,1)S(1)}, bf16[2,8,1024]{2,1,0:T(8,128)(2,1)S(1)}, u32[]{:S(2)}, u32[]{:S(2)}) collective-permute-start(bf16[2,8,1024]{2,1,0:T(8,128)(2,1)S(1)} %get-tuple-element.57), channel_id=1, source_target_pairs={{0,8},{4,12},{8,0},{12,4},{16,24},{20,28},{24,16},{28,20},{1,9},{5... | collective-permute-start | bytes 98312 | tf_op jit(solution)/shard_map/ppermute | solution.py:183
  49.6 10.7 %collective-permute-start.20 = (bf16[2,8,1024]{2,1,0:T(8,128)(2,1)S(1)}, bf16[2,8,1024]{2,1,0:T(8,128)(2,1)S(1)}, u32[]{:S(2)}, u32[]{:S(2)}) collective-permute-start(bf16[2,8,1024]{2,1,0:T(8,128)(2,1)S(1)} %get-tuple-element.59), channel_id=1, source_target_pairs={{0,16},{4,20},{8,24},{12,28},{16,0},{20,4},{24,8},{28,12},{1,17},{... | collective-permute-start | bytes 98312 | tf_op jit(solution)/shard_map/ppermute | solution.py:183
  50.5 9.9 %collective-permute-start.21 = (bf16[2,8,1024]{2,1,0:T(8,128)(2,1)S(1)}, bf16[2,8,1024]{2,1,0:T(8,128)(2,1)S(1)}, u32[]{:S(2)}, u32[]{:S(2)}) collective-permute-start(bf16[2,8,1024]{2,1,0:T(8,128)(2,1)S(1)} %get-tuple-element.58), channel_id=1, source_target_pairs={{0,24},{4,28},{8,16},{12,20},{16,8},{20,12},{24,0},{28,4},{1,25},{... | collective-permute-start | bytes 98312 | tf_op jit(solution)/shard_map/ppermute | solution.py:183
  56.7 4.1 %collective-permute-start.26 = (bf16[2,8,1280]{2,1,0:T(8,128)(2,1)S(1)}, bf16[2,8,1280]{2,1,0:T(8,128)(2,1)S(1)}, u32[]{:S(2)}, u32[]{:S(2)}) collective-permute-start(bf16[2,8,1280]{2,1,0:T(8,128)(2,1)S(1)} %get-tuple-element.52), channel_id=1, source_target_pairs={{0,8},{4,12},{8,0},{12,4},{16,24},{20,28},{24,16},{28,20},{1,9},{5... | collective-permute-start | bytes 122888 | tf_op jit(solution)/shard_map/ppermute | solution.py:183
  58.2 4.2 %collective-permute-start.27 = (bf16[2,8,1280]{2,1,0:T(8,128)(2,1)S(1)}, bf16[2,8,1280]{2,1,0:T(8,128)(2,1)S(1)}, u32[]{:S(2)}, u32[]{:S(2)}) collective-permute-start(bf16[2,8,1280]{2,1,0:T(8,128)(2,1)S(1)} %get-tuple-element.54), channel_id=1, source_target_pairs={{0,16},{4,20},{8,24},{12,28},{16,0},{20,4},{24,8},{28,12},{1,17},{... | collective-permute-start | bytes 122888 | tf_op jit(solution)/shard_map/ppermute | solution.py:183
  59.1 4.9 %collective-permute-start.28 = (bf16[2,8,1280]{2,1,0:T(8,128)(2,1)S(1)}, bf16[2,8,1280]{2,1,0:T(8,128)(2,1)S(1)}, u32[]{:S(2)}, u32[]{:S(2)}) collective-permute-start(bf16[2,8,1280]{2,1,0:T(8,128)(2,1)S(1)} %get-tuple-element.53), channel_id=1, source_target_pairs={{0,24},{4,28},{8,16},{12,20},{16,8},{20,12},{24,0},{28,4},{1,25},{... | collective-permute-start | bytes 122888 | tf_op jit(solution)/shard_map/ppermute | solution.py:183
  60.4 3.8 %collective-permute-start.22 = (bf16[4,8,1024]{2,1,0:T(8,128)(2,1)S(1)}, bf16[4,8,1024]{2,1,0:T(8,128)(2,1)S(1)}, u32[]{:S(2)}, u32[]{:S(2)}) collective-permute-start(bf16[4,8,1024]{2,1,0:T(8,128)(2,1)S(1)} %pad_maximum_fusion.7), channel_id=1, source_target_pairs={{0,4},{4,0},{8,12},{12,8},{16,20},{20,16},{24,28},{28,24},{1,5},{5... | collective-permute-start | bytes 196616 | tf_op jit(solution)/shard_map/ppermute | solution.py:183
  71.1 4.7 %collective-permute-start.39 = (bf16[8,4096]{1,0:T(8,128)(2,1)S(1)}, bf16[8,4096]{1,0:T(8,128)(2,1)S(1)}, u32[]{:S(2)}, u32[]{:S(2)}) collective-permute-start(bf16[8,4096]{1,0:T(8,128)(2,1)S(1)} %get-tuple-element.43), channel_id=1, source_target_pairs={{0,1},{1,0},{2,3},{3,2},{4,5},{5,4},{6,7},{7,6},{8,9},{9,8},{10,11... | collective-permute-start | bytes 196616 | tf_op jit(solution)/shard_map/ppermute | solution.py:183
  72.6 7.2 %collective-permute-start.30 = (bf16[8,4096]{1,0:T(8,128)(2,1)S(1)}, bf16[8,4096]{1,0:T(8,128)(2,1)S(1)}, u32[]{:S(2)}, u32[]{:S(2)}) collective-permute-start(bf16[8,4096]{1,0:T(8,128)(2,1)S(1)} %get-tuple-element.45), channel_id=1, source_target_pairs={{0,2},{1,3},{2,0},{3,1},{4,6},{5,7},{6,4},{7,5},{8,10},{9,11},{10,... | collective-permute-start | bytes 196616 | tf_op jit(solution)/shard_map/ppermute | solution.py:183
  74.9 7.1 %collective-permute-start.31 = (bf16[8,4096]{1,0:T(8,128)(2,1)S(1)}, bf16[8,4096]{1,0:T(8,128)(2,1)S(1)}, u32[]{:S(2)}, u32[]{:S(2)}) collective-permute-start(bf16[8,4096]{1,0:T(8,128)(2,1)S(1)} %get-tuple-element.44), channel_id=1, source_target_pairs={{0,3},{1,2},{2,1},{3,0},{4,7},{5,6},{6,5},{7,4},{8,11},{9,10},{10,... | collective-permute-start | bytes 196616 | tf_op jit(solution)/shard_map/ppermute | solution.py:183
  75.8 6.4 %collective-permute-start.40 = (bf16[16,4096]{1,0:T(8,128)(2,1)S(1)}, bf16[16,4096]{1,0:T(8,128)(2,1)S(1)}, u32[]{:S(2)}, u32[]{:S(2)}) collective-permute-start(bf16[16,4096]{1,0:T(8,128)(2,1)S(1)} %pad_maximum_fusion.5), channel_id=1, source_target_pairs={{0,4},{4,0},{8,12},{12,8},{16,20},{20,16},{24,28},{28,24},{1,5},{5... | collective-permute-start | bytes 393224 | tf_op jit(solution)/shard_map/ppermute | solution.py:183
  76.0 9.3 %collective-permute-start.41 = (bf16[16,4096]{1,0:T(8,128)(2,1)S(1)}, bf16[16,4096]{1,0:T(8,128)(2,1)S(1)}, u32[]{:S(2)}, u32[]{:S(2)}) collective-permute-start(bf16[16,4096]{1,0:T(8,128)(2,1)S(1)} %pad_maximum_fusion.5), channel_id=1, source_target_pairs={{0,8},{4,12},{8,0},{12,4},{16,24},{20,28},{24,16},{28,20},{1,9},{5... | collective-permute-start | bytes 393224 | tf_op jit(solution)/shard_map/ppermute | solution.py:183
  79.9 9.8 %collective-permute-start.43 = (bf16[16,4096]{1,0:T(8,128)(2,1)S(1)}, bf16[16,4096]{1,0:T(8,128)(2,1)S(1)}, u32[]{:S(2)}, u32[]{:S(2)}) collective-permute-start(bf16[16,4096]{1,0:T(8,128)(2,1)S(1)} %pad_maximum_fusion.5), channel_id=1, source_target_pairs={{0,16},{4,20},{8,24},{12,28},{16,0},{20,4},{24,8},{28,12},{1,17},{... | collective-permute-start | bytes 393224 | tf_op jit(solution)/shard_map/ppermute | solution.py:183
  79.9 10.4 %collective-permute-start.45 = (bf16[16,4096]{1,0:T(8,128)(2,1)S(1)}, bf16[16,4096]{1,0:T(8,128)(2,1)S(1)}, u32[]{:S(2)}, u32[]{:S(2)}) collective-permute-start(bf16[16,4096]{1,0:T(8,128)(2,1)S(1)} %pad_maximum_fusion.5), channel_id=1, source_target_pairs={{0,24},{4,28},{8,16},{12,20},{16,8},{20,12},{24,0},{28,4},{1,25},{... | collective-permute-start | bytes 393224 | tf_op jit(solution)/shard_map/ppermute | solution.py:183
  82.1 3.4 %collective-permute-start.32 = (bf16[16,4096]{1,0:T(8,128)(2,1)S(1)}, bf16[16,4096]{1,0:T(8,128)(2,1)S(1)}, u32[]{:S(2)}, u32[]{:S(2)}) collective-permute-start(bf16[16,4096]{1,0:T(8,128)(2,1)S(1)} %constant_dynamic-update-slice_fusion.10), channel_id=1, source_target_pairs={{0,4},{4,0},{8,12},{12,8},{16,20},{20,16},{24,28},{28,24},{1,5},{5... | collective-permute-start | bytes 393224 | tf_op jit(solution)/shard_map/ppermute | solution.py:183
  82.2 7.5 %collective-permute-start.33 = (bf16[16,4096]{1,0:T(8,128)(2,1)S(1)}, bf16[16,4096]{1,0:T(8,128)(2,1)S(1)}, u32[]{:S(2)}, u32[]{:S(2)}) collective-permute-start(bf16[16,4096]{1,0:T(8,128)(2,1)S(1)} %constant_dynamic-update-slice_fusion.10), channel_id=1, source_target_pairs={{0,8},{4,12},{8,0},{12,4},{16,24},{20,28},{24,16},{28,20},{1,9},{5... | collective-permute-start | bytes 393224 | tf_op jit(solution)/shard_map/ppermute | solution.py:183
  85.4 8.5 %collective-permute-start.35 = (bf16[16,4096]{1,0:T(8,128)(2,1)S(1)}, bf16[16,4096]{1,0:T(8,128)(2,1)S(1)}, u32[]{:S(2)}, u32[]{:S(2)}) collective-permute-start(bf16[16,4096]{1,0:T(8,128)(2,1)S(1)} %constant_dynamic-update-slice_fusion.10), channel_id=1, source_target_pairs={{0,16},{4,20},{8,24},{12,28},{16,0},{20,4},{24,8},{28,12},{1,17},{... | collective-permute-start | bytes 393224 | tf_op jit(solution)/shard_map/ppermute | solution.py:183
  85.5 8.4 %collective-permute-start.37 = (bf16[16,4096]{1,0:T(8,128)(2,1)S(1)}, bf16[16,4096]{1,0:T(8,128)(2,1)S(1)}, u32[]{:S(2)}, u32[]{:S(2)}) collective-permute-start(bf16[16,4096]{1,0:T(8,128)(2,1)S(1)} %constant_dynamic-update-slice_fusion.10), channel_id=1, source_target_pairs={{0,24},{4,28},{8,16},{12,20},{16,8},{20,12},{24,0},{28,4},{1,25},{... | collective-permute-start | bytes 393224 | tf_op jit(solution)/shard_map/ppermute | solution.py:183
  89.7 4.7 %collective-permute-start.42 = (bf16[16,4096]{1,0:T(8,128)(2,1)S(1)}, bf16[16,4096]{1,0:T(8,128)(2,1)S(1)}, u32[]{:S(2)}, u32[]{:S(2)}) collective-permute-start(bf16[16,4096]{1,0:T(8,128)(2,1)S(1)} %collective-permute-done.41), channel_id=1, source_target_pairs={{0,4},{4,0},{8,12},{12,8},{16,20},{20,16},{24,28},{28,24},{1,5},{5... | collective-permute-start | bytes 393224 | tf_op jit(solution)/shard_map/ppermute | solution.py:183
  89.7 4.8 %collective-permute-start.34 = (bf16[16,4096]{1,0:T(8,128)(2,1)S(1)}, bf16[16,4096]{1,0:T(8,128)(2,1)S(1)}, u32[]{:S(2)}, u32[]{:S(2)}) collective-permute-start(bf16[16,4096]{1,0:T(8,128)(2,1)S(1)} %collective-permute-done.33), channel_id=1, source_target_pairs={{0,4},{4,0},{8,12},{12,8},{16,20},{20,16},{24,28},{28,24},{1,5},{5... | collective-permute-start | bytes 393224 | tf_op jit(solution)/shard_map/ppermute | solution.py:183
  90.3 4.2 %collective-permute-start.44 = (bf16[16,4096]{1,0:T(8,128)(2,1)S(1)}, bf16[16,4096]{1,0:T(8,128)(2,1)S(1)}, u32[]{:S(2)}, u32[]{:S(2)}) collective-permute-start(bf16[16,4096]{1,0:T(8,128)(2,1)S(1)} %collective-permute-done.43), channel_id=1, source_target_pairs={{0,4},{4,0},{8,12},{12,8},{16,20},{20,16},{24,28},{28,24},{1,5},{5... | collective-permute-start | bytes 393224 | tf_op jit(solution)/shard_map/ppermute | solution.py:183
  100.4 9.1 %collective-permute-start.47 = (f16[2,8,8,1024]{3,2,1,0:T(8,128)(2,1)S(1)}, f16[2,8,8,1024]{3,2,1,0:T(8,128)(2,1)S(1)}, u32[]{:S(2)}, u32[]{:S(2)}) collective-permute-start(f16[2,8,8,1024]{3,2,1,0:T(8,128)(2,1)S(1)} %fusion.20), channel_id=1, source_target_pairs={{0,1},{1,0},{2,3},{3,2},{4,5},{5,4},{6,7},{7,6},{8,9},{9,8},{10,11... | collective-permute-start | bytes 786440 | tf_op jit(solution)/shard_map/ppermute | solution.py:183
  105.5 6.1 %collective-permute-start.50 = (f16[8,8,1024]{2,1,0:T(8,128)(2,1)S(1)}, f16[8,8,1024]{2,1,0:T(8,128)(2,1)S(1)}, u32[]{:S(2)}, u32[]{:S(2)}) collective-permute-start(f16[8,8,1024]{2,1,0:T(8,128)(2,1)S(1)} %get-tuple-element.34), channel_id=1, source_target_pairs={{0,1},{1,0},{2,3},{3,2},{4,5},{5,4},{6,7},{7,6},{8,9},{9,8},{10,11... | collective-permute-start | bytes 393224 | tf_op jit(solution)/shard_map/ppermute | solution.py:183
  109.6 12.1 %collective-permute-start.48 = (f16[8,8,1024]{2,1,0:T(8,128)(2,1)S(1)}, f16[8,8,1024]{2,1,0:T(8,128)(2,1)S(1)}, u32[]{:S(2)}, u32[]{:S(2)}) collective-permute-start(f16[8,8,1024]{2,1,0:T(8,128)(2,1)S(1)} %fusion.42), channel_id=1, source_target_pairs={{0,2},{1,3},{2,0},{3,1},{4,6},{5,7},{6,4},{7,5},{8,10},{9,11},{10,... | collective-permute-start | bytes 393224 | tf_op jit(solution)/shard_map/ppermute | solution.py:183
  111.7 11.7 %collective-permute-start.51 = (f16[8,8,1024]{2,1,0:T(8,128)(2,1)S(1)}, f16[8,8,1024]{2,1,0:T(8,128)(2,1)S(1)}, u32[]{:S(2)}, u32[]{:S(2)}) collective-permute-start(f16[8,8,1024]{2,1,0:T(8,128)(2,1)S(1)} %fusion.28), channel_id=1, source_target_pairs={{0,2},{1,3},{2,0},{3,1},{4,6},{5,7},{6,4},{7,5},{8,10},{9,11},{10,... | collective-permute-start | bytes 393224 | tf_op jit(solution)/shard_map/ppermute | solution.py:183
  115.6 8.4 %collective-permute-start.49 = (f16[8,8,1024]{2,1,0:T(8,128)(2,1)S(1)}, f16[8,8,1024]{2,1,0:T(8,128)(2,1)S(1)}, u32[]{:S(2)}, u32[]{:S(2)}) collective-permute-start(f16[8,8,1024]{2,1,0:T(8,128)(2,1)S(1)} %get-tuple-element.24), channel_id=1, source_target_pairs={{0,1},{1,0},{2,3},{3,2},{4,5},{5,4},{6,7},{7,6},{8,9},{9,8},{10,11... | collective-permute-start | bytes 393224 | tf_op jit(solution)/shard_map/ppermute | solution.py:183
  124.0 4.3 %collective-permute-start.52 = (bf16[2,8,2048]{2,1,0:T(8,128)(2,1)S(1)}, bf16[2,8,2048]{2,1,0:T(8,128)(2,1)S(1)}, u32[]{:S(2)}, u32[]{:S(2)}) collective-permute-start(bf16[2,8,2048]{2,1,0:T(8,128)(2,1)S(1)} %get-tuple-element.39), channel_id=1, source_target_pairs={{0,8},{4,12},{8,0},{12,4},{16,24},{20,28},{24,16},{28,20},{1,9},{5... | collective-permute-start | bytes 196616 | tf_op jit(solution)/shard_map/ppermute | solution.py:183
  124.7 4.3 %collective-permute-start.53 = (bf16[2,8,2048]{2,1,0:T(8,128)(2,1)S(1)}, bf16[2,8,2048]{2,1,0:T(8,128)(2,1)S(1)}, u32[]{:S(2)}, u32[]{:S(2)}) collective-permute-start(bf16[2,8,2048]{2,1,0:T(8,128)(2,1)S(1)} %get-tuple-element.40), channel_id=1, source_target_pairs={{0,16},{4,20},{8,24},{12,28},{16,0},{20,4},{24,8},{28,12},{1,17},{... | collective-permute-start | bytes 196616 | tf_op jit(solution)/shard_map/ppermute | solution.py:183
  125.7 5.2 %collective-permute-start.54 = (bf16[2,8,2048]{2,1,0:T(8,128)(2,1)S(1)}, bf16[2,8,2048]{2,1,0:T(8,128)(2,1)S(1)}, u32[]{:S(2)}, u32[]{:S(2)}) collective-permute-start(bf16[2,8,2048]{2,1,0:T(8,128)(2,1)S(1)} %get-tuple-element.41), channel_id=1, source_target_pairs={{0,24},{4,28},{8,16},{12,20},{16,8},{20,12},{24,0},{28,4},{1,25},{... | collective-permute-start | bytes 196616 | tf_op jit(solution)/shard_map/ppermute | solution.py:183
  (9 other events, 40.7 us)
